TPU v7x, 32 devices: a whole 2x2x4 slice. The times are simulated.
32 devices in a mesh: lat: 4 (over x, core), lon: 8 (over z, y).
Axes of the slice: x: 2, y: 2, z: 4, core: 2. Of those that a mesh axis runs over, the one named last changes fastest.
Arguments:
- inputs_below: bfloat16 [64, 32, 1024], P(None, 'lat', 'lon'), may hold values from -6 to 6
- hidden_prev: bfloat16 [64, 32, 1024], P(None, 'lat', 'lon'), may hold values from -0.8984375 to 0.8984375
- cell_prev: float32 [64, 32, 1024], P(None, 'lat', 'lon'), may hold values from -5 to 5
- kernel_weights: bfloat16 [9, 256, 128], replicated, may hold values from -0.1875 to 0.1875
- gate_bias: float32 [256], replicated, may hold values from -4 to 4
- readout: float32 [64], replicated, may hold values from -0.75 to 0.75
- target_field: float32 [32, 1024], P('lat', 'lon'), may hold values from -6 to 6
- land_mask: int32 [32, 1024], P('lat', 'lon'), may hold values 0 or 1
- fire_mask: int32 [32, 1024], P('lat', 'lon'), may hold values 0 or 1
- hidden_grad: bfloat16 [64, 32, 1024], P(None, 'lat', 'lon'), may hold values from -10 to 10
Outputs:
- hidden_next: bfloat16 [64, 32, 1024], P(None, 'lat', 'lon')
- cell_next: float32 [64, 32, 1024], P(None, 'lat', 'lon')
- grad_inputs: bfloat16 [64, 32, 1024], P(None, 'lat', 'lon')
- grad_hidden: bfloat16 [64, 32, 1024], P(None, 'lat', 'lon')
- grad_cell: float32 [64, 32, 1024], P(None, 'lat', 'lon')
- grad_kernel: float32 [9, 256, 128], replicated
- grad_bias: float32 [256], replicated
Inputs may be any that keep to these rules, and one draw needn't show every extreme that they name: `land_mask`: 1 marks land cells, 0 sea cells. `fire_mask`: 1 marks cells where fire danger is observed.
All inputs are finite; a program needn't handle non-finite values. No bound on the sum of `land_mask` or of `fire_mask` on one device may be relied on, other than what follows from the above.
Results may differ from a plain program's by a relative error of at most 0.0049.
Values may be sent and summed in bfloat16 or wider, within the bound.
No kernel may reach another device: no remote copies, remote signals or barrier semaphores. Data moves between devices by JAX's collectives and lax.ppermute only.
A program may use at most 64 MiB of HBM per device.

v0:
```python
import functools
import math

import jax
import jax.numpy as jnp
from jax import lax
from jax.experimental import pallas as pl
from jax.experimental.pallas import tpu as pltpu
from jax.sharding import Mesh, PartitionSpec as P

F32 = jnp.float32
BF16 = jnp.bfloat16
AXES = ("band", "core", "reach", "near")
BIAS_ROWS = 16
LAST = 16
VMEM = pl.BlockSpec(memory_space=pltpu.VMEM)
HBM = pl.BlockSpec(memory_space=pltpu.HBM)
ACROSS = (((1,), (1,)), ((), ()))


def sds(shape, dtype):
    return jax.ShapeDtypeStruct(shape, dtype)


def call(
    kernel,
    out_shape,
    scratch=(),
    remote=0,
    leaving=0,
    aliases=None,
    flops=0,
    moved=0,
    transcendentals=0,
):
    several = isinstance(out_shape, tuple)
    shapes = out_shape if several else (out_shape,)
    out_specs = tuple([HBM] * leaving + [VMEM] * (len(shapes) - leaving))

    def run(*args):
        near = len(args) - remote
        far = [pltpu.with_memory_space_constraint(arg, pltpu.HBM) for arg in args[near:]]
        return pl.pallas_call(
            kernel,
            out_shape=out_shape,
            in_specs=[VMEM] * near + [HBM] * remote,
            out_specs=out_specs if several else out_specs[0],
            input_output_aliases=aliases or {},
            scratch_shapes=list(scratch),
            cost_estimate=pl.CostEstimate(
                flops=flops, bytes_accessed=moved, transcendentals=transcendentals
            ),
            compiler_params=pltpu.CompilerParams(vmem_limit_bytes=24 * 1024 * 1024),
        )(*args[:near], *far)

    return run


class Layout:
    def __init__(self, lat_count, lon_count, kernel_rows):
        self.lat, self.lon = lat_count, lon_count
        self.half = lon_count // 2
        self.plane = lat_count
        whole = [("lon", 1 << k) for k in range(1, lon_count.bit_length() - 1)]
        self.orders = ([("lat", 1)] + whole, [("lat", 1)] + whole[::-1])
        step = 16 * self.plane
        self.rows = -(-kernel_rows // step) * step
        self.half_rows = self.rows // 2
        self.chunk = self.half_rows // self.plane

    def position(self):
        lat = 2 * lax.axis_index("band") + lax.axis_index("core")
        return lat, 2 * lax.axis_index("reach") + lax.axis_index("near")

    def rank(self, phase):
        lat, lon = self.position()

        def digit(order):
            axis, bit = order[phase]
            return ((lat if axis == "lat" else lon) // bit) % 2

        return jnp.where(lat % 2 == 0, digit(self.orders[0]), digit(self.orders[1]))

    def pairs(self, partner):
        result = []
        for lat in range(self.lat):
            for lon in range(self.lon):
                there = partner(lat, lon)
                result.append((lat * self.lon + lon, there[0] * self.lon + there[1]))
        return result

    def phase_pairs(self, phase):
        def partner(lat, lon):
            axis, bit = self.orders[lat % 2][phase]
            return (lat ^ bit, lon) if axis == "lat" else (lat, lon ^ bit)

        return self.pairs(partner)

    def plane_rank(self):
        return 2 * lax.axis_index("band") + lax.axis_index("near")

    def plane_pairs(self, step):
        def partner(lat, lon):
            there = (lat // 2 * 2 + lon % 2) ^ step
            return there // 2 * 2 + lat % 2, lon // 2 * 2 + there % 2

        return self.pairs(partner)

    def inner_rows(self, lat, lon):
        return lat ^ 1, lon

    def outer_rows(self, lat, lon):
        there = lat + 1 if lat % 2 else lat - 1
        if 0 <= there < self.lat:
            return there, lon
        return lat, (lon + self.half) % self.lon

    def inner_columns(self, lat, lon):
        return lat, lon ^ 1

    def outer_columns(self, lat, lon):
        return lat, (lon + (1 if lon % 2 else -1)) % self.lon


def permuted(value, pairs):
    return lax.ppermute(value, AXES, pairs)


def lanes(shape):
    return lax.broadcasted_iota(jnp.int32, shape, len(shape) - 1)


def rolled(value, shift):
    shift %= value.shape[1]
    return pltpu.roll(value, shift, 1) if shift else value


def edge_columns(row, position, columns):
    lane = lanes(row.shape)
    columns = jnp.where(lane == position, rolled(row, position), columns)
    return jnp.where(lane == LAST + position, rolled(row, LAST + position + 1), columns)


def pick(flag, yes, no):
    return jnp.where(flag, yes, no)


def is_odd(axis):
    return lax.axis_index(axis) % 2 == 1


def row_sends(first, last, inner_out, outer_out):
    odd = is_odd("core")
    inner_out[...] = pick(odd, first, last).astype(BF16)
    outer_out[...] = pick(odd, last, first).astype(BF16)


def row_halo(inner, outer):
    odd = is_odd("core")
    inner, outer = inner[...].astype(F32), outer[...].astype(F32)
    return pick(odd, inner, outer), pick(odd, outer, inner)


def column_halo(inner, outer):
    odd = is_odd("near")
    inner, outer = inner[...].astype(F32), outer[...].astype(F32)
    return pick(odd, inner, outer), pick(odd, outer, inner)


def widened(row_count, rows, row_blocks, column_blocks, emit):
    north, south = row_halo(*row_blocks)
    west, east = column_halo(*column_blocks)
    width = west.shape[1]
    lane = lanes(west.shape)
    for position in range(row_count + 2):
        if position == 0:
            row = north
        elif position == row_count + 1:
            row = south
        else:
            row = rows(position - 1)
        left = rolled(west, -LAST - position)
        right = rolled(east, width - 1 - position)
        emit(
            position,
            jnp.where(lane == 0, left, rolled(row, 1)),
            row,
            jnp.where(lane == width - 1, right, rolled(row, -1)),
        )


def pack_kernel(below, hidden, inner_out, outer_out, wide_out, below_here, hidden_here, arrived):
    first = pltpu.make_async_copy(below, below_here, arrived.at[0])
    second = pltpu.make_async_copy(hidden, hidden_here, arrived.at[1])
    first.start()
    second.start()
    channels, row_count, width = below.shape
    size = channels * row_count
    first.wait()
    wide_out[0:size, :] = below_here[...].astype(F32).reshape(size, width)
    second.wait()
    wide_out[size : 2 * size, :] = hidden_here[...].astype(F32).reshape(size, width)
    edges = [
        wide_out[pl.ds(index, 2 * channels, stride=row_count), :] for index in (0, row_count - 1)
    ]
    row_sends(edges[0], edges[1], inner_out, outer_out)


def down_rows(values, width):
    count = values.shape[0]
    return jnp.broadcast_to(values[None, :], (width, count)).T


def prepare_kernel(
    wide,
    cell_hbm,
    weights_hbm,
    hidden_grad_hbm,
    target_hbm,
    land_hbm,
    fire_hbm,
    gate_bias_hbm,
    readout_hbm,
    rows_out,
    columns_out,
    cell_out,
    weights_out,
    hidden_grad_out,
    target_out,
    land_out,
    fire_out,
    bias_wide_out,
    readout_wide_out,
    hidden_grad_here,
    gate_bias_here,
    readout_here,
    arrived,
):
    copies = [
        pltpu.make_async_copy(source, target, arrived.at[index])
        for index, (source, target) in enumerate(
            (
                (cell_hbm, cell_out),
                (weights_hbm, weights_out),
                (hidden_grad_hbm, hidden_grad_here),
                (target_hbm, target_out),
                (land_hbm, land_out),
                (fire_hbm, fire_out),
                (gate_bias_hbm, gate_bias_here),
                (readout_hbm, readout_here),
            )
        )
    ]
    for copy in copies:
        copy.start()
    row_count, channels, width = rows_out.shape
    columns = jnp.zeros((channels, width), F32)
    for index in range(row_count):
        row = wide[pl.ds(index, channels, stride=row_count), :]
        rows_out[index] = row.astype(BF16)
        columns = edge_columns(row, index + 1, columns)
    columns_out[...] = columns
    for copy in copies:
        copy.wait()
    hidden_grad_out[...] = hidden_grad_here[...].astype(F32).reshape(hidden_grad_out.shape)
    bias_wide_out[...] = down_rows(gate_bias_here[...], width)
    readout_wide_out[...] = down_rows(readout_here[...], width)


def columns_kernel(row_count, columns, inner, outer, out):
    north, south = row_halo(inner, outer)
    value = edge_columns(north, 0, columns[...])
    out[...] = edge_columns(south, row_count + 1, value).astype(BF16)


def pre_columns_kernel(row_count, pre, inner, outer, out):
    width = out.shape[1]
    north, south = row_halo(inner, outer)
    value = edge_columns(north, 0, jnp.zeros(north.shape, F32))
    for index in range(row_count):
        row = pre[:, pl.ds(index * width, width)].astype(F32)
        value = edge_columns(row, index + 1, value)
    out[...] = edge_columns(south, row_count + 1, value).astype(BF16)


def encode(bias):
    high = bias.astype(BF16).astype(F32)
    return jnp.concatenate([high, bias - high], axis=0)


def decode(block):
    return block[0:8] + block[8:16]


def split_sum(place, phase, bias, sums, rows, send_out, keep_out):
    half = rows // 2
    rank = place.rank(phase)
    send_out[0:BIAS_ROWS, :] = encode(bias).astype(BF16)
    away = pl.ds(pl.multiple_of((1 - rank) * half, 8), half)
    send_out[BIAS_ROWS:, :] = sums[away, :].astype(BF16)
    keep_out[...] = sums[pl.ds(pl.multiple_of(rank * half, 8), half), :]


def gates_kernel(
    place,
    rows_in,
    inner_row,
    outer_row,
    inner_column,
    outer_column,
    cell_prev,
    weights,
    hidden_grad,
    target,
    land,
    fire,
    bias_wide,
    readout_wide,
    hidden_hbm,
    cell_hbm,
    grad_cell_hbm,
    pre_out,
    inner_out,
    outer_out,
    send_out,
    keep_out,
    bias_out,
    shifted,
    hidden_wide,
    hidden_low,
    cell_out,
    grad_cell_out,
    sums,
    left,
):
    row_count, channels, width = rows_in.shape
    gate_count = weights.shape[1]
    hid = gate_count // 4

    def emit(position, left, row, right):
        at = pl.ds(position * width, width)
        shifted[0:channels, at] = left.astype(BF16)
        shifted[channels : 2 * channels, at] = row.astype(BF16)
        shifted[2 * channels : 3 * channels, at] = right.astype(BF16)

    widened(
        row_count,
        lambda index: rows_in[index].astype(F32),
        (inner_row, outer_row),
        (inner_column, outer_column),
        emit,
    )

    taps = [
        jnp.concatenate([weights[3 * a], weights[3 * a + 1], weights[3 * a + 2]], axis=1)
        for a in range(3)
    ]
    bias_total = jnp.zeros((gate_count, width), F32)
    edges = []
    readout = readout_wide[...]
    pair = 2 if row_count % 2 == 0 else 1
    for base in range(0, row_count, pair):
        preact = jnp.zeros((gate_count, pair * width), F32)
        for a in range(3):
            preact += jnp.dot(
                taps[a],
                shifted[:, pl.ds((base + a) * width, pair * width)],
                preferred_element_type=F32,
            )
        for offset in range(pair):
            index = base + offset
            strided = pl.ds(index, hid, stride=row_count)
            part = preact[:, offset * width : (offset + 1) * width] + bias_wide[...]
            input_gate = 0.5 + 0.5 * jnp.tanh(0.5 * part[0:hid])
            forget_gate = 0.5 + 0.5 * jnp.tanh(0.5 * part[hid : 2 * hid])
            output_gate = 0.5 + 0.5 * jnp.tanh(0.5 * part[2 * hid : 3 * hid])
            candidate = jnp.tanh(part[3 * hid : 4 * hid])
            cell_before = cell_prev[strided, :]
            land_row = land[index : index + 1, :].astype(F32)
            fire_row = fire[index : index + 1, :].astype(F32)
            cell_next = land_row * (forget_gate * cell_before + input_gate * candidate)
            squashed = jnp.tanh(cell_next)
            hidden_next = (output_gate * squashed).astype(BF16).astype(F32)
            predicted = jnp.sum(readout * hidden_next, axis=0, keepdims=True)
            miss = 2.0 * (fire_row * (predicted - target[index : index + 1, :]))
            total_grad = hidden_grad[strided, :] + miss * readout
            cell_grad = land_row * total_grad * output_gate * (1.0 - squashed * squashed)
            cell_out[strided, :] = cell_next
            hidden_wide[strided, :] = hidden_next
            grad_cell_out[strided, :] = cell_grad * forget_gate
            pre_grad = jnp.concatenate(
                [
                    cell_grad * candidate * input_gate * (1.0 - input_gate),
                    cell_grad * cell_before * forget_gate * (1.0 - forget_gate),
                    total_grad * squashed * output_gate * (1.0 - output_gate),
                    cell_grad * input_gate * (1.0 - candidate * candidate),
                ],
                axis=0,
            )
            bias_total += pre_grad
            pre_out[:, pl.ds(index * width, width)] = pre_grad.astype(BF16)
            if index in (0, row_count - 1):
                edges.append(pre_grad)
    hidden_low[...] = hidden_wide[...].reshape(hidden_low.shape).astype(BF16)
    leaving = [
        pltpu.make_async_copy(source, target, left.at[index])
        for index, (source, target) in enumerate(
            ((hidden_low, hidden_hbm), (cell_out, cell_hbm), (grad_cell_out, grad_cell_hbm))
        )
    ]
    for copy in leaving:
        copy.start()
    row_sends(edges[0], edges[-1], inner_out, outer_out)

    for a in range(3):
        product = lax.dot_general(
            pre_out[...],
            shifted[:, pl.ds(a * width, row_count * width)],
            ACROSS,
            preferred_element_type=F32,
        )
        for b in range(3):
            at = (3 * a + b) * gate_count
            sums[at : at + gate_count, :] = product[:, b * channels : (b + 1) * channels]
    used = 9 * gate_count
    if place.rows > used:
        sums[used:, :] = jnp.zeros((place.rows - used, channels), F32)

    ones = jnp.ones((8, width), BF16)
    high = bias_total.astype(BF16)
    low = (bias_total - high.astype(F32)).astype(BF16)
    flat = lax.dot_general(ones, high, ACROSS, preferred_element_type=F32)
    flat += lax.dot_general(ones, low, ACROSS, preferred_element_type=F32)
    odd = lax.broadcasted_iota(jnp.int32, (8, channels), 0) % 2 == 1
    bias_rows = jnp.where(odd, flat[:, channels : 2 * channels], flat[:, 0:channels])
    bias_out[...] = bias_rows
    split_sum(place, 0, bias_rows, sums, place.rows, send_out, keep_out)
    for copy in leaving:
        copy.wait()


def pair_kernel(place, keep, bias, received, *outs):
    sends, keep_out, bias_out, scratch = outs[:-3], outs[-3], outs[-2], outs[-1]
    chunk = place.chunk
    rank = place.plane_rank()
    scratch[...] = keep[...] + received[BIAS_ROWS:, :].astype(F32)
    bias_total = bias[...] + decode(received[0:BIAS_ROWS, :].astype(F32))
    block = encode(bias_total).astype(BF16)
    for step, send in enumerate(sends, 1):
        send[0:BIAS_ROWS, :] = block
        at = pl.ds(pl.multiple_of((rank ^ step) * chunk, 8), chunk)
        send[BIAS_ROWS:, :] = scratch[at, :].astype(BF16)
    keep_out[...] = scratch[pl.ds(pl.multiple_of(rank * chunk, 8), chunk), :]
    bias_out[...] = bias_total


def plane_kernel(keep, bias, *refs):
    received, out = refs[:-2], refs[-1]
    total, bias_total = keep[...], bias[...]
    for ref in received:
        total += ref[BIAS_ROWS:, :].astype(F32)
        bias_total += decode(ref[0:BIAS_ROWS, :].astype(F32))
    out[0:BIAS_ROWS, :] = encode(bias_total).astype(BF16)
    out[BIAS_ROWS:, :] = total.astype(BF16)


def join_kernel(place, *refs):
    blocks, out = refs[:-2], refs[-1]
    rank = place.plane_rank()
    for step, block in enumerate(blocks):
        out[rank ^ step] = block[...]


def add_kernel(scale, own, received, out, done_out):
    here, there = own[...].astype(F32), received[...].astype(F32)
    bias = (decode(here[0:BIAS_ROWS]) + decode(there[0:BIAS_ROWS])) * scale
    out[0:BIAS_ROWS, :] = encode(bias).astype(BF16)
    out[BIAS_ROWS:, :] = ((here[BIAS_ROWS:] + there[BIAS_ROWS:]) * scale).astype(BF16)
    done_out[...] = jnp.zeros(done_out.shape, F32)


def unpack(blocks, wide):
    chunk = blocks.shape[1] - BIAS_ROWS
    for index in range(blocks.shape[0]):
        wide[index * chunk : (index + 1) * chunk, :] = blocks[index, BIAS_ROWS:, :].astype(F32)


def own_half_kernel(place, own, out, wide, left):
    unpack(own, wide)
    at = pl.ds(pl.multiple_of(place.rank(0) * place.half_rows, 8), place.half_rows)
    copy = pltpu.make_async_copy(wide, out.at[at, :], left.at[0])
    copy.start()
    copy.wait()


def other_half_kernel(place, own, received, out_before, out, bias_out, wide, bias_here, left):
    del out_before
    rank = place.rank(0)
    here, there = own[0, 0:BIAS_ROWS, :].astype(F32), received[0, 0:BIAS_ROWS, :].astype(F32)
    bias = decode(pick(rank == 1, there, here))
    width = bias.shape[1]
    for index in range(bias_here.shape[0] // width):
        bias_here[pl.ds(index * width, width)] = bias[index]
    bias_copy = pltpu.make_async_copy(bias_here, bias_out, left.at[1])
    bias_copy.start()
    unpack(received, wide)
    at = pl.ds(pl.multiple_of((1 - rank) * place.half_rows, 8), place.half_rows)
    copy = pltpu.make_async_copy(wide, out.at[at, :], left.at[0])
    copy.start()
    bias_copy.wait()
    copy.wait()


def field_kernel(
    place,
    pre,
    inner_row,
    outer_row,
    inner_column,
    outer_column,
    weights,
    after,
    inputs_out,
    hidden_out,
    done_out,
    shifted,
    turned,
    wide,
):
    del after
    gate_count = pre.shape[0]
    channels = weights.shape[2]
    done_out[...] = jnp.zeros(done_out.shape, F32)
    hid, row_count, width = hidden_out.shape

    def emit(position, left, row, right):
        at = pl.ds(position * width, width)
        shifted[0:gate_count, at] = right.astype(BF16)
        shifted[gate_count : 2 * gate_count, at] = row.astype(BF16)
        shifted[2 * gate_count : 3 * gate_count, at] = left.astype(BF16)

    widened(
        row_count,
        lambda index: pre[:, pl.ds(index * width, width)].astype(F32),
        (inner_row, outer_row),
        (inner_column, outer_column),
        emit,
    )
    for a in range(3):
        for b in range(3):
            turned[a, :, b * gate_count : (b + 1) * gate_count] = weights[3 * a + b].T
    lat = place.position()[0]
    top = turned[jnp.where(lat == 0, 0, 2)]
    bottom = turned[jnp.where(lat == place.lat - 1, 2, 0)]

    def product(matrix, position, count):
        return jnp.dot(
            matrix, shifted[:, pl.ds(position * width, count * width)], preferred_element_type=F32
        )

    pair = 2 if row_count % 2 == 0 else 1
    for base in range(0, row_count, pair):
        total = product(turned[1], base + 1, pair)
        if base == 0:
            above = product(top, 0, 1)
            if pair == 2:
                above = jnp.concatenate([above, product(turned[2], 1, 1)], axis=1)
        else:
            above = product(turned[2], base, pair)
        if base + pair == row_count:
            below = product(bottom, row_count + 1, 1)
            if pair == 2:
                below = jnp.concatenate([product(turned[0], row_count, 1), below], axis=1)
        else:
            below = product(turned[0], base + 2, pair)
        total = total + above + below
        for offset in range(pair):
            value = total[:, offset * width : (offset + 1) * width]
            wide[pl.ds(base + offset, channels, stride=row_count), :] = value
    size = (channels - hid) * row_count
    inputs_out[...] = wide[0:size, :].reshape(inputs_out.shape).astype(BF16)
    hidden_out[...] = wide[size:, :].reshape(hidden_out.shape).astype(BF16)


def body(
    place,
    inputs_below,
    hidden_prev,
    cell_prev,
    kernel_weights,
    gate_bias,
    readout,
    target_field,
    land_mask,
    fire_mask,
    hidden_grad,
):
    hid, row_count, width = hidden_prev.shape
    gate_count, channels = kernel_weights.shape[1:]
    cells = row_count * width
    halo_cells = (row_count + 2) * width
    scaling = 1.0 / math.sqrt(cells * place.lat * place.lon)
    bind = functools.partial
    inner_rows, outer_rows = place.pairs(place.inner_rows), place.pairs(place.outer_rows)
    inner_columns = place.pairs(place.inner_columns)
    outer_columns = place.pairs(place.outer_columns)
    flat = sds((hid * row_count, width), F32)

    inner, outer, wide = call(
        pack_kernel,
        (
            sds((channels, width), BF16),
            sds((channels, width), BF16),
            sds((channels * row_count, width), F32),
        ),
        [
            pltpu.VMEM(inputs_below.shape, BF16),
            pltpu.VMEM(hidden_prev.shape, BF16),
            pltpu.SemaphoreType.DMA((2,)),
        ],
        remote=2,
        moved=4 * channels * cells,
    )(inputs_below, hidden_prev)
    inner, outer = permuted(inner, inner_rows), permuted(outer, outer_rows)
    (
        rows,
        columns,
        cell_here,
        weights_here,
        hidden_grad_here,
        target_here,
        land_here,
        fire_here,
        bias_wide,
        readout_wide,
    ) = call(
        prepare_kernel,
        (
            sds((row_count, channels, width), BF16),
            sds((channels, width), F32),
            flat,
            sds(kernel_weights.shape, BF16),
            flat,
            sds(target_field.shape, F32),
            sds(land_mask.shape, jnp.int32),
            sds(fire_mask.shape, jnp.int32),
            sds((gate_count, width), F32),
            sds((hid, width), F32),
        ),
        [
            pltpu.VMEM(hidden_grad.shape, BF16),
            pltpu.VMEM(gate_bias.shape, F32),
            pltpu.VMEM(readout.shape, F32),
            pltpu.SemaphoreType.DMA((8,)),
        ],
        remote=8,
        moved=6_000_000,
    )(
        wide,
        cell_prev.reshape(hid * row_count, width),
        kernel_weights,
        hidden_grad,
        target_field,
        land_mask,
        fire_mask,
        gate_bias,
        readout,
    )
    columns = call(bind(columns_kernel, row_count), sds((channels, width), BF16))(
        columns, inner, outer
    )

    (
        hidden_next,
        cell_next,
        grad_cell,
        pre,
        pre_inner,
        pre_outer,
        send,
        keep,
        bias,
    ) = call(
        bind(gates_kernel, place),
        (
            sds((hid, row_count, width), BF16),
            flat,
            flat,
            sds((gate_count, cells), BF16),
            sds((gate_count, width), BF16),
            sds((gate_count, width), BF16),
            sds((BIAS_ROWS + place.half_rows, channels), BF16),
            sds((place.half_rows, channels), F32),
            sds((8, channels), F32),
        ),
        [
            pltpu.VMEM((3 * channels, halo_cells), BF16),
            pltpu.VMEM((hid * row_count, width), F32),
            pltpu.VMEM((hid, row_count, width), BF16),
            pltpu.VMEM((hid * row_count, width), F32),
            pltpu.VMEM((hid * row_count, width), F32),
            pltpu.VMEM((place.rows, channels), F32),
            pltpu.SemaphoreType.DMA((3,)),
        ],
        leaving=3,
        flops=4 * 9 * gate_count * channels * cells,
        moved=4_000_000,
        transcendentals=5 * hid * cells,
    )(
        rows,
        inner,
        outer,
        permuted(columns, inner_columns),
        permuted(columns, outer_columns),
        cell_here,
        weights_here,
        hidden_grad_here,
        target_here,
        land_here,
        fire_here,
        bias_wide,
        readout_wide,
    )

    pre_inner, pre_outer = permuted(pre_inner, inner_rows), permuted(pre_outer, outer_rows)
    pre_columns = call(bind(pre_columns_kernel, row_count), sds((gate_count, width), BF16))(
        pre, pre_inner, pre_outer
    )
    block = sds((BIAS_ROWS + place.chunk, channels), BF16)
    token = sds((8, width), F32)
    steps = range(1, place.plane)
    *sends, keep, bias = call(
        bind(pair_kernel, place),
        (*[block for _ in steps], sds((place.chunk, channels), F32), sds((8, channels), F32)),
        [pltpu.VMEM((place.half_rows, channels), F32)],
    )(keep, bias, permuted(send, place.phase_pairs(0)))
    received = [permuted(send, place.plane_pairs(step)) for step, send in zip(steps, sends)]
    part = call(plane_kernel, block)(keep, bias, *received, pre_columns)
    pre_inner_columns = permuted(pre_columns, inner_columns)
    pre_outer_columns = permuted(pre_columns, outer_columns)
    phases = len(place.orders[0])
    for phase in range(1, phases):
        is_last = phase == phases - 1
        part, summed = call(bind(add_kernel, scaling if is_last else 1.0), (block, token))(
            part,
            permuted(part, place.phase_pairs(phase)),
        )
    grad_inputs, grad_hidden, field_done = call(
        bind(field_kernel, place),
        (
            sds((channels - hid, row_count, width), BF16),
            sds((hid, row_count, width), BF16),
            sds((8, width), F32),
        ),
        [
            pltpu.VMEM((3 * gate_count, halo_cells), BF16),
            pltpu.VMEM((3, channels, 3 * gate_count), BF16),
            pltpu.VMEM((channels * row_count, width), F32),
        ],
        flops=2 * 9 * gate_count * channels * cells,
        moved=2_000_000,
    )(
        pre,
        pre_inner,
        pre_outer,
        pre_inner_columns,
        pre_outer_columns,
        weights_here,
        summed,
    )
    received = [permuted(part, place.plane_pairs(step)) for step in steps]
    gathered = call(bind(join_kernel, place), sds((place.plane, *block.shape), BF16))(
        part, *received, field_done
    )
    received = permuted(gathered, place.phase_pairs(0))
    half = [pltpu.VMEM((place.half_rows, channels), F32)]
    grad_kernel = call(
        bind(own_half_kernel, place),
        (sds((place.rows, channels), F32),),
        half + [pltpu.SemaphoreType.DMA((1,))],
        leaving=1,
        moved=6 * place.half_rows * channels,
    )(gathered)[0]
    grad_kernel, grad_bias = call(
        bind(other_half_kernel, place),
        (sds((place.rows, channels), F32), sds((gate_count,), F32)),
        half + [pltpu.VMEM((gate_count,), F32), pltpu.SemaphoreType.DMA((2,))],
        remote=1,
        leaving=2,
        aliases={2: 0},
        moved=6 * place.half_rows * channels,
    )(gathered, received, grad_kernel)
    shape = hidden_prev.shape
    return (
        hidden_next,
        cell_next.reshape(shape),
        grad_inputs,
        grad_hidden,
        grad_cell.reshape(shape),
        grad_kernel[: 9 * gate_count].reshape(kernel_weights.shape),
        grad_bias,
    )


def solution(mesh):
    lat_count, lon_count = mesh.shape["lat"], mesh.shape["lon"]
    split = Mesh(mesh.devices.reshape(lat_count // 2, 2, lon_count // 2, 2), AXES)
    field = P(None, ("band", "core"), ("reach", "near"))
    flat = P(("band", "core"), ("reach", "near"))

    def run(*args):
        place = Layout(lat_count, lon_count, args[3].shape[0] * args[3].shape[1])
        return jax.shard_map(
            functools.partial(body, place),
            mesh=split,
            in_specs=(field, field, field, P(), P(), P(), flat, flat, flat, field),
            out_specs=(field, field, field, field, field, P(), P()),
            check_vma=False,
        )(*args)

    return run
```

profile of v0, /device:TPU:0, one launch (start us, length us, event | category | flops | bytes accessed | tf_op | source)
XLA Modules:
  0.0 52.0 jit_solution(4591603841806209178)
XLA Ops:
  0.6 1.0 %shard_map.153 = (bf16[128,128]{1,0:T(8,128)(2,1)S(1)}, bf16[128,128]{1,0:T(8,128)(2,1)S(1)}, f32[1024,128]{1,0:T(8,128)S(1)}) custom-call(bf16[64,8,128]{2,1,0:T(8,128)(2,1)} %below.1, bf16[64,8,128]{2,1,0:T(8,128)(2,1)} %hidden.1), custom_call_target="tpu_custom_call" | custom-call | bytes 524288 | tf_op jit(solution)/shard_map/pallas_call | solution.py:43
  1.7 0.5 collective-permute-start
  2.2 3.7 %collective-permute-start.1 = (bf16[128,128]{1,0:T(8,128)(2,1)S(1)}, bf16[128,128]{1,0:T(8,128)(2,1)S(1)}, u32[]{:S(2)}, u32[]{:S(2)}) collective-permute-start(bf16[128,128]{1,0:T(8,128)(2,1)S(1)} %get-tuple-element.45), channel_id=1, source_target_pairs={{0,4},{1,5},{2,6},{3,7},{4,0},{5,1},{6,2},{7,3},{8,16},{9,17},{10,... | collective-permute-start | bytes 98312 | tf_op jit(solution)/shard_map/ppermute | solution.py:126
  5.8 1.5 %shard_map.154 = (bf16[8,128,128]{2,1,0:T(8,128)(2,1)S(1)}, f32[128,128]{1,0:T(8,128)S(1)}, f32[512,128]{1,0:T(8,128)S(1)}, bf16[9,256,128]{2,1,0:T(8,128)(2,1)S...) custom-call(f32[1024,128]{1,0:T(8,128)S(1)} %get-tuple-element.42.wi, ...), custom_call_target="tpu_custom_call" | custom-call | bytes 6000000 | tf_op jit(solution)/shard_map/pallas_call | solution.py:43
  7.4 0.0 collective-permute-done.inner.inner_row
  7.4 0.4 collective-permute-done.1.outer.outer_row
  7.7 0.1 shard_map.155
  7.8 5.2 %collective-permute-start.3 = (bf16[128,128]{1,0:T(8,128)(2,1)S(1)}, bf16[128,128]{1,0:T(8,128)(2,1)S(1)}, u32[]{:S(2)}, u32[]{:S(2)}) collective-permute-start(bf16[128,128]{1,0:T(8,128)(2,1)S(1)} %shard_map.155), channel_id=1, source_target_pairs={{0,7},{1,2},{2,1},{3,4},{4,3},{5,6},{6,5},{7,0},{8,15},{9,10},{10,... | collective-permute-start | bytes 98312 | tf_op jit(solution)/shard_map/ppermute | solution.py:126
  13.0 0.0 collective-permute-start.2
  13.0 1.9 %collective-permute-done.3.outer_column = bf16[128,128]{1,0:T(8,128)(2,1)S(1)} collective-permute-done((bf16[128,128]{1,0:T(8,128)(2,1)S(1)}, bf16[128,128]{1,0:T(8,128)(2,1)S(1)}, u32[]{:S(2)}, u32[]{:S(2)}) %collective-permute-start.3) | collective-permute-done | bytes 32800 | tf_op jit(solution)/shard_map/ppermute | solution.py:126
  14.9 2.0 %collective-permute-done.2.inner_column = bf16[128,128]{1,0:T(8,128)(2,1)S(1)} collective-permute-done((bf16[128,128]{1,0:T(8,128)(2,1)S(1)}, bf16[128,128]{1,0:T(8,128)(2,1)S(1)}, u32[]{:S(2)}, u32[]{:S(2)}) %collective-permute-start.2) | collective-permute-done | bytes 32800 | tf_op jit(solution)/shard_map/ppermute | solution.py:126
  16.9 2.5 %shard_map.156 = (bf16[64,8,128]{2,1,0:T(8,128)(2,1)}, f32[512,128]{1,0:T(8,128)}, f32[512,128]{1,0:T(8,128)}, bf16[256,1024]{1,0:T(8,128)(2,1)S(1)}, bf16[256,1...) custom-call(bf16[8,128,128]{2,1,0:T(8,128)(2,1)S(1)} %get-tuple-elem, ...), custom_call_target="tpu_custom_call" | custom-call | flops 1207959552 | bytes 4000000 | tf_op jit(solution)/shard_map/pallas_call | solution.py:43
  19.5 0.1 collective-permute-start.8
  19.5 1.6 %collective-permute-done.8.received = bf16[1168,128]{1,0:T(8,128)(2,1)S(1)} collective-permute-done((bf16[1168,128]{1,0:T(8,128)(2,1)S(1)}, bf16[1168,128]{1,0:T(8,128)(2,1)S(1)}, u32[]{:S(2)}, u32[]{:S(2)}) %collective-permute-start.8) | collective-permute-done | bytes 299040 | tf_op jit(solution)/shard_map/ppermute | solution.py:126
  21.1 0.1 shard_map.158
  21.2 0.1 collective-permute-start.9
  21.3 0.1 collective-permute-start.10
  21.4 3.4 %collective-permute-start.11 = (bf16[304,128]{1,0:T(8,128)(2,1)S(1)}, bf16[304,128]{1,0:T(8,128)(2,1)S(1)}, u32[]{:S(2)}, u32[]{:S(2)}) collective-permute-start(bf16[304,128]{1,0:T(8,128)(2,1)S(1)} %get-tuple-element.67), channel_id=1, source_target_pairs={{0,17},{1,16},{2,19},{3,18},{4,21},{5,20},{6,23},{7,22},{8,25},{9,... | collective-permute-start | bytes 233480 | tf_op jit(solution)/shard_map/ppermute | solution.py:126
  24.8 0.0 collective-permute-start.4
  24.8 0.0 collective-permute-start.5
  24.8 1.2 %collective-permute-done.4.inner.inner_row = bf16[256,128]{1,0:T(8,128)(2,1)S(1)} collective-permute-done((bf16[256,128]{1,0:T(8,128)(2,1)S(1)}, bf16[256,128]{1,0:T(8,128)(2,1)S(1)}, u32[]{:S(2)}, u32[]{:S(2)}) %collective-permute-start.4) | collective-permute-done | bytes 65568 | tf_op jit(solution)/shard_map/ppermute | solution.py:126
  26.0 3.9 %collective-permute-done.5.outer.outer_row = bf16[256,128]{1,0:T(8,128)(2,1)S(1)} collective-permute-done((bf16[256,128]{1,0:T(8,128)(2,1)S(1)}, bf16[256,128]{1,0:T(8,128)(2,1)S(1)}, u32[]{:S(2)}, u32[]{:S(2)}) %collective-permute-start.5) | collective-permute-done | bytes 65568 | tf_op jit(solution)/shard_map/ppermute | solution.py:126
  29.9 0.4 shard_map.157.refs_3_
  30.4 0.0 collective-permute-done.9.refs_0_
  30.4 0.0 collective-permute-done.10.refs_1_
  30.4 0.0 collective-permute-done.11.refs_2_
  30.4 0.1 collective-permute-start.12
  30.5 4.6 %collective-permute-done.12.received = bf16[304,128]{1,0:T(8,128)(2,1)S(1)} collective-permute-done((bf16[304,128]{1,0:T(8,128)(2,1)S(1)}, bf16[304,128]{1,0:T(8,128)(2,1)S(1)}, u32[]{:S(2)}, u32[]{:S(2)}) %collective-permute-start.12) | collective-permute-done | bytes 77856 | tf_op jit(solution)/shard_map/ppermute | solution.py:126
  35.1 0.6 %shard_map.160 = (bf16[304,128]{1,0:T(8,128)(2,1)S(1)}, f32[8,128]{1,0:T(8,128)}) custom-call(bf16[304,128]{1,0:T(8,128)(2,1)S(1)} %shard_map.159.own, bf16[304,128]{1,0:T(8,128)(2,1)S(1)} %collective-permute-done.12.received), custom_call_target="tpu_custom_call" | custom-call | tf_op jit(solution)/shard_map/pallas_call | solution.py:43
  35.7 0.0 collective-permute-start.13
  35.7 2.6 %collective-permute-start.7 = (bf16[256,128]{1,0:T(8,128)(2,1)S(1)}, bf16[256,128]{1,0:T(8,128)(2,1)S(1)}, u32[]{:S(2)}, u32[]{:S(2)}) collective-permute-start(bf16[256,128]{1,0:T(8,128)(2,1)S(1)} %shard_map.157.refs_3_), channel_id=1, source_target_pairs={{0,7},{1,2},{2,1},{3,4},{4,3},{5,6},{6,5},{7,0},{8,15},{9,10},{10,... | collective-permute-start | bytes 196616 | tf_op jit(solution)/shard_map/ppermute | solution.py:126
  38.3 1.2 %collective-permute-start.6 = (bf16[256,128]{1,0:T(8,128)(2,1)S(1)}, bf16[256,128]{1,0:T(8,128)(2,1)S(1)}, u32[]{:S(2)}, u32[]{:S(2)}) collective-permute-start(bf16[256,128]{1,0:T(8,128)(2,1)S(1)} %shard_map.157.refs_3_), channel_id=1, source_target_pairs={{0,1},{1,0},{2,3},{3,2},{4,5},{5,4},{6,7},{7,6},{8,9},{9,8},{10,11... | collective-permute-start | bytes 196616 | tf_op jit(solution)/shard_map/ppermute | solution.py:126
  39.5 1.9 %collective-permute-done.13.received = bf16[304,128]{1,0:T(8,128)(2,1)S(1)} collective-permute-done((bf16[304,128]{1,0:T(8,128)(2,1)S(1)}, bf16[304,128]{1,0:T(8,128)(2,1)S(1)}, u32[]{:S(2)}, u32[]{:S(2)}) %collective-permute-start.13) | collective-permute-done | bytes 77856 | tf_op jit(solution)/shard_map/ppermute | solution.py:126
  41.5 1.0 %collective-permute-start.16 = (bf16[304,128]{1,0:T(8,128)(2,1)S(1)}, bf16[304,128]{1,0:T(8,128)(2,1)S(1)}, u32[]{:S(2)}, u32[]{:S(2)}) collective-permute-start(bf16[304,128]{1,0:T(8,128)(2,1)S(1)} %get-tuple-element.73.refs_0_), channel_id=1, source_target_pairs={{0,17},{1,16},{2,19},{3,18},{4,21},{5,20},{6,23},{7,22},{8,25},{9,... | collective-permute-start | bytes 233480 | tf_op jit(solution)/shard_map/ppermute | solution.py:126
  42.5 2.6 %collective-permute-start.15 = (bf16[304,128]{1,0:T(8,128)(2,1)S(1)}, bf16[304,128]{1,0:T(8,128)(2,1)S(1)}, u32[]{:S(2)}, u32[]{:S(2)}) collective-permute-start(bf16[304,128]{1,0:T(8,128)(2,1)S(1)} %get-tuple-element.73.refs_0_), channel_id=1, source_target_pairs={{0,16},{1,17},{2,18},{3,19},{4,20},{5,21},{6,22},{7,23},{8,24},{9,... | collective-permute-start | bytes 233480 | tf_op jit(solution)/shard_map/ppermute | solution.py:126
  45.0 0.0 collective-permute-start.14
  45.1 0.0 collective-permute-done.7.outer_column
  45.1 0.0 collective-permute-done.6.inner_column
  45.1 2.1 %shard_map.162 = (bf16[64,8,128]{2,1,0:T(8,128)(2,1)}, bf16[64,8,128]{2,1,0:T(8,128)(2,1)}, f32[8,128]{1,0:T(8,128)S(1)}) custom-call(bf16[256,1024]{1,0:T(8,128)(2,1)S(1)} %get-tuple-element.57.pre, bf16[256,128]{1,0:T(8,128)(2,1)S(1)} %collective-permute-done.4.inner.inner_row, bf16[256,128]{1,0:T(8,128)(2,1)S(1)} %collective-permute-done.5.outer.outer_row, ...), custom_call_target="tpu_custom_call" | custom-call | flops 603979776 | bytes 2000000 | tf_op jit(solution)/shard_map/pallas_call | solution.py:43
  47.2 0.0 collective-permute-done.16.refs_3_
  47.2 1.1 %collective-permute-done.15.refs_2_ = bf16[304,128]{1,0:T(8,128)(2,1)S(1)} collective-permute-done((bf16[304,128]{1,0:T(8,128)(2,1)S(1)}, bf16[304,128]{1,0:T(8,128)(2,1)S(1)}, u32[]{:S(2)}, u32[]{:S(2)}) %collective-permute-start.15) | collective-permute-done | bytes 77856 | tf_op jit(solution)/shard_map/ppermute | solution.py:126
  48.3 1.2 %collective-permute-done.14.refs_1_ = bf16[304,128]{1,0:T(8,128)(2,1)S(1)} collective-permute-done((bf16[304,128]{1,0:T(8,128)(2,1)S(1)}, bf16[304,128]{1,0:T(8,128)(2,1)S(1)}, u32[]{:S(2)}, u32[]{:S(2)}) %collective-permute-start.14) | collective-permute-done | bytes 77856 | tf_op jit(solution)/shard_map/ppermute | solution.py:126
  49.5 0.1 collective-permute-start.17
  49.6 0.9 %shard_map.164.out_before = f32[2304,128]{1,0:T(8,128)} custom-call(bf16[4,304,128]{2,1,0:T(8,128)(2,1)S(1)} %shard_map.163.own), custom_call_target="tpu_custom_call" | custom-call | bytes 884736 | tf_op jit(solution)/shard_map/pallas_call | solution.py:43
  50.4 0.7 %collective-permute-done.17.received = bf16[4,304,128]{2,1,0:T(8,128)(2,1)S(1)} collective-permute-done((bf16[4,304,128]{2,1,0:T(8,128)(2,1)S(1)}, bf16[4,304,128]{2,1,0:T(8,128)(2,1)S(1)}, u32[]{:S(2)}, u32[]{:S(2)}) %collective-permute-start.17) | collective-permute-done | bytes 311328 | tf_op jit(solution)/shard_map/ppermute | solution.py:126
  51.2 0.9 %shard_map.165 = (f32[2304,128]{1,0:T(8,128)}, f32[256]{0:T(256)}) custom-call(bf16[4,304,128]{2,1,0:T(8,128)(2,1)S(1)} %shard_map.163.own, bf16[4,304,128]{2,1,0:T(8,128)(2,1)S(1)} %collective-permute-done.17.received, f32[2304,128]{1,0:T(8,128)} %shard_map.164.out_before), custom_call_target="tpu_custom_call", output_to_operand_aliasing={{0}: (2, {})} | custom-call | bytes 884736 | tf_op jit(solution)/shard_map/pallas_call | solution.py:43
  (3 shorter events, 0.1 us)
Async XLA Ops:
  1.7 5.7 %collective-permute-start = (bf16[128,128]{1,0:T(8,128)(2,1)S(1)}, bf16[128,128]{1,0:T(8,128)(2,1)S(1)}, u32[]{:S(2)}, u32[]{:S(2)}) collective-permute-start(bf16[128,128]{1,0:T(8,128)(2,1)S(1)} %get-tuple-element.44), channel_id=1, source_target_pairs={{0,8},{1,9},{2,10},{3,11},{4,12},{5,13},{6,14},{7,15},{8,0},{9,1},... | collective-permute-start | bytes 98312 | tf_op jit(solution)/shard_map/ppermute | solution.py:126
  2.2 5.6 %collective-permute-start.1 = (bf16[128,128]{1,0:T(8,128)(2,1)S(1)}, bf16[128,128]{1,0:T(8,128)(2,1)S(1)}, u32[]{:S(2)}, u32[]{:S(2)}) collective-permute-start(bf16[128,128]{1,0:T(8,128)(2,1)S(1)} %get-tuple-element.45), channel_id=1, source_target_pairs={{0,4},{1,5},{2,6},{3,7},{4,0},{5,1},{6,2},{7,3},{8,16},{9,17},{10,... | collective-permute-start | bytes 98312 | tf_op jit(solution)/shard_map/ppermute | solution.py:126
  7.8 7.1 %collective-permute-start.3 = (bf16[128,128]{1,0:T(8,128)(2,1)S(1)}, bf16[128,128]{1,0:T(8,128)(2,1)S(1)}, u32[]{:S(2)}, u32[]{:S(2)}) collective-permute-start(bf16[128,128]{1,0:T(8,128)(2,1)S(1)} %shard_map.155), channel_id=1, source_target_pairs={{0,7},{1,2},{2,1},{3,4},{4,3},{5,6},{6,5},{7,0},{8,15},{9,10},{10,... | collective-permute-start | bytes 98312 | tf_op jit(solution)/shard_map/ppermute | solution.py:126
  13.0 3.9 %collective-permute-start.2 = (bf16[128,128]{1,0:T(8,128)(2,1)S(1)}, bf16[128,128]{1,0:T(8,128)(2,1)S(1)}, u32[]{:S(2)}, u32[]{:S(2)}) collective-permute-start(bf16[128,128]{1,0:T(8,128)(2,1)S(1)} %shard_map.155), channel_id=1, source_target_pairs={{0,1},{1,0},{2,3},{3,2},{4,5},{5,4},{6,7},{7,6},{8,9},{9,8},{10,11... | collective-permute-start | bytes 98312 | tf_op jit(solution)/shard_map/ppermute | solution.py:126
  19.5 1.7 %collective-permute-start.8 = (bf16[1168,128]{1,0:T(8,128)(2,1)S(1)}, bf16[1168,128]{1,0:T(8,128)(2,1)S(1)}, u32[]{:S(2)}, u32[]{:S(2)}) collective-permute-start(bf16[1168,128]{1,0:T(8,128)(2,1)S(1)} %get-tuple-element.62), channel_id=1, source_target_pairs={{0,8},{1,9},{2,10},{3,11},{4,12},{5,13},{6,14},{7,15},{8,0},{9,1},... | collective-permute-start | bytes 897032 | tf_op jit(solution)/shard_map/ppermute | solution.py:126
  21.2 9.2 %collective-permute-start.9 = (bf16[304,128]{1,0:T(8,128)(2,1)S(1)}, bf16[304,128]{1,0:T(8,128)(2,1)S(1)}, u32[]{:S(2)}, u32[]{:S(2)}) collective-permute-start(bf16[304,128]{1,0:T(8,128)(2,1)S(1)} %get-tuple-element.65), channel_id=1, source_target_pairs={{0,1},{1,0},{2,3},{3,2},{4,5},{5,4},{6,7},{7,6},{8,9},{9,8},{10,11... | collective-permute-start | bytes 233480 | tf_op jit(solution)/shard_map/ppermute | solution.py:126
  21.3 9.1 %collective-permute-start.10 = (bf16[304,128]{1,0:T(8,128)(2,1)S(1)}, bf16[304,128]{1,0:T(8,128)(2,1)S(1)}, u32[]{:S(2)}, u32[]{:S(2)}) collective-permute-start(bf16[304,128]{1,0:T(8,128)(2,1)S(1)} %get-tuple-element.66), channel_id=1, source_target_pairs={{0,16},{1,17},{2,18},{3,19},{4,20},{5,21},{6,22},{7,23},{8,24},{9,... | collective-permute-start | bytes 233480 | tf_op jit(solution)/shard_map/ppermute | solution.py:126
  21.4 9.0 %collective-permute-start.11 = (bf16[304,128]{1,0:T(8,128)(2,1)S(1)}, bf16[304,128]{1,0:T(8,128)(2,1)S(1)}, u32[]{:S(2)}, u32[]{:S(2)}) collective-permute-start(bf16[304,128]{1,0:T(8,128)(2,1)S(1)} %get-tuple-element.67), channel_id=1, source_target_pairs={{0,17},{1,16},{2,19},{3,18},{4,21},{5,20},{6,23},{7,22},{8,25},{9,... | collective-permute-start | bytes 233480 | tf_op jit(solution)/shard_map/ppermute | solution.py:126
  24.8 1.3 %collective-permute-start.4 = (bf16[256,128]{1,0:T(8,128)(2,1)S(1)}, bf16[256,128]{1,0:T(8,128)(2,1)S(1)}, u32[]{:S(2)}, u32[]{:S(2)}) collective-permute-start(bf16[256,128]{1,0:T(8,128)(2,1)S(1)} %get-tuple-element.58), channel_id=1, source_target_pairs={{0,8},{1,9},{2,10},{3,11},{4,12},{5,13},{6,14},{7,15},{8,0},{9,1},... | collective-permute-start | bytes 196616 | tf_op jit(solution)/shard_map/ppermute | solution.py:126
  24.8 5.2 %collective-permute-start.5 = (bf16[256,128]{1,0:T(8,128)(2,1)S(1)}, bf16[256,128]{1,0:T(8,128)(2,1)S(1)}, u32[]{:S(2)}, u32[]{:S(2)}) collective-permute-start(bf16[256,128]{1,0:T(8,128)(2,1)S(1)} %get-tuple-element.59), channel_id=1, source_target_pairs={{0,4},{1,5},{2,6},{3,7},{4,0},{5,1},{6,2},{7,3},{8,16},{9,17},{10,... | collective-permute-start | bytes 196616 | tf_op jit(solution)/shard_map/ppermute | solution.py:126
  30.4 4.6 %collective-permute-start.12 = (bf16[304,128]{1,0:T(8,128)(2,1)S(1)}, bf16[304,128]{1,0:T(8,128)(2,1)S(1)}, u32[]{:S(2)}, u32[]{:S(2)}) collective-permute-start(bf16[304,128]{1,0:T(8,128)(2,1)S(1)} %shard_map.159.own), channel_id=1, source_target_pairs={{0,2},{1,3},{2,0},{3,1},{4,6},{5,7},{6,4},{7,5},{8,12},{9,13},{10,... | collective-permute-start | bytes 233480 | tf_op jit(solution)/shard_map/ppermute | solution.py:126
  35.7 5.8 %collective-permute-start.13 = (bf16[304,128]{1,0:T(8,128)(2,1)S(1)}, bf16[304,128]{1,0:T(8,128)(2,1)S(1)}, u32[]{:S(2)}, u32[]{:S(2)}) collective-permute-start(bf16[304,128]{1,0:T(8,128)(2,1)S(1)} %get-tuple-element.68.own), channel_id=1, source_target_pairs={{0,4},{1,5},{2,6},{3,7},{4,0},{5,1},{6,2},{7,3},{8,10},{9,11},{10,... | collective-permute-start | bytes 233480 | tf_op jit(solution)/shard_map/ppermute | solution.py:126
  35.7 9.4 %collective-permute-start.7 = (bf16[256,128]{1,0:T(8,128)(2,1)S(1)}, bf16[256,128]{1,0:T(8,128)(2,1)S(1)}, u32[]{:S(2)}, u32[]{:S(2)}) collective-permute-start(bf16[256,128]{1,0:T(8,128)(2,1)S(1)} %shard_map.157.refs_3_), channel_id=1, source_target_pairs={{0,7},{1,2},{2,1},{3,4},{4,3},{5,6},{6,5},{7,0},{8,15},{9,10},{10,... | collective-permute-start | bytes 196616 | tf_op jit(solution)/shard_map/ppermute | solution.py:126
  38.3 6.7 %collective-permute-start.6 = (bf16[256,128]{1,0:T(8,128)(2,1)S(1)}, bf16[256,128]{1,0:T(8,128)(2,1)S(1)}, u32[]{:S(2)}, u32[]{:S(2)}) collective-permute-start(bf16[256,128]{1,0:T(8,128)(2,1)S(1)} %shard_map.157.refs_3_), channel_id=1, source_target_pairs={{0,1},{1,0},{2,3},{3,2},{4,5},{5,4},{6,7},{7,6},{8,9},{9,8},{10,11... | collective-permute-start | bytes 196616 | tf_op jit(solution)/shard_map/ppermute | solution.py:126
  41.5 5.7 %collective-permute-start.16 = (bf16[304,128]{1,0:T(8,128)(2,1)S(1)}, bf16[304,128]{1,0:T(8,128)(2,1)S(1)}, u32[]{:S(2)}, u32[]{:S(2)}) collective-permute-start(bf16[304,128]{1,0:T(8,128)(2,1)S(1)} %get-tuple-element.73.refs_0_), channel_id=1, source_target_pairs={{0,17},{1,16},{2,19},{3,18},{4,21},{5,20},{6,23},{7,22},{8,25},{9,... | collective-permute-start | bytes 233480 | tf_op jit(solution)/shard_map/ppermute | solution.py:126
  42.5 5.8 %collective-permute-start.15 = (bf16[304,128]{1,0:T(8,128)(2,1)S(1)}, bf16[304,128]{1,0:T(8,128)(2,1)S(1)}, u32[]{:S(2)}, u32[]{:S(2)}) collective-permute-start(bf16[304,128]{1,0:T(8,128)(2,1)S(1)} %get-tuple-element.73.refs_0_), channel_id=1, source_target_pairs={{0,16},{1,17},{2,18},{3,19},{4,20},{5,21},{6,22},{7,23},{8,24},{9,... | collective-permute-start | bytes 233480 | tf_op jit(solution)/shard_map/ppermute | solution.py:126
  45.0 4.4 %collective-permute-start.14 = (bf16[304,128]{1,0:T(8,128)(2,1)S(1)}, bf16[304,128]{1,0:T(8,128)(2,1)S(1)}, u32[]{:S(2)}, u32[]{:S(2)}) collective-permute-start(bf16[304,128]{1,0:T(8,128)(2,1)S(1)} %get-tuple-element.73.refs_0_), channel_id=1, source_target_pairs={{0,1},{1,0},{2,3},{3,2},{4,5},{5,4},{6,7},{7,6},{8,9},{9,8},{10,11... | collective-permute-start | bytes 233480 | tf_op jit(solution)/shard_map/ppermute | solution.py:126
  49.5 1.7 %collective-permute-start.17 = (bf16[4,304,128]{2,1,0:T(8,128)(2,1)S(1)}, bf16[4,304,128]{2,1,0:T(8,128)(2,1)S(1)}, u32[]{:S(2)}, u32[]{:S(2)}) collective-permute-start(bf16[4,304,128]{2,1,0:T(8,128)(2,1)S(1)} %shard_map.163.own), channel_id=1, source_target_pairs={{0,8},{1,9},{2,10},{3,11},{4,12},{5,13},{6,14},{7,15},{8,0},{9,1},... | collective-permute-start | bytes 933896 | tf_op jit(solution)/shard_map/ppermute | solution.py:126
where the time goes:
time: 52.2 us; the launch traced here: 52 us
  starting transfers between devices  20.5 us (39%)
  waiting for transfers between devices  20.5 us (39%)
  Pallas kernels  10.2 us (20%)
  between operations  0.77 us (1%)
    ppermute x18, starting transfers between devices, permuted(): return lax.ppermute(value, AXES, pairs)  20.5 us
    ppermute x18, waiting for transfers between devices, permuted(): return lax.ppermute(value, AXES, pairs)  20.5 us
    pallas_call x13, Pallas kernels, run(): pl.pallas_call(kernel, out_shape=out_shape, in_specs=[VMEM] * near + [HBM...  10.2 us
  transfers between devices with their start and end apart: 18, of which 11 were waited for; matrix products, arithmetic and copies ran while one was open for 0% of the time, Pallas kernels for 9%

commit v1 on v0

--- a/solution.py
+++ b/solution.py
@@ -455,7 +455,7 @@
 
 
 def plane_kernel(keep, bias, *refs):
-    received, out = refs[:-2], refs[-1]
+    received, out = refs[:-1], refs[-1]
     total, bias_total = keep[...], bias[...]
     for ref in received:
         total += ref[BIAS_ROWS:, :].astype(F32)
@@ -471,12 +471,13 @@
         out[rank ^ step] = block[...]
 
 
-def add_kernel(scale, own, received, out, done_out):
+def add_kernel(scale, own, received, out, *done_out):
     here, there = own[...].astype(F32), received[...].astype(F32)
     bias = (decode(here[0:BIAS_ROWS]) + decode(there[0:BIAS_ROWS])) * scale
     out[0:BIAS_ROWS, :] = encode(bias).astype(BF16)
     out[BIAS_ROWS:, :] = ((here[BIAS_ROWS:] + there[BIAS_ROWS:]) * scale).astype(BF16)
-    done_out[...] = jnp.zeros(done_out.shape, F32)
+    for done in done_out:
+        done[...] = jnp.zeros(done.shape, F32)
 
 
 def unpack(blocks, wide):
@@ -735,16 +736,15 @@
         [pltpu.VMEM((place.half_rows, channels), F32)],
     )(keep, bias, permuted(send, place.phase_pairs(0)))
     received = [permuted(send, place.plane_pairs(step)) for step, send in zip(steps, sends)]
-    part = call(plane_kernel, block)(keep, bias, *received, pre_columns)
+    part = call(plane_kernel, block)(keep, bias, *received)
     pre_inner_columns = permuted(pre_columns, inner_columns)
     pre_outer_columns = permuted(pre_columns, outer_columns)
     phases = len(place.orders[0])
     for phase in range(1, phases):
         is_last = phase == phases - 1
-        part, summed = call(bind(add_kernel, scaling if is_last else 1.0), (block, token))(
-            part,
-            permuted(part, place.phase_pairs(phase)),
-        )
+        part, *summed = call(
+            bind(add_kernel, scaling if is_last else 1.0), (block, token) if is_last else (block,)
+        )(part, permuted(part, place.phase_pairs(phase)))
     grad_inputs, grad_hidden, field_done = call(
         bind(field_kernel, place),
         (
@@ -766,7 +766,7 @@
         pre_inner_columns,
         pre_outer_columns,
         weights_here,
-        summed,
+        *summed,
     )
     received = [permuted(part, place.plane_pairs(step)) for step in steps]
     gathered = call(bind(join_kernel, place), sds((place.plane, *block.shape), BF16))(

time: 52.2 us -> 49 us (0.939)
  waiting for transfers between devices: 20.5 us -> 15.6 us
  starting transfers between devices: 20.5 us -> 22.9 us
  Pallas kernels: 10.2 us -> 9.62 us
    ppermute x18, waiting for transfers between devices: 20.5 us -> 15.6 us  [permuted(): return lax.ppermute(value, AXES, pairs)]
    ppermute x18, starting transfers between devices: 20.5 us -> 22.9 us  [permuted(): return lax.ppermute(value, AXES, pairs)]
    pallas_call x13, Pallas kernels: 10.2 us -> 9.62 us  [run(): pl.pallas_call(kernel, out_shape=out_shape, in_specs=[VMEM] * near + [HBM...]
  transfers between devices with their start and end apart: 18 -> 18, of which waited for: 11 -> 12; matrix products, arithmetic and copies ran while one was open for 0% -> 0% of each run, Pallas kernels for 9% -> 10%
where the time goes in v1:
time: 49 us; the launch traced here: 48.9 us
  starting transfers between devices  22.9 us (47%)
  waiting for transfers between devices  15.6 us (32%)
  Pallas kernels  9.62 us (20%)
  between operations  0.76 us (2%)
    ppermute x18, starting transfers between devices, permuted(): return lax.ppermute(value, AXES, pairs)  22.9 us
    ppermute x18, waiting for transfers between devices, permuted(): return lax.ppermute(value, AXES, pairs)  15.6 us
    pallas_call x13, Pallas kernels, run(): pl.pallas_call(kernel, out_shape=out_shape, in_specs=[VMEM] * near + [HBM...  9.62 us
  transfers between devices with their start and end apart: 18, of which 12 were waited for; matrix products, arithmetic and copies ran while one was open for 0% of the time, Pallas kernels for 10%

profile of v1, /device:TPU:0, one launch (start us, length us, event | category | flops | bytes accessed | tf_op | source)
XLA Modules:
  0.0 48.9 jit_solution(16549265242164885365)
XLA Ops:
  0.6 1.0 %shard_map.153 = (bf16[128,128]{1,0:T(8,128)(2,1)S(1)}, bf16[128,128]{1,0:T(8,128)(2,1)S(1)}, f32[1024,128]{1,0:T(8,128)S(1)}) custom-call(bf16[64,8,128]{2,1,0:T(8,128)(2,1)} %below.1, bf16[64,8,128]{2,1,0:T(8,128)(2,1)} %hidden.1), custom_call_target="tpu_custom_call" | custom-call | bytes 524288 | tf_op jit(solution)/shard_map/pallas_call | solution.py:43
  1.7 0.5 %collective-permute-start = (bf16[128,128]{1,0:T(8,128)(2,1)S(1)}, bf16[128,128]{1,0:T(8,128)(2,1)S(1)}, u32[]{:S(2)}, u32[]{:S(2)}) collective-permute-start(bf16[128,128]{1,0:T(8,128)(2,1)S(1)} %get-tuple-element.43), channel_id=1, source_target_pairs={{0,8},{1,9},{2,10},{3,11},{4,12},{5,13},{6,14},{7,15},{8,0},{9,1},... | collective-permute-start | bytes 98312 | tf_op jit(solution)/shard_map/ppermute | solution.py:126
  2.2 3.7 %collective-permute-start.1 = (bf16[128,128]{1,0:T(8,128)(2,1)S(1)}, bf16[128,128]{1,0:T(8,128)(2,1)S(1)}, u32[]{:S(2)}, u32[]{:S(2)}) collective-permute-start(bf16[128,128]{1,0:T(8,128)(2,1)S(1)} %get-tuple-element.44), channel_id=1, source_target_pairs={{0,4},{1,5},{2,6},{3,7},{4,0},{5,1},{6,2},{7,3},{8,16},{9,17},{10,... | collective-permute-start | bytes 98312 | tf_op jit(solution)/shard_map/ppermute | solution.py:126
  5.8 1.5 %shard_map.154 = (bf16[8,128,128]{2,1,0:T(8,128)(2,1)S(1)}, f32[128,128]{1,0:T(8,128)S(1)}, f32[512,128]{1,0:T(8,128)S(1)}, bf16[9,256,128]{2,1,0:T(8,128)(2,1)S...) custom-call(f32[1024,128]{1,0:T(8,128)S(1)} %get-tuple-element.41.wi, ...), custom_call_target="tpu_custom_call" | custom-call | bytes 6000000 | tf_op jit(solution)/shard_map/pallas_call | solution.py:43
  7.4 0.0 collective-permute-done.inner.inner_row
  7.4 0.4 collective-permute-done.1.outer.outer_row
  7.7 0.1 shard_map.155
  7.8 5.2 %collective-permute-start.3 = (bf16[128,128]{1,0:T(8,128)(2,1)S(1)}, bf16[128,128]{1,0:T(8,128)(2,1)S(1)}, u32[]{:S(2)}, u32[]{:S(2)}) collective-permute-start(bf16[128,128]{1,0:T(8,128)(2,1)S(1)} %shard_map.155), channel_id=1, source_target_pairs={{0,7},{1,2},{2,1},{3,4},{4,3},{5,6},{6,5},{7,0},{8,15},{9,10},{10,... | collective-permute-start | bytes 98312 | tf_op jit(solution)/shard_map/ppermute | solution.py:126
  13.0 0.0 collective-permute-start.2
  13.0 1.9 %collective-permute-done.3.outer_column = bf16[128,128]{1,0:T(8,128)(2,1)S(1)} collective-permute-done((bf16[128,128]{1,0:T(8,128)(2,1)S(1)}, bf16[128,128]{1,0:T(8,128)(2,1)S(1)}, u32[]{:S(2)}, u32[]{:S(2)}) %collective-permute-start.3) | collective-permute-done | bytes 32800 | tf_op jit(solution)/shard_map/ppermute | solution.py:126
  14.9 2.0 %collective-permute-done.2.inner_column = bf16[128,128]{1,0:T(8,128)(2,1)S(1)} collective-permute-done((bf16[128,128]{1,0:T(8,128)(2,1)S(1)}, bf16[128,128]{1,0:T(8,128)(2,1)S(1)}, u32[]{:S(2)}, u32[]{:S(2)}) %collective-permute-start.2) | collective-permute-done | bytes 32800 | tf_op jit(solution)/shard_map/ppermute | solution.py:126
  16.9 2.5 %shard_map.156 = (bf16[64,8,128]{2,1,0:T(8,128)(2,1)}, f32[512,128]{1,0:T(8,128)}, f32[512,128]{1,0:T(8,128)}, bf16[256,1024]{1,0:T(8,128)(2,1)S(1)}, bf16[256,1...) custom-call(bf16[8,128,128]{2,1,0:T(8,128)(2,1)S(1)} %get-tuple-elem, ...), custom_call_target="tpu_custom_call" | custom-call | flops 1207959552 | bytes 4000000 | tf_op jit(solution)/shard_map/pallas_call | solution.py:43
  19.5 0.1 collective-permute-start.8
  19.5 1.6 %collective-permute-done.8.received = bf16[1168,128]{1,0:T(8,128)(2,1)S(1)} collective-permute-done((bf16[1168,128]{1,0:T(8,128)(2,1)S(1)}, bf16[1168,128]{1,0:T(8,128)(2,1)S(1)}, u32[]{:S(2)}, u32[]{:S(2)}) %collective-permute-start.8) | collective-permute-done | bytes 299040 | tf_op jit(solution)/shard_map/ppermute | solution.py:126
  21.1 0.1 shard_map.158
  21.2 0.1 collective-permute-start.9
  21.3 0.1 collective-permute-start.10
  21.4 3.4 %collective-permute-start.11 = (bf16[304,128]{1,0:T(8,128)(2,1)S(1)}, bf16[304,128]{1,0:T(8,128)(2,1)S(1)}, u32[]{:S(2)}, u32[]{:S(2)}) collective-permute-start(bf16[304,128]{1,0:T(8,128)(2,1)S(1)} %get-tuple-element.66), channel_id=1, source_target_pairs={{0,17},{1,16},{2,19},{3,18},{4,21},{5,20},{6,23},{7,22},{8,25},{9,... | collective-permute-start | bytes 233480 | tf_op jit(solution)/shard_map/ppermute | solution.py:126
  24.8 0.9 %collective-permute-done.9.refs_0_ = bf16[304,128]{1,0:T(8,128)(2,1)S(1)} collective-permute-done((bf16[304,128]{1,0:T(8,128)(2,1)S(1)}, bf16[304,128]{1,0:T(8,128)(2,1)S(1)}, u32[]{:S(2)}, u32[]{:S(2)}) %collective-permute-start.9) | collective-permute-done | bytes 77856 | tf_op jit(solution)/shard_map/ppermute | solution.py:126
  25.7 0.6 %collective-permute-done.10.refs_1_ = bf16[304,128]{1,0:T(8,128)(2,1)S(1)} collective-permute-done((bf16[304,128]{1,0:T(8,128)(2,1)S(1)}, bf16[304,128]{1,0:T(8,128)(2,1)S(1)}, u32[]{:S(2)}, u32[]{:S(2)}) %collective-permute-start.10) | collective-permute-done | bytes 77856 | tf_op jit(solution)/shard_map/ppermute | solution.py:126
  26.3 2.2 %collective-permute-done.11.refs_2_ = bf16[304,128]{1,0:T(8,128)(2,1)S(1)} collective-permute-done((bf16[304,128]{1,0:T(8,128)(2,1)S(1)}, bf16[304,128]{1,0:T(8,128)(2,1)S(1)}, u32[]{:S(2)}, u32[]{:S(2)}) %collective-permute-start.11) | collective-permute-done | bytes 77856 | tf_op jit(solution)/shard_map/ppermute | solution.py:126
  28.6 0.1 collective-permute-start.12
  28.7 0.1 collective-permute-start.4
  28.7 2.1 %collective-permute-start.5 = (bf16[256,128]{1,0:T(8,128)(2,1)S(1)}, bf16[256,128]{1,0:T(8,128)(2,1)S(1)}, u32[]{:S(2)}, u32[]{:S(2)}) collective-permute-start(bf16[256,128]{1,0:T(8,128)(2,1)S(1)} %get-tuple-element.58), channel_id=1, source_target_pairs={{0,4},{1,5},{2,6},{3,7},{4,0},{5,1},{6,2},{7,3},{8,16},{9,17},{10,... | collective-permute-start | bytes 196616 | tf_op jit(solution)/shard_map/ppermute | solution.py:126
  30.8 2.2 %collective-permute-done.12.received = bf16[304,128]{1,0:T(8,128)(2,1)S(1)} collective-permute-done((bf16[304,128]{1,0:T(8,128)(2,1)S(1)}, bf16[304,128]{1,0:T(8,128)(2,1)S(1)}, u32[]{:S(2)}, u32[]{:S(2)}) %collective-permute-start.12) | collective-permute-done | bytes 77856 | tf_op jit(solution)/shard_map/ppermute | solution.py:126
  33.1 0.2 collective-permute-start.13
  33.3 0.0 collective-permute-done.4.inner.inner_row
  33.3 0.7 %collective-permute-done.5.outer.outer_row = bf16[256,128]{1,0:T(8,128)(2,1)S(1)} collective-permute-done((bf16[256,128]{1,0:T(8,128)(2,1)S(1)}, bf16[256,128]{1,0:T(8,128)(2,1)S(1)}, u32[]{:S(2)}, u32[]{:S(2)}) %collective-permute-start.5) | collective-permute-done | bytes 65568 | tf_op jit(solution)/shard_map/ppermute | solution.py:126
  34.0 0.4 shard_map.157
  34.4 2.8 %collective-permute-start.7 = (bf16[256,128]{1,0:T(8,128)(2,1)S(1)}, bf16[256,128]{1,0:T(8,128)(2,1)S(1)}, u32[]{:S(2)}, u32[]{:S(2)}) collective-permute-start(bf16[256,128]{1,0:T(8,128)(2,1)S(1)} %shard_map.157), channel_id=1, source_target_pairs={{0,7},{1,2},{2,1},{3,4},{4,3},{5,6},{6,5},{7,0},{8,15},{9,10},{10,... | collective-permute-start | bytes 196616 | tf_op jit(solution)/shard_map/ppermute | solution.py:126
  37.2 1.1 %collective-permute-start.6 = (bf16[256,128]{1,0:T(8,128)(2,1)S(1)}, bf16[256,128]{1,0:T(8,128)(2,1)S(1)}, u32[]{:S(2)}, u32[]{:S(2)}) collective-permute-start(bf16[256,128]{1,0:T(8,128)(2,1)S(1)} %shard_map.157), channel_id=1, source_target_pairs={{0,1},{1,0},{2,3},{3,2},{4,5},{5,4},{6,7},{7,6},{8,9},{9,8},{10,11... | collective-permute-start | bytes 196616 | tf_op jit(solution)/shard_map/ppermute | solution.py:126
  38.3 1.2 %collective-permute-done.13.received = bf16[304,128]{1,0:T(8,128)(2,1)S(1)} collective-permute-done((bf16[304,128]{1,0:T(8,128)(2,1)S(1)}, bf16[304,128]{1,0:T(8,128)(2,1)S(1)}, u32[]{:S(2)}, u32[]{:S(2)}) %collective-permute-start.13) | collective-permute-done | bytes 77856 | tf_op jit(solution)/shard_map/ppermute | solution.py:126
  39.5 1.2 %collective-permute-start.16 = (bf16[304,128]{1,0:T(8,128)(2,1)S(1)}, bf16[304,128]{1,0:T(8,128)(2,1)S(1)}, u32[]{:S(2)}, u32[]{:S(2)}) collective-permute-start(bf16[304,128]{1,0:T(8,128)(2,1)S(1)} %get-tuple-element.71.refs_0_), channel_id=1, source_target_pairs={{0,17},{1,16},{2,19},{3,18},{4,21},{5,20},{6,23},{7,22},{8,25},{9,... | collective-permute-start | bytes 233480 | tf_op jit(solution)/shard_map/ppermute | solution.py:126
  40.8 1.1 %collective-permute-start.15 = (bf16[304,128]{1,0:T(8,128)(2,1)S(1)}, bf16[304,128]{1,0:T(8,128)(2,1)S(1)}, u32[]{:S(2)}, u32[]{:S(2)}) collective-permute-start(bf16[304,128]{1,0:T(8,128)(2,1)S(1)} %get-tuple-element.71.refs_0_), channel_id=1, source_target_pairs={{0,16},{1,17},{2,18},{3,19},{4,20},{5,21},{6,22},{7,23},{8,24},{9,... | collective-permute-start | bytes 233480 | tf_op jit(solution)/shard_map/ppermute | solution.py:126
  41.9 1.2 %collective-permute-start.14 = (bf16[304,128]{1,0:T(8,128)(2,1)S(1)}, bf16[304,128]{1,0:T(8,128)(2,1)S(1)}, u32[]{:S(2)}, u32[]{:S(2)}) collective-permute-start(bf16[304,128]{1,0:T(8,128)(2,1)S(1)} %get-tuple-element.71.refs_0_), channel_id=1, source_target_pairs={{0,1},{1,0},{2,3},{3,2},{4,5},{5,4},{6,7},{7,6},{8,9},{9,8},{10,11... | collective-permute-start | bytes 233480 | tf_op jit(solution)/shard_map/ppermute | solution.py:126
  43.1 0.0 collective-permute-done.7.outer_column
  43.1 0.0 collective-permute-done.6.inner_column
  43.1 2.1 %shard_map.162 = (bf16[64,8,128]{2,1,0:T(8,128)(2,1)}, bf16[64,8,128]{2,1,0:T(8,128)(2,1)}, f32[8,128]{1,0:T(8,128)S(1)}) custom-call(bf16[256,1024]{1,0:T(8,128)(2,1)S(1)} %get-tuple-element.56.pre, bf16[256,128]{1,0:T(8,128)(2,1)S(1)} %collective-permute-done.4.inner.inner_row, bf16[256,128]{1,0:T(8,128)(2,1)S(1)} %collective-permute-done.5.outer.outer_row, ...), custom_call_target="tpu_custom_call" | custom-call | flops 603979776 | bytes 2000000 | tf_op jit(solution)/shard_map/pallas_call | solution.py:43
  45.2 0.0 collective-permute-done.16.refs_3_
  45.2 0.0 collective-permute-done.15.refs_2_
  45.2 1.1 %collective-permute-done.14.refs_1_ = bf16[304,128]{1,0:T(8,128)(2,1)S(1)} collective-permute-done((bf16[304,128]{1,0:T(8,128)(2,1)S(1)}, bf16[304,128]{1,0:T(8,128)(2,1)S(1)}, u32[]{:S(2)}, u32[]{:S(2)}) %collective-permute-start.14) | collective-permute-done | bytes 77856 | tf_op jit(solution)/shard_map/ppermute | solution.py:126
  46.3 0.1 collective-permute-start.17
  46.4 0.9 %shard_map.164.out_before = f32[2304,128]{1,0:T(8,128)} custom-call(bf16[4,304,128]{2,1,0:T(8,128)(2,1)S(1)} %shard_map.163.own), custom_call_target="tpu_custom_call" | custom-call | bytes 884736 | tf_op jit(solution)/shard_map/pallas_call | solution.py:43
  47.3 0.7 %collective-permute-done.17.received = bf16[4,304,128]{2,1,0:T(8,128)(2,1)S(1)} collective-permute-done((bf16[4,304,128]{2,1,0:T(8,128)(2,1)S(1)}, bf16[4,304,128]{2,1,0:T(8,128)(2,1)S(1)}, u32[]{:S(2)}, u32[]{:S(2)}) %collective-permute-start.17) | collective-permute-done | bytes 311328 | tf_op jit(solution)/shard_map/ppermute | solution.py:126
  48.0 0.9 %shard_map.165 = (f32[2304,128]{1,0:T(8,128)}, f32[256]{0:T(256)}) custom-call(bf16[4,304,128]{2,1,0:T(8,128)(2,1)S(1)} %shard_map.163.own, bf16[4,304,128]{2,1,0:T(8,128)(2,1)S(1)} %collective-permute-done.17.received, f32[2304,128]{1,0:T(8,128)} %shard_map.164.out_before), custom_call_target="tpu_custom_call", output_to_operand_aliasing={{0}: (2, {})} | custom-call | bytes 884736 | tf_op jit(solution)/shard_map/pallas_call | solution.py:43
  (4 shorter events, 0.1 us)
Async XLA Ops:
  1.7 5.7 %collective-permute-start = (bf16[128,128]{1,0:T(8,128)(2,1)S(1)}, bf16[128,128]{1,0:T(8,128)(2,1)S(1)}, u32[]{:S(2)}, u32[]{:S(2)}) collective-permute-start(bf16[128,128]{1,0:T(8,128)(2,1)S(1)} %get-tuple-element.43), channel_id=1, source_target_pairs={{0,8},{1,9},{2,10},{3,11},{4,12},{5,13},{6,14},{7,15},{8,0},{9,1},... | collective-permute-start | bytes 98312 | tf_op jit(solution)/shard_map/ppermute | solution.py:126
  2.2 5.6 %collective-permute-start.1 = (bf16[128,128]{1,0:T(8,128)(2,1)S(1)}, bf16[128,128]{1,0:T(8,128)(2,1)S(1)}, u32[]{:S(2)}, u32[]{:S(2)}) collective-permute-start(bf16[128,128]{1,0:T(8,128)(2,1)S(1)} %get-tuple-element.44), channel_id=1, source_target_pairs={{0,4},{1,5},{2,6},{3,7},{4,0},{5,1},{6,2},{7,3},{8,16},{9,17},{10,... | collective-permute-start | bytes 98312 | tf_op jit(solution)/shard_map/ppermute | solution.py:126
  7.8 7.1 %collective-permute-start.3 = (bf16[128,128]{1,0:T(8,128)(2,1)S(1)}, bf16[128,128]{1,0:T(8,128)(2,1)S(1)}, u32[]{:S(2)}, u32[]{:S(2)}) collective-permute-start(bf16[128,128]{1,0:T(8,128)(2,1)S(1)} %shard_map.155), channel_id=1, source_target_pairs={{0,7},{1,2},{2,1},{3,4},{4,3},{5,6},{6,5},{7,0},{8,15},{9,10},{10,... | collective-permute-start | bytes 98312 | tf_op jit(solution)/shard_map/ppermute | solution.py:126
  13.0 3.9 %collective-permute-start.2 = (bf16[128,128]{1,0:T(8,128)(2,1)S(1)}, bf16[128,128]{1,0:T(8,128)(2,1)S(1)}, u32[]{:S(2)}, u32[]{:S(2)}) collective-permute-start(bf16[128,128]{1,0:T(8,128)(2,1)S(1)} %shard_map.155), channel_id=1, source_target_pairs={{0,1},{1,0},{2,3},{3,2},{4,5},{5,4},{6,7},{7,6},{8,9},{9,8},{10,11... | collective-permute-start | bytes 98312 | tf_op jit(solution)/shard_map/ppermute | solution.py:126
  19.5 1.7 %collective-permute-start.8 = (bf16[1168,128]{1,0:T(8,128)(2,1)S(1)}, bf16[1168,128]{1,0:T(8,128)(2,1)S(1)}, u32[]{:S(2)}, u32[]{:S(2)}) collective-permute-start(bf16[1168,128]{1,0:T(8,128)(2,1)S(1)} %get-tuple-element.61), channel_id=1, source_target_pairs={{0,8},{1,9},{2,10},{3,11},{4,12},{5,13},{6,14},{7,15},{8,0},{9,1},... | collective-permute-start | bytes 897032 | tf_op jit(solution)/shard_map/ppermute | solution.py:126
  21.2 4.5 %collective-permute-start.9 = (bf16[304,128]{1,0:T(8,128)(2,1)S(1)}, bf16[304,128]{1,0:T(8,128)(2,1)S(1)}, u32[]{:S(2)}, u32[]{:S(2)}) collective-permute-start(bf16[304,128]{1,0:T(8,128)(2,1)S(1)} %get-tuple-element.64), channel_id=1, source_target_pairs={{0,1},{1,0},{2,3},{3,2},{4,5},{5,4},{6,7},{7,6},{8,9},{9,8},{10,11... | collective-permute-start | bytes 233480 | tf_op jit(solution)/shard_map/ppermute | solution.py:126
  21.3 5.0 %collective-permute-start.10 = (bf16[304,128]{1,0:T(8,128)(2,1)S(1)}, bf16[304,128]{1,0:T(8,128)(2,1)S(1)}, u32[]{:S(2)}, u32[]{:S(2)}) collective-permute-start(bf16[304,128]{1,0:T(8,128)(2,1)S(1)} %get-tuple-element.65), channel_id=1, source_target_pairs={{0,16},{1,17},{2,18},{3,19},{4,20},{5,21},{6,22},{7,23},{8,24},{9,... | collective-permute-start | bytes 233480 | tf_op jit(solution)/shard_map/ppermute | solution.py:126
  21.4 7.1 %collective-permute-start.11 = (bf16[304,128]{1,0:T(8,128)(2,1)S(1)}, bf16[304,128]{1,0:T(8,128)(2,1)S(1)}, u32[]{:S(2)}, u32[]{:S(2)}) collective-permute-start(bf16[304,128]{1,0:T(8,128)(2,1)S(1)} %get-tuple-element.66), channel_id=1, source_target_pairs={{0,17},{1,16},{2,19},{3,18},{4,21},{5,20},{6,23},{7,22},{8,25},{9,... | collective-permute-start | bytes 233480 | tf_op jit(solution)/shard_map/ppermute | solution.py:126
  28.6 4.5 %collective-permute-start.12 = (bf16[304,128]{1,0:T(8,128)(2,1)S(1)}, bf16[304,128]{1,0:T(8,128)(2,1)S(1)}, u32[]{:S(2)}, u32[]{:S(2)}) collective-permute-start(bf16[304,128]{1,0:T(8,128)(2,1)S(1)} %shard_map.159.own), channel_id=1, source_target_pairs={{0,2},{1,3},{2,0},{3,1},{4,6},{5,7},{6,4},{7,5},{8,12},{9,13},{10,... | collective-permute-start | bytes 233480 | tf_op jit(solution)/shard_map/ppermute | solution.py:126
  28.7 4.6 %collective-permute-start.4 = (bf16[256,128]{1,0:T(8,128)(2,1)S(1)}, bf16[256,128]{1,0:T(8,128)(2,1)S(1)}, u32[]{:S(2)}, u32[]{:S(2)}) collective-permute-start(bf16[256,128]{1,0:T(8,128)(2,1)S(1)} %get-tuple-element.57), channel_id=1, source_target_pairs={{0,8},{1,9},{2,10},{3,11},{4,12},{5,13},{6,14},{7,15},{8,0},{9,1},... | collective-permute-start | bytes 196616 | tf_op jit(solution)/shard_map/ppermute | solution.py:126
  28.7 5.2 %collective-permute-start.5 = (bf16[256,128]{1,0:T(8,128)(2,1)S(1)}, bf16[256,128]{1,0:T(8,128)(2,1)S(1)}, u32[]{:S(2)}, u32[]{:S(2)}) collective-permute-start(bf16[256,128]{1,0:T(8,128)(2,1)S(1)} %get-tuple-element.58), channel_id=1, source_target_pairs={{0,4},{1,5},{2,6},{3,7},{4,0},{5,1},{6,2},{7,3},{8,16},{9,17},{10,... | collective-permute-start | bytes 196616 | tf_op jit(solution)/shard_map/ppermute | solution.py:126
  33.1 6.4 %collective-permute-start.13 = (bf16[304,128]{1,0:T(8,128)(2,1)S(1)}, bf16[304,128]{1,0:T(8,128)(2,1)S(1)}, u32[]{:S(2)}, u32[]{:S(2)}) collective-permute-start(bf16[304,128]{1,0:T(8,128)(2,1)S(1)} %shard_map.160.own), channel_id=1, source_target_pairs={{0,4},{1,5},{2,6},{3,7},{4,0},{5,1},{6,2},{7,3},{8,10},{9,11},{10,... | collective-permute-start | bytes 233480 | tf_op jit(solution)/shard_map/ppermute | solution.py:126
  34.4 8.7 %collective-permute-start.7 = (bf16[256,128]{1,0:T(8,128)(2,1)S(1)}, bf16[256,128]{1,0:T(8,128)(2,1)S(1)}, u32[]{:S(2)}, u32[]{:S(2)}) collective-permute-start(bf16[256,128]{1,0:T(8,128)(2,1)S(1)} %shard_map.157), channel_id=1, source_target_pairs={{0,7},{1,2},{2,1},{3,4},{4,3},{5,6},{6,5},{7,0},{8,15},{9,10},{10,... | collective-permute-start | bytes 196616 | tf_op jit(solution)/shard_map/ppermute | solution.py:126
  37.2 5.9 %collective-permute-start.6 = (bf16[256,128]{1,0:T(8,128)(2,1)S(1)}, bf16[256,128]{1,0:T(8,128)(2,1)S(1)}, u32[]{:S(2)}, u32[]{:S(2)}) collective-permute-start(bf16[256,128]{1,0:T(8,128)(2,1)S(1)} %shard_map.157), channel_id=1, source_target_pairs={{0,1},{1,0},{2,3},{3,2},{4,5},{5,4},{6,7},{7,6},{8,9},{9,8},{10,11... | collective-permute-start | bytes 196616 | tf_op jit(solution)/shard_map/ppermute | solution.py:126
  39.5 5.7 %collective-permute-start.16 = (bf16[304,128]{1,0:T(8,128)(2,1)S(1)}, bf16[304,128]{1,0:T(8,128)(2,1)S(1)}, u32[]{:S(2)}, u32[]{:S(2)}) collective-permute-start(bf16[304,128]{1,0:T(8,128)(2,1)S(1)} %get-tuple-element.71.refs_0_), channel_id=1, source_target_pairs={{0,17},{1,16},{2,19},{3,18},{4,21},{5,20},{6,23},{7,22},{8,25},{9,... | collective-permute-start | bytes 233480 | tf_op jit(solution)/shard_map/ppermute | solution.py:126
  40.8 4.4 %collective-permute-start.15 = (bf16[304,128]{1,0:T(8,128)(2,1)S(1)}, bf16[304,128]{1,0:T(8,128)(2,1)S(1)}, u32[]{:S(2)}, u32[]{:S(2)}) collective-permute-start(bf16[304,128]{1,0:T(8,128)(2,1)S(1)} %get-tuple-element.71.refs_0_), channel_id=1, source_target_pairs={{0,16},{1,17},{2,18},{3,19},{4,20},{5,21},{6,22},{7,23},{8,24},{9,... | collective-permute-start | bytes 233480 | tf_op jit(solution)/shard_map/ppermute | solution.py:126
  41.9 4.4 %collective-permute-start.14 = (bf16[304,128]{1,0:T(8,128)(2,1)S(1)}, bf16[304,128]{1,0:T(8,128)(2,1)S(1)}, u32[]{:S(2)}, u32[]{:S(2)}) collective-permute-start(bf16[304,128]{1,0:T(8,128)(2,1)S(1)} %get-tuple-element.71.refs_0_), channel_id=1, source_target_pairs={{0,1},{1,0},{2,3},{3,2},{4,5},{5,4},{6,7},{7,6},{8,9},{9,8},{10,11... | collective-permute-start | bytes 233480 | tf_op jit(solution)/shard_map/ppermute | solution.py:126
  46.3 1.7 %collective-permute-start.17 = (bf16[4,304,128]{2,1,0:T(8,128)(2,1)S(1)}, bf16[4,304,128]{2,1,0:T(8,128)(2,1)S(1)}, u32[]{:S(2)}, u32[]{:S(2)}) collective-permute-start(bf16[4,304,128]{2,1,0:T(8,128)(2,1)S(1)} %shard_map.163.own), channel_id=1, source_target_pairs={{0,8},{1,9},{2,10},{3,11},{4,12},{5,13},{6,14},{7,15},{8,0},{9,1},... | collective-permute-start | bytes 933896 | tf_op jit(solution)/shard_map/ppermute | solution.py:126

commit v2 on v1

--- a/solution.py
+++ b/solution.py
@@ -57,15 +57,15 @@
 
 
 class Layout:
-    def __init__(self, lat_count, lon_count, kernel_rows):
+    def __init__(self, lat_count, lon_count, taps, gate_count):
         self.lat, self.lon = lat_count, lon_count
         self.half = lon_count // 2
+        self.taps, self.half_gates = taps, gate_count // 2
         self.plane = lat_count
         whole = [("lon", 1 << k) for k in range(1, lon_count.bit_length() - 1)]
         self.orders = ([("lat", 1)] + whole, [("lat", 1)] + whole[::-1])
-        step = 16 * self.plane
-        self.rows = -(-kernel_rows // step) * step
-        self.half_rows = self.rows // 2
+        step = 8 * self.plane
+        self.half_rows = -(-taps * self.half_gates // step) * step
         self.chunk = self.half_rows // self.plane
 
     def position(self):
@@ -139,6 +139,19 @@
     lane = lanes(row.shape)
     columns = jnp.where(lane == position, rolled(row, position), columns)
     return jnp.where(lane == LAST + position, rolled(row, LAST + position + 1), columns)
+
+
+def second_columns(row, position, columns):
+    lane = lanes(row.shape)
+    columns = jnp.where(lane == position, rolled(row, position - 1), columns)
+    return jnp.where(lane == LAST + position, rolled(row, LAST + position + 2), columns)
+
+
+def at_edges(row, position, columns):
+    lane = lanes(row.shape)
+    width = row.shape[1]
+    row = jnp.where(lane == 0, rolled(columns, -position), row)
+    return jnp.where(lane == width - 1, rolled(columns, width - 1 - LAST - position), row)
 
 
 def pick(flag, yes, no):
@@ -223,6 +236,10 @@
     readout_hbm,
     rows_out,
     columns_out,
+    second_out,
+    cell_strip_out,
+    hidden_grad_strip_out,
+    fields_strip_out,
     cell_out,
     weights_out,
     hidden_grad_out,
@@ -255,31 +272,39 @@
         copy.start()
     row_count, channels, width = rows_out.shape
     columns = jnp.zeros((channels, width), F32)
+    second = jnp.zeros((channels, width), F32)
     for index in range(row_count):
         row = wide[pl.ds(index, channels, stride=row_count), :]
         rows_out[index] = row.astype(BF16)
         columns = edge_columns(row, index + 1, columns)
+        second = second_columns(row, index + 1, second)
     columns_out[...] = columns
+    second_out[...] = second
     for copy in copies:
         copy.wait()
     hidden_grad_out[...] = hidden_grad_here[...].astype(F32).reshape(hidden_grad_out.shape)
     bias_wide_out[...] = down_rows(gate_bias_here[...], width)
     readout_wide_out[...] = down_rows(readout_here[...], width)
+    hid = hidden_grad_here.shape[0]
+    cell_strip = jnp.zeros((hid, width), F32)
+    hidden_grad_strip = jnp.zeros((hid, width), F32)
+    fields_strip = jnp.zeros((8, width), F32)
+    for index in range(row_count):
+        strided = pl.ds(index, hid, stride=row_count)
+        cell_strip = edge_columns(cell_out[strided, :], index + 1, cell_strip)
+        hidden_grad_strip = edge_columns(hidden_grad_out[strided, :], index + 1, hidden_grad_strip)
+        at = slice(index, index + 1)
+        fields = [target_out[at, :], land_out[at, :].astype(F32), fire_out[at, :].astype(F32)]
+        fields = jnp.concatenate(fields + [jnp.zeros((5, width), F32)], axis=0)
+        fields_strip = edge_columns(fields, index + 1, fields_strip)
+    cell_strip_out[...] = cell_strip
+    hidden_grad_strip_out[...] = hidden_grad_strip
+    fields_strip_out[...] = fields_strip
 
 
 def columns_kernel(row_count, columns, inner, outer, out):
     north, south = row_halo(inner, outer)
-    value = edge_columns(north, 0, columns[...])
-    out[...] = edge_columns(south, row_count + 1, value).astype(BF16)
-
-
-def pre_columns_kernel(row_count, pre, inner, outer, out):
-    width = out.shape[1]
-    north, south = row_halo(inner, outer)
-    value = edge_columns(north, 0, jnp.zeros(north.shape, F32))
-    for index in range(row_count):
-        row = pre[:, pl.ds(index * width, width)].astype(F32)
-        value = edge_columns(row, index + 1, value)
+    value = edge_columns(north, 0, columns[...].astype(F32))
     out[...] = edge_columns(south, row_count + 1, value).astype(BF16)
 
 
@@ -292,13 +317,28 @@
     return block[0:8] + block[8:16]
 
 
-def split_sum(place, phase, bias, sums, rows, send_out, keep_out):
-    half = rows // 2
-    rank = place.rank(phase)
-    send_out[0:BIAS_ROWS, :] = encode(bias).astype(BF16)
-    away = pl.ds(pl.multiple_of((1 - rank) * half, 8), half)
-    send_out[BIAS_ROWS:, :] = sums[away, :].astype(BF16)
-    keep_out[...] = sums[pl.ds(pl.multiple_of(rank * half, 8), half), :]
+def cell_step(part, cell_before, hidden_grad, target, land, fire, readout):
+    hid = part.shape[0] // 4
+    input_gate = 0.5 + 0.5 * jnp.tanh(0.5 * part[0:hid])
+    forget_gate = 0.5 + 0.5 * jnp.tanh(0.5 * part[hid : 2 * hid])
+    output_gate = 0.5 + 0.5 * jnp.tanh(0.5 * part[2 * hid : 3 * hid])
+    candidate = jnp.tanh(part[3 * hid : 4 * hid])
+    cell_next = land * (forget_gate * cell_before + input_gate * candidate)
+    squashed = jnp.tanh(cell_next)
+    hidden_next = (output_gate * squashed).astype(BF16).astype(F32)
+    predicted = jnp.sum(readout * hidden_next, axis=0, keepdims=True)
+    total_grad = hidden_grad + 2.0 * (fire * (predicted - target)) * readout
+    cell_grad = land * total_grad * output_gate * (1.0 - squashed * squashed)
+    pre_grad = jnp.concatenate(
+        [
+            cell_grad * candidate * input_gate * (1.0 - input_gate),
+            cell_grad * cell_before * forget_gate * (1.0 - forget_gate),
+            total_grad * squashed * output_gate * (1.0 - output_gate),
+            cell_grad * input_gate * (1.0 - candidate * candidate),
+        ],
+        axis=0,
+    )
+    return hidden_next, cell_next, cell_grad * forget_gate, pre_grad
 
 
 def gates_kernel(
@@ -306,8 +346,7 @@
     rows_in,
     inner_row,
     outer_row,
-    inner_column,
-    outer_column,
+    second,
     cell_prev,
     weights,
     hidden_grad,
@@ -316,47 +355,41 @@
     fire,
     bias_wide,
     readout_wide,
-    hidden_hbm,
-    cell_hbm,
-    grad_cell_hbm,
+    hidden_out,
+    cell_out,
+    grad_cell_out,
     pre_out,
-    inner_out,
-    outer_out,
-    send_out,
-    keep_out,
+    second_out,
+    sums,
     bias_out,
     shifted,
-    hidden_wide,
-    hidden_low,
-    cell_out,
-    grad_cell_out,
-    sums,
-    left,
 ):
     row_count, channels, width = rows_in.shape
     gate_count = weights.shape[1]
     hid = gate_count // 4
-
-    def emit(position, left, row, right):
+    half_gates = place.half_gates
+    north, south = row_halo(inner_row, outer_row)
+    columns = second_columns(north, 0, second[...])
+    second_out[...] = second_columns(south, row_count + 1, columns).astype(BF16)
+    for position in range(row_count + 2):
+        if position == 0:
+            row = north
+        elif position == row_count + 1:
+            row = south
+        else:
+            row = rows_in[position - 1].astype(F32)
         at = pl.ds(position * width, width)
-        shifted[0:channels, at] = left.astype(BF16)
+        shifted[0:channels, at] = rolled(row, 1).astype(BF16)
         shifted[channels : 2 * channels, at] = row.astype(BF16)
-        shifted[2 * channels : 3 * channels, at] = right.astype(BF16)
-
-    widened(
-        row_count,
-        lambda index: rows_in[index].astype(F32),
-        (inner_row, outer_row),
-        (inner_column, outer_column),
-        emit,
-    )
+        shifted[2 * channels : 3 * channels, at] = rolled(row, -1).astype(BF16)
 
     taps = [
         jnp.concatenate([weights[3 * a], weights[3 * a + 1], weights[3 * a + 2]], axis=1)
         for a in range(3)
     ]
     bias_total = jnp.zeros((gate_count, width), F32)
-    edges = []
+    lane = lanes((gate_count, width))
+    inside = (lane > 0) & (lane < width - 1)
     readout = readout_wide[...]
     pair = 2 if row_count % 2 == 0 else 1
     for base in range(0, row_count, pair):
@@ -370,47 +403,23 @@
         for offset in range(pair):
             index = base + offset
             strided = pl.ds(index, hid, stride=row_count)
-            part = preact[:, offset * width : (offset + 1) * width] + bias_wide[...]
-            input_gate = 0.5 + 0.5 * jnp.tanh(0.5 * part[0:hid])
-            forget_gate = 0.5 + 0.5 * jnp.tanh(0.5 * part[hid : 2 * hid])
-            output_gate = 0.5 + 0.5 * jnp.tanh(0.5 * part[2 * hid : 3 * hid])
-            candidate = jnp.tanh(part[3 * hid : 4 * hid])
-            cell_before = cell_prev[strided, :]
-            land_row = land[index : index + 1, :].astype(F32)
-            fire_row = fire[index : index + 1, :].astype(F32)
-            cell_next = land_row * (forget_gate * cell_before + input_gate * candidate)
-            squashed = jnp.tanh(cell_next)
-            hidden_next = (output_gate * squashed).astype(BF16).astype(F32)
-            predicted = jnp.sum(readout * hidden_next, axis=0, keepdims=True)
-            miss = 2.0 * (fire_row * (predicted - target[index : index + 1, :]))
-            total_grad = hidden_grad[strided, :] + miss * readout
-            cell_grad = land_row * total_grad * output_gate * (1.0 - squashed * squashed)
+            at = slice(index, index + 1)
+            hidden_next, cell_next, grad_cell, pre_grad = cell_step(
+                preact[:, offset * width : (offset + 1) * width] + bias_wide[...],
+                cell_prev[strided, :],
+                hidden_grad[strided, :],
+                target[at, :],
+                land[at, :].astype(F32),
+                fire[at, :].astype(F32),
+                readout,
+            )
+            hidden_out[strided, :] = hidden_next
             cell_out[strided, :] = cell_next
-            hidden_wide[strided, :] = hidden_next
-            grad_cell_out[strided, :] = cell_grad * forget_gate
-            pre_grad = jnp.concatenate(
-                [
-                    cell_grad * candidate * input_gate * (1.0 - input_gate),
-                    cell_grad * cell_before * forget_gate * (1.0 - forget_gate),
-                    total_grad * squashed * output_gate * (1.0 - output_gate),
-                    cell_grad * input_gate * (1.0 - candidate * candidate),
-                ],
-                axis=0,
-            )
+            grad_cell_out[strided, :] = grad_cell
+            pre_grad = jnp.where(inside, pre_grad, 0.0)
             bias_total += pre_grad
             pre_out[:, pl.ds(index * width, width)] = pre_grad.astype(BF16)
-            if index in (0, row_count - 1):
-                edges.append(pre_grad)
-    hidden_low[...] = hidden_wide[...].reshape(hidden_low.shape).astype(BF16)
-    leaving = [
-        pltpu.make_async_copy(source, target, left.at[index])
-        for index, (source, target) in enumerate(
-            ((hidden_low, hidden_hbm), (cell_out, cell_hbm), (grad_cell_out, grad_cell_hbm))
-        )
-    ]
-    for copy in leaving:
-        copy.start()
-    row_sends(edges[0], edges[-1], inner_out, outer_out)
+    bias_out[...] = bias_total
 
     for a in range(3):
         product = lax.dot_general(
@@ -420,12 +429,94 @@
             preferred_element_type=F32,
         )
         for b in range(3):
-            at = (3 * a + b) * gate_count
-            sums[at : at + gate_count, :] = product[:, b * channels : (b + 1) * channels]
-    used = 9 * gate_count
-    if place.rows > used:
-        sums[used:, :] = jnp.zeros((place.rows - used, channels), F32)
-
+            for half in range(2):
+                at = half * place.half_rows + (3 * a + b) * half_gates
+                sums[at : at + half_gates, :] = product[
+                    half * half_gates : (half + 1) * half_gates, b * channels : (b + 1) * channels
+                ]
+    used = place.taps * half_gates
+    if place.half_rows > used:
+        for half in range(2):
+            at = half * place.half_rows
+            sums[at + used : at + place.half_rows, :] = jnp.zeros(
+                (place.half_rows - used, channels), F32
+            )
+
+
+def add_strip(place, half, sums, pre_strip, patches, out, start):
+    half_gates, channels = place.half_gates, sums.shape[1]
+    gates = pre_strip[pl.ds(pl.multiple_of(half * half_gates, half_gates), half_gates), :]
+    product = lax.dot_general(gates, patches[...], ACROSS, preferred_element_type=F32)
+    base = half * place.half_rows
+    for tap in range(place.taps):
+        at = pl.ds(pl.multiple_of(base + tap * half_gates, 8), half_gates)
+        value = sums[at, :] + product[:, tap * channels : (tap + 1) * channels]
+        to = start + tap * half_gates
+        out[to : to + half_gates, :] = value.astype(out.dtype)
+    used = place.taps * half_gates
+    if place.half_rows > used:
+        rest = jnp.zeros((place.half_rows - used, channels), out.dtype)
+        out[start + used : start + place.half_rows, :] = rest
+
+
+def strip_kernel(
+    place,
+    row_count,
+    edge,
+    second,
+    inner_column,
+    outer_column,
+    weights,
+    bias_wide,
+    readout_wide,
+    cell_strip,
+    hidden_grad_strip,
+    fields_strip,
+    sums,
+    bias_partial,
+    send_out,
+    bias_out,
+    pre_out,
+    patches,
+    hidden_out,
+    cell_out,
+    grad_cell_out,
+):
+    channels, width = edge.shape
+    west, east = column_halo(inner_column, outer_column)
+    near_first = lanes((channels, width)) < LAST
+    inner = second[...].astype(F32)
+    columns = (
+        jnp.where(near_first, rolled(west, -LAST), inner),
+        edge[...].astype(F32),
+        jnp.where(near_first, inner, rolled(east, LAST)),
+    )
+    for a in range(3):
+        for b in range(3):
+            at = (3 * a + b) * channels
+            patches[at : at + channels, :] = rolled(columns[b], 1 - a).astype(BF16)
+    taps = jnp.concatenate([weights[tap] for tap in range(place.taps)], axis=1)
+    preact = jnp.dot(taps, patches[...], preferred_element_type=F32) + bias_wide[...]
+    hidden_next, cell_next, grad_cell, pre_grad = cell_step(
+        preact,
+        cell_strip[...],
+        hidden_grad_strip[...],
+        fields_strip[0:1, :],
+        fields_strip[1:2, :],
+        fields_strip[2:3, :],
+        readout_wide[...],
+    )
+    hidden_out[...] = hidden_next
+    cell_out[...] = cell_next
+    grad_cell_out[...] = grad_cell
+    lane = lanes(pre_grad.shape)
+    lane = jnp.where(lane >= LAST, lane - LAST, lane)
+    pre_grad = jnp.where((lane >= 1) & (lane <= row_count), pre_grad, 0.0)
+    pre_out[...] = pre_grad.astype(BF16)
+    rank = place.rank(0)
+    add_strip(place, 1 - rank, sums, pre_out, patches, send_out, BIAS_ROWS)
+
+    bias_total = bias_partial[...] + pre_grad
     ones = jnp.ones((8, width), BF16)
     high = bias_total.astype(BF16)
     low = (bias_total - high.astype(F32)).astype(BF16)
@@ -434,9 +525,66 @@
     odd = lax.broadcasted_iota(jnp.int32, (8, channels), 0) % 2 == 1
     bias_rows = jnp.where(odd, flat[:, channels : 2 * channels], flat[:, 0:channels])
     bias_out[...] = bias_rows
-    split_sum(place, 0, bias_rows, sums, place.rows, send_out, keep_out)
+    send_out[0:BIAS_ROWS, :] = encode(bias_rows).astype(BF16)
+
+
+def keep_kernel(place, sums, pre_strip, patches, out):
+    add_strip(place, place.rank(0), sums, pre_strip, patches, out, 0)
+
+
+def edges_kernel(
+    row_count,
+    hidden,
+    cell,
+    grad_cell,
+    pre,
+    hidden_strip,
+    cell_strip,
+    grad_cell_strip,
+    pre_strip,
+    hidden_hbm,
+    cell_hbm,
+    grad_cell_hbm,
+    pre_out,
+    inner_out,
+    outer_out,
+    hidden_low,
+    cell_here,
+    grad_cell_here,
+    left,
+):
+    hid, _, width = hidden_low.shape
+    pairs = (
+        (cell, cell_strip, cell_here, cell_hbm),
+        (grad_cell, grad_cell_strip, grad_cell_here, grad_cell_hbm),
+    )
+    leaving = []
+    for source, strip, here, target in pairs:
+        columns = strip[...]
+        for index in range(row_count):
+            strided = pl.ds(index, hid, stride=row_count)
+            here[strided, :] = at_edges(source[strided, :], index + 1, columns)
+        leaving.append(pltpu.make_async_copy(here, target, left.at[len(leaving)]))
+        leaving[-1].start()
+    first, last = None, None
+    columns = pre_strip[...].astype(F32)
+    for index in range(row_count):
+        at = pl.ds(index * width, width)
+        row = at_edges(pre[:, at].astype(F32), index + 1, columns)
+        pre_out[:, at] = row.astype(BF16)
+        first = row if index == 0 else first
+        last = row
+    row_sends(first, last, inner_out, outer_out)
     for copy in leaving:
         copy.wait()
+    columns = hidden_strip[...]
+    for index in range(row_count):
+        strided = pl.ds(index, hid, stride=row_count)
+        cell_here[strided, :] = at_edges(hidden[strided, :], index + 1, columns)
+    hidden_low[...] = cell_here[...].reshape(hidden_low.shape).astype(BF16)
+    copy = pltpu.make_async_copy(hidden_low, hidden_hbm, left.at[2])
+    copy.start()
+    copy.wait()
 
 
 def pair_kernel(place, keep, bias, received, *outs):
@@ -446,7 +594,7 @@
     scratch[...] = keep[...] + received[BIAS_ROWS:, :].astype(F32)
     bias_total = bias[...] + decode(received[0:BIAS_ROWS, :].astype(F32))
     block = encode(bias_total).astype(BF16)
-    for step, send in enumerate(sends, 1):
+    for step, send in zip(range(place.plane - 1, 0, -1), sends):
         send[0:BIAS_ROWS, :] = block
         at = pl.ds(pl.multiple_of((rank ^ step) * chunk, 8), chunk)
         send[BIAS_ROWS:, :] = scratch[at, :].astype(BF16)
@@ -455,7 +603,7 @@
 
 
 def plane_kernel(keep, bias, *refs):
-    received, out = refs[:-1], refs[-1]
+    received, out = refs[:-2], refs[-1]
     total, bias_total = keep[...], bias[...]
     for ref in received:
         total += ref[BIAS_ROWS:, :].astype(F32)
@@ -480,18 +628,23 @@
         done[...] = jnp.zeros(done.shape, F32)
 
 
-def unpack(blocks, wide):
-    chunk = blocks.shape[1] - BIAS_ROWS
-    for index in range(blocks.shape[0]):
+def store_half(place, half, blocks, out, wide, left):
+    chunk, half_gates = place.chunk, place.half_gates
+    gates = pl.ds(pl.multiple_of(half * half_gates, half_gates), half_gates)
+    copies = []
+    for index in range(place.plane):
         wide[index * chunk : (index + 1) * chunk, :] = blocks[index, BIAS_ROWS:, :].astype(F32)
+        while len(copies) < min(place.taps, (index + 1) * chunk // half_gates):
+            tap = len(copies)
+            source = wide.at[tap * half_gates : (tap + 1) * half_gates, :]
+            copies.append(pltpu.make_async_copy(source, out.at[tap, gates, :], left.at[tap]))
+            copies[-1].start()
+    return copies
 
 
 def own_half_kernel(place, own, out, wide, left):
-    unpack(own, wide)
-    at = pl.ds(pl.multiple_of(place.rank(0) * place.half_rows, 8), place.half_rows)
-    copy = pltpu.make_async_copy(wide, out.at[at, :], left.at[0])
-    copy.start()
-    copy.wait()
+    for copy in store_half(place, place.rank(0), own, out, wide, left):
+        copy.wait()
 
 
 def other_half_kernel(place, own, received, out_before, out, bias_out, wide, bias_here, left):
@@ -502,14 +655,12 @@
     width = bias.shape[1]
     for index in range(bias_here.shape[0] // width):
         bias_here[pl.ds(index * width, width)] = bias[index]
-    bias_copy = pltpu.make_async_copy(bias_here, bias_out, left.at[1])
+    bias_copy = pltpu.make_async_copy(bias_here, bias_out, left.at[place.taps])
     bias_copy.start()
-    unpack(received, wide)
-    at = pl.ds(pl.multiple_of((1 - rank) * place.half_rows, 8), place.half_rows)
-    copy = pltpu.make_async_copy(wide, out.at[at, :], left.at[0])
-    copy.start()
+    copies = store_half(place, 1 - rank, received, out, wide, left)
     bias_copy.wait()
-    copy.wait()
+    for copy in copies:
+        copy.wait()
 
 
 def field_kernel(
@@ -606,6 +757,7 @@
     inner_columns = place.pairs(place.inner_columns)
     outer_columns = place.pairs(place.outer_columns)
     flat = sds((hid * row_count, width), F32)
+    strip = sds((hid, width), F32)
 
     inner, outer, wide = call(
         pack_kernel,
@@ -626,6 +778,10 @@
     (
         rows,
         columns,
+        second,
+        cell_strip,
+        hidden_grad_strip,
+        fields_strip,
         cell_here,
         weights_here,
         hidden_grad_here,
@@ -639,6 +795,10 @@
         (
             sds((row_count, channels, width), BF16),
             sds((channels, width), F32),
+            sds((channels, width), F32),
+            strip,
+            strip,
+            sds((8, width), F32),
             flat,
             sds(kernel_weights.shape, BF16),
             flat,
@@ -667,52 +827,30 @@
         gate_bias,
         readout,
     )
-    columns = call(bind(columns_kernel, row_count), sds((channels, width), BF16))(
+    edge = call(bind(columns_kernel, row_count), sds((channels, width), BF16))(
         columns, inner, outer
     )
-
-    (
-        hidden_next,
-        cell_next,
-        grad_cell,
-        pre,
-        pre_inner,
-        pre_outer,
-        send,
-        keep,
-        bias,
-    ) = call(
+    inner_column, outer_column = permuted(edge, inner_columns), permuted(edge, outer_columns)
+    hidden_rows, cell_rows, grad_cell_rows, pre, second, sums, bias = call(
         bind(gates_kernel, place),
         (
-            sds((hid, row_count, width), BF16),
+            flat,
             flat,
             flat,
             sds((gate_count, cells), BF16),
-            sds((gate_count, width), BF16),
-            sds((gate_count, width), BF16),
-            sds((BIAS_ROWS + place.half_rows, channels), BF16),
-            sds((place.half_rows, channels), F32),
-            sds((8, channels), F32),
+            sds((channels, width), BF16),
+            sds((2 * place.half_rows, channels), F32),
+            sds((gate_count, width), F32),
         ),
-        [
-            pltpu.VMEM((3 * channels, halo_cells), BF16),
-            pltpu.VMEM((hid * row_count, width), F32),
-            pltpu.VMEM((hid, row_count, width), BF16),
-            pltpu.VMEM((hid * row_count, width), F32),
-            pltpu.VMEM((hid * row_count, width), F32),
-            pltpu.VMEM((place.rows, channels), F32),
-            pltpu.SemaphoreType.DMA((3,)),
-        ],
-        leaving=3,
+        [pltpu.VMEM((3 * channels, halo_cells), BF16)],
         flops=4 * 9 * gate_count * channels * cells,
-        moved=4_000_000,
+        moved=6_000_000,
         transcendentals=5 * hid * cells,
     )(
         rows,
         inner,
         outer,
-        permuted(columns, inner_columns),
-        permuted(columns, outer_columns),
+        second,
         cell_here,
         weights_here,
         hidden_grad_here,
@@ -722,21 +860,69 @@
         bias_wide,
         readout_wide,
     )
-
+    send, bias, pre_strip, patches, *strips = call(
+        bind(strip_kernel, place, row_count),
+        (
+            sds((BIAS_ROWS + place.half_rows, channels), BF16),
+            sds((8, channels), F32),
+            sds((gate_count, width), BF16),
+            sds((place.taps * channels, width), BF16),
+            strip,
+            strip,
+            strip,
+        ),
+    )(
+        edge,
+        second,
+        inner_column,
+        outer_column,
+        weights_here,
+        bias_wide,
+        readout_wide,
+        cell_strip,
+        hidden_grad_strip,
+        fields_strip,
+        sums,
+        bias,
+    )
+    keep = call(bind(keep_kernel, place), sds((place.half_rows, channels), F32))(
+        sums, pre_strip, patches
+    )
+    hidden_next, cell_next, grad_cell, pre, pre_inner, pre_outer = call(
+        bind(edges_kernel, row_count),
+        (
+            sds((hid, row_count, width), BF16),
+            flat,
+            flat,
+            sds((gate_count, cells), BF16),
+            sds((gate_count, width), BF16),
+            sds((gate_count, width), BF16),
+        ),
+        [
+            pltpu.VMEM((hid, row_count, width), BF16),
+            pltpu.VMEM(flat.shape, F32),
+            pltpu.VMEM(flat.shape, F32),
+            pltpu.SemaphoreType.DMA((3,)),
+        ],
+        leaving=3,
+        moved=4_000_000,
+    )(hidden_rows, cell_rows, grad_cell_rows, pre, *strips, pre_strip)
+    after = pre_inner
     pre_inner, pre_outer = permuted(pre_inner, inner_rows), permuted(pre_outer, outer_rows)
-    pre_columns = call(bind(pre_columns_kernel, row_count), sds((gate_count, width), BF16))(
-        pre, pre_inner, pre_outer
-    )
+    pre_columns = call(bind(columns_kernel, row_count), sds((gate_count, width), BF16))(
+        pre_strip, pre_inner, pre_outer
+    )
+
     block = sds((BIAS_ROWS + place.chunk, channels), BF16)
     token = sds((8, width), F32)
-    steps = range(1, place.plane)
+    steps = range(place.plane - 1, 0, -1)
     *sends, keep, bias = call(
         bind(pair_kernel, place),
         (*[block for _ in steps], sds((place.chunk, channels), F32), sds((8, channels), F32)),
         [pltpu.VMEM((place.half_rows, channels), F32)],
     )(keep, bias, permuted(send, place.phase_pairs(0)))
     received = [permuted(send, place.plane_pairs(step)) for step, send in zip(steps, sends)]
-    part = call(plane_kernel, block)(keep, bias, *received)
+    part = call(plane_kernel, block)(keep, bias, *received, after)
     pre_inner_columns = permuted(pre_columns, inner_columns)
     pre_outer_columns = permuted(pre_columns, outer_columns)
     phases = len(place.orders[0])
@@ -768,7 +954,7 @@
         weights_here,
         *summed,
     )
-    received = [permuted(part, place.plane_pairs(step)) for step in steps]
+    received = [permuted(part, place.plane_pairs(step)) for step in steps[::-1]]
     gathered = call(bind(join_kernel, place), sds((place.plane, *block.shape), BF16))(
         part, *received, field_done
     )
@@ -776,15 +962,15 @@
     half = [pltpu.VMEM((place.half_rows, channels), F32)]
     grad_kernel = call(
         bind(own_half_kernel, place),
-        (sds((place.rows, channels), F32),),
-        half + [pltpu.SemaphoreType.DMA((1,))],
+        (sds(kernel_weights.shape, F32),),
+        half + [pltpu.SemaphoreType.DMA((place.taps,))],
         leaving=1,
         moved=6 * place.half_rows * channels,
     )(gathered)[0]
     grad_kernel, grad_bias = call(
         bind(other_half_kernel, place),
-        (sds((place.rows, channels), F32), sds((gate_count,), F32)),
-        half + [pltpu.VMEM((gate_count,), F32), pltpu.SemaphoreType.DMA((2,))],
+        (sds(kernel_weights.shape, F32), sds((gate_count,), F32)),
+        half + [pltpu.VMEM((gate_count,), F32), pltpu.SemaphoreType.DMA((place.taps + 1,))],
         remote=1,
         leaving=2,
         aliases={2: 0},
@@ -797,7 +983,7 @@
         grad_inputs,
         grad_hidden,
         grad_cell.reshape(shape),
-        grad_kernel[: 9 * gate_count].reshape(kernel_weights.shape),
+        grad_kernel,
         grad_bias,
     )
 
@@ -809,7 +995,7 @@
     flat = P(("band", "core"), ("reach", "near"))
 
     def run(*args):
-        place = Layout(lat_count, lon_count, args[3].shape[0] * args[3].shape[1])
+        place = Layout(lat_count, lon_count, *args[3].shape[:2])
         return jax.shard_map(
             functools.partial(body, place),
             mesh=split,

time: 49 us -> 47.3 us (0.965)
  waiting for transfers between devices: 15.6 us -> 6.23 us
  starting transfers between devices: 22.9 us -> 27.3 us
  Pallas kernels: 9.62 us -> 12.8 us
    ppermute x18, waiting for transfers between devices: 15.6 us -> 6.23 us  [permuted(): return lax.ppermute(value, AXES, pairs)]
    ppermute x18, starting transfers between devices: 22.9 us -> 27.3 us  [permuted(): return lax.ppermute(value, AXES, pairs)]
    pallas_call x13 -> x16, Pallas kernels: 9.62 us -> 12.8 us  [run(): pl.pallas_call(kernel, out_shape=out_shape, in_specs=[VMEM] * near + [HBM...]
  transfers between devices with their start and end apart: 18 -> 18, of which waited for: 12 -> 8; matrix products, arithmetic and copies ran while one was open for 0% -> 0% of each run, Pallas kernels for 10% -> 21%
where the time goes in v2:
time: 47.3 us; the launch traced here: 47.1 us
  starting transfers between devices  27.3 us (58%)
  Pallas kernels  12.8 us (27%)
  waiting for transfers between devices  6.23 us (13%)
  between operations  0.8 us (2%)
    ppermute x18, starting transfers between devices, permuted(): return lax.ppermute(value, AXES, pairs)  27.3 us
    pallas_call x16, Pallas kernels, run(): pl.pallas_call(kernel, out_shape=out_shape, in_specs=[VMEM] * near + [HBM...  12.8 us
    ppermute x18, waiting for transfers between devices, permuted(): return lax.ppermute(value, AXES, pairs)  6.23 us
  transfers between devices with their start and end apart: 18, of which 8 were waited for; matrix products, arithmetic and copies ran while one was open for 0% of the time, Pallas kernels for 21%

profile of v2, /device:TPU:0, one launch (start us, length us, event | category | flops | bytes accessed | tf_op | source)
XLA Modules:
  0.0 47.1 jit_solution(12869950334626251212)
XLA Ops:
  0.6 1.0 %shard_map.153 = (bf16[128,128]{1,0:T(8,128)(2,1)S(1)}, bf16[128,128]{1,0:T(8,128)(2,1)S(1)}, f32[1024,128]{1,0:T(8,128)S(1)}) custom-call(bf16[64,8,128]{2,1,0:T(8,128)(2,1)} %below.1, bf16[64,8,128]{2,1,0:T(8,128)(2,1)} %hidden.1), custom_call_target="tpu_custom_call" | custom-call | bytes 524288 | tf_op jit(solution)/shard_map/pallas_call | solution.py:43
  1.7 0.5 %collective-permute-start = (bf16[128,128]{1,0:T(8,128)(2,1)S(1)}, bf16[128,128]{1,0:T(8,128)(2,1)S(1)}, u32[]{:S(2)}, u32[]{:S(2)}) collective-permute-start(bf16[128,128]{1,0:T(8,128)(2,1)S(1)} %get-tuple-element.58), channel_id=1, source_target_pairs={{0,8},{1,9},{2,10},{3,11},{4,12},{5,13},{6,14},{7,15},{8,0},{9,1},... | collective-permute-start | bytes 98312 | tf_op jit(solution)/shard_map/ppermute | solution.py:126
  2.2 3.7 %collective-permute-start.1 = (bf16[128,128]{1,0:T(8,128)(2,1)S(1)}, bf16[128,128]{1,0:T(8,128)(2,1)S(1)}, u32[]{:S(2)}, u32[]{:S(2)}) collective-permute-start(bf16[128,128]{1,0:T(8,128)(2,1)S(1)} %get-tuple-element.59), channel_id=1, source_target_pairs={{0,4},{1,5},{2,6},{3,7},{4,0},{5,1},{6,2},{7,3},{8,16},{9,17},{10,... | collective-permute-start | bytes 98312 | tf_op jit(solution)/shard_map/ppermute | solution.py:126
  5.8 2.2 %shard_map.154 = (bf16[8,128,128]{2,1,0:T(8,128)(2,1)S(1)}, f32[128,128]{1,0:T(8,128)S(1)}, f32[128,128]{1,0:T(8,128)S(1)}, f32[64,128]{1,0:T(8,128)S(1)}, f32[6...) custom-call(f32[1024,128]{1,0:T(8,128)S(1)} %get-tuple-element.56.wi, ...), custom_call_target="tpu_custom_call" | custom-call | bytes 6000000 | tf_op jit(solution)/shard_map/pallas_call | solution.py:43
  8.0 0.0 collective-permute-done.inner_row.inner
  8.0 0.0 collective-permute-done.1.outer_row.outer
  8.0 0.1 shard_map.156.edge
  8.2 1.6 %collective-permute-start.2 = (bf16[128,128]{1,0:T(8,128)(2,1)S(1)}, bf16[128,128]{1,0:T(8,128)(2,1)S(1)}, u32[]{:S(2)}, u32[]{:S(2)}) collective-permute-start(bf16[128,128]{1,0:T(8,128)(2,1)S(1)} %shard_map.156.edge), channel_id=1, source_target_pairs={{0,1},{1,0},{2,3},{3,2},{4,5},{5,4},{6,7},{7,6},{8,9},{9,8},{10,11... | collective-permute-start | bytes 98312 | tf_op jit(solution)/shard_map/ppermute | solution.py:126
  9.8 3.8 %collective-permute-start.3 = (bf16[128,128]{1,0:T(8,128)(2,1)S(1)}, bf16[128,128]{1,0:T(8,128)(2,1)S(1)}, u32[]{:S(2)}, u32[]{:S(2)}) collective-permute-start(bf16[128,128]{1,0:T(8,128)(2,1)S(1)} %shard_map.156.edge), channel_id=1, source_target_pairs={{0,7},{1,2},{2,1},{3,4},{4,3},{5,6},{6,5},{7,0},{8,15},{9,10},{10,... | collective-permute-start | bytes 98312 | tf_op jit(solution)/shard_map/ppermute | solution.py:126
  13.5 2.2 %shard_map.155 = (f32[512,128]{1,0:T(8,128)S(1)}, f32[512,128]{1,0:T(8,128)S(1)}, f32[512,128]{1,0:T(8,128)S(1)}, bf16[256,1024]{1,0:T(8,128)(2,1)S(1)}, bf16[12...) custom-call(bf16[8,128,128]{2,1,0:T(8,128)(2,1)S(1)} %get-tuple-element.57.rows_in, ...), custom_call_target="tpu_custom_call" | custom-call | flops 1207959552 | bytes 6000000 | tf_op jit(solution)/shard_map/pallas_call | solution.py:43
  15.8 0.0 collective-permute-done.2.inner_column
  15.8 0.6 %collective-permute-done.3.outer_column = bf16[128,128]{1,0:T(8,128)(2,1)S(1)} collective-permute-done((bf16[128,128]{1,0:T(8,128)(2,1)S(1)}, bf16[128,128]{1,0:T(8,128)(2,1)S(1)}, u32[]{:S(2)}, u32[]{:S(2)}) %collective-permute-start.3) | collective-permute-done | bytes 32800 | tf_op jit(solution)/shard_map/ppermute | solution.py:126
  16.4 0.8 %shard_map.157 = (bf16[1168,128]{1,0:T(8,128)(2,1)S(1)}, f32[8,128]{1,0:T(8,128)S(1)}, bf16[256,128]{1,0:T(8,128)(2,1)S(1)}, bf16[1152,128]{1,0:T(8,128)(2,1)S(1...) custom-call(bf16[128,128]{1,0:T(8,128)(2,1)S(1)} %shard_map.156.edge, ...), custom_call_target="tpu_custom_call" | custom-call | tf_op jit(solution)/shard_map/pallas_call | solution.py:43
  17.2 0.1 collective-permute-start.8
  17.3 0.2 shard_map.160.keep
  17.5 1.3 %collective-permute-done.8.received = bf16[1168,128]{1,0:T(8,128)(2,1)S(1)} collective-permute-done((bf16[1168,128]{1,0:T(8,128)(2,1)S(1)}, bf16[1168,128]{1,0:T(8,128)(2,1)S(1)}, u32[]{:S(2)}, u32[]{:S(2)}) %collective-permute-start.8) | collective-permute-done | bytes 299040 | tf_op jit(solution)/shard_map/ppermute | solution.py:126
  18.8 0.1 shard_map.161
  18.9 0.1 collective-permute-start.10
  19.0 0.1 collective-permute-start.11
  19.1 3.4 %collective-permute-start.9 = (bf16[304,128]{1,0:T(8,128)(2,1)S(1)}, bf16[304,128]{1,0:T(8,128)(2,1)S(1)}, u32[]{:S(2)}, u32[]{:S(2)}) collective-permute-start(bf16[304,128]{1,0:T(8,128)(2,1)S(1)} %get-tuple-element.94), channel_id=1, source_target_pairs={{0,17},{1,16},{2,19},{3,18},{4,21},{5,20},{6,23},{7,22},{8,25},{9,... | collective-permute-start | bytes 233480 | tf_op jit(solution)/shard_map/ppermute | solution.py:126
  22.5 2.0 %shard_map.158 = (bf16[64,8,128]{2,1,0:T(8,128)(2,1)}, f32[512,128]{1,0:T(8,128)}, f32[512,128]{1,0:T(8,128)}, bf16[256,1024]{1,0:T(8,128)(2,1)S(1)}, bf16[256,1...) custom-call(f32[512,128]{1,0:T(8,128)S(1)} %get-tuple-element.69.hidden, f32[512,128]{1,0:T(8,128)S(1)} %get-tuple-element.70.cell, ...), custom_call_target="tpu_custom_call" | custom-call | bytes 4000000 | tf_op jit(solution)/shard_map/pallas_call | solution.py:43
  24.5 0.0 collective-permute-done.10.refs_1_
  24.5 0.7 %collective-permute-done.11.refs_2_ = bf16[304,128]{1,0:T(8,128)(2,1)S(1)} collective-permute-done((bf16[304,128]{1,0:T(8,128)(2,1)S(1)}, bf16[304,128]{1,0:T(8,128)(2,1)S(1)}, u32[]{:S(2)}, u32[]{:S(2)}) %collective-permute-start.11) | collective-permute-done | bytes 77856 | tf_op jit(solution)/shard_map/ppermute | solution.py:126
  25.2 0.0 collective-permute-done.9.refs_0_
  25.2 0.1 collective-permute-start.12
  25.3 0.1 collective-permute-start.4
  25.4 4.2 %collective-permute-start.5 = (bf16[256,128]{1,0:T(8,128)(2,1)S(1)}, bf16[256,128]{1,0:T(8,128)(2,1)S(1)}, u32[]{:S(2)}, u32[]{:S(2)}) collective-permute-start(bf16[256,128]{1,0:T(8,128)(2,1)S(1)} %get-tuple-element.88), channel_id=1, source_target_pairs={{0,4},{1,5},{2,6},{3,7},{4,0},{5,1},{6,2},{7,3},{8,16},{9,17},{10,... | collective-permute-start | bytes 196616 | tf_op jit(solution)/shard_map/ppermute | solution.py:126
  29.5 0.1 collective-permute-done.12.received
  29.7 2.3 %collective-permute-start.13 = (bf16[304,128]{1,0:T(8,128)(2,1)S(1)}, bf16[304,128]{1,0:T(8,128)(2,1)S(1)}, u32[]{:S(2)}, u32[]{:S(2)}) collective-permute-start(bf16[304,128]{1,0:T(8,128)(2,1)S(1)} %shard_map.163.own), channel_id=1, source_target_pairs={{0,4},{1,5},{2,6},{3,7},{4,0},{5,1},{6,2},{7,3},{8,10},{9,11},{10,... | collective-permute-start | bytes 233480 | tf_op jit(solution)/shard_map/ppermute | solution.py:126
  32.0 0.0 collective-permute-done.4.inner.inner_row
  32.0 0.0 collective-permute-done.5.outer.outer_row
  32.0 0.1 shard_map.159
  32.1 0.7 %collective-permute-start.6 = (bf16[256,128]{1,0:T(8,128)(2,1)S(1)}, bf16[256,128]{1,0:T(8,128)(2,1)S(1)}, u32[]{:S(2)}, u32[]{:S(2)}) collective-permute-start(bf16[256,128]{1,0:T(8,128)(2,1)S(1)} %shard_map.159), channel_id=1, source_target_pairs={{0,1},{1,0},{2,3},{3,2},{4,5},{5,4},{6,7},{7,6},{8,9},{9,8},{10,11... | collective-permute-start | bytes 196616 | tf_op jit(solution)/shard_map/ppermute | solution.py:126
  32.9 3.1 %collective-permute-start.7 = (bf16[256,128]{1,0:T(8,128)(2,1)S(1)}, bf16[256,128]{1,0:T(8,128)(2,1)S(1)}, u32[]{:S(2)}, u32[]{:S(2)}) collective-permute-start(bf16[256,128]{1,0:T(8,128)(2,1)S(1)} %shard_map.159), channel_id=1, source_target_pairs={{0,7},{1,2},{2,1},{3,4},{4,3},{5,6},{6,5},{7,0},{8,15},{9,10},{10,... | collective-permute-start | bytes 196616 | tf_op jit(solution)/shard_map/ppermute | solution.py:126
  35.9 0.0 collective-permute-done.13.received
  36.0 2.1 %collective-permute-start.14 = (bf16[304,128]{1,0:T(8,128)(2,1)S(1)}, bf16[304,128]{1,0:T(8,128)(2,1)S(1)}, u32[]{:S(2)}, u32[]{:S(2)}) collective-permute-start(bf16[304,128]{1,0:T(8,128)(2,1)S(1)} %get-tuple-element.101.refs_0_), channel_id=1, source_target_pairs={{0,1},{1,0},{2,3},{3,2},{4,5},{5,4},{6,7},{7,6},{8,9},{9,8},{10,11... | collective-permute-start | bytes 233480 | tf_op jit(solution)/shard_map/ppermute | solution.py:126
  38.1 1.1 %collective-permute-start.15 = (bf16[304,128]{1,0:T(8,128)(2,1)S(1)}, bf16[304,128]{1,0:T(8,128)(2,1)S(1)}, u32[]{:S(2)}, u32[]{:S(2)}) collective-permute-start(bf16[304,128]{1,0:T(8,128)(2,1)S(1)} %get-tuple-element.101.refs_0_), channel_id=1, source_target_pairs={{0,16},{1,17},{2,18},{3,19},{4,20},{5,21},{6,22},{7,23},{8,24},{9,... | collective-permute-start | bytes 233480 | tf_op jit(solution)/shard_map/ppermute | solution.py:126
  39.2 0.4 collective-permute-start.16
  39.6 0.0 collective-permute-done.6.inner_column
  39.7 0.2 collective-permute-done.7.outer_column
  39.8 2.1 %shard_map.165 = (bf16[64,8,128]{2,1,0:T(8,128)(2,1)}, bf16[64,8,128]{2,1,0:T(8,128)(2,1)}, f32[8,128]{1,0:T(8,128)S(1)}) custom-call(bf16[256,1024]{1,0:T(8,128)(2,1)S(1)} %get-tuple-element.86.pre, bf16[256,128]{1,0:T(8,128)(2,1)S(1)} %collective-permute-done.4.inner.inner_row, bf16[256,128]{1,0:T(8,128)(2,1)S(1)} %collective-permute-done.5.outer.outer_row, ...), custom_call_target="tpu_custom_call" | custom-call | flops 603979776 | bytes 2000000 | tf_op jit(solution)/shard_map/pallas_call | solution.py:43
  41.9 0.0 collective-permute-done.14.refs_1_
  41.9 0.6 %collective-permute-done.15.refs_2_ = bf16[304,128]{1,0:T(8,128)(2,1)S(1)} collective-permute-done((bf16[304,128]{1,0:T(8,128)(2,1)S(1)}, bf16[304,128]{1,0:T(8,128)(2,1)S(1)}, u32[]{:S(2)}, u32[]{:S(2)}) %collective-permute-start.15) | collective-permute-done | bytes 77856 | tf_op jit(solution)/shard_map/ppermute | solution.py:126
  42.5 2.0 %collective-permute-done.16.refs_3_ = bf16[304,128]{1,0:T(8,128)(2,1)S(1)} collective-permute-done((bf16[304,128]{1,0:T(8,128)(2,1)S(1)}, bf16[304,128]{1,0:T(8,128)(2,1)S(1)}, u32[]{:S(2)}, u32[]{:S(2)}) %collective-permute-start.16) | collective-permute-done | bytes 77856 | tf_op jit(solution)/shard_map/ppermute | solution.py:126
  44.5 0.1 collective-permute-start.17
  44.6 0.9 %shard_map.167.out_before = f32[9,256,128]{2,1,0:T(8,128)} custom-call(bf16[4,304,128]{2,1,0:T(8,128)(2,1)S(1)} %shard_map.166.own), custom_call_target="tpu_custom_call" | custom-call | bytes 884736 | tf_op jit(solution)/shard_map/pallas_call | solution.py:43
  45.5 0.7 %collective-permute-done.17.received = bf16[4,304,128]{2,1,0:T(8,128)(2,1)S(1)} collective-permute-done((bf16[4,304,128]{2,1,0:T(8,128)(2,1)S(1)}, bf16[4,304,128]{2,1,0:T(8,128)(2,1)S(1)}, u32[]{:S(2)}, u32[]{:S(2)}) %collective-permute-start.17) | collective-permute-done | bytes 311328 | tf_op jit(solution)/shard_map/ppermute | solution.py:126
  46.2 0.9 %shard_map.168 = (f32[9,256,128]{2,1,0:T(8,128)}, f32[256]{0:T(256)}) custom-call(bf16[4,304,128]{2,1,0:T(8,128)(2,1)S(1)} %shard_map.166.own, bf16[4,304,128]{2,1,0:T(8,128)(2,1)S(1)} %collective-permute-done.17.received, f32[9,256,128]{2,1,0:T(8,128)} %shard_map.167.out_before), custom_call_target="tpu_custom_call", output_to_operand_aliasing={{0}: (2, {})} | custom-call | bytes 884736 | tf_op jit(solution)/shard_map/pallas_call | solution.py:43
  (4 shorter events, 0.1 us)
Async XLA Ops:
  1.7 6.4 %collective-permute-start = (bf16[128,128]{1,0:T(8,128)(2,1)S(1)}, bf16[128,128]{1,0:T(8,128)(2,1)S(1)}, u32[]{:S(2)}, u32[]{:S(2)}) collective-permute-start(bf16[128,128]{1,0:T(8,128)(2,1)S(1)} %get-tuple-element.58), channel_id=1, source_target_pairs={{0,8},{1,9},{2,10},{3,11},{4,12},{5,13},{6,14},{7,15},{8,0},{9,1},... | collective-permute-start | bytes 98312 | tf_op jit(solution)/shard_map/ppermute | solution.py:126
  2.2 5.9 %collective-permute-start.1 = (bf16[128,128]{1,0:T(8,128)(2,1)S(1)}, bf16[128,128]{1,0:T(8,128)(2,1)S(1)}, u32[]{:S(2)}, u32[]{:S(2)}) collective-permute-start(bf16[128,128]{1,0:T(8,128)(2,1)S(1)} %get-tuple-element.59), channel_id=1, source_target_pairs={{0,4},{1,5},{2,6},{3,7},{4,0},{5,1},{6,2},{7,3},{8,16},{9,17},{10,... | collective-permute-start | bytes 98312 | tf_op jit(solution)/shard_map/ppermute | solution.py:126
  8.2 7.6 %collective-permute-start.2 = (bf16[128,128]{1,0:T(8,128)(2,1)S(1)}, bf16[128,128]{1,0:T(8,128)(2,1)S(1)}, u32[]{:S(2)}, u32[]{:S(2)}) collective-permute-start(bf16[128,128]{1,0:T(8,128)(2,1)S(1)} %shard_map.156.edge), channel_id=1, source_target_pairs={{0,1},{1,0},{2,3},{3,2},{4,5},{5,4},{6,7},{7,6},{8,9},{9,8},{10,11... | collective-permute-start | bytes 98312 | tf_op jit(solution)/shard_map/ppermute | solution.py:126
  9.8 6.6 %collective-permute-start.3 = (bf16[128,128]{1,0:T(8,128)(2,1)S(1)}, bf16[128,128]{1,0:T(8,128)(2,1)S(1)}, u32[]{:S(2)}, u32[]{:S(2)}) collective-permute-start(bf16[128,128]{1,0:T(8,128)(2,1)S(1)} %shard_map.156.edge), channel_id=1, source_target_pairs={{0,7},{1,2},{2,1},{3,4},{4,3},{5,6},{6,5},{7,0},{8,15},{9,10},{10,... | collective-permute-start | bytes 98312 | tf_op jit(solution)/shard_map/ppermute | solution.py:126
  17.2 1.6 %collective-permute-start.8 = (bf16[1168,128]{1,0:T(8,128)(2,1)S(1)}, bf16[1168,128]{1,0:T(8,128)(2,1)S(1)}, u32[]{:S(2)}, u32[]{:S(2)}) collective-permute-start(bf16[1168,128]{1,0:T(8,128)(2,1)S(1)} %get-tuple-element.91), channel_id=1, source_target_pairs={{0,8},{1,9},{2,10},{3,11},{4,12},{5,13},{6,14},{7,15},{8,0},{9,1},... | collective-permute-start | bytes 897032 | tf_op jit(solution)/shard_map/ppermute | solution.py:126
  18.9 5.5 %collective-permute-start.10 = (bf16[304,128]{1,0:T(8,128)(2,1)S(1)}, bf16[304,128]{1,0:T(8,128)(2,1)S(1)}, u32[]{:S(2)}, u32[]{:S(2)}) collective-permute-start(bf16[304,128]{1,0:T(8,128)(2,1)S(1)} %get-tuple-element.95), channel_id=1, source_target_pairs={{0,16},{1,17},{2,18},{3,19},{4,20},{5,21},{6,22},{7,23},{8,24},{9,... | collective-permute-start | bytes 233480 | tf_op jit(solution)/shard_map/ppermute | solution.py:126
  19.0 6.1 %collective-permute-start.11 = (bf16[304,128]{1,0:T(8,128)(2,1)S(1)}, bf16[304,128]{1,0:T(8,128)(2,1)S(1)}, u32[]{:S(2)}, u32[]{:S(2)}) collective-permute-start(bf16[304,128]{1,0:T(8,128)(2,1)S(1)} %get-tuple-element.96), channel_id=1, source_target_pairs={{0,1},{1,0},{2,3},{3,2},{4,5},{5,4},{6,7},{7,6},{8,9},{9,8},{10,11... | collective-permute-start | bytes 233480 | tf_op jit(solution)/shard_map/ppermute | solution.py:126
  19.1 6.1 %collective-permute-start.9 = (bf16[304,128]{1,0:T(8,128)(2,1)S(1)}, bf16[304,128]{1,0:T(8,128)(2,1)S(1)}, u32[]{:S(2)}, u32[]{:S(2)}) collective-permute-start(bf16[304,128]{1,0:T(8,128)(2,1)S(1)} %get-tuple-element.94), channel_id=1, source_target_pairs={{0,17},{1,16},{2,19},{3,18},{4,21},{5,20},{6,23},{7,22},{8,25},{9,... | collective-permute-start | bytes 233480 | tf_op jit(solution)/shard_map/ppermute | solution.py:126
  25.2 4.5 %collective-permute-start.12 = (bf16[304,128]{1,0:T(8,128)(2,1)S(1)}, bf16[304,128]{1,0:T(8,128)(2,1)S(1)}, u32[]{:S(2)}, u32[]{:S(2)}) collective-permute-start(bf16[304,128]{1,0:T(8,128)(2,1)S(1)} %shard_map.162.own), channel_id=1, source_target_pairs={{0,2},{1,3},{2,0},{3,1},{4,6},{5,7},{6,4},{7,5},{8,12},{9,13},{10,... | collective-permute-start | bytes 233480 | tf_op jit(solution)/shard_map/ppermute | solution.py:126
  25.3 6.7 %collective-permute-start.4 = (bf16[256,128]{1,0:T(8,128)(2,1)S(1)}, bf16[256,128]{1,0:T(8,128)(2,1)S(1)}, u32[]{:S(2)}, u32[]{:S(2)}) collective-permute-start(bf16[256,128]{1,0:T(8,128)(2,1)S(1)} %get-tuple-element.87.refs_3_), channel_id=1, source_target_pairs={{0,8},{1,9},{2,10},{3,11},{4,12},{5,13},{6,14},{7,15},{8,0},{9,1},... | collective-permute-start | bytes 196616 | tf_op jit(solution)/shard_map/ppermute | solution.py:126
  25.4 6.6 %collective-permute-start.5 = (bf16[256,128]{1,0:T(8,128)(2,1)S(1)}, bf16[256,128]{1,0:T(8,128)(2,1)S(1)}, u32[]{:S(2)}, u32[]{:S(2)}) collective-permute-start(bf16[256,128]{1,0:T(8,128)(2,1)S(1)} %get-tuple-element.88), channel_id=1, source_target_pairs={{0,4},{1,5},{2,6},{3,7},{4,0},{5,1},{6,2},{7,3},{8,16},{9,17},{10,... | collective-permute-start | bytes 196616 | tf_op jit(solution)/shard_map/ppermute | solution.py:126
  29.7 6.3 %collective-permute-start.13 = (bf16[304,128]{1,0:T(8,128)(2,1)S(1)}, bf16[304,128]{1,0:T(8,128)(2,1)S(1)}, u32[]{:S(2)}, u32[]{:S(2)}) collective-permute-start(bf16[304,128]{1,0:T(8,128)(2,1)S(1)} %shard_map.163.own), channel_id=1, source_target_pairs={{0,4},{1,5},{2,6},{3,7},{4,0},{5,1},{6,2},{7,3},{8,10},{9,11},{10,... | collective-permute-start | bytes 233480 | tf_op jit(solution)/shard_map/ppermute | solution.py:126
  32.1 7.5 %collective-permute-start.6 = (bf16[256,128]{1,0:T(8,128)(2,1)S(1)}, bf16[256,128]{1,0:T(8,128)(2,1)S(1)}, u32[]{:S(2)}, u32[]{:S(2)}) collective-permute-start(bf16[256,128]{1,0:T(8,128)(2,1)S(1)} %shard_map.159), channel_id=1, source_target_pairs={{0,1},{1,0},{2,3},{3,2},{4,5},{5,4},{6,7},{7,6},{8,9},{9,8},{10,11... | collective-permute-start | bytes 196616 | tf_op jit(solution)/shard_map/ppermute | solution.py:126
  32.9 7.0 %collective-permute-start.7 = (bf16[256,128]{1,0:T(8,128)(2,1)S(1)}, bf16[256,128]{1,0:T(8,128)(2,1)S(1)}, u32[]{:S(2)}, u32[]{:S(2)}) collective-permute-start(bf16[256,128]{1,0:T(8,128)(2,1)S(1)} %shard_map.159), channel_id=1, source_target_pairs={{0,7},{1,2},{2,1},{3,4},{4,3},{5,6},{6,5},{7,0},{8,15},{9,10},{10,... | collective-permute-start | bytes 196616 | tf_op jit(solution)/shard_map/ppermute | solution.py:126
  36.0 6.0 %collective-permute-start.14 = (bf16[304,128]{1,0:T(8,128)(2,1)S(1)}, bf16[304,128]{1,0:T(8,128)(2,1)S(1)}, u32[]{:S(2)}, u32[]{:S(2)}) collective-permute-start(bf16[304,128]{1,0:T(8,128)(2,1)S(1)} %get-tuple-element.101.refs_0_), channel_id=1, source_target_pairs={{0,1},{1,0},{2,3},{3,2},{4,5},{5,4},{6,7},{7,6},{8,9},{9,8},{10,11... | collective-permute-start | bytes 233480 | tf_op jit(solution)/shard_map/ppermute | solution.py:126
  38.1 4.4 %collective-permute-start.15 = (bf16[304,128]{1,0:T(8,128)(2,1)S(1)}, bf16[304,128]{1,0:T(8,128)(2,1)S(1)}, u32[]{:S(2)}, u32[]{:S(2)}) collective-permute-start(bf16[304,128]{1,0:T(8,128)(2,1)S(1)} %get-tuple-element.101.refs_0_), channel_id=1, source_target_pairs={{0,16},{1,17},{2,18},{3,19},{4,20},{5,21},{6,22},{7,23},{8,24},{9,... | collective-permute-start | bytes 233480 | tf_op jit(solution)/shard_map/ppermute | solution.py:126
  39.2 5.3 %collective-permute-start.16 = (bf16[304,128]{1,0:T(8,128)(2,1)S(1)}, bf16[304,128]{1,0:T(8,128)(2,1)S(1)}, u32[]{:S(2)}, u32[]{:S(2)}) collective-permute-start(bf16[304,128]{1,0:T(8,128)(2,1)S(1)} %get-tuple-element.101.refs_0_), channel_id=1, source_target_pairs={{0,17},{1,16},{2,19},{3,18},{4,21},{5,20},{6,23},{7,22},{8,25},{9,... | collective-permute-start | bytes 233480 | tf_op jit(solution)/shard_map/ppermute | solution.py:126
  44.5 1.7 %collective-permute-start.17 = (bf16[4,304,128]{2,1,0:T(8,128)(2,1)S(1)}, bf16[4,304,128]{2,1,0:T(8,128)(2,1)S(1)}, u32[]{:S(2)}, u32[]{:S(2)}) collective-permute-start(bf16[4,304,128]{2,1,0:T(8,128)(2,1)S(1)} %shard_map.166.own), channel_id=1, source_target_pairs={{0,8},{1,9},{2,10},{3,11},{4,12},{5,13},{6,14},{7,15},{8,0},{9,1},... | collective-permute-start | bytes 933896 | tf_op jit(solution)/shard_map/ppermute | solution.py:126

commit v3 on v2

--- a/solution.py
+++ b/solution.py
@@ -12,6 +12,8 @@
 BF16 = jnp.bfloat16
 AXES = ("band", "core", "reach", "near")
 BIAS_ROWS = 16
+GROUPS = 4
+PRE_GROUPS = 1
 LAST = 16
 VMEM = pl.BlockSpec(memory_space=pltpu.VMEM)
 HBM = pl.BlockSpec(memory_space=pltpu.HBM)
@@ -174,15 +176,30 @@
     return pick(odd, inner, outer), pick(odd, outer, inner)
 
 
-def column_halo(inner, outer):
+def packed(columns, groups):
+    count, width = columns.shape[0] // groups, columns.shape[1] // groups
+    lane = lanes((count, columns.shape[1]))
+    value = columns[0:count]
+    for group in range(1, groups):
+        part = rolled(columns[group * count : (group + 1) * count], group * width)
+        value = jnp.where(lane >= group * width, part, value)
+    return value
+
+
+def unpacked(value, groups):
+    width = value.shape[1] // groups
+    return jnp.concatenate([rolled(value, -group * width) for group in range(groups)], axis=0)
+
+
+def column_halo(inner, outer, groups):
     odd = is_odd("near")
     inner, outer = inner[...].astype(F32), outer[...].astype(F32)
-    return pick(odd, inner, outer), pick(odd, outer, inner)
+    return unpacked(pick(odd, inner, outer), groups), unpacked(pick(odd, outer, inner), groups)
 
 
 def widened(row_count, rows, row_blocks, column_blocks, emit):
     north, south = row_halo(*row_blocks)
-    west, east = column_halo(*column_blocks)
+    west, east = column_halo(*column_blocks, PRE_GROUPS)
     width = west.shape[1]
     lane = lanes(west.shape)
     for position in range(row_count + 2):
@@ -302,10 +319,13 @@
     fields_strip_out[...] = fields_strip
 
 
-def columns_kernel(row_count, columns, inner, outer, out):
+def columns_kernel(row_count, groups, columns, inner, outer, packed_out, *whole_out):
     north, south = row_halo(inner, outer)
     value = edge_columns(north, 0, columns[...].astype(F32))
-    out[...] = edge_columns(south, row_count + 1, value).astype(BF16)
+    value = edge_columns(south, row_count + 1, value)
+    packed_out[...] = packed(value, groups).astype(BF16)
+    for out in whole_out:
+        out[...] = value.astype(BF16)
 
 
 def encode(bias):
@@ -443,7 +463,7 @@
             )
 
 
-def add_strip(place, half, sums, pre_strip, patches, out, start):
+def add_strip(place, half, sums, pre_strip, patches, out):
     half_gates, channels = place.half_gates, sums.shape[1]
     gates = pre_strip[pl.ds(pl.multiple_of(half * half_gates, half_gates), half_gates), :]
     product = lax.dot_general(gates, patches[...], ACROSS, preferred_element_type=F32)
@@ -451,12 +471,11 @@
     for tap in range(place.taps):
         at = pl.ds(pl.multiple_of(base + tap * half_gates, 8), half_gates)
         value = sums[at, :] + product[:, tap * channels : (tap + 1) * channels]
-        to = start + tap * half_gates
-        out[to : to + half_gates, :] = value.astype(out.dtype)
+        out[tap * half_gates : (tap + 1) * half_gates, :] = value.astype(out.dtype)
     used = place.taps * half_gates
     if place.half_rows > used:
         rest = jnp.zeros((place.half_rows - used, channels), out.dtype)
-        out[start + used : start + place.half_rows, :] = rest
+        out[used:, :] = rest
 
 
 def strip_kernel(
@@ -473,17 +492,16 @@
     hidden_grad_strip,
     fields_strip,
     sums,
-    bias_partial,
     send_out,
-    bias_out,
     pre_out,
+    pre_wide_out,
     patches,
     hidden_out,
     cell_out,
     grad_cell_out,
 ):
     channels, width = edge.shape
-    west, east = column_halo(inner_column, outer_column)
+    west, east = column_halo(inner_column, outer_column, GROUPS)
     near_first = lanes((channels, width)) < LAST
     inner = second[...].astype(F32)
     columns = (
@@ -513,23 +531,21 @@
     lane = jnp.where(lane >= LAST, lane - LAST, lane)
     pre_grad = jnp.where((lane >= 1) & (lane <= row_count), pre_grad, 0.0)
     pre_out[...] = pre_grad.astype(BF16)
-    rank = place.rank(0)
-    add_strip(place, 1 - rank, sums, pre_out, patches, send_out, BIAS_ROWS)
-
-    bias_total = bias_partial[...] + pre_grad
-    ones = jnp.ones((8, width), BF16)
+    pre_wide_out[...] = pre_grad
+    add_strip(place, 1 - place.rank(0), sums, pre_out, patches, send_out)
+
+
+def keep_kernel(place, sums, pre_strip, patches, bias_partial, pre_wide, out, bias_out):
+    add_strip(place, place.rank(0), sums, pre_strip, patches, out)
+    channels = sums.shape[1]
+    bias_total = bias_partial[...] + pre_wide[...]
+    ones = jnp.ones((8, bias_total.shape[1]), BF16)
     high = bias_total.astype(BF16)
     low = (bias_total - high.astype(F32)).astype(BF16)
     flat = lax.dot_general(ones, high, ACROSS, preferred_element_type=F32)
     flat += lax.dot_general(ones, low, ACROSS, preferred_element_type=F32)
     odd = lax.broadcasted_iota(jnp.int32, (8, channels), 0) % 2 == 1
-    bias_rows = jnp.where(odd, flat[:, channels : 2 * channels], flat[:, 0:channels])
-    bias_out[...] = bias_rows
-    send_out[0:BIAS_ROWS, :] = encode(bias_rows).astype(BF16)
-
-
-def keep_kernel(place, sums, pre_strip, patches, out):
-    add_strip(place, place.rank(0), sums, pre_strip, patches, out, 0)
+    bias_out[...] = jnp.where(odd, flat[:, channels : 2 * channels], flat[:, 0:channels])
 
 
 def edges_kernel(
@@ -588,18 +604,16 @@
 
 
 def pair_kernel(place, keep, bias, received, *outs):
-    sends, keep_out, bias_out, scratch = outs[:-3], outs[-3], outs[-2], outs[-1]
+    sends, keep_out, scratch = outs[:-2], outs[-2], outs[-1]
     chunk = place.chunk
     rank = place.plane_rank()
-    scratch[...] = keep[...] + received[BIAS_ROWS:, :].astype(F32)
-    bias_total = bias[...] + decode(received[0:BIAS_ROWS, :].astype(F32))
-    block = encode(bias_total).astype(BF16)
+    scratch[...] = keep[...] + received[...].astype(F32)
+    block = encode(bias[...]).astype(BF16)
     for step, send in zip(range(place.plane - 1, 0, -1), sends):
         send[0:BIAS_ROWS, :] = block
         at = pl.ds(pl.multiple_of((rank ^ step) * chunk, 8), chunk)
         send[BIAS_ROWS:, :] = scratch[at, :].astype(BF16)
     keep_out[...] = scratch[pl.ds(pl.multiple_of(rank * chunk, 8), chunk), :]
-    bias_out[...] = bias_total
 
 
 def plane_kernel(keep, bias, *refs):
@@ -651,7 +665,7 @@
     del out_before
     rank = place.rank(0)
     here, there = own[0, 0:BIAS_ROWS, :].astype(F32), received[0, 0:BIAS_ROWS, :].astype(F32)
-    bias = decode(pick(rank == 1, there, here))
+    bias = decode(here) + decode(there)
     width = bias.shape[1]
     for index in range(bias_here.shape[0] // width):
         bias_here[pl.ds(index * width, width)] = bias[index]
@@ -827,10 +841,12 @@
         gate_bias,
         readout,
     )
-    edge = call(bind(columns_kernel, row_count), sds((channels, width), BF16))(
-        columns, inner, outer
-    )
-    inner_column, outer_column = permuted(edge, inner_columns), permuted(edge, outer_columns)
+    columns, edge = call(
+        bind(columns_kernel, row_count, GROUPS),
+        (sds((channels // GROUPS, width), BF16), sds((channels, width), BF16)),
+    )(columns, inner, outer)
+    outer_column = permuted(columns, outer_columns)
+    inner_column = permuted(columns, inner_columns)
     hidden_rows, cell_rows, grad_cell_rows, pre, second, sums, bias = call(
         bind(gates_kernel, place),
         (
@@ -860,12 +876,12 @@
         bias_wide,
         readout_wide,
     )
-    send, bias, pre_strip, patches, *strips = call(
+    send, pre_strip, pre_wide, patches, *strips = call(
         bind(strip_kernel, place, row_count),
         (
-            sds((BIAS_ROWS + place.half_rows, channels), BF16),
-            sds((8, channels), F32),
+            sds((place.half_rows, channels), BF16),
             sds((gate_count, width), BF16),
+            sds((gate_count, width), F32),
             sds((place.taps * channels, width), BF16),
             strip,
             strip,
@@ -883,11 +899,11 @@
         hidden_grad_strip,
         fields_strip,
         sums,
-        bias,
     )
-    keep = call(bind(keep_kernel, place), sds((place.half_rows, channels), F32))(
-        sums, pre_strip, patches
-    )
+    keep, bias = call(
+        bind(keep_kernel, place),
+        (sds((place.half_rows, channels), F32), sds((8, channels), F32)),
+    )(sums, pre_strip, patches, bias, pre_wide)
     hidden_next, cell_next, grad_cell, pre, pre_inner, pre_outer = call(
         bind(edges_kernel, row_count),
         (
@@ -909,22 +925,23 @@
     )(hidden_rows, cell_rows, grad_cell_rows, pre, *strips, pre_strip)
     after = pre_inner
     pre_inner, pre_outer = permuted(pre_inner, inner_rows), permuted(pre_outer, outer_rows)
-    pre_columns = call(bind(columns_kernel, row_count), sds((gate_count, width), BF16))(
-        pre_strip, pre_inner, pre_outer
-    )
+    pre_columns = call(
+        bind(columns_kernel, row_count, PRE_GROUPS),
+        (sds((gate_count // PRE_GROUPS, width), BF16),),
+    )(pre_strip, pre_inner, pre_outer)[0]
 
     block = sds((BIAS_ROWS + place.chunk, channels), BF16)
     token = sds((8, width), F32)
     steps = range(place.plane - 1, 0, -1)
-    *sends, keep, bias = call(
+    *sends, keep = call(
         bind(pair_kernel, place),
-        (*[block for _ in steps], sds((place.chunk, channels), F32), sds((8, channels), F32)),
+        (*[block for _ in steps], sds((place.chunk, channels), F32)),
         [pltpu.VMEM((place.half_rows, channels), F32)],
     )(keep, bias, permuted(send, place.phase_pairs(0)))
     received = [permuted(send, place.plane_pairs(step)) for step, send in zip(steps, sends)]
     part = call(plane_kernel, block)(keep, bias, *received, after)
+    pre_outer_columns = permuted(pre_columns, outer_columns)
     pre_inner_columns = permuted(pre_columns, inner_columns)
-    pre_outer_columns = permuted(pre_columns, outer_columns)
     phases = len(place.orders[0])
     for phase in range(1, phases):
         is_last = phase == phases - 1

time: 47.3 us -> 48.4 us (1.023)
  waiting for transfers between devices: 6.23 us -> 11.2 us
  starting transfers between devices: 27.3 us -> 23.4 us
    ppermute x18, waiting for transfers between devices: 6.23 us -> 11.2 us  [permuted(): return lax.ppermute(value, AXES, pairs)]
    ppermute x18, starting transfers between devices: 27.3 us -> 23.4 us  [permuted(): return lax.ppermute(value, AXES, pairs)]
  transfers between devices with their start and end apart: 18 -> 18, of which waited for: 8 -> 10; matrix products, arithmetic and copies ran while one was open for 0% -> 0% of each run, Pallas kernels for 21% -> 20%
where the time goes in v3:
time: 48.4 us; the launch traced here: 48.3 us
  starting transfers between devices  23.4 us (48%)
  Pallas kernels  12.9 us (27%)
  waiting for transfers between devices  11.2 us (23%)
  between operations  0.78 us (2%)
    ppermute x18, starting transfers between devices, permuted(): return lax.ppermute(value, AXES, pairs)  23.4 us
    pallas_call x16, Pallas kernels, run(): pl.pallas_call(kernel, out_shape=out_shape, in_specs=[VMEM] * near + [HBM...  12.9 us
    ppermute x18, waiting for transfers between devices, permuted(): return lax.ppermute(value, AXES, pairs)  11.2 us
  transfers between devices with their start and end apart: 18, of which 10 were waited for; matrix products, arithmetic and copies ran while one was open for 0% of the time, Pallas kernels for 20%

profile of v3, /device:TPU:0, one launch (start us, length us, event | category | flops | bytes accessed | tf_op | source)
XLA Modules:
  0.0 48.3 jit_solution(10953539532779425832)
XLA Ops:
  0.6 1.0 %shard_map.153 = (bf16[128,128]{1,0:T(8,128)(2,1)S(1)}, bf16[128,128]{1,0:T(8,128)(2,1)S(1)}, f32[1024,128]{1,0:T(8,128)S(1)}) custom-call(bf16[64,8,128]{2,1,0:T(8,128)(2,1)} %below.1, bf16[64,8,128]{2,1,0:T(8,128)(2,1)} %hidden.1), custom_call_target="tpu_custom_call" | custom-call | bytes 524288 | tf_op jit(solution)/shard_map/pallas_call | solution.py:45
  1.7 0.5 %collective-permute-start = (bf16[128,128]{1,0:T(8,128)(2,1)S(1)}, bf16[128,128]{1,0:T(8,128)(2,1)S(1)}, u32[]{:S(2)}, u32[]{:S(2)}) collective-permute-start(bf16[128,128]{1,0:T(8,128)(2,1)S(1)} %get-tuple-element.61), channel_id=1, source_target_pairs={{0,8},{1,9},{2,10},{3,11},{4,12},{5,13},{6,14},{7,15},{8,0},{9,1},... | collective-permute-start | bytes 98312 | tf_op jit(solution)/shard_map/ppermute | solution.py:128
  2.2 3.7 %collective-permute-start.1 = (bf16[128,128]{1,0:T(8,128)(2,1)S(1)}, bf16[128,128]{1,0:T(8,128)(2,1)S(1)}, u32[]{:S(2)}, u32[]{:S(2)}) collective-permute-start(bf16[128,128]{1,0:T(8,128)(2,1)S(1)} %get-tuple-element.62), channel_id=1, source_target_pairs={{0,4},{1,5},{2,6},{3,7},{4,0},{5,1},{6,2},{7,3},{8,16},{9,17},{10,... | collective-permute-start | bytes 98312 | tf_op jit(solution)/shard_map/ppermute | solution.py:128
  5.8 2.2 %shard_map.154 = (bf16[8,128,128]{2,1,0:T(8,128)(2,1)S(1)}, f32[128,128]{1,0:T(8,128)S(1)}, f32[128,128]{1,0:T(8,128)S(1)}, f32[64,128]{1,0:T(8,128)S(1)}, f32[6...) custom-call(f32[1024,128]{1,0:T(8,128)S(1)} %get-tuple-element.59.wi, ...), custom_call_target="tpu_custom_call" | custom-call | bytes 6000000 | tf_op jit(solution)/shard_map/pallas_call | solution.py:45
  8.0 0.0 collective-permute-done.inner_row.inner
  8.0 0.0 collective-permute-done.1.outer_row.outer
  8.0 0.2 shard_map.156
  8.2 4.8 %collective-permute-start.3 = (bf16[32,128]{1,0:T(8,128)(2,1)S(1)}, bf16[32,128]{1,0:T(8,128)(2,1)S(1)}, u32[]{:S(2)}, u32[]{:S(2)}) collective-permute-start(bf16[32,128]{1,0:T(8,128)(2,1)S(1)} %get-tuple-element.79), channel_id=1, source_target_pairs={{0,7},{1,2},{2,1},{3,4},{4,3},{5,6},{6,5},{7,0},{8,15},{9,10},{10,... | collective-permute-start | bytes 24584 | tf_op jit(solution)/shard_map/ppermute | solution.py:128
  13.0 0.0 collective-permute-start.2
  13.0 2.2 %shard_map.155 = (f32[512,128]{1,0:T(8,128)S(1)}, f32[512,128]{1,0:T(8,128)S(1)}, f32[512,128]{1,0:T(8,128)S(1)}, bf16[256,1024]{1,0:T(8,128)(2,1)S(1)}, bf16[12...) custom-call(bf16[8,128,128]{2,1,0:T(8,128)(2,1)S(1)} %get-tuple-element.60.rows_in, ...), custom_call_target="tpu_custom_call" | custom-call | flops 1207959552 | bytes 6000000 | tf_op jit(solution)/shard_map/pallas_call | solution.py:45
  15.3 0.0 collective-permute-done.3.outer_column
  15.3 1.4 %collective-permute-done.2.inner_column = bf16[32,128]{1,0:T(8,128)(2,1)S(1)} collective-permute-done((bf16[32,128]{1,0:T(8,128)(2,1)S(1)}, bf16[32,128]{1,0:T(8,128)(2,1)S(1)}, u32[]{:S(2)}, u32[]{:S(2)}) %collective-permute-start.2) | collective-permute-done | bytes 8224 | tf_op jit(solution)/shard_map/ppermute | solution.py:128
  16.7 0.9 %shard_map.157 = (bf16[1152,128]{1,0:T(8,128)(2,1)S(1)}, bf16[256,128]{1,0:T(8,128)(2,1)S(1)}, f32[256,128]{1,0:T(8,128)S(1)}, bf16[1152,128]{1,0:T(8,128)(2,1)S...) custom-call(bf16[128,128]{1,0:T(8,128)(2,1)S(1)} %get-tuple-element.77.edge, ...), custom_call_target="tpu_custom_call" | custom-call | tf_op jit(solution)/shard_map/pallas_call | solution.py:45
  17.6 0.1 collective-permute-start.8
  17.6 0.3 shard_map.160
  17.9 1.3 %collective-permute-done.8.received = bf16[1152,128]{1,0:T(8,128)(2,1)S(1)} collective-permute-done((bf16[1152,128]{1,0:T(8,128)(2,1)S(1)}, bf16[1152,128]{1,0:T(8,128)(2,1)S(1)}, u32[]{:S(2)}, u32[]{:S(2)}) %collective-permute-start.8) | collective-permute-done | bytes 294944 | tf_op jit(solution)/shard_map/ppermute | solution.py:128
  19.2 0.1 shard_map.161
  19.3 0.1 collective-permute-start.9
  19.4 2.1 %collective-permute-start.10 = (bf16[304,128]{1,0:T(8,128)(2,1)S(1)}, bf16[304,128]{1,0:T(8,128)(2,1)S(1)}, u32[]{:S(2)}, u32[]{:S(2)}) collective-permute-start(bf16[304,128]{1,0:T(8,128)(2,1)S(1)} %get-tuple-element.101), channel_id=1, source_target_pairs={{0,16},{1,17},{2,18},{3,19},{4,20},{5,21},{6,22},{7,23},{8,24},{9,... | collective-permute-start | bytes 233480 | tf_op jit(solution)/shard_map/ppermute | solution.py:128
  21.5 1.4 %collective-permute-start.11 = (bf16[304,128]{1,0:T(8,128)(2,1)S(1)}, bf16[304,128]{1,0:T(8,128)(2,1)S(1)}, u32[]{:S(2)}, u32[]{:S(2)}) collective-permute-start(bf16[304,128]{1,0:T(8,128)(2,1)S(1)} %get-tuple-element.102), channel_id=1, source_target_pairs={{0,1},{1,0},{2,3},{3,2},{4,5},{5,4},{6,7},{7,6},{8,9},{9,8},{10,11... | collective-permute-start | bytes 233480 | tf_op jit(solution)/shard_map/ppermute | solution.py:128
  22.9 2.0 %shard_map.158 = (bf16[64,8,128]{2,1,0:T(8,128)(2,1)}, f32[512,128]{1,0:T(8,128)}, f32[512,128]{1,0:T(8,128)}, bf16[256,1024]{1,0:T(8,128)(2,1)S(1)}, bf16[256,1...) custom-call(f32[512,128]{1,0:T(8,128)S(1)} %get-tuple-element.72.hidden, f32[512,128]{1,0:T(8,128)S(1)} %get-tuple-element.73.cell, ...), custom_call_target="tpu_custom_call" | custom-call | bytes 4000000 | tf_op jit(solution)/shard_map/pallas_call | solution.py:45
  24.8 0.6 %collective-permute-done.9.refs_0_ = bf16[304,128]{1,0:T(8,128)(2,1)S(1)} collective-permute-done((bf16[304,128]{1,0:T(8,128)(2,1)S(1)}, bf16[304,128]{1,0:T(8,128)(2,1)S(1)}, u32[]{:S(2)}, u32[]{:S(2)}) %collective-permute-start.9) | collective-permute-done | bytes 77856 | tf_op jit(solution)/shard_map/ppermute | solution.py:128
  25.5 0.0 collective-permute-done.10.refs_1_
  25.5 0.8 %collective-permute-done.11.refs_2_ = bf16[304,128]{1,0:T(8,128)(2,1)S(1)} collective-permute-done((bf16[304,128]{1,0:T(8,128)(2,1)S(1)}, bf16[304,128]{1,0:T(8,128)(2,1)S(1)}, u32[]{:S(2)}, u32[]{:S(2)}) %collective-permute-start.11) | collective-permute-done | bytes 77856 | tf_op jit(solution)/shard_map/ppermute | solution.py:128
  26.4 0.1 collective-permute-start.12
  26.5 2.7 %collective-permute-start.5 = (bf16[256,128]{1,0:T(8,128)(2,1)S(1)}, bf16[256,128]{1,0:T(8,128)(2,1)S(1)}, u32[]{:S(2)}, u32[]{:S(2)}) collective-permute-start(bf16[256,128]{1,0:T(8,128)(2,1)S(1)} %get-tuple-element.92), channel_id=1, source_target_pairs={{0,4},{1,5},{2,6},{3,7},{4,0},{5,1},{6,2},{7,3},{8,16},{9,17},{10,... | collective-permute-start | bytes 196616 | tf_op jit(solution)/shard_map/ppermute | solution.py:128
  29.2 0.0 collective-permute-start.4
  29.2 1.9 %collective-permute-done.12.received = bf16[304,128]{1,0:T(8,128)(2,1)S(1)} collective-permute-done((bf16[304,128]{1,0:T(8,128)(2,1)S(1)}, bf16[304,128]{1,0:T(8,128)(2,1)S(1)}, u32[]{:S(2)}, u32[]{:S(2)}) %collective-permute-start.12) | collective-permute-done | bytes 77856 | tf_op jit(solution)/shard_map/ppermute | solution.py:128
  31.1 0.5 %collective-permute-start.13 = (bf16[304,128]{1,0:T(8,128)(2,1)S(1)}, bf16[304,128]{1,0:T(8,128)(2,1)S(1)}, u32[]{:S(2)}, u32[]{:S(2)}) collective-permute-start(bf16[304,128]{1,0:T(8,128)(2,1)S(1)} %shard_map.163.own), channel_id=1, source_target_pairs={{0,4},{1,5},{2,6},{3,7},{4,0},{5,1},{6,2},{7,3},{8,10},{9,11},{10,... | collective-permute-start | bytes 233480 | tf_op jit(solution)/shard_map/ppermute | solution.py:128
  31.6 0.2 collective-permute-done.5.outer.outer_row
  31.8 0.0 collective-permute-done.4.inner.inner_row
  31.8 0.1 shard_map.159
  31.9 3.3 %collective-permute-start.7 = (bf16[256,128]{1,0:T(8,128)(2,1)S(1)}, bf16[256,128]{1,0:T(8,128)(2,1)S(1)}, u32[]{:S(2)}, u32[]{:S(2)}) collective-permute-start(bf16[256,128]{1,0:T(8,128)(2,1)S(1)} %shard_map.159), channel_id=1, source_target_pairs={{0,7},{1,2},{2,1},{3,4},{4,3},{5,6},{6,5},{7,0},{8,15},{9,10},{10,... | collective-permute-start | bytes 196616 | tf_op jit(solution)/shard_map/ppermute | solution.py:128
  35.2 0.3 collective-permute-start.6
  35.4 1.9 %collective-permute-done.13.received = bf16[304,128]{1,0:T(8,128)(2,1)S(1)} collective-permute-done((bf16[304,128]{1,0:T(8,128)(2,1)S(1)}, bf16[304,128]{1,0:T(8,128)(2,1)S(1)}, u32[]{:S(2)}, u32[]{:S(2)}) %collective-permute-start.13) | collective-permute-done | bytes 77856 | tf_op jit(solution)/shard_map/ppermute | solution.py:128
  37.3 1.2 %collective-permute-start.16 = (bf16[304,128]{1,0:T(8,128)(2,1)S(1)}, bf16[304,128]{1,0:T(8,128)(2,1)S(1)}, u32[]{:S(2)}, u32[]{:S(2)}) collective-permute-start(bf16[304,128]{1,0:T(8,128)(2,1)S(1)} %get-tuple-element.107.refs_0_), channel_id=1, source_target_pairs={{0,17},{1,16},{2,19},{3,18},{4,21},{5,20},{6,23},{7,22},{8,25},{9,... | collective-permute-start | bytes 233480 | tf_op jit(solution)/shard_map/ppermute | solution.py:128
  38.5 2.7 %collective-permute-start.15 = (bf16[304,128]{1,0:T(8,128)(2,1)S(1)}, bf16[304,128]{1,0:T(8,128)(2,1)S(1)}, u32[]{:S(2)}, u32[]{:S(2)}) collective-permute-start(bf16[304,128]{1,0:T(8,128)(2,1)S(1)} %get-tuple-element.107.refs_0_), channel_id=1, source_target_pairs={{0,16},{1,17},{2,18},{3,19},{4,20},{5,21},{6,22},{7,23},{8,24},{9,... | collective-permute-start | bytes 233480 | tf_op jit(solution)/shard_map/ppermute | solution.py:128
  41.3 0.0 collective-permute-start.14
  41.3 0.0 collective-permute-done.7.outer_column
  41.3 0.0 collective-permute-done.6.inner_column
  41.3 2.1 %shard_map.165 = (bf16[64,8,128]{2,1,0:T(8,128)(2,1)}, bf16[64,8,128]{2,1,0:T(8,128)(2,1)}, f32[8,128]{1,0:T(8,128)S(1)}) custom-call(bf16[256,1024]{1,0:T(8,128)(2,1)S(1)} %get-tuple-element.90.pre, bf16[256,128]{1,0:T(8,128)(2,1)S(1)} %collective-permute-done.4.inner.inner_row, bf16[256,128]{1,0:T(8,128)(2,1)S(1)} %collective-permute-done.5.outer.outer_row, ...), custom_call_target="tpu_custom_call" | custom-call | flops 603979776 | bytes 2000000 | tf_op jit(solution)/shard_map/pallas_call | solution.py:45
  43.4 0.0 collective-permute-done.16.refs_3_
  43.4 1.1 %collective-permute-done.15.refs_2_ = bf16[304,128]{1,0:T(8,128)(2,1)S(1)} collective-permute-done((bf16[304,128]{1,0:T(8,128)(2,1)S(1)}, bf16[304,128]{1,0:T(8,128)(2,1)S(1)}, u32[]{:S(2)}, u32[]{:S(2)}) %collective-permute-start.15) | collective-permute-done | bytes 77856 | tf_op jit(solution)/shard_map/ppermute | solution.py:128
  44.5 1.2 %collective-permute-done.14.refs_1_ = bf16[304,128]{1,0:T(8,128)(2,1)S(1)} collective-permute-done((bf16[304,128]{1,0:T(8,128)(2,1)S(1)}, bf16[304,128]{1,0:T(8,128)(2,1)S(1)}, u32[]{:S(2)}, u32[]{:S(2)}) %collective-permute-start.14) | collective-permute-done | bytes 77856 | tf_op jit(solution)/shard_map/ppermute | solution.py:128
  45.7 0.1 collective-permute-start.17
  45.8 0.9 %shard_map.167.out_before = f32[9,256,128]{2,1,0:T(8,128)} custom-call(bf16[4,304,128]{2,1,0:T(8,128)(2,1)S(1)} %shard_map.166.own), custom_call_target="tpu_custom_call" | custom-call | bytes 884736 | tf_op jit(solution)/shard_map/pallas_call | solution.py:45
  46.7 0.7 %collective-permute-done.17.received = bf16[4,304,128]{2,1,0:T(8,128)(2,1)S(1)} collective-permute-done((bf16[4,304,128]{2,1,0:T(8,128)(2,1)S(1)}, bf16[4,304,128]{2,1,0:T(8,128)(2,1)S(1)}, u32[]{:S(2)}, u32[]{:S(2)}) %collective-permute-start.17) | collective-permute-done | bytes 311328 | tf_op jit(solution)/shard_map/ppermute | solution.py:128
  47.4 0.9 %shard_map.168 = (f32[9,256,128]{2,1,0:T(8,128)}, f32[256]{0:T(256)}) custom-call(bf16[4,304,128]{2,1,0:T(8,128)(2,1)S(1)} %shard_map.166.own, bf16[4,304,128]{2,1,0:T(8,128)(2,1)S(1)} %collective-permute-done.17.received, f32[9,256,128]{2,1,0:T(8,128)} %shard_map.167.out_before), custom_call_target="tpu_custom_call", output_to_operand_aliasing={{0}: (2, {})} | custom-call | bytes 884736 | tf_op jit(solution)/shard_map/pallas_call | solution.py:45
  (4 shorter events, 0.1 us)
Async XLA Ops:
  1.7 6.4 %collective-permute-start = (bf16[128,128]{1,0:T(8,128)(2,1)S(1)}, bf16[128,128]{1,0:T(8,128)(2,1)S(1)}, u32[]{:S(2)}, u32[]{:S(2)}) collective-permute-start(bf16[128,128]{1,0:T(8,128)(2,1)S(1)} %get-tuple-element.61), channel_id=1, source_target_pairs={{0,8},{1,9},{2,10},{3,11},{4,12},{5,13},{6,14},{7,15},{8,0},{9,1},... | collective-permute-start | bytes 98312 | tf_op jit(solution)/shard_map/ppermute | solution.py:128
  2.2 5.9 %collective-permute-start.1 = (bf16[128,128]{1,0:T(8,128)(2,1)S(1)}, bf16[128,128]{1,0:T(8,128)(2,1)S(1)}, u32[]{:S(2)}, u32[]{:S(2)}) collective-permute-start(bf16[128,128]{1,0:T(8,128)(2,1)S(1)} %get-tuple-element.62), channel_id=1, source_target_pairs={{0,4},{1,5},{2,6},{3,7},{4,0},{5,1},{6,2},{7,3},{8,16},{9,17},{10,... | collective-permute-start | bytes 98312 | tf_op jit(solution)/shard_map/ppermute | solution.py:128
  8.2 7.0 %collective-permute-start.3 = (bf16[32,128]{1,0:T(8,128)(2,1)S(1)}, bf16[32,128]{1,0:T(8,128)(2,1)S(1)}, u32[]{:S(2)}, u32[]{:S(2)}) collective-permute-start(bf16[32,128]{1,0:T(8,128)(2,1)S(1)} %get-tuple-element.79), channel_id=1, source_target_pairs={{0,7},{1,2},{2,1},{3,4},{4,3},{5,6},{6,5},{7,0},{8,15},{9,10},{10,... | collective-permute-start | bytes 24584 | tf_op jit(solution)/shard_map/ppermute | solution.py:128
  13.0 3.7 %collective-permute-start.2 = (bf16[32,128]{1,0:T(8,128)(2,1)S(1)}, bf16[32,128]{1,0:T(8,128)(2,1)S(1)}, u32[]{:S(2)}, u32[]{:S(2)}) collective-permute-start(bf16[32,128]{1,0:T(8,128)(2,1)S(1)} %get-tuple-element.79), channel_id=1, source_target_pairs={{0,1},{1,0},{2,3},{3,2},{4,5},{5,4},{6,7},{7,6},{8,9},{9,8},{10,11... | collective-permute-start | bytes 24584 | tf_op jit(solution)/shard_map/ppermute | solution.py:128
  17.6 1.6 %collective-permute-start.8 = (bf16[1152,128]{1,0:T(8,128)(2,1)S(1)}, bf16[1152,128]{1,0:T(8,128)(2,1)S(1)}, u32[]{:S(2)}, u32[]{:S(2)}) collective-permute-start(bf16[1152,128]{1,0:T(8,128)(2,1)S(1)} %get-tuple-element.98), channel_id=1, source_target_pairs={{0,8},{1,9},{2,10},{3,11},{4,12},{5,13},{6,14},{7,15},{8,0},{9,1},... | collective-permute-start | bytes 884744 | tf_op jit(solution)/shard_map/ppermute | solution.py:128
  19.3 6.2 %collective-permute-start.9 = (bf16[304,128]{1,0:T(8,128)(2,1)S(1)}, bf16[304,128]{1,0:T(8,128)(2,1)S(1)}, u32[]{:S(2)}, u32[]{:S(2)}) collective-permute-start(bf16[304,128]{1,0:T(8,128)(2,1)S(1)} %get-tuple-element.100), channel_id=1, source_target_pairs={{0,17},{1,16},{2,19},{3,18},{4,21},{5,20},{6,23},{7,22},{8,25},{9,... | collective-permute-start | bytes 233480 | tf_op jit(solution)/shard_map/ppermute | solution.py:128
  19.4 6.1 %collective-permute-start.10 = (bf16[304,128]{1,0:T(8,128)(2,1)S(1)}, bf16[304,128]{1,0:T(8,128)(2,1)S(1)}, u32[]{:S(2)}, u32[]{:S(2)}) collective-permute-start(bf16[304,128]{1,0:T(8,128)(2,1)S(1)} %get-tuple-element.101), channel_id=1, source_target_pairs={{0,16},{1,17},{2,18},{3,19},{4,20},{5,21},{6,22},{7,23},{8,24},{9,... | collective-permute-start | bytes 233480 | tf_op jit(solution)/shard_map/ppermute | solution.py:128
  21.5 4.9 %collective-permute-start.11 = (bf16[304,128]{1,0:T(8,128)(2,1)S(1)}, bf16[304,128]{1,0:T(8,128)(2,1)S(1)}, u32[]{:S(2)}, u32[]{:S(2)}) collective-permute-start(bf16[304,128]{1,0:T(8,128)(2,1)S(1)} %get-tuple-element.102), channel_id=1, source_target_pairs={{0,1},{1,0},{2,3},{3,2},{4,5},{5,4},{6,7},{7,6},{8,9},{9,8},{10,11... | collective-permute-start | bytes 233480 | tf_op jit(solution)/shard_map/ppermute | solution.py:128
  26.4 4.7 %collective-permute-start.12 = (bf16[304,128]{1,0:T(8,128)(2,1)S(1)}, bf16[304,128]{1,0:T(8,128)(2,1)S(1)}, u32[]{:S(2)}, u32[]{:S(2)}) collective-permute-start(bf16[304,128]{1,0:T(8,128)(2,1)S(1)} %shard_map.162.own), channel_id=1, source_target_pairs={{0,2},{1,3},{2,0},{3,1},{4,6},{5,7},{6,4},{7,5},{8,12},{9,13},{10,... | collective-permute-start | bytes 233480 | tf_op jit(solution)/shard_map/ppermute | solution.py:128
  26.5 5.3 %collective-permute-start.5 = (bf16[256,128]{1,0:T(8,128)(2,1)S(1)}, bf16[256,128]{1,0:T(8,128)(2,1)S(1)}, u32[]{:S(2)}, u32[]{:S(2)}) collective-permute-start(bf16[256,128]{1,0:T(8,128)(2,1)S(1)} %get-tuple-element.92), channel_id=1, source_target_pairs={{0,4},{1,5},{2,6},{3,7},{4,0},{5,1},{6,2},{7,3},{8,16},{9,17},{10,... | collective-permute-start | bytes 196616 | tf_op jit(solution)/shard_map/ppermute | solution.py:128
  29.2 2.6 %collective-permute-start.4 = (bf16[256,128]{1,0:T(8,128)(2,1)S(1)}, bf16[256,128]{1,0:T(8,128)(2,1)S(1)}, u32[]{:S(2)}, u32[]{:S(2)}) collective-permute-start(bf16[256,128]{1,0:T(8,128)(2,1)S(1)} %get-tuple-element.91.refs_3_), channel_id=1, source_target_pairs={{0,8},{1,9},{2,10},{3,11},{4,12},{5,13},{6,14},{7,15},{8,0},{9,1},... | collective-permute-start | bytes 196616 | tf_op jit(solution)/shard_map/ppermute | solution.py:128
  31.1 6.2 %collective-permute-start.13 = (bf16[304,128]{1,0:T(8,128)(2,1)S(1)}, bf16[304,128]{1,0:T(8,128)(2,1)S(1)}, u32[]{:S(2)}, u32[]{:S(2)}) collective-permute-start(bf16[304,128]{1,0:T(8,128)(2,1)S(1)} %shard_map.163.own), channel_id=1, source_target_pairs={{0,4},{1,5},{2,6},{3,7},{4,0},{5,1},{6,2},{7,3},{8,10},{9,11},{10,... | collective-permute-start | bytes 233480 | tf_op jit(solution)/shard_map/ppermute | solution.py:128
  31.9 9.3 %collective-permute-start.7 = (bf16[256,128]{1,0:T(8,128)(2,1)S(1)}, bf16[256,128]{1,0:T(8,128)(2,1)S(1)}, u32[]{:S(2)}, u32[]{:S(2)}) collective-permute-start(bf16[256,128]{1,0:T(8,128)(2,1)S(1)} %shard_map.159), channel_id=1, source_target_pairs={{0,7},{1,2},{2,1},{3,4},{4,3},{5,6},{6,5},{7,0},{8,15},{9,10},{10,... | collective-permute-start | bytes 196616 | tf_op jit(solution)/shard_map/ppermute | solution.py:128
  35.2 6.1 %collective-permute-start.6 = (bf16[256,128]{1,0:T(8,128)(2,1)S(1)}, bf16[256,128]{1,0:T(8,128)(2,1)S(1)}, u32[]{:S(2)}, u32[]{:S(2)}) collective-permute-start(bf16[256,128]{1,0:T(8,128)(2,1)S(1)} %shard_map.159), channel_id=1, source_target_pairs={{0,1},{1,0},{2,3},{3,2},{4,5},{5,4},{6,7},{7,6},{8,9},{9,8},{10,11... | collective-permute-start | bytes 196616 | tf_op jit(solution)/shard_map/ppermute | solution.py:128
  37.3 6.0 %collective-permute-start.16 = (bf16[304,128]{1,0:T(8,128)(2,1)S(1)}, bf16[304,128]{1,0:T(8,128)(2,1)S(1)}, u32[]{:S(2)}, u32[]{:S(2)}) collective-permute-start(bf16[304,128]{1,0:T(8,128)(2,1)S(1)} %get-tuple-element.107.refs_0_), channel_id=1, source_target_pairs={{0,17},{1,16},{2,19},{3,18},{4,21},{5,20},{6,23},{7,22},{8,25},{9,... | collective-permute-start | bytes 233480 | tf_op jit(solution)/shard_map/ppermute | solution.py:128
  38.5 5.9 %collective-permute-start.15 = (bf16[304,128]{1,0:T(8,128)(2,1)S(1)}, bf16[304,128]{1,0:T(8,128)(2,1)S(1)}, u32[]{:S(2)}, u32[]{:S(2)}) collective-permute-start(bf16[304,128]{1,0:T(8,128)(2,1)S(1)} %get-tuple-element.107.refs_0_), channel_id=1, source_target_pairs={{0,16},{1,17},{2,18},{3,19},{4,20},{5,21},{6,22},{7,23},{8,24},{9,... | collective-permute-start | bytes 233480 | tf_op jit(solution)/shard_map/ppermute | solution.py:128
  41.3 4.4 %collective-permute-start.14 = (bf16[304,128]{1,0:T(8,128)(2,1)S(1)}, bf16[304,128]{1,0:T(8,128)(2,1)S(1)}, u32[]{:S(2)}, u32[]{:S(2)}) collective-permute-start(bf16[304,128]{1,0:T(8,128)(2,1)S(1)} %get-tuple-element.107.refs_0_), channel_id=1, source_target_pairs={{0,1},{1,0},{2,3},{3,2},{4,5},{5,4},{6,7},{7,6},{8,9},{9,8},{10,11... | collective-permute-start | bytes 233480 | tf_op jit(solution)/shard_map/ppermute | solution.py:128
  45.7 1.7 %collective-permute-start.17 = (bf16[4,304,128]{2,1,0:T(8,128)(2,1)S(1)}, bf16[4,304,128]{2,1,0:T(8,128)(2,1)S(1)}, u32[]{:S(2)}, u32[]{:S(2)}) collective-permute-start(bf16[4,304,128]{2,1,0:T(8,128)(2,1)S(1)} %shard_map.166.own), channel_id=1, source_target_pairs={{0,8},{1,9},{2,10},{3,11},{4,12},{5,13},{6,14},{7,15},{8,0},{9,1},... | collective-permute-start | bytes 933896 | tf_op jit(solution)/shard_map/ppermute | solution.py:128

commit v4 on v3

--- a/solution.py
+++ b/solution.py
@@ -319,7 +319,7 @@
     fields_strip_out[...] = fields_strip
 
 
-def columns_kernel(row_count, groups, columns, inner, outer, packed_out, *whole_out):
+def columns_kernel(row_count, groups, columns, outer, inner, packed_out, *whole_out):
     north, south = row_halo(inner, outer)
     value = edge_columns(north, 0, columns[...].astype(F32))
     value = edge_columns(south, row_count + 1, value)
@@ -483,8 +483,8 @@
     row_count,
     edge,
     second,
+    outer_column,
     inner_column,
-    outer_column,
     weights,
     bias_wide,
     readout_wide,
@@ -680,10 +680,10 @@
 def field_kernel(
     place,
     pre,
+    outer_row,
     inner_row,
-    outer_row,
+    outer_column,
     inner_column,
-    outer_column,
     weights,
     after,
     inputs_out,
@@ -844,9 +844,9 @@
     columns, edge = call(
         bind(columns_kernel, row_count, GROUPS),
         (sds((channels // GROUPS, width), BF16), sds((channels, width), BF16)),
-    )(columns, inner, outer)
+    )(columns, outer, inner)
+    inner_column = permuted(columns, inner_columns)
     outer_column = permuted(columns, outer_columns)
-    inner_column = permuted(columns, inner_columns)
     hidden_rows, cell_rows, grad_cell_rows, pre, second, sums, bias = call(
         bind(gates_kernel, place),
         (
@@ -890,8 +890,8 @@
     )(
         edge,
         second,
+        outer_column,
         inner_column,
-        outer_column,
         weights_here,
         bias_wide,
         readout_wide,
@@ -928,7 +928,7 @@
     pre_columns = call(
         bind(columns_kernel, row_count, PRE_GROUPS),
         (sds((gate_count // PRE_GROUPS, width), BF16),),
-    )(pre_strip, pre_inner, pre_outer)[0]
+    )(pre_strip, pre_outer, pre_inner)[0]
 
     block = sds((BIAS_ROWS + place.chunk, channels), BF16)
     token = sds((8, width), F32)
@@ -940,8 +940,8 @@
     )(keep, bias, permuted(send, place.phase_pairs(0)))
     received = [permuted(send, place.plane_pairs(step)) for step, send in zip(steps, sends)]
     part = call(plane_kernel, block)(keep, bias, *received, after)
+    pre_inner_columns = permuted(pre_columns, inner_columns)
     pre_outer_columns = permuted(pre_columns, outer_columns)
-    pre_inner_columns = permuted(pre_columns, inner_columns)
     phases = len(place.orders[0])
     for phase in range(1, phases):
         is_last = phase == phases - 1
@@ -964,10 +964,10 @@
         moved=2_000_000,
     )(
         pre,
+        pre_outer,
         pre_inner,
-        pre_outer,
+        pre_outer_columns,
         pre_inner_columns,
-        pre_outer_columns,
         weights_here,
         *summed,
     )

time: 48.4 us -> 47 us (0.971)
  waiting for transfers between devices: 11.2 us -> 8.23 us
  starting transfers between devices: 23.4 us -> 24.9 us
    ppermute x18, waiting for transfers between devices: 11.2 us -> 8.23 us  [permuted(): return lax.ppermute(value, AXES, pairs)]
    ppermute x18, starting transfers between devices: 23.4 us -> 24.9 us  [permuted(): return lax.ppermute(value, AXES, pairs)]
  transfers between devices with their start and end apart: 18 -> 18, of which waited for: 10 -> 10; matrix products, arithmetic and copies ran while one was open for 0% -> 0% of each run, Pallas kernels for 20% -> 21%
where the time goes in v4:
time: 47 us; the launch traced here: 46.8 us
  starting transfers between devices  24.9 us (53%)
  Pallas kernels  12.9 us (27%)
  waiting for transfers between devices  8.23 us (18%)
  between operations  0.78 us (2%)
    ppermute x18, starting transfers between devices, permuted(): return lax.ppermute(value, AXES, pairs)  24.9 us
    pallas_call x16, Pallas kernels, run(): pl.pallas_call(kernel, out_shape=out_shape, in_specs=[VMEM] * near + [HBM...  12.9 us
    ppermute x18, waiting for transfers between devices, permuted(): return lax.ppermute(value, AXES, pairs)  8.23 us
  transfers between devices with their start and end apart: 18, of which 10 were waited for; matrix products, arithmetic and copies ran while one was open for 0% of the time, Pallas kernels for 21%

profile of v4, /device:TPU:0, one launch (start us, length us, event | category | flops | bytes accessed | tf_op | source)
XLA Modules:
  0.0 46.8 jit_solution(8517978809874553546)
XLA Ops:
  0.6 1.0 %shard_map.153 = (bf16[128,128]{1,0:T(8,128)(2,1)S(1)}, bf16[128,128]{1,0:T(8,128)(2,1)S(1)}, f32[1024,128]{1,0:T(8,128)S(1)}) custom-call(bf16[64,8,128]{2,1,0:T(8,128)(2,1)} %below.1, bf16[64,8,128]{2,1,0:T(8,128)(2,1)} %hidden.1), custom_call_target="tpu_custom_call" | custom-call | bytes 524288 | tf_op jit(solution)/shard_map/pallas_call | solution.py:45
  1.7 0.5 %collective-permute-start = (bf16[128,128]{1,0:T(8,128)(2,1)S(1)}, bf16[128,128]{1,0:T(8,128)(2,1)S(1)}, u32[]{:S(2)}, u32[]{:S(2)}) collective-permute-start(bf16[128,128]{1,0:T(8,128)(2,1)S(1)} %get-tuple-element.61), channel_id=1, source_target_pairs={{0,8},{1,9},{2,10},{3,11},{4,12},{5,13},{6,14},{7,15},{8,0},{9,1},... | collective-permute-start | bytes 98312 | tf_op jit(solution)/shard_map/ppermute | solution.py:128
  2.2 3.7 %collective-permute-start.1 = (bf16[128,128]{1,0:T(8,128)(2,1)S(1)}, bf16[128,128]{1,0:T(8,128)(2,1)S(1)}, u32[]{:S(2)}, u32[]{:S(2)}) collective-permute-start(bf16[128,128]{1,0:T(8,128)(2,1)S(1)} %get-tuple-element.62), channel_id=1, source_target_pairs={{0,4},{1,5},{2,6},{3,7},{4,0},{5,1},{6,2},{7,3},{8,16},{9,17},{10,... | collective-permute-start | bytes 98312 | tf_op jit(solution)/shard_map/ppermute | solution.py:128
  5.8 2.2 %shard_map.154 = (bf16[8,128,128]{2,1,0:T(8,128)(2,1)S(1)}, f32[128,128]{1,0:T(8,128)S(1)}, f32[128,128]{1,0:T(8,128)S(1)}, f32[64,128]{1,0:T(8,128)S(1)}, f32[6...) custom-call(f32[1024,128]{1,0:T(8,128)S(1)} %get-tuple-element.59.wi, ...), custom_call_target="tpu_custom_call" | custom-call | bytes 6000000 | tf_op jit(solution)/shard_map/pallas_call | solution.py:45
  8.0 0.0 collective-permute-done.inner_row.inner
  8.0 0.0 collective-permute-done.1.outer_row.outer
  8.0 0.2 shard_map.156
  8.2 1.5 %collective-permute-start.3 = (bf16[32,128]{1,0:T(8,128)(2,1)S(1)}, bf16[32,128]{1,0:T(8,128)(2,1)S(1)}, u32[]{:S(2)}, u32[]{:S(2)}) collective-permute-start(bf16[32,128]{1,0:T(8,128)(2,1)S(1)} %get-tuple-element.79), channel_id=1, source_target_pairs={{0,1},{1,0},{2,3},{3,2},{4,5},{5,4},{6,7},{7,6},{8,9},{9,8},{10,11... | collective-permute-start | bytes 24584 | tf_op jit(solution)/shard_map/ppermute | solution.py:128
  9.8 3.8 %collective-permute-start.2 = (bf16[32,128]{1,0:T(8,128)(2,1)S(1)}, bf16[32,128]{1,0:T(8,128)(2,1)S(1)}, u32[]{:S(2)}, u32[]{:S(2)}) collective-permute-start(bf16[32,128]{1,0:T(8,128)(2,1)S(1)} %get-tuple-element.79), channel_id=1, source_target_pairs={{0,7},{1,2},{2,1},{3,4},{4,3},{5,6},{6,5},{7,0},{8,15},{9,10},{10,... | collective-permute-start | bytes 24584 | tf_op jit(solution)/shard_map/ppermute | solution.py:128
  13.5 2.2 %shard_map.155 = (f32[512,128]{1,0:T(8,128)S(1)}, f32[512,128]{1,0:T(8,128)S(1)}, f32[512,128]{1,0:T(8,128)S(1)}, bf16[256,1024]{1,0:T(8,128)(2,1)S(1)}, bf16[12...) custom-call(bf16[8,128,128]{2,1,0:T(8,128)(2,1)S(1)} %get-tuple-element.60.rows_in, ...), custom_call_target="tpu_custom_call" | custom-call | flops 1207959552 | bytes 6000000 | tf_op jit(solution)/shard_map/pallas_call | solution.py:45
  15.8 0.0 collective-permute-done.3.inner_column
  15.8 0.3 collective-permute-done.2.outer_column
  16.1 0.9 %shard_map.157 = (bf16[1152,128]{1,0:T(8,128)(2,1)S(1)}, bf16[256,128]{1,0:T(8,128)(2,1)S(1)}, f32[256,128]{1,0:T(8,128)S(1)}, bf16[1152,128]{1,0:T(8,128)(2,1)S...) custom-call(bf16[128,128]{1,0:T(8,128)(2,1)S(1)} %get-tuple-element.77.edge, ...), custom_call_target="tpu_custom_call" | custom-call | tf_op jit(solution)/shard_map/pallas_call | solution.py:45
  17.0 0.1 collective-permute-start.8
  17.1 0.3 shard_map.160
  17.3 1.3 %collective-permute-done.8.received = bf16[1152,128]{1,0:T(8,128)(2,1)S(1)} collective-permute-done((bf16[1152,128]{1,0:T(8,128)(2,1)S(1)}, bf16[1152,128]{1,0:T(8,128)(2,1)S(1)}, u32[]{:S(2)}, u32[]{:S(2)}) %collective-permute-start.8) | collective-permute-done | bytes 294944 | tf_op jit(solution)/shard_map/ppermute | solution.py:128
  18.6 0.1 shard_map.161
  18.7 0.1 collective-permute-start.9
  18.8 0.4 collective-permute-start.10
  19.2 3.1 %collective-permute-start.11 = (bf16[304,128]{1,0:T(8,128)(2,1)S(1)}, bf16[304,128]{1,0:T(8,128)(2,1)S(1)}, u32[]{:S(2)}, u32[]{:S(2)}) collective-permute-start(bf16[304,128]{1,0:T(8,128)(2,1)S(1)} %get-tuple-element.102), channel_id=1, source_target_pairs={{0,1},{1,0},{2,3},{3,2},{4,5},{5,4},{6,7},{7,6},{8,9},{9,8},{10,11... | collective-permute-start | bytes 233480 | tf_op jit(solution)/shard_map/ppermute | solution.py:128
  22.3 2.0 %shard_map.158 = (bf16[64,8,128]{2,1,0:T(8,128)(2,1)}, f32[512,128]{1,0:T(8,128)}, f32[512,128]{1,0:T(8,128)}, bf16[256,1024]{1,0:T(8,128)(2,1)S(1)}, bf16[256,1...) custom-call(f32[512,128]{1,0:T(8,128)S(1)} %get-tuple-element.72.hidden, f32[512,128]{1,0:T(8,128)S(1)} %get-tuple-element.73.cell, ...), custom_call_target="tpu_custom_call" | custom-call | bytes 4000000 | tf_op jit(solution)/shard_map/pallas_call | solution.py:45
  24.2 0.6 %collective-permute-done.9.refs_0_ = bf16[304,128]{1,0:T(8,128)(2,1)S(1)} collective-permute-done((bf16[304,128]{1,0:T(8,128)(2,1)S(1)}, bf16[304,128]{1,0:T(8,128)(2,1)S(1)}, u32[]{:S(2)}, u32[]{:S(2)}) %collective-permute-start.9) | collective-permute-done | bytes 77856 | tf_op jit(solution)/shard_map/ppermute | solution.py:128
  24.9 0.0 collective-permute-done.10.refs_1_
  24.9 0.9 %collective-permute-done.11.refs_2_ = bf16[304,128]{1,0:T(8,128)(2,1)S(1)} collective-permute-done((bf16[304,128]{1,0:T(8,128)(2,1)S(1)}, bf16[304,128]{1,0:T(8,128)(2,1)S(1)}, u32[]{:S(2)}, u32[]{:S(2)}) %collective-permute-start.11) | collective-permute-done | bytes 77856 | tf_op jit(solution)/shard_map/ppermute | solution.py:128
  25.8 0.1 collective-permute-start.12
  25.9 3.8 %collective-permute-start.4 = (bf16[256,128]{1,0:T(8,128)(2,1)S(1)}, bf16[256,128]{1,0:T(8,128)(2,1)S(1)}, u32[]{:S(2)}, u32[]{:S(2)}) collective-permute-start(bf16[256,128]{1,0:T(8,128)(2,1)S(1)} %get-tuple-element.91), channel_id=1, source_target_pairs={{0,4},{1,5},{2,6},{3,7},{4,0},{5,1},{6,2},{7,3},{8,16},{9,17},{10,... | collective-permute-start | bytes 196616 | tf_op jit(solution)/shard_map/ppermute | solution.py:128
  29.7 0.0 collective-permute-start.5
  29.7 1.4 %collective-permute-done.12.received = bf16[304,128]{1,0:T(8,128)(2,1)S(1)} collective-permute-done((bf16[304,128]{1,0:T(8,128)(2,1)S(1)}, bf16[304,128]{1,0:T(8,128)(2,1)S(1)}, u32[]{:S(2)}, u32[]{:S(2)}) %collective-permute-start.12) | collective-permute-done | bytes 77856 | tf_op jit(solution)/shard_map/ppermute | solution.py:128
  31.1 1.0 %collective-permute-start.13 = (bf16[304,128]{1,0:T(8,128)(2,1)S(1)}, bf16[304,128]{1,0:T(8,128)(2,1)S(1)}, u32[]{:S(2)}, u32[]{:S(2)}) collective-permute-start(bf16[304,128]{1,0:T(8,128)(2,1)S(1)} %shard_map.163.own), channel_id=1, source_target_pairs={{0,4},{1,5},{2,6},{3,7},{4,0},{5,1},{6,2},{7,3},{8,10},{9,11},{10,... | collective-permute-start | bytes 233480 | tf_op jit(solution)/shard_map/ppermute | solution.py:128
  32.1 0.5 %collective-permute-done.4.outer.outer_row = bf16[256,128]{1,0:T(8,128)(2,1)S(1)} collective-permute-done((bf16[256,128]{1,0:T(8,128)(2,1)S(1)}, bf16[256,128]{1,0:T(8,128)(2,1)S(1)}, u32[]{:S(2)}, u32[]{:S(2)}) %collective-permute-start.4) | collective-permute-done | bytes 65568 | tf_op jit(solution)/shard_map/ppermute | solution.py:128
  32.6 0.0 collective-permute-done.5.inner.inner_row
  32.6 0.1 shard_map.159
  32.8 1.6 %collective-permute-start.7 = (bf16[256,128]{1,0:T(8,128)(2,1)S(1)}, bf16[256,128]{1,0:T(8,128)(2,1)S(1)}, u32[]{:S(2)}, u32[]{:S(2)}) collective-permute-start(bf16[256,128]{1,0:T(8,128)(2,1)S(1)} %shard_map.159), channel_id=1, source_target_pairs={{0,1},{1,0},{2,3},{3,2},{4,5},{5,4},{6,7},{7,6},{8,9},{9,8},{10,11... | collective-permute-start | bytes 196616 | tf_op jit(solution)/shard_map/ppermute | solution.py:128
  34.3 1.7 %collective-permute-start.6 = (bf16[256,128]{1,0:T(8,128)(2,1)S(1)}, bf16[256,128]{1,0:T(8,128)(2,1)S(1)}, u32[]{:S(2)}, u32[]{:S(2)}) collective-permute-start(bf16[256,128]{1,0:T(8,128)(2,1)S(1)} %shard_map.159), channel_id=1, source_target_pairs={{0,7},{1,2},{2,1},{3,4},{4,3},{5,6},{6,5},{7,0},{8,15},{9,10},{10,... | collective-permute-start | bytes 196616 | tf_op jit(solution)/shard_map/ppermute | solution.py:128
  36.0 1.5 %collective-permute-done.13.received = bf16[304,128]{1,0:T(8,128)(2,1)S(1)} collective-permute-done((bf16[304,128]{1,0:T(8,128)(2,1)S(1)}, bf16[304,128]{1,0:T(8,128)(2,1)S(1)}, u32[]{:S(2)}, u32[]{:S(2)}) %collective-permute-start.13) | collective-permute-done | bytes 77856 | tf_op jit(solution)/shard_map/ppermute | solution.py:128
  37.5 0.1 collective-permute-start.16
  37.6 2.2 %collective-permute-start.15 = (bf16[304,128]{1,0:T(8,128)(2,1)S(1)}, bf16[304,128]{1,0:T(8,128)(2,1)S(1)}, u32[]{:S(2)}, u32[]{:S(2)}) collective-permute-start(bf16[304,128]{1,0:T(8,128)(2,1)S(1)} %get-tuple-element.107.refs_0_), channel_id=1, source_target_pairs={{0,16},{1,17},{2,18},{3,19},{4,20},{5,21},{6,22},{7,23},{8,24},{9,... | collective-permute-start | bytes 233480 | tf_op jit(solution)/shard_map/ppermute | solution.py:128
  39.8 1.3 %collective-permute-start.14 = (bf16[304,128]{1,0:T(8,128)(2,1)S(1)}, bf16[304,128]{1,0:T(8,128)(2,1)S(1)}, u32[]{:S(2)}, u32[]{:S(2)}) collective-permute-start(bf16[304,128]{1,0:T(8,128)(2,1)S(1)} %get-tuple-element.107.refs_0_), channel_id=1, source_target_pairs={{0,1},{1,0},{2,3},{3,2},{4,5},{5,4},{6,7},{7,6},{8,9},{9,8},{10,11... | collective-permute-start | bytes 233480 | tf_op jit(solution)/shard_map/ppermute | solution.py:128
  41.1 0.0 collective-permute-done.7.inner_column
  41.1 0.2 collective-permute-done.6.outer_column
  41.3 2.1 %shard_map.165 = (bf16[64,8,128]{2,1,0:T(8,128)(2,1)}, bf16[64,8,128]{2,1,0:T(8,128)(2,1)}, f32[8,128]{1,0:T(8,128)S(1)}) custom-call(bf16[256,1024]{1,0:T(8,128)(2,1)S(1)} %get-tuple-element.90.pre, bf16[256,128]{1,0:T(8,128)(2,1)S(1)} %collective-permute-done.4.outer.outer_row, bf16[256,128]{1,0:T(8,128)(2,1)S(1)} %collective-permute-done.5.inner.inner_row, ...), custom_call_target="tpu_custom_call" | custom-call | flops 603979776 | bytes 2000000 | tf_op jit(solution)/shard_map/pallas_call | solution.py:45
  43.4 0.0 collective-permute-done.16.refs_3_
  43.4 0.0 collective-permute-done.15.refs_2_
  43.4 0.8 %collective-permute-done.14.refs_1_ = bf16[304,128]{1,0:T(8,128)(2,1)S(1)} collective-permute-done((bf16[304,128]{1,0:T(8,128)(2,1)S(1)}, bf16[304,128]{1,0:T(8,128)(2,1)S(1)}, u32[]{:S(2)}, u32[]{:S(2)}) %collective-permute-start.14) | collective-permute-done | bytes 77856 | tf_op jit(solution)/shard_map/ppermute | solution.py:128
  44.3 0.1 collective-permute-start.17
  44.3 0.9 %shard_map.167.out_before = f32[9,256,128]{2,1,0:T(8,128)} custom-call(bf16[4,304,128]{2,1,0:T(8,128)(2,1)S(1)} %shard_map.166.own), custom_call_target="tpu_custom_call" | custom-call | bytes 884736 | tf_op jit(solution)/shard_map/pallas_call | solution.py:45
  45.2 0.7 %collective-permute-done.17.received = bf16[4,304,128]{2,1,0:T(8,128)(2,1)S(1)} collective-permute-done((bf16[4,304,128]{2,1,0:T(8,128)(2,1)S(1)}, bf16[4,304,128]{2,1,0:T(8,128)(2,1)S(1)}, u32[]{:S(2)}, u32[]{:S(2)}) %collective-permute-start.17) | collective-permute-done | bytes 311328 | tf_op jit(solution)/shard_map/ppermute | solution.py:128
  45.9 0.9 %shard_map.168 = (f32[9,256,128]{2,1,0:T(8,128)}, f32[256]{0:T(256)}) custom-call(bf16[4,304,128]{2,1,0:T(8,128)(2,1)S(1)} %shard_map.166.own, bf16[4,304,128]{2,1,0:T(8,128)(2,1)S(1)} %collective-permute-done.17.received, f32[9,256,128]{2,1,0:T(8,128)} %shard_map.167.out_before), custom_call_target="tpu_custom_call", output_to_operand_aliasing={{0}: (2, {})} | custom-call | bytes 884736 | tf_op jit(solution)/shard_map/pallas_call | solution.py:45
  (4 shorter events, 0.1 us)
Async XLA Ops:
  1.7 6.4 %collective-permute-start = (bf16[128,128]{1,0:T(8,128)(2,1)S(1)}, bf16[128,128]{1,0:T(8,128)(2,1)S(1)}, u32[]{:S(2)}, u32[]{:S(2)}) collective-permute-start(bf16[128,128]{1,0:T(8,128)(2,1)S(1)} %get-tuple-element.61), channel_id=1, source_target_pairs={{0,8},{1,9},{2,10},{3,11},{4,12},{5,13},{6,14},{7,15},{8,0},{9,1},... | collective-permute-start | bytes 98312 | tf_op jit(solution)/shard_map/ppermute | solution.py:128
  2.2 5.9 %collective-permute-start.1 = (bf16[128,128]{1,0:T(8,128)(2,1)S(1)}, bf16[128,128]{1,0:T(8,128)(2,1)S(1)}, u32[]{:S(2)}, u32[]{:S(2)}) collective-permute-start(bf16[128,128]{1,0:T(8,128)(2,1)S(1)} %get-tuple-element.62), channel_id=1, source_target_pairs={{0,4},{1,5},{2,6},{3,7},{4,0},{5,1},{6,2},{7,3},{8,16},{9,17},{10,... | collective-permute-start | bytes 98312 | tf_op jit(solution)/shard_map/ppermute | solution.py:128
  8.2 7.6 %collective-permute-start.3 = (bf16[32,128]{1,0:T(8,128)(2,1)S(1)}, bf16[32,128]{1,0:T(8,128)(2,1)S(1)}, u32[]{:S(2)}, u32[]{:S(2)}) collective-permute-start(bf16[32,128]{1,0:T(8,128)(2,1)S(1)} %get-tuple-element.79), channel_id=1, source_target_pairs={{0,1},{1,0},{2,3},{3,2},{4,5},{5,4},{6,7},{7,6},{8,9},{9,8},{10,11... | collective-permute-start | bytes 24584 | tf_op jit(solution)/shard_map/ppermute | solution.py:128
  9.8 6.3 %collective-permute-start.2 = (bf16[32,128]{1,0:T(8,128)(2,1)S(1)}, bf16[32,128]{1,0:T(8,128)(2,1)S(1)}, u32[]{:S(2)}, u32[]{:S(2)}) collective-permute-start(bf16[32,128]{1,0:T(8,128)(2,1)S(1)} %get-tuple-element.79), channel_id=1, source_target_pairs={{0,7},{1,2},{2,1},{3,4},{4,3},{5,6},{6,5},{7,0},{8,15},{9,10},{10,... | collective-permute-start | bytes 24584 | tf_op jit(solution)/shard_map/ppermute | solution.py:128
  17.0 1.6 %collective-permute-start.8 = (bf16[1152,128]{1,0:T(8,128)(2,1)S(1)}, bf16[1152,128]{1,0:T(8,128)(2,1)S(1)}, u32[]{:S(2)}, u32[]{:S(2)}) collective-permute-start(bf16[1152,128]{1,0:T(8,128)(2,1)S(1)} %get-tuple-element.98), channel_id=1, source_target_pairs={{0,8},{1,9},{2,10},{3,11},{4,12},{5,13},{6,14},{7,15},{8,0},{9,1},... | collective-permute-start | bytes 884744 | tf_op jit(solution)/shard_map/ppermute | solution.py:128
  18.7 6.2 %collective-permute-start.9 = (bf16[304,128]{1,0:T(8,128)(2,1)S(1)}, bf16[304,128]{1,0:T(8,128)(2,1)S(1)}, u32[]{:S(2)}, u32[]{:S(2)}) collective-permute-start(bf16[304,128]{1,0:T(8,128)(2,1)S(1)} %get-tuple-element.100), channel_id=1, source_target_pairs={{0,17},{1,16},{2,19},{3,18},{4,21},{5,20},{6,23},{7,22},{8,25},{9,... | collective-permute-start | bytes 233480 | tf_op jit(solution)/shard_map/ppermute | solution.py:128
  18.8 6.1 %collective-permute-start.10 = (bf16[304,128]{1,0:T(8,128)(2,1)S(1)}, bf16[304,128]{1,0:T(8,128)(2,1)S(1)}, u32[]{:S(2)}, u32[]{:S(2)}) collective-permute-start(bf16[304,128]{1,0:T(8,128)(2,1)S(1)} %get-tuple-element.101), channel_id=1, source_target_pairs={{0,16},{1,17},{2,18},{3,19},{4,20},{5,21},{6,22},{7,23},{8,24},{9,... | collective-permute-start | bytes 233480 | tf_op jit(solution)/shard_map/ppermute | solution.py:128
  19.2 6.6 %collective-permute-start.11 = (bf16[304,128]{1,0:T(8,128)(2,1)S(1)}, bf16[304,128]{1,0:T(8,128)(2,1)S(1)}, u32[]{:S(2)}, u32[]{:S(2)}) collective-permute-start(bf16[304,128]{1,0:T(8,128)(2,1)S(1)} %get-tuple-element.102), channel_id=1, source_target_pairs={{0,1},{1,0},{2,3},{3,2},{4,5},{5,4},{6,7},{7,6},{8,9},{9,8},{10,11... | collective-permute-start | bytes 233480 | tf_op jit(solution)/shard_map/ppermute | solution.py:128
  25.8 5.3 %collective-permute-start.12 = (bf16[304,128]{1,0:T(8,128)(2,1)S(1)}, bf16[304,128]{1,0:T(8,128)(2,1)S(1)}, u32[]{:S(2)}, u32[]{:S(2)}) collective-permute-start(bf16[304,128]{1,0:T(8,128)(2,1)S(1)} %shard_map.162.own), channel_id=1, source_target_pairs={{0,2},{1,3},{2,0},{3,1},{4,6},{5,7},{6,4},{7,5},{8,12},{9,13},{10,... | collective-permute-start | bytes 233480 | tf_op jit(solution)/shard_map/ppermute | solution.py:128
  25.9 6.7 %collective-permute-start.4 = (bf16[256,128]{1,0:T(8,128)(2,1)S(1)}, bf16[256,128]{1,0:T(8,128)(2,1)S(1)}, u32[]{:S(2)}, u32[]{:S(2)}) collective-permute-start(bf16[256,128]{1,0:T(8,128)(2,1)S(1)} %get-tuple-element.91), channel_id=1, source_target_pairs={{0,4},{1,5},{2,6},{3,7},{4,0},{5,1},{6,2},{7,3},{8,16},{9,17},{10,... | collective-permute-start | bytes 196616 | tf_op jit(solution)/shard_map/ppermute | solution.py:128
  29.7 2.9 %collective-permute-start.5 = (bf16[256,128]{1,0:T(8,128)(2,1)S(1)}, bf16[256,128]{1,0:T(8,128)(2,1)S(1)}, u32[]{:S(2)}, u32[]{:S(2)}) collective-permute-start(bf16[256,128]{1,0:T(8,128)(2,1)S(1)} %get-tuple-element.92.refs_3_), channel_id=1, source_target_pairs={{0,8},{1,9},{2,10},{3,11},{4,12},{5,13},{6,14},{7,15},{8,0},{9,1},... | collective-permute-start | bytes 196616 | tf_op jit(solution)/shard_map/ppermute | solution.py:128
  31.1 6.4 %collective-permute-start.13 = (bf16[304,128]{1,0:T(8,128)(2,1)S(1)}, bf16[304,128]{1,0:T(8,128)(2,1)S(1)}, u32[]{:S(2)}, u32[]{:S(2)}) collective-permute-start(bf16[304,128]{1,0:T(8,128)(2,1)S(1)} %shard_map.163.own), channel_id=1, source_target_pairs={{0,4},{1,5},{2,6},{3,7},{4,0},{5,1},{6,2},{7,3},{8,10},{9,11},{10,... | collective-permute-start | bytes 233480 | tf_op jit(solution)/shard_map/ppermute | solution.py:128
  32.8 8.3 %collective-permute-start.7 = (bf16[256,128]{1,0:T(8,128)(2,1)S(1)}, bf16[256,128]{1,0:T(8,128)(2,1)S(1)}, u32[]{:S(2)}, u32[]{:S(2)}) collective-permute-start(bf16[256,128]{1,0:T(8,128)(2,1)S(1)} %shard_map.159), channel_id=1, source_target_pairs={{0,1},{1,0},{2,3},{3,2},{4,5},{5,4},{6,7},{7,6},{8,9},{9,8},{10,11... | collective-permute-start | bytes 196616 | tf_op jit(solution)/shard_map/ppermute | solution.py:128
  34.3 7.0 %collective-permute-start.6 = (bf16[256,128]{1,0:T(8,128)(2,1)S(1)}, bf16[256,128]{1,0:T(8,128)(2,1)S(1)}, u32[]{:S(2)}, u32[]{:S(2)}) collective-permute-start(bf16[256,128]{1,0:T(8,128)(2,1)S(1)} %shard_map.159), channel_id=1, source_target_pairs={{0,7},{1,2},{2,1},{3,4},{4,3},{5,6},{6,5},{7,0},{8,15},{9,10},{10,... | collective-permute-start | bytes 196616 | tf_op jit(solution)/shard_map/ppermute | solution.py:128
  37.5 5.9 %collective-permute-start.16 = (bf16[304,128]{1,0:T(8,128)(2,1)S(1)}, bf16[304,128]{1,0:T(8,128)(2,1)S(1)}, u32[]{:S(2)}, u32[]{:S(2)}) collective-permute-start(bf16[304,128]{1,0:T(8,128)(2,1)S(1)} %get-tuple-element.107.refs_0_), channel_id=1, source_target_pairs={{0,17},{1,16},{2,19},{3,18},{4,21},{5,20},{6,23},{7,22},{8,25},{9,... | collective-permute-start | bytes 233480 | tf_op jit(solution)/shard_map/ppermute | solution.py:128
  37.6 5.8 %collective-permute-start.15 = (bf16[304,128]{1,0:T(8,128)(2,1)S(1)}, bf16[304,128]{1,0:T(8,128)(2,1)S(1)}, u32[]{:S(2)}, u32[]{:S(2)}) collective-permute-start(bf16[304,128]{1,0:T(8,128)(2,1)S(1)} %get-tuple-element.107.refs_0_), channel_id=1, source_target_pairs={{0,16},{1,17},{2,18},{3,19},{4,20},{5,21},{6,22},{7,23},{8,24},{9,... | collective-permute-start | bytes 233480 | tf_op jit(solution)/shard_map/ppermute | solution.py:128
  39.8 4.4 %collective-permute-start.14 = (bf16[304,128]{1,0:T(8,128)(2,1)S(1)}, bf16[304,128]{1,0:T(8,128)(2,1)S(1)}, u32[]{:S(2)}, u32[]{:S(2)}) collective-permute-start(bf16[304,128]{1,0:T(8,128)(2,1)S(1)} %get-tuple-element.107.refs_0_), channel_id=1, source_target_pairs={{0,1},{1,0},{2,3},{3,2},{4,5},{5,4},{6,7},{7,6},{8,9},{9,8},{10,11... | collective-permute-start | bytes 233480 | tf_op jit(solution)/shard_map/ppermute | solution.py:128
  44.3 1.7 %collective-permute-start.17 = (bf16[4,304,128]{2,1,0:T(8,128)(2,1)S(1)}, bf16[4,304,128]{2,1,0:T(8,128)(2,1)S(1)}, u32[]{:S(2)}, u32[]{:S(2)}) collective-permute-start(bf16[4,304,128]{2,1,0:T(8,128)(2,1)S(1)} %shard_map.166.own), channel_id=1, source_target_pairs={{0,8},{1,9},{2,10},{3,11},{4,12},{5,13},{6,14},{7,15},{8,0},{9,1},... | collective-permute-start | bytes 933896 | tf_op jit(solution)/shard_map/ppermute | solution.py:128

commit v5 on v4

--- a/solution.py
+++ b/solution.py
@@ -13,7 +13,7 @@
 AXES = ("band", "core", "reach", "near")
 BIAS_ROWS = 16
 GROUPS = 4
-PRE_GROUPS = 1
+PRE_GROUPS = 4
 LAST = 16
 VMEM = pl.BlockSpec(memory_space=pltpu.VMEM)
 HBM = pl.BlockSpec(memory_space=pltpu.HBM)
@@ -195,28 +195,6 @@
     odd = is_odd("near")
     inner, outer = inner[...].astype(F32), outer[...].astype(F32)
     return unpacked(pick(odd, inner, outer), groups), unpacked(pick(odd, outer, inner), groups)
-
-
-def widened(row_count, rows, row_blocks, column_blocks, emit):
-    north, south = row_halo(*row_blocks)
-    west, east = column_halo(*column_blocks, PRE_GROUPS)
-    width = west.shape[1]
-    lane = lanes(west.shape)
-    for position in range(row_count + 2):
-        if position == 0:
-            row = north
-        elif position == row_count + 1:
-            row = south
-        else:
-            row = rows(position - 1)
-        left = rolled(west, -LAST - position)
-        right = rolled(east, width - 1 - position)
-        emit(
-            position,
-            jnp.where(lane == 0, left, rolled(row, 1)),
-            row,
-            jnp.where(lane == width - 1, right, rolled(row, -1)),
-        )
 
 
 def pack_kernel(below, hidden, inner_out, outer_out, wide_out, below_here, hidden_here, arrived):
@@ -565,22 +543,25 @@
     inner_out,
     outer_out,
     hidden_low,
+    hidden_here,
     cell_here,
     grad_cell_here,
     left,
 ):
     hid, _, width = hidden_low.shape
-    pairs = (
-        (cell, cell_strip, cell_here, cell_hbm),
-        (grad_cell, grad_cell_strip, grad_cell_here, grad_cell_hbm),
-    )
     leaving = []
-    for source, strip, here, target in pairs:
+    for source, strip, here, ready, target in (
+        (cell, cell_strip, cell_here, cell_here, cell_hbm),
+        (grad_cell, grad_cell_strip, grad_cell_here, grad_cell_here, grad_cell_hbm),
+        (hidden, hidden_strip, hidden_here, hidden_low, hidden_hbm),
+    ):
         columns = strip[...]
         for index in range(row_count):
             strided = pl.ds(index, hid, stride=row_count)
             here[strided, :] = at_edges(source[strided, :], index + 1, columns)
-        leaving.append(pltpu.make_async_copy(here, target, left.at[len(leaving)]))
+        if ready is hidden_low:
+            hidden_low[...] = here[...].reshape(hidden_low.shape).astype(BF16)
+        leaving.append(pltpu.make_async_copy(ready, target, left.at[len(leaving)]))
         leaving[-1].start()
     first, last = None, None
     columns = pre_strip[...].astype(F32)
@@ -593,14 +574,6 @@
     row_sends(first, last, inner_out, outer_out)
     for copy in leaving:
         copy.wait()
-    columns = hidden_strip[...]
-    for index in range(row_count):
-        strided = pl.ds(index, hid, stride=row_count)
-        cell_here[strided, :] = at_edges(hidden[strided, :], index + 1, columns)
-    hidden_low[...] = cell_here[...].reshape(hidden_low.shape).astype(BF16)
-    copy = pltpu.make_async_copy(hidden_low, hidden_hbm, left.at[2])
-    copy.start()
-    copy.wait()
 
 
 def pair_kernel(place, keep, bias, received, *outs):
@@ -633,13 +606,11 @@
         out[rank ^ step] = block[...]
 
 
-def add_kernel(scale, own, received, out, *done_out):
+def add_kernel(scale, own, received, out):
     here, there = own[...].astype(F32), received[...].astype(F32)
     bias = (decode(here[0:BIAS_ROWS]) + decode(there[0:BIAS_ROWS])) * scale
     out[0:BIAS_ROWS, :] = encode(bias).astype(BF16)
     out[BIAS_ROWS:, :] = ((here[BIAS_ROWS:] + there[BIAS_ROWS:]) * scale).astype(BF16)
-    for done in done_out:
-        done[...] = jnp.zeros(done.shape, F32)
 
 
 def store_half(place, half, blocks, out, wide, left):
@@ -661,8 +632,10 @@
         copy.wait()
 
 
-def other_half_kernel(place, own, received, out_before, out, bias_out, wide, bias_here, left):
-    del out_before
+def other_half_kernel(
+    place, own, received, after, out_before, out, bias_out, wide, bias_here, left
+):
+    del after, out_before
     rank = place.rank(0)
     here, there = own[0, 0:BIAS_ROWS, :].astype(F32), received[0, 0:BIAS_ROWS, :].astype(F32)
     bias = decode(here) + decode(there)
@@ -677,75 +650,102 @@
         copy.wait()
 
 
-def field_kernel(
+def field_kernel(pre, weights, wide_out, turned_out, done_out, shifted):
+    done_out[...] = jnp.zeros(done_out.shape, F32)
+    gate_count, cells = pre.shape
+    channels, width = weights.shape[2], wide_out.shape[1]
+    row_count = cells // width
+    lane = lanes((gate_count, width))
+    for index in range(row_count):
+        at = pl.ds(index * width, width)
+        row = pre[:, at].astype(F32)
+        left = jnp.where(lane == 0, 0.0, rolled(row, 1))
+        right = jnp.where(lane == width - 1, 0.0, rolled(row, -1))
+        shifted[0:gate_count, at] = right.astype(BF16)
+        shifted[gate_count : 2 * gate_count, at] = pre[:, at]
+        shifted[2 * gate_count : 3 * gate_count, at] = left.astype(BF16)
+    for a in range(3):
+        for b in range(3):
+            turned_out[a, :, b * gate_count : (b + 1) * gate_count] = weights[3 * a + b].T
+
+    def product(a, index, count):
+        return jnp.dot(
+            turned_out[a],
+            shifted[:, pl.ds(index * width, count * width)],
+            preferred_element_type=F32,
+        )
+
+    pair = 2 if row_count % 2 == 0 else 1
+    for base in range(0, row_count, pair):
+        total = product(1, base, pair)
+        for a, first in ((2, base - 1), (0, base + 1)):
+            low, high = max(first, 0), min(first + pair, row_count)
+            if low >= high:
+                continue
+            part = product(a, low, high - low)
+            blank = jnp.zeros((channels, width), F32)
+            parts = [blank] * (low - first) + [part] + [blank] * (first + pair - high)
+            total += jnp.concatenate(parts, axis=1)
+        for offset in range(pair):
+            value = total[:, offset * width : (offset + 1) * width]
+            wide_out[pl.ds(base + offset, channels, stride=row_count), :] = value
+
+
+def field_halo_kernel(
     place,
-    pre,
+    wide,
+    turned,
     outer_row,
     inner_row,
     outer_column,
     inner_column,
-    weights,
-    after,
     inputs_out,
     hidden_out,
     done_out,
-    shifted,
-    turned,
-    wide,
+    total,
 ):
-    del after
-    gate_count = pre.shape[0]
-    channels = weights.shape[2]
     done_out[...] = jnp.zeros(done_out.shape, F32)
     hid, row_count, width = hidden_out.shape
-
-    def emit(position, left, row, right):
-        at = pl.ds(position * width, width)
-        shifted[0:gate_count, at] = right.astype(BF16)
-        shifted[gate_count : 2 * gate_count, at] = row.astype(BF16)
-        shifted[2 * gate_count : 3 * gate_count, at] = left.astype(BF16)
-
-    widened(
-        row_count,
-        lambda index: pre[:, pl.ds(index * width, width)].astype(F32),
-        (inner_row, outer_row),
-        (inner_column, outer_column),
-        emit,
+    channels = turned.shape[1]
+    gate_count = turned.shape[2] // 3
+    north, south = row_halo(inner_row, outer_row)
+    west, east = column_halo(inner_column, outer_column, PRE_GROUPS)
+    lane = lanes((gate_count, width))
+    lat = place.position()[0]
+
+    def row_part(taps, row, position):
+        left = jnp.where(lane == 0, rolled(west, -LAST - position), rolled(row, 1))
+        right = rolled(east, width - 1 - position)
+        right = jnp.where(lane == width - 1, right, rolled(row, -1))
+        stack = jnp.concatenate([right, row, left], axis=0).astype(BF16)
+        return jnp.dot(taps, stack, preferred_element_type=F32)
+
+    above = row_part(turned[jnp.where(lat == 0, 0, 2)], north, 0)
+    below = row_part(turned[jnp.where(lat == place.lat - 1, 2, 0)], south, row_count + 1)
+
+    inside = (lane >= 1) & (lane <= row_count)
+    west = jnp.where(inside, rolled(west, -LAST), 0.0)
+    east = jnp.where(inside, east, 0.0)
+    sides = [rolled(west, a - 1) for a in range(3)] + [rolled(east, LAST + a - 1) for a in range(3)]
+    taps = [turned[a, :, 2 * gate_count : 3 * gate_count] for a in range(3)]
+    taps += [turned[a, :, 0:gate_count] for a in range(3)]
+    columns = jnp.dot(
+        jnp.concatenate(taps, axis=1),
+        jnp.concatenate(sides, axis=0).astype(BF16),
+        preferred_element_type=F32,
     )
-    for a in range(3):
-        for b in range(3):
-            turned[a, :, b * gate_count : (b + 1) * gate_count] = weights[3 * a + b].T
-    lat = place.position()[0]
-    top = turned[jnp.where(lat == 0, 0, 2)]
-    bottom = turned[jnp.where(lat == place.lat - 1, 2, 0)]
-
-    def product(matrix, position, count):
-        return jnp.dot(
-            matrix, shifted[:, pl.ds(position * width, count * width)], preferred_element_type=F32
-        )
-
-    pair = 2 if row_count % 2 == 0 else 1
-    for base in range(0, row_count, pair):
-        total = product(turned[1], base + 1, pair)
-        if base == 0:
-            above = product(top, 0, 1)
-            if pair == 2:
-                above = jnp.concatenate([above, product(turned[2], 1, 1)], axis=1)
-        else:
-            above = product(turned[2], base, pair)
-        if base + pair == row_count:
-            below = product(bottom, row_count + 1, 1)
-            if pair == 2:
-                below = jnp.concatenate([product(turned[0], row_count, 1), below], axis=1)
-        else:
-            below = product(turned[0], base + 2, pair)
-        total = total + above + below
-        for offset in range(pair):
-            value = total[:, offset * width : (offset + 1) * width]
-            wide[pl.ds(base + offset, channels, stride=row_count), :] = value
+    blank = jnp.zeros((channels, width), F32)
+    for index in range(row_count):
+        strided = pl.ds(index, channels, stride=row_count)
+        value = wide[strided, :] + at_edges(blank, index + 1, columns)
+        if index == 0:
+            value += above
+        if index == row_count - 1:
+            value += below
+        total[strided, :] = value
     size = (channels - hid) * row_count
-    inputs_out[...] = wide[0:size, :].reshape(inputs_out.shape).astype(BF16)
-    hidden_out[...] = wide[size:, :].reshape(hidden_out.shape).astype(BF16)
+    inputs_out[...] = total[0:size, :].reshape(inputs_out.shape).astype(BF16)
+    hidden_out[...] = total[size:, :].reshape(hidden_out.shape).astype(BF16)
 
 
 def body(
@@ -918,12 +918,12 @@
             pltpu.VMEM((hid, row_count, width), BF16),
             pltpu.VMEM(flat.shape, F32),
             pltpu.VMEM(flat.shape, F32),
+            pltpu.VMEM(flat.shape, F32),
             pltpu.SemaphoreType.DMA((3,)),
         ],
         leaving=3,
         moved=4_000_000,
     )(hidden_rows, cell_rows, grad_cell_rows, pre, *strips, pre_strip)
-    after = pre_inner
     pre_inner, pre_outer = permuted(pre_inner, inner_rows), permuted(pre_outer, outer_rows)
     pre_columns = call(
         bind(columns_kernel, row_count, PRE_GROUPS),
@@ -939,39 +939,38 @@
         [pltpu.VMEM((place.half_rows, channels), F32)],
     )(keep, bias, permuted(send, place.phase_pairs(0)))
     received = [permuted(send, place.plane_pairs(step)) for step, send in zip(steps, sends)]
-    part = call(plane_kernel, block)(keep, bias, *received, after)
+    field, turned, field_done = call(
+        field_kernel,
+        (
+            sds((channels * row_count, width), F32),
+            sds((3, channels, 3 * gate_count), BF16),
+            token,
+        ),
+        [pltpu.VMEM((3 * gate_count, cells), BF16)],
+        flops=2 * 9 * gate_count * channels * cells,
+        moved=3_000_000,
+    )(pre, weights_here)
+    part = call(plane_kernel, block)(keep, bias, *received, field_done)
     pre_inner_columns = permuted(pre_columns, inner_columns)
     pre_outer_columns = permuted(pre_columns, outer_columns)
     phases = len(place.orders[0])
     for phase in range(1, phases):
         is_last = phase == phases - 1
-        part, *summed = call(
-            bind(add_kernel, scaling if is_last else 1.0), (block, token) if is_last else (block,)
-        )(part, permuted(part, place.phase_pairs(phase)))
+        part = call(bind(add_kernel, scaling if is_last else 1.0), block)(
+            part, permuted(part, place.phase_pairs(phase))
+        )
+    received = [permuted(part, place.plane_pairs(step)) for step in steps[::-1]]
     grad_inputs, grad_hidden, field_done = call(
-        bind(field_kernel, place),
+        bind(field_halo_kernel, place),
         (
             sds((channels - hid, row_count, width), BF16),
             sds((hid, row_count, width), BF16),
-            sds((8, width), F32),
+            token,
         ),
-        [
-            pltpu.VMEM((3 * gate_count, halo_cells), BF16),
-            pltpu.VMEM((3, channels, 3 * gate_count), BF16),
-            pltpu.VMEM((channels * row_count, width), F32),
-        ],
-        flops=2 * 9 * gate_count * channels * cells,
+        [pltpu.VMEM((channels * row_count, width), F32)],
+        flops=40 * gate_count * channels * cells * 9,
         moved=2_000_000,
-    )(
-        pre,
-        pre_outer,
-        pre_inner,
-        pre_outer_columns,
-        pre_inner_columns,
-        weights_here,
-        *summed,
-    )
-    received = [permuted(part, place.plane_pairs(step)) for step in steps[::-1]]
+    )(field, turned, pre_outer, pre_inner, pre_outer_columns, pre_inner_columns)
     gathered = call(bind(join_kernel, place), sds((place.plane, *block.shape), BF16))(
         part, *received, field_done
     )
@@ -990,9 +989,9 @@
         half + [pltpu.VMEM((gate_count,), F32), pltpu.SemaphoreType.DMA((place.taps + 1,))],
         remote=1,
         leaving=2,
-        aliases={2: 0},
+        aliases={3: 0},
         moved=6 * place.half_rows * channels,
-    )(gathered, received, grad_kernel)
+    )(gathered, received, target_here, grad_kernel)
     shape = hidden_prev.shape
     return (
         hidden_next,

time: 47 us -> 47 us (level)
    pallas_call x16 -> x17, Pallas kernels: 12.9 us -> 13 us  [run(): pl.pallas_call(kernel, out_shape=out_shape, in_specs=[VMEM] * near + [HBM...]
  transfers between devices with their start and end apart: 18 -> 18, of which waited for: 10 -> 11; matrix products, arithmetic and copies ran while one was open for 0% -> 0% of each run, Pallas kernels for 21% -> 21%
where the time goes in v5:
time: 47 us; the launch traced here: 46.9 us
  starting transfers between devices  24.9 us (53%)
  Pallas kernels  13 us (28%)
  waiting for transfers between devices  8.2 us (17%)
  between operations  0.78 us (2%)
    ppermute x18, starting transfers between devices, permuted(): return lax.ppermute(value, AXES, pairs)  24.9 us
    pallas_call x17, Pallas kernels, run(): pl.pallas_call(kernel, out_shape=out_shape, in_specs=[VMEM] * near + [HBM...  13 us
    ppermute x18, waiting for transfers between devices, permuted(): return lax.ppermute(value, AXES, pairs)  8.2 us
  transfers between devices with their start and end apart: 18, of which 11 were waited for; matrix products, arithmetic and copies ran while one was open for 0% of the time, Pallas kernels for 21%

profile of v5, /device:TPU:0, one launch (start us, length us, event | category | flops | bytes accessed | tf_op | source)
XLA Modules:
  0.0 46.9 jit_solution(8916087641766384792)
XLA Ops:
  0.6 1.0 %shard_map.153 = (bf16[128,128]{1,0:T(8,128)(2,1)S(1)}, bf16[128,128]{1,0:T(8,128)(2,1)S(1)}, f32[1024,128]{1,0:T(8,128)S(1)}) custom-call(bf16[64,8,128]{2,1,0:T(8,128)(2,1)} %below.1, bf16[64,8,128]{2,1,0:T(8,128)(2,1)} %hidden.1), custom_call_target="tpu_custom_call" | custom-call | bytes 524288 | tf_op jit(solution)/shard_map/pallas_call | solution.py:45
  1.7 0.5 %collective-permute-start = (bf16[128,128]{1,0:T(8,128)(2,1)S(1)}, bf16[128,128]{1,0:T(8,128)(2,1)S(1)}, u32[]{:S(2)}, u32[]{:S(2)}) collective-permute-start(bf16[128,128]{1,0:T(8,128)(2,1)S(1)} %get-tuple-element.62), channel_id=1, source_target_pairs={{0,8},{1,9},{2,10},{3,11},{4,12},{5,13},{6,14},{7,15},{8,0},{9,1},... | collective-permute-start | bytes 98312 | tf_op jit(solution)/shard_map/ppermute | solution.py:128
  2.2 3.7 %collective-permute-start.1 = (bf16[128,128]{1,0:T(8,128)(2,1)S(1)}, bf16[128,128]{1,0:T(8,128)(2,1)S(1)}, u32[]{:S(2)}, u32[]{:S(2)}) collective-permute-start(bf16[128,128]{1,0:T(8,128)(2,1)S(1)} %get-tuple-element.63), channel_id=1, source_target_pairs={{0,4},{1,5},{2,6},{3,7},{4,0},{5,1},{6,2},{7,3},{8,16},{9,17},{10,... | collective-permute-start | bytes 98312 | tf_op jit(solution)/shard_map/ppermute | solution.py:128
  5.8 2.2 %shard_map.154 = (bf16[8,128,128]{2,1,0:T(8,128)(2,1)S(1)}, f32[128,128]{1,0:T(8,128)S(1)}, f32[128,128]{1,0:T(8,128)S(1)}, f32[64,128]{1,0:T(8,128)S(1)}, f32[6...) custom-call(f32[1024,128]{1,0:T(8,128)S(1)} %get-tuple-element.60.wi, ...), custom_call_target="tpu_custom_call" | custom-call | bytes 6000000 | tf_op jit(solution)/shard_map/pallas_call | solution.py:45
  8.0 0.0 collective-permute-done.inner_row.inner
  8.0 0.0 collective-permute-done.1.outer_row.outer
  8.0 0.2 shard_map.156
  8.2 1.5 %collective-permute-start.3 = (bf16[32,128]{1,0:T(8,128)(2,1)S(1)}, bf16[32,128]{1,0:T(8,128)(2,1)S(1)}, u32[]{:S(2)}, u32[]{:S(2)}) collective-permute-start(bf16[32,128]{1,0:T(8,128)(2,1)S(1)} %get-tuple-element.80), channel_id=1, source_target_pairs={{0,1},{1,0},{2,3},{3,2},{4,5},{5,4},{6,7},{7,6},{8,9},{9,8},{10,11... | collective-permute-start | bytes 24584 | tf_op jit(solution)/shard_map/ppermute | solution.py:128
  9.8 3.8 %collective-permute-start.2 = (bf16[32,128]{1,0:T(8,128)(2,1)S(1)}, bf16[32,128]{1,0:T(8,128)(2,1)S(1)}, u32[]{:S(2)}, u32[]{:S(2)}) collective-permute-start(bf16[32,128]{1,0:T(8,128)(2,1)S(1)} %get-tuple-element.80), channel_id=1, source_target_pairs={{0,7},{1,2},{2,1},{3,4},{4,3},{5,6},{6,5},{7,0},{8,15},{9,10},{10,... | collective-permute-start | bytes 24584 | tf_op jit(solution)/shard_map/ppermute | solution.py:128
  13.5 2.2 %shard_map.155 = (f32[512,128]{1,0:T(8,128)S(1)}, f32[512,128]{1,0:T(8,128)S(1)}, f32[512,128]{1,0:T(8,128)S(1)}, bf16[256,1024]{1,0:T(8,128)(2,1)S(1)}, bf16[12...) custom-call(bf16[8,128,128]{2,1,0:T(8,128)(2,1)S(1)} %get-tuple-element.61.rows_in, ...), custom_call_target="tpu_custom_call" | custom-call | flops 1207959552 | bytes 6000000 | tf_op jit(solution)/shard_map/pallas_call | solution.py:45
  15.8 0.0 collective-permute-done.3.inner_column
  15.8 0.3 collective-permute-done.2.outer_column
  16.1 0.9 %shard_map.157 = (bf16[1152,128]{1,0:T(8,128)(2,1)S(1)}, bf16[256,128]{1,0:T(8,128)(2,1)S(1)}, f32[256,128]{1,0:T(8,128)S(1)}, bf16[1152,128]{1,0:T(8,128)(2,1)S...) custom-call(bf16[128,128]{1,0:T(8,128)(2,1)S(1)} %get-tuple-element.78.edge, ...), custom_call_target="tpu_custom_call" | custom-call | tf_op jit(solution)/shard_map/pallas_call | solution.py:45
  17.0 0.1 collective-permute-start.8
  17.1 0.3 shard_map.162
  17.3 1.3 %collective-permute-done.8.received = bf16[1152,128]{1,0:T(8,128)(2,1)S(1)} collective-permute-done((bf16[1152,128]{1,0:T(8,128)(2,1)S(1)}, bf16[1152,128]{1,0:T(8,128)(2,1)S(1)}, u32[]{:S(2)}, u32[]{:S(2)}) %collective-permute-start.8) | collective-permute-done | bytes 294944 | tf_op jit(solution)/shard_map/ppermute | solution.py:128
  18.6 0.1 shard_map.163
  18.7 0.1 collective-permute-start.9
  18.8 0.4 collective-permute-start.10
  19.2 3.1 %collective-permute-start.11 = (bf16[304,128]{1,0:T(8,128)(2,1)S(1)}, bf16[304,128]{1,0:T(8,128)(2,1)S(1)}, u32[]{:S(2)}, u32[]{:S(2)}) collective-permute-start(bf16[304,128]{1,0:T(8,128)(2,1)S(1)} %get-tuple-element.108), channel_id=1, source_target_pairs={{0,1},{1,0},{2,3},{3,2},{4,5},{5,4},{6,7},{7,6},{8,9},{9,8},{10,11... | collective-permute-start | bytes 233480 | tf_op jit(solution)/shard_map/ppermute | solution.py:128
  22.3 1.4 %shard_map.158 = (bf16[64,8,128]{2,1,0:T(8,128)(2,1)}, f32[512,128]{1,0:T(8,128)}, f32[512,128]{1,0:T(8,128)}, bf16[256,1024]{1,0:T(8,128)(2,1)S(1)}, bf16[256,1...) custom-call(f32[512,128]{1,0:T(8,128)S(1)} %get-tuple-element.73.hidden, f32[512,128]{1,0:T(8,128)S(1)} %get-tuple-element.74.cell, ...), custom_call_target="tpu_custom_call" | custom-call | bytes 4000000 | tf_op jit(solution)/shard_map/pallas_call | solution.py:45
  23.6 1.1 %shard_map.159 = (f32[1024,128]{1,0:T(8,128)S(1)}, bf16[3,128,768]{2,1,0:T(8,128)(2,1)S(1)}, f32[8,128]{1,0:T(8,128)S(1)}) custom-call(bf16[256,1024]{1,0:T(8,128)(2,1)S(1)} %get-tuple-element.91.pre, bf16[9,256,128]{2,1,0:T(8,128)(2,1)S(1)} %get-tuple-element.66.weights), custom_call_target="tpu_custom_call" | custom-call | flops 603979776 | bytes 3000000 | tf_op jit(solution)/shard_map/pallas_call | solution.py:45
  24.8 0.1 collective-permute-done.9.refs_0_
  24.9 0.0 collective-permute-done.10.refs_1_
  24.9 0.9 %collective-permute-done.11.refs_2_ = bf16[304,128]{1,0:T(8,128)(2,1)S(1)} collective-permute-done((bf16[304,128]{1,0:T(8,128)(2,1)S(1)}, bf16[304,128]{1,0:T(8,128)(2,1)S(1)}, u32[]{:S(2)}, u32[]{:S(2)}) %collective-permute-start.11) | collective-permute-done | bytes 77856 | tf_op jit(solution)/shard_map/ppermute | solution.py:128
  25.8 0.1 collective-permute-start.12
  25.9 3.8 %collective-permute-start.4 = (bf16[256,128]{1,0:T(8,128)(2,1)S(1)}, bf16[256,128]{1,0:T(8,128)(2,1)S(1)}, u32[]{:S(2)}, u32[]{:S(2)}) collective-permute-start(bf16[256,128]{1,0:T(8,128)(2,1)S(1)} %get-tuple-element.94), channel_id=1, source_target_pairs={{0,4},{1,5},{2,6},{3,7},{4,0},{5,1},{6,2},{7,3},{8,16},{9,17},{10,... | collective-permute-start | bytes 196616 | tf_op jit(solution)/shard_map/ppermute | solution.py:128
  29.7 0.0 collective-permute-start.5
  29.7 1.4 %collective-permute-done.12.received = bf16[304,128]{1,0:T(8,128)(2,1)S(1)} collective-permute-done((bf16[304,128]{1,0:T(8,128)(2,1)S(1)}, bf16[304,128]{1,0:T(8,128)(2,1)S(1)}, u32[]{:S(2)}, u32[]{:S(2)}) %collective-permute-start.12) | collective-permute-done | bytes 77856 | tf_op jit(solution)/shard_map/ppermute | solution.py:128
  31.1 1.0 %collective-permute-start.13 = (bf16[304,128]{1,0:T(8,128)(2,1)S(1)}, bf16[304,128]{1,0:T(8,128)(2,1)S(1)}, u32[]{:S(2)}, u32[]{:S(2)}) collective-permute-start(bf16[304,128]{1,0:T(8,128)(2,1)S(1)} %shard_map.165.own), channel_id=1, source_target_pairs={{0,4},{1,5},{2,6},{3,7},{4,0},{5,1},{6,2},{7,3},{8,10},{9,11},{10,... | collective-permute-start | bytes 233480 | tf_op jit(solution)/shard_map/ppermute | solution.py:128
  32.1 0.5 %collective-permute-done.4.outer.outer_row = bf16[256,128]{1,0:T(8,128)(2,1)S(1)} collective-permute-done((bf16[256,128]{1,0:T(8,128)(2,1)S(1)}, bf16[256,128]{1,0:T(8,128)(2,1)S(1)}, u32[]{:S(2)}, u32[]{:S(2)}) %collective-permute-start.4) | collective-permute-done | bytes 65568 | tf_op jit(solution)/shard_map/ppermute | solution.py:128
  32.6 0.0 collective-permute-done.5.inner.inner_row
  32.6 0.2 shard_map.160
  32.8 1.6 %collective-permute-start.7 = (bf16[64,128]{1,0:T(8,128)(2,1)S(1)}, bf16[64,128]{1,0:T(8,128)(2,1)S(1)}, u32[]{:S(2)}, u32[]{:S(2)}) collective-permute-start(bf16[64,128]{1,0:T(8,128)(2,1)S(1)} %shard_map.160), channel_id=1, source_target_pairs={{0,1},{1,0},{2,3},{3,2},{4,5},{5,4},{6,7},{7,6},{8,9},{9,8},{10,11... | collective-permute-start | bytes 49160 | tf_op jit(solution)/shard_map/ppermute | solution.py:128
  34.4 1.7 %collective-permute-start.6 = (bf16[64,128]{1,0:T(8,128)(2,1)S(1)}, bf16[64,128]{1,0:T(8,128)(2,1)S(1)}, u32[]{:S(2)}, u32[]{:S(2)}) collective-permute-start(bf16[64,128]{1,0:T(8,128)(2,1)S(1)} %shard_map.160), channel_id=1, source_target_pairs={{0,7},{1,2},{2,1},{3,4},{4,3},{5,6},{6,5},{7,0},{8,15},{9,10},{10,... | collective-permute-start | bytes 49160 | tf_op jit(solution)/shard_map/ppermute | solution.py:128
  36.1 0.9 %collective-permute-done.13.received = bf16[304,128]{1,0:T(8,128)(2,1)S(1)} collective-permute-done((bf16[304,128]{1,0:T(8,128)(2,1)S(1)}, bf16[304,128]{1,0:T(8,128)(2,1)S(1)}, u32[]{:S(2)}, u32[]{:S(2)}) %collective-permute-start.13) | collective-permute-done | bytes 77856 | tf_op jit(solution)/shard_map/ppermute | solution.py:128
  37.0 0.5 %collective-permute-start.16 = (bf16[304,128]{1,0:T(8,128)(2,1)S(1)}, bf16[304,128]{1,0:T(8,128)(2,1)S(1)}, u32[]{:S(2)}, u32[]{:S(2)}) collective-permute-start(bf16[304,128]{1,0:T(8,128)(2,1)S(1)} %shard_map.166.refs_0_), channel_id=1, source_target_pairs={{0,17},{1,16},{2,19},{3,18},{4,21},{5,20},{6,23},{7,22},{8,25},{9,... | collective-permute-start | bytes 233480 | tf_op jit(solution)/shard_map/ppermute | solution.py:128
  37.5 2.3 %collective-permute-start.15 = (bf16[304,128]{1,0:T(8,128)(2,1)S(1)}, bf16[304,128]{1,0:T(8,128)(2,1)S(1)}, u32[]{:S(2)}, u32[]{:S(2)}) collective-permute-start(bf16[304,128]{1,0:T(8,128)(2,1)S(1)} %shard_map.166.refs_0_), channel_id=1, source_target_pairs={{0,16},{1,17},{2,18},{3,19},{4,20},{5,21},{6,22},{7,23},{8,24},{9,... | collective-permute-start | bytes 233480 | tf_op jit(solution)/shard_map/ppermute | solution.py:128
  39.9 0.7 %collective-permute-start.14 = (bf16[304,128]{1,0:T(8,128)(2,1)S(1)}, bf16[304,128]{1,0:T(8,128)(2,1)S(1)}, u32[]{:S(2)}, u32[]{:S(2)}) collective-permute-start(bf16[304,128]{1,0:T(8,128)(2,1)S(1)} %shard_map.166.refs_0_), channel_id=1, source_target_pairs={{0,1},{1,0},{2,3},{3,2},{4,5},{5,4},{6,7},{7,6},{8,9},{9,8},{10,11... | collective-permute-start | bytes 233480 | tf_op jit(solution)/shard_map/ppermute | solution.py:128
  40.6 0.3 collective-permute-done.6.outer_column
  40.8 1.6 %shard_map.161 = (bf16[64,8,128]{2,1,0:T(8,128)(2,1)}, bf16[64,8,128]{2,1,0:T(8,128)(2,1)}, f32[8,128]{1,0:T(8,128)S(1)}) custom-call(f32[1024,128]{1,0:T(8,128)S(1)} %get-tuple-element.92.wide, bf16[3,128,768]{2,1,0:T(8,128)(2,1)S(1)} %get-tuple-element.93.turned, bf16[256,128]{1,0:T(8,128)(2,1)S(1)} %collective-permute-done.4.outer.outer_row, ...), custom_call_target="tpu_custom_call" | custom-call | flops 12079595520 | bytes 2000000 | tf_op jit(solution)/shard_map/pallas_call | solution.py:45
  42.4 0.0 collective-permute-done.16.refs_3_
  42.4 0.7 %collective-permute-done.15.refs_2_ = bf16[304,128]{1,0:T(8,128)(2,1)S(1)} collective-permute-done((bf16[304,128]{1,0:T(8,128)(2,1)S(1)}, bf16[304,128]{1,0:T(8,128)(2,1)S(1)}, u32[]{:S(2)}, u32[]{:S(2)}) %collective-permute-start.15) | collective-permute-done | bytes 77856 | tf_op jit(solution)/shard_map/ppermute | solution.py:128
  43.1 1.2 %collective-permute-done.14.refs_1_ = bf16[304,128]{1,0:T(8,128)(2,1)S(1)} collective-permute-done((bf16[304,128]{1,0:T(8,128)(2,1)S(1)}, bf16[304,128]{1,0:T(8,128)(2,1)S(1)}, u32[]{:S(2)}, u32[]{:S(2)}) %collective-permute-start.14) | collective-permute-done | bytes 77856 | tf_op jit(solution)/shard_map/ppermute | solution.py:128
  44.3 0.1 collective-permute-start.17
  44.4 0.9 %shard_map.168.out_before = f32[9,256,128]{2,1,0:T(8,128)} custom-call(bf16[4,304,128]{2,1,0:T(8,128)(2,1)S(1)} %shard_map.167.own), custom_call_target="tpu_custom_call" | custom-call | bytes 884736 | tf_op jit(solution)/shard_map/pallas_call | solution.py:45
  45.3 0.7 %collective-permute-done.17.received = bf16[4,304,128]{2,1,0:T(8,128)(2,1)S(1)} collective-permute-done((bf16[4,304,128]{2,1,0:T(8,128)(2,1)S(1)}, bf16[4,304,128]{2,1,0:T(8,128)(2,1)S(1)}, u32[]{:S(2)}, u32[]{:S(2)}) %collective-permute-start.17) | collective-permute-done | bytes 311328 | tf_op jit(solution)/shard_map/ppermute | solution.py:128
  46.0 0.9 %shard_map.169 = (f32[9,256,128]{2,1,0:T(8,128)}, f32[256]{0:T(256)}) custom-call(bf16[4,304,128]{2,1,0:T(8,128)(2,1)S(1)} %shard_map.167.own, bf16[4,304,128]{2,1,0:T(8,128)(2,1)S(1)} %collective-permute-done.17.received, f32[8,128]{1,0:T(8,128)S(1)} %get-tuple-element.68.target.after, ...), custom_call_target="tpu_custom_call", output_to_operand_aliasing={{0}: (3, {})} | custom-call | bytes 884736 | tf_op jit(solution)/shard_map/pallas_call | solution.py:45
  (5 shorter events, 0.1 us)
Async XLA Ops:
  1.7 6.4 %collective-permute-start = (bf16[128,128]{1,0:T(8,128)(2,1)S(1)}, bf16[128,128]{1,0:T(8,128)(2,1)S(1)}, u32[]{:S(2)}, u32[]{:S(2)}) collective-permute-start(bf16[128,128]{1,0:T(8,128)(2,1)S(1)} %get-tuple-element.62), channel_id=1, source_target_pairs={{0,8},{1,9},{2,10},{3,11},{4,12},{5,13},{6,14},{7,15},{8,0},{9,1},... | collective-permute-start | bytes 98312 | tf_op jit(solution)/shard_map/ppermute | solution.py:128
  2.2 5.9 %collective-permute-start.1 = (bf16[128,128]{1,0:T(8,128)(2,1)S(1)}, bf16[128,128]{1,0:T(8,128)(2,1)S(1)}, u32[]{:S(2)}, u32[]{:S(2)}) collective-permute-start(bf16[128,128]{1,0:T(8,128)(2,1)S(1)} %get-tuple-element.63), channel_id=1, source_target_pairs={{0,4},{1,5},{2,6},{3,7},{4,0},{5,1},{6,2},{7,3},{8,16},{9,17},{10,... | collective-permute-start | bytes 98312 | tf_op jit(solution)/shard_map/ppermute | solution.py:128
  8.2 7.6 %collective-permute-start.3 = (bf16[32,128]{1,0:T(8,128)(2,1)S(1)}, bf16[32,128]{1,0:T(8,128)(2,1)S(1)}, u32[]{:S(2)}, u32[]{:S(2)}) collective-permute-start(bf16[32,128]{1,0:T(8,128)(2,1)S(1)} %get-tuple-element.80), channel_id=1, source_target_pairs={{0,1},{1,0},{2,3},{3,2},{4,5},{5,4},{6,7},{7,6},{8,9},{9,8},{10,11... | collective-permute-start | bytes 24584 | tf_op jit(solution)/shard_map/ppermute | solution.py:128
  9.8 6.3 %collective-permute-start.2 = (bf16[32,128]{1,0:T(8,128)(2,1)S(1)}, bf16[32,128]{1,0:T(8,128)(2,1)S(1)}, u32[]{:S(2)}, u32[]{:S(2)}) collective-permute-start(bf16[32,128]{1,0:T(8,128)(2,1)S(1)} %get-tuple-element.80), channel_id=1, source_target_pairs={{0,7},{1,2},{2,1},{3,4},{4,3},{5,6},{6,5},{7,0},{8,15},{9,10},{10,... | collective-permute-start | bytes 24584 | tf_op jit(solution)/shard_map/ppermute | solution.py:128
  17.0 1.6 %collective-permute-start.8 = (bf16[1152,128]{1,0:T(8,128)(2,1)S(1)}, bf16[1152,128]{1,0:T(8,128)(2,1)S(1)}, u32[]{:S(2)}, u32[]{:S(2)}) collective-permute-start(bf16[1152,128]{1,0:T(8,128)(2,1)S(1)} %get-tuple-element.104), channel_id=1, source_target_pairs={{0,8},{1,9},{2,10},{3,11},{4,12},{5,13},{6,14},{7,15},{8,0},{9,1},... | collective-permute-start | bytes 884744 | tf_op jit(solution)/shard_map/ppermute | solution.py:128
  18.7 6.2 %collective-permute-start.9 = (bf16[304,128]{1,0:T(8,128)(2,1)S(1)}, bf16[304,128]{1,0:T(8,128)(2,1)S(1)}, u32[]{:S(2)}, u32[]{:S(2)}) collective-permute-start(bf16[304,128]{1,0:T(8,128)(2,1)S(1)} %get-tuple-element.106), channel_id=1, source_target_pairs={{0,17},{1,16},{2,19},{3,18},{4,21},{5,20},{6,23},{7,22},{8,25},{9,... | collective-permute-start | bytes 233480 | tf_op jit(solution)/shard_map/ppermute | solution.py:128
  18.8 6.1 %collective-permute-start.10 = (bf16[304,128]{1,0:T(8,128)(2,1)S(1)}, bf16[304,128]{1,0:T(8,128)(2,1)S(1)}, u32[]{:S(2)}, u32[]{:S(2)}) collective-permute-start(bf16[304,128]{1,0:T(8,128)(2,1)S(1)} %get-tuple-element.107), channel_id=1, source_target_pairs={{0,16},{1,17},{2,18},{3,19},{4,20},{5,21},{6,22},{7,23},{8,24},{9,... | collective-permute-start | bytes 233480 | tf_op jit(solution)/shard_map/ppermute | solution.py:128
  19.2 6.6 %collective-permute-start.11 = (bf16[304,128]{1,0:T(8,128)(2,1)S(1)}, bf16[304,128]{1,0:T(8,128)(2,1)S(1)}, u32[]{:S(2)}, u32[]{:S(2)}) collective-permute-start(bf16[304,128]{1,0:T(8,128)(2,1)S(1)} %get-tuple-element.108), channel_id=1, source_target_pairs={{0,1},{1,0},{2,3},{3,2},{4,5},{5,4},{6,7},{7,6},{8,9},{9,8},{10,11... | collective-permute-start | bytes 233480 | tf_op jit(solution)/shard_map/ppermute | solution.py:128
  25.8 5.3 %collective-permute-start.12 = (bf16[304,128]{1,0:T(8,128)(2,1)S(1)}, bf16[304,128]{1,0:T(8,128)(2,1)S(1)}, u32[]{:S(2)}, u32[]{:S(2)}) collective-permute-start(bf16[304,128]{1,0:T(8,128)(2,1)S(1)} %shard_map.164.own), channel_id=1, source_target_pairs={{0,2},{1,3},{2,0},{3,1},{4,6},{5,7},{6,4},{7,5},{8,12},{9,13},{10,... | collective-permute-start | bytes 233480 | tf_op jit(solution)/shard_map/ppermute | solution.py:128
  25.9 6.7 %collective-permute-start.4 = (bf16[256,128]{1,0:T(8,128)(2,1)S(1)}, bf16[256,128]{1,0:T(8,128)(2,1)S(1)}, u32[]{:S(2)}, u32[]{:S(2)}) collective-permute-start(bf16[256,128]{1,0:T(8,128)(2,1)S(1)} %get-tuple-element.94), channel_id=1, source_target_pairs={{0,4},{1,5},{2,6},{3,7},{4,0},{5,1},{6,2},{7,3},{8,16},{9,17},{10,... | collective-permute-start | bytes 196616 | tf_op jit(solution)/shard_map/ppermute | solution.py:128
  29.7 2.9 %collective-permute-start.5 = (bf16[256,128]{1,0:T(8,128)(2,1)S(1)}, bf16[256,128]{1,0:T(8,128)(2,1)S(1)}, u32[]{:S(2)}, u32[]{:S(2)}) collective-permute-start(bf16[256,128]{1,0:T(8,128)(2,1)S(1)} %get-tuple-element.95), channel_id=1, source_target_pairs={{0,8},{1,9},{2,10},{3,11},{4,12},{5,13},{6,14},{7,15},{8,0},{9,1},... | collective-permute-start | bytes 196616 | tf_op jit(solution)/shard_map/ppermute | solution.py:128
  31.1 5.9 %collective-permute-start.13 = (bf16[304,128]{1,0:T(8,128)(2,1)S(1)}, bf16[304,128]{1,0:T(8,128)(2,1)S(1)}, u32[]{:S(2)}, u32[]{:S(2)}) collective-permute-start(bf16[304,128]{1,0:T(8,128)(2,1)S(1)} %shard_map.165.own), channel_id=1, source_target_pairs={{0,4},{1,5},{2,6},{3,7},{4,0},{5,1},{6,2},{7,3},{8,10},{9,11},{10,... | collective-permute-start | bytes 233480 | tf_op jit(solution)/shard_map/ppermute | solution.py:128
  32.8 7.8 %collective-permute-start.7 = (bf16[64,128]{1,0:T(8,128)(2,1)S(1)}, bf16[64,128]{1,0:T(8,128)(2,1)S(1)}, u32[]{:S(2)}, u32[]{:S(2)}) collective-permute-start(bf16[64,128]{1,0:T(8,128)(2,1)S(1)} %shard_map.160), channel_id=1, source_target_pairs={{0,1},{1,0},{2,3},{3,2},{4,5},{5,4},{6,7},{7,6},{8,9},{9,8},{10,11... | collective-permute-start | bytes 49160 | tf_op jit(solution)/shard_map/ppermute | solution.py:128
  34.4 6.4 %collective-permute-start.6 = (bf16[64,128]{1,0:T(8,128)(2,1)S(1)}, bf16[64,128]{1,0:T(8,128)(2,1)S(1)}, u32[]{:S(2)}, u32[]{:S(2)}) collective-permute-start(bf16[64,128]{1,0:T(8,128)(2,1)S(1)} %shard_map.160), channel_id=1, source_target_pairs={{0,7},{1,2},{2,1},{3,4},{4,3},{5,6},{6,5},{7,0},{8,15},{9,10},{10,... | collective-permute-start | bytes 49160 | tf_op jit(solution)/shard_map/ppermute | solution.py:128
  37.0 5.4 %collective-permute-start.16 = (bf16[304,128]{1,0:T(8,128)(2,1)S(1)}, bf16[304,128]{1,0:T(8,128)(2,1)S(1)}, u32[]{:S(2)}, u32[]{:S(2)}) collective-permute-start(bf16[304,128]{1,0:T(8,128)(2,1)S(1)} %shard_map.166.refs_0_), channel_id=1, source_target_pairs={{0,17},{1,16},{2,19},{3,18},{4,21},{5,20},{6,23},{7,22},{8,25},{9,... | collective-permute-start | bytes 233480 | tf_op jit(solution)/shard_map/ppermute | solution.py:128
  37.5 5.5 %collective-permute-start.15 = (bf16[304,128]{1,0:T(8,128)(2,1)S(1)}, bf16[304,128]{1,0:T(8,128)(2,1)S(1)}, u32[]{:S(2)}, u32[]{:S(2)}) collective-permute-start(bf16[304,128]{1,0:T(8,128)(2,1)S(1)} %shard_map.166.refs_0_), channel_id=1, source_target_pairs={{0,16},{1,17},{2,18},{3,19},{4,20},{5,21},{6,22},{7,23},{8,24},{9,... | collective-permute-start | bytes 233480 | tf_op jit(solution)/shard_map/ppermute | solution.py:128
  39.9 4.4 %collective-permute-start.14 = (bf16[304,128]{1,0:T(8,128)(2,1)S(1)}, bf16[304,128]{1,0:T(8,128)(2,1)S(1)}, u32[]{:S(2)}, u32[]{:S(2)}) collective-permute-start(bf16[304,128]{1,0:T(8,128)(2,1)S(1)} %shard_map.166.refs_0_), channel_id=1, source_target_pairs={{0,1},{1,0},{2,3},{3,2},{4,5},{5,4},{6,7},{7,6},{8,9},{9,8},{10,11... | collective-permute-start | bytes 233480 | tf_op jit(solution)/shard_map/ppermute | solution.py:128
  44.3 1.7 %collective-permute-start.17 = (bf16[4,304,128]{2,1,0:T(8,128)(2,1)S(1)}, bf16[4,304,128]{2,1,0:T(8,128)(2,1)S(1)}, u32[]{:S(2)}, u32[]{:S(2)}) collective-permute-start(bf16[4,304,128]{2,1,0:T(8,128)(2,1)S(1)} %shard_map.167.own), channel_id=1, source_target_pairs={{0,8},{1,9},{2,10},{3,11},{4,12},{5,13},{6,14},{7,15},{8,0},{9,1},... | collective-permute-start | bytes 933896 | tf_op jit(solution)/shard_map/ppermute | solution.py:128

commit v6 on v5

--- a/solution.py
+++ b/solution.py
@@ -65,7 +65,7 @@
         self.taps, self.half_gates = taps, gate_count // 2
         self.plane = lat_count
         whole = [("lon", 1 << k) for k in range(1, lon_count.bit_length() - 1)]
-        self.orders = ([("lat", 1)] + whole, [("lat", 1)] + whole[::-1])
+        self.orders = ([("lat", 1)] + whole[::-1], [("lat", 1)] + whole)
         step = 8 * self.plane
         self.half_rows = -(-taps * self.half_gates // step) * step
         self.chunk = self.half_rows // self.plane

time: 47 us -> 47.8 us (1.017)
  starting transfers between devices: 24.9 us -> 25.9 us
    ppermute x18, starting transfers between devices: 24.9 us -> 25.9 us  [permuted(): return lax.ppermute(value, AXES, pairs)]
  transfers between devices with their start and end apart: 18 -> 18, of which waited for: 11 -> 9; matrix products, arithmetic and copies ran while one was open for 0% -> 0% of each run, Pallas kernels for 21% -> 21%
where the time goes in v6:
time: 47.8 us; the launch traced here: 47.7 us
  starting transfers between devices  25.9 us (54%)
  Pallas kernels  13 us (27%)
  waiting for transfers between devices  8.01 us (17%)
  between operations  0.78 us (2%)
    ppermute x18, starting transfers between devices, permuted(): return lax.ppermute(value, AXES, pairs)  25.9 us
    pallas_call x17, Pallas kernels, run(): pl.pallas_call(kernel, out_shape=out_shape, in_specs=[VMEM] * near + [HBM...  13 us
    ppermute x18, waiting for transfers between devices, permuted(): return lax.ppermute(value, AXES, pairs)  8.01 us
  transfers between devices with their start and end apart: 18, of which 9 were waited for; matrix products, arithmetic and copies ran while one was open for 0% of the time, Pallas kernels for 21%

profile of v6, /device:TPU:0, one launch (start us, length us, event | category | flops | bytes accessed | tf_op | source)
XLA Modules:
  0.0 47.7 jit_solution(2702519287146347627)
XLA Ops:
  0.6 1.0 %shard_map.153 = (bf16[128,128]{1,0:T(8,128)(2,1)S(1)}, bf16[128,128]{1,0:T(8,128)(2,1)S(1)}, f32[1024,128]{1,0:T(8,128)S(1)}) custom-call(bf16[64,8,128]{2,1,0:T(8,128)(2,1)} %below.1, bf16[64,8,128]{2,1,0:T(8,128)(2,1)} %hidden.1), custom_call_target="tpu_custom_call" | custom-call | bytes 524288 | tf_op jit(solution)/shard_map/pallas_call | solution.py:45
  1.7 0.5 %collective-permute-start = (bf16[128,128]{1,0:T(8,128)(2,1)S(1)}, bf16[128,128]{1,0:T(8,128)(2,1)S(1)}, u32[]{:S(2)}, u32[]{:S(2)}) collective-permute-start(bf16[128,128]{1,0:T(8,128)(2,1)S(1)} %get-tuple-element.62), channel_id=1, source_target_pairs={{0,8},{1,9},{2,10},{3,11},{4,12},{5,13},{6,14},{7,15},{8,0},{9,1},... | collective-permute-start | bytes 98312 | tf_op jit(solution)/shard_map/ppermute | solution.py:128
  2.2 3.7 %collective-permute-start.1 = (bf16[128,128]{1,0:T(8,128)(2,1)S(1)}, bf16[128,128]{1,0:T(8,128)(2,1)S(1)}, u32[]{:S(2)}, u32[]{:S(2)}) collective-permute-start(bf16[128,128]{1,0:T(8,128)(2,1)S(1)} %get-tuple-element.63), channel_id=1, source_target_pairs={{0,4},{1,5},{2,6},{3,7},{4,0},{5,1},{6,2},{7,3},{8,16},{9,17},{10,... | collective-permute-start | bytes 98312 | tf_op jit(solution)/shard_map/ppermute | solution.py:128
  5.8 2.2 %shard_map.154 = (bf16[8,128,128]{2,1,0:T(8,128)(2,1)S(1)}, f32[128,128]{1,0:T(8,128)S(1)}, f32[128,128]{1,0:T(8,128)S(1)}, f32[64,128]{1,0:T(8,128)S(1)}, f32[6...) custom-call(f32[1024,128]{1,0:T(8,128)S(1)} %get-tuple-element.60.wi, ...), custom_call_target="tpu_custom_call" | custom-call | bytes 6000000 | tf_op jit(solution)/shard_map/pallas_call | solution.py:45
  8.0 0.0 collective-permute-done.inner_row.inner
  8.0 0.0 collective-permute-done.1.outer_row.outer
  8.0 0.2 shard_map.156
  8.2 1.5 %collective-permute-start.3 = (bf16[32,128]{1,0:T(8,128)(2,1)S(1)}, bf16[32,128]{1,0:T(8,128)(2,1)S(1)}, u32[]{:S(2)}, u32[]{:S(2)}) collective-permute-start(bf16[32,128]{1,0:T(8,128)(2,1)S(1)} %get-tuple-element.80), channel_id=1, source_target_pairs={{0,1},{1,0},{2,3},{3,2},{4,5},{5,4},{6,7},{7,6},{8,9},{9,8},{10,11... | collective-permute-start | bytes 24584 | tf_op jit(solution)/shard_map/ppermute | solution.py:128
  9.8 3.8 %collective-permute-start.2 = (bf16[32,128]{1,0:T(8,128)(2,1)S(1)}, bf16[32,128]{1,0:T(8,128)(2,1)S(1)}, u32[]{:S(2)}, u32[]{:S(2)}) collective-permute-start(bf16[32,128]{1,0:T(8,128)(2,1)S(1)} %get-tuple-element.80), channel_id=1, source_target_pairs={{0,7},{1,2},{2,1},{3,4},{4,3},{5,6},{6,5},{7,0},{8,15},{9,10},{10,... | collective-permute-start | bytes 24584 | tf_op jit(solution)/shard_map/ppermute | solution.py:128
  13.5 2.2 %shard_map.155 = (f32[512,128]{1,0:T(8,128)S(1)}, f32[512,128]{1,0:T(8,128)S(1)}, f32[512,128]{1,0:T(8,128)S(1)}, bf16[256,1024]{1,0:T(8,128)(2,1)S(1)}, bf16[12...) custom-call(bf16[8,128,128]{2,1,0:T(8,128)(2,1)S(1)} %get-tuple-element.61.rows_in, ...), custom_call_target="tpu_custom_call" | custom-call | flops 1207959552 | bytes 6000000 | tf_op jit(solution)/shard_map/pallas_call | solution.py:45
  15.8 0.0 collective-permute-done.3.inner_column
  15.8 0.3 collective-permute-done.2.outer_column
  16.1 0.9 %shard_map.157 = (bf16[1152,128]{1,0:T(8,128)(2,1)S(1)}, bf16[256,128]{1,0:T(8,128)(2,1)S(1)}, f32[256,128]{1,0:T(8,128)S(1)}, bf16[1152,128]{1,0:T(8,128)(2,1)S...) custom-call(bf16[128,128]{1,0:T(8,128)(2,1)S(1)} %get-tuple-element.78.edge, ...), custom_call_target="tpu_custom_call" | custom-call | tf_op jit(solution)/shard_map/pallas_call | solution.py:45
  17.0 0.1 collective-permute-start.8
  17.1 0.3 shard_map.162
  17.3 1.3 %collective-permute-done.8.received = bf16[1152,128]{1,0:T(8,128)(2,1)S(1)} collective-permute-done((bf16[1152,128]{1,0:T(8,128)(2,1)S(1)}, bf16[1152,128]{1,0:T(8,128)(2,1)S(1)}, u32[]{:S(2)}, u32[]{:S(2)}) %collective-permute-start.8) | collective-permute-done | bytes 294944 | tf_op jit(solution)/shard_map/ppermute | solution.py:128
  18.6 0.1 shard_map.163
  18.7 0.1 collective-permute-start.9
  18.8 0.4 collective-permute-start.10
  19.2 3.1 %collective-permute-start.11 = (bf16[304,128]{1,0:T(8,128)(2,1)S(1)}, bf16[304,128]{1,0:T(8,128)(2,1)S(1)}, u32[]{:S(2)}, u32[]{:S(2)}) collective-permute-start(bf16[304,128]{1,0:T(8,128)(2,1)S(1)} %get-tuple-element.108), channel_id=1, source_target_pairs={{0,1},{1,0},{2,3},{3,2},{4,5},{5,4},{6,7},{7,6},{8,9},{9,8},{10,11... | collective-permute-start | bytes 233480 | tf_op jit(solution)/shard_map/ppermute | solution.py:128
  22.3 1.4 %shard_map.158 = (bf16[64,8,128]{2,1,0:T(8,128)(2,1)}, f32[512,128]{1,0:T(8,128)}, f32[512,128]{1,0:T(8,128)}, bf16[256,1024]{1,0:T(8,128)(2,1)S(1)}, bf16[256,1...) custom-call(f32[512,128]{1,0:T(8,128)S(1)} %get-tuple-element.73.hidden, f32[512,128]{1,0:T(8,128)S(1)} %get-tuple-element.74.cell, ...), custom_call_target="tpu_custom_call" | custom-call | bytes 4000000 | tf_op jit(solution)/shard_map/pallas_call | solution.py:45
  23.6 1.1 %shard_map.159 = (f32[1024,128]{1,0:T(8,128)S(1)}, bf16[3,128,768]{2,1,0:T(8,128)(2,1)S(1)}, f32[8,128]{1,0:T(8,128)S(1)}) custom-call(bf16[256,1024]{1,0:T(8,128)(2,1)S(1)} %get-tuple-element.91.pre, bf16[9,256,128]{2,1,0:T(8,128)(2,1)S(1)} %get-tuple-element.66.weights), custom_call_target="tpu_custom_call" | custom-call | flops 603979776 | bytes 3000000 | tf_op jit(solution)/shard_map/pallas_call | solution.py:45
  24.8 0.1 collective-permute-done.9.refs_0_
  24.9 0.0 collective-permute-done.10.refs_1_
  24.9 0.9 %collective-permute-done.11.refs_2_ = bf16[304,128]{1,0:T(8,128)(2,1)S(1)} collective-permute-done((bf16[304,128]{1,0:T(8,128)(2,1)S(1)}, bf16[304,128]{1,0:T(8,128)(2,1)S(1)}, u32[]{:S(2)}, u32[]{:S(2)}) %collective-permute-start.11) | collective-permute-done | bytes 77856 | tf_op jit(solution)/shard_map/ppermute | solution.py:128
  25.8 0.9 %collective-permute-start.12 = (bf16[304,128]{1,0:T(8,128)(2,1)S(1)}, bf16[304,128]{1,0:T(8,128)(2,1)S(1)}, u32[]{:S(2)}, u32[]{:S(2)}) collective-permute-start(bf16[304,128]{1,0:T(8,128)(2,1)S(1)} %shard_map.164.own), channel_id=1, source_target_pairs={{0,4},{1,5},{2,6},{3,7},{4,0},{5,1},{6,2},{7,3},{8,10},{9,11},{10,... | collective-permute-start | bytes 233480 | tf_op jit(solution)/shard_map/ppermute | solution.py:128
  26.7 2.1 %collective-permute-start.4 = (bf16[256,128]{1,0:T(8,128)(2,1)S(1)}, bf16[256,128]{1,0:T(8,128)(2,1)S(1)}, u32[]{:S(2)}, u32[]{:S(2)}) collective-permute-start(bf16[256,128]{1,0:T(8,128)(2,1)S(1)} %get-tuple-element.94), channel_id=1, source_target_pairs={{0,4},{1,5},{2,6},{3,7},{4,0},{5,1},{6,2},{7,3},{8,16},{9,17},{10,... | collective-permute-start | bytes 196616 | tf_op jit(solution)/shard_map/ppermute | solution.py:128
  28.8 0.0 collective-permute-start.5
  28.8 3.2 %collective-permute-done.12.received = bf16[304,128]{1,0:T(8,128)(2,1)S(1)} collective-permute-done((bf16[304,128]{1,0:T(8,128)(2,1)S(1)}, bf16[304,128]{1,0:T(8,128)(2,1)S(1)}, u32[]{:S(2)}, u32[]{:S(2)}) %collective-permute-start.12) | collective-permute-done | bytes 77856 | tf_op jit(solution)/shard_map/ppermute | solution.py:128
  32.0 0.2 collective-permute-start.13
  32.2 0.5 collective-permute-done.4.outer.outer_row
  32.7 0.0 collective-permute-done.5.inner.inner_row
  32.7 0.2 shard_map.160
  32.9 1.0 %collective-permute-start.7 = (bf16[64,128]{1,0:T(8,128)(2,1)S(1)}, bf16[64,128]{1,0:T(8,128)(2,1)S(1)}, u32[]{:S(2)}, u32[]{:S(2)}) collective-permute-start(bf16[64,128]{1,0:T(8,128)(2,1)S(1)} %shard_map.160), channel_id=1, source_target_pairs={{0,1},{1,0},{2,3},{3,2},{4,5},{5,4},{6,7},{7,6},{8,9},{9,8},{10,11... | collective-permute-start | bytes 49160 | tf_op jit(solution)/shard_map/ppermute | solution.py:128
  33.9 4.9 %collective-permute-start.6 = (bf16[64,128]{1,0:T(8,128)(2,1)S(1)}, bf16[64,128]{1,0:T(8,128)(2,1)S(1)}, u32[]{:S(2)}, u32[]{:S(2)}) collective-permute-start(bf16[64,128]{1,0:T(8,128)(2,1)S(1)} %shard_map.160), channel_id=1, source_target_pairs={{0,7},{1,2},{2,1},{3,4},{4,3},{5,6},{6,5},{7,0},{8,15},{9,10},{10,... | collective-permute-start | bytes 49160 | tf_op jit(solution)/shard_map/ppermute | solution.py:128
  38.8 0.0 collective-permute-done.13.received
  38.9 0.1 collective-permute-start.16
  38.9 1.0 %collective-permute-start.15 = (bf16[304,128]{1,0:T(8,128)(2,1)S(1)}, bf16[304,128]{1,0:T(8,128)(2,1)S(1)}, u32[]{:S(2)}, u32[]{:S(2)}) collective-permute-start(bf16[304,128]{1,0:T(8,128)(2,1)S(1)} %shard_map.166.refs_0_), channel_id=1, source_target_pairs={{0,16},{1,17},{2,18},{3,19},{4,20},{5,21},{6,22},{7,23},{8,24},{9,... | collective-permute-start | bytes 233480 | tf_op jit(solution)/shard_map/ppermute | solution.py:128
  40.0 2.4 %collective-permute-start.14 = (bf16[304,128]{1,0:T(8,128)(2,1)S(1)}, bf16[304,128]{1,0:T(8,128)(2,1)S(1)}, u32[]{:S(2)}, u32[]{:S(2)}) collective-permute-start(bf16[304,128]{1,0:T(8,128)(2,1)S(1)} %shard_map.166.refs_0_), channel_id=1, source_target_pairs={{0,1},{1,0},{2,3},{3,2},{4,5},{5,4},{6,7},{7,6},{8,9},{9,8},{10,11... | collective-permute-start | bytes 233480 | tf_op jit(solution)/shard_map/ppermute | solution.py:128
  42.4 0.0 collective-permute-done.7.inner_column
  42.4 0.0 collective-permute-done.6.outer_column
  42.4 1.6 %shard_map.161 = (bf16[64,8,128]{2,1,0:T(8,128)(2,1)}, bf16[64,8,128]{2,1,0:T(8,128)(2,1)}, f32[8,128]{1,0:T(8,128)S(1)}) custom-call(f32[1024,128]{1,0:T(8,128)S(1)} %get-tuple-element.92.wide, bf16[3,128,768]{2,1,0:T(8,128)(2,1)S(1)} %get-tuple-element.93.turned, bf16[256,128]{1,0:T(8,128)(2,1)S(1)} %collective-permute-done.4.outer.outer_row, ...), custom_call_target="tpu_custom_call" | custom-call | flops 12079595520 | bytes 2000000 | tf_op jit(solution)/shard_map/pallas_call | solution.py:45
  44.0 0.2 collective-permute-done.16.refs_3_
  44.2 0.8 %collective-permute-done.14.refs_1_ = bf16[304,128]{1,0:T(8,128)(2,1)S(1)} collective-permute-done((bf16[304,128]{1,0:T(8,128)(2,1)S(1)}, bf16[304,128]{1,0:T(8,128)(2,1)S(1)}, u32[]{:S(2)}, u32[]{:S(2)}) %collective-permute-start.14) | collective-permute-done | bytes 77856 | tf_op jit(solution)/shard_map/ppermute | solution.py:128
  45.1 0.1 collective-permute-start.17
  45.2 0.9 %shard_map.168.out_before = f32[9,256,128]{2,1,0:T(8,128)} custom-call(bf16[4,304,128]{2,1,0:T(8,128)(2,1)S(1)} %shard_map.167.own), custom_call_target="tpu_custom_call" | custom-call | bytes 884736 | tf_op jit(solution)/shard_map/pallas_call | solution.py:45
  46.1 0.7 %collective-permute-done.17.received = bf16[4,304,128]{2,1,0:T(8,128)(2,1)S(1)} collective-permute-done((bf16[4,304,128]{2,1,0:T(8,128)(2,1)S(1)}, bf16[4,304,128]{2,1,0:T(8,128)(2,1)S(1)}, u32[]{:S(2)}, u32[]{:S(2)}) %collective-permute-start.17) | collective-permute-done | bytes 311328 | tf_op jit(solution)/shard_map/ppermute | solution.py:128
  46.8 0.9 %shard_map.169 = (f32[9,256,128]{2,1,0:T(8,128)}, f32[256]{0:T(256)}) custom-call(bf16[4,304,128]{2,1,0:T(8,128)(2,1)S(1)} %shard_map.167.own, bf16[4,304,128]{2,1,0:T(8,128)(2,1)S(1)} %collective-permute-done.17.received, f32[8,128]{1,0:T(8,128)S(1)} %get-tuple-element.68.target.after, ...), custom_call_target="tpu_custom_call", output_to_operand_aliasing={{0}: (3, {})} | custom-call | bytes 884736 | tf_op jit(solution)/shard_map/pallas_call | solution.py:45
  (5 shorter events, 0.1 us)
Async XLA Ops:
  1.7 6.4 %collective-permute-start = (bf16[128,128]{1,0:T(8,128)(2,1)S(1)}, bf16[128,128]{1,0:T(8,128)(2,1)S(1)}, u32[]{:S(2)}, u32[]{:S(2)}) collective-permute-start(bf16[128,128]{1,0:T(8,128)(2,1)S(1)} %get-tuple-element.62), channel_id=1, source_target_pairs={{0,8},{1,9},{2,10},{3,11},{4,12},{5,13},{6,14},{7,15},{8,0},{9,1},... | collective-permute-start | bytes 98312 | tf_op jit(solution)/shard_map/ppermute | solution.py:128
  2.2 5.9 %collective-permute-start.1 = (bf16[128,128]{1,0:T(8,128)(2,1)S(1)}, bf16[128,128]{1,0:T(8,128)(2,1)S(1)}, u32[]{:S(2)}, u32[]{:S(2)}) collective-permute-start(bf16[128,128]{1,0:T(8,128)(2,1)S(1)} %get-tuple-element.63), channel_id=1, source_target_pairs={{0,4},{1,5},{2,6},{3,7},{4,0},{5,1},{6,2},{7,3},{8,16},{9,17},{10,... | collective-permute-start | bytes 98312 | tf_op jit(solution)/shard_map/ppermute | solution.py:128
  8.2 7.6 %collective-permute-start.3 = (bf16[32,128]{1,0:T(8,128)(2,1)S(1)}, bf16[32,128]{1,0:T(8,128)(2,1)S(1)}, u32[]{:S(2)}, u32[]{:S(2)}) collective-permute-start(bf16[32,128]{1,0:T(8,128)(2,1)S(1)} %get-tuple-element.80), channel_id=1, source_target_pairs={{0,1},{1,0},{2,3},{3,2},{4,5},{5,4},{6,7},{7,6},{8,9},{9,8},{10,11... | collective-permute-start | bytes 24584 | tf_op jit(solution)/shard_map/ppermute | solution.py:128
  9.8 6.3 %collective-permute-start.2 = (bf16[32,128]{1,0:T(8,128)(2,1)S(1)}, bf16[32,128]{1,0:T(8,128)(2,1)S(1)}, u32[]{:S(2)}, u32[]{:S(2)}) collective-permute-start(bf16[32,128]{1,0:T(8,128)(2,1)S(1)} %get-tuple-element.80), channel_id=1, source_target_pairs={{0,7},{1,2},{2,1},{3,4},{4,3},{5,6},{6,5},{7,0},{8,15},{9,10},{10,... | collective-permute-start | bytes 24584 | tf_op jit(solution)/shard_map/ppermute | solution.py:128
  17.0 1.6 %collective-permute-start.8 = (bf16[1152,128]{1,0:T(8,128)(2,1)S(1)}, bf16[1152,128]{1,0:T(8,128)(2,1)S(1)}, u32[]{:S(2)}, u32[]{:S(2)}) collective-permute-start(bf16[1152,128]{1,0:T(8,128)(2,1)S(1)} %get-tuple-element.104), channel_id=1, source_target_pairs={{0,8},{1,9},{2,10},{3,11},{4,12},{5,13},{6,14},{7,15},{8,0},{9,1},... | collective-permute-start | bytes 884744 | tf_op jit(solution)/shard_map/ppermute | solution.py:128
  18.7 6.2 %collective-permute-start.9 = (bf16[304,128]{1,0:T(8,128)(2,1)S(1)}, bf16[304,128]{1,0:T(8,128)(2,1)S(1)}, u32[]{:S(2)}, u32[]{:S(2)}) collective-permute-start(bf16[304,128]{1,0:T(8,128)(2,1)S(1)} %get-tuple-element.106), channel_id=1, source_target_pairs={{0,17},{1,16},{2,19},{3,18},{4,21},{5,20},{6,23},{7,22},{8,25},{9,... | collective-permute-start | bytes 233480 | tf_op jit(solution)/shard_map/ppermute | solution.py:128
  18.8 6.1 %collective-permute-start.10 = (bf16[304,128]{1,0:T(8,128)(2,1)S(1)}, bf16[304,128]{1,0:T(8,128)(2,1)S(1)}, u32[]{:S(2)}, u32[]{:S(2)}) collective-permute-start(bf16[304,128]{1,0:T(8,128)(2,1)S(1)} %get-tuple-element.107), channel_id=1, source_target_pairs={{0,16},{1,17},{2,18},{3,19},{4,20},{5,21},{6,22},{7,23},{8,24},{9,... | collective-permute-start | bytes 233480 | tf_op jit(solution)/shard_map/ppermute | solution.py:128
  19.2 6.6 %collective-permute-start.11 = (bf16[304,128]{1,0:T(8,128)(2,1)S(1)}, bf16[304,128]{1,0:T(8,128)(2,1)S(1)}, u32[]{:S(2)}, u32[]{:S(2)}) collective-permute-start(bf16[304,128]{1,0:T(8,128)(2,1)S(1)} %get-tuple-element.108), channel_id=1, source_target_pairs={{0,1},{1,0},{2,3},{3,2},{4,5},{5,4},{6,7},{7,6},{8,9},{9,8},{10,11... | collective-permute-start | bytes 233480 | tf_op jit(solution)/shard_map/ppermute | solution.py:128
  25.8 6.2 %collective-permute-start.12 = (bf16[304,128]{1,0:T(8,128)(2,1)S(1)}, bf16[304,128]{1,0:T(8,128)(2,1)S(1)}, u32[]{:S(2)}, u32[]{:S(2)}) collective-permute-start(bf16[304,128]{1,0:T(8,128)(2,1)S(1)} %shard_map.164.own), channel_id=1, source_target_pairs={{0,4},{1,5},{2,6},{3,7},{4,0},{5,1},{6,2},{7,3},{8,10},{9,11},{10,... | collective-permute-start | bytes 233480 | tf_op jit(solution)/shard_map/ppermute | solution.py:128
  26.7 6.0 %collective-permute-start.4 = (bf16[256,128]{1,0:T(8,128)(2,1)S(1)}, bf16[256,128]{1,0:T(8,128)(2,1)S(1)}, u32[]{:S(2)}, u32[]{:S(2)}) collective-permute-start(bf16[256,128]{1,0:T(8,128)(2,1)S(1)} %get-tuple-element.94), channel_id=1, source_target_pairs={{0,4},{1,5},{2,6},{3,7},{4,0},{5,1},{6,2},{7,3},{8,16},{9,17},{10,... | collective-permute-start | bytes 196616 | tf_op jit(solution)/shard_map/ppermute | solution.py:128
  28.8 3.9 %collective-permute-start.5 = (bf16[256,128]{1,0:T(8,128)(2,1)S(1)}, bf16[256,128]{1,0:T(8,128)(2,1)S(1)}, u32[]{:S(2)}, u32[]{:S(2)}) collective-permute-start(bf16[256,128]{1,0:T(8,128)(2,1)S(1)} %get-tuple-element.95), channel_id=1, source_target_pairs={{0,8},{1,9},{2,10},{3,11},{4,12},{5,13},{6,14},{7,15},{8,0},{9,1},... | collective-permute-start | bytes 196616 | tf_op jit(solution)/shard_map/ppermute | solution.py:128
  32.0 6.8 %collective-permute-start.13 = (bf16[304,128]{1,0:T(8,128)(2,1)S(1)}, bf16[304,128]{1,0:T(8,128)(2,1)S(1)}, u32[]{:S(2)}, u32[]{:S(2)}) collective-permute-start(bf16[304,128]{1,0:T(8,128)(2,1)S(1)} %shard_map.165.own), channel_id=1, source_target_pairs={{0,2},{1,3},{2,0},{3,1},{4,6},{5,7},{6,4},{7,5},{8,12},{9,13},{10,... | collective-permute-start | bytes 233480 | tf_op jit(solution)/shard_map/ppermute | solution.py:128
  32.9 9.5 %collective-permute-start.7 = (bf16[64,128]{1,0:T(8,128)(2,1)S(1)}, bf16[64,128]{1,0:T(8,128)(2,1)S(1)}, u32[]{:S(2)}, u32[]{:S(2)}) collective-permute-start(bf16[64,128]{1,0:T(8,128)(2,1)S(1)} %shard_map.160), channel_id=1, source_target_pairs={{0,1},{1,0},{2,3},{3,2},{4,5},{5,4},{6,7},{7,6},{8,9},{9,8},{10,11... | collective-permute-start | bytes 49160 | tf_op jit(solution)/shard_map/ppermute | solution.py:128
  33.9 8.5 %collective-permute-start.6 = (bf16[64,128]{1,0:T(8,128)(2,1)S(1)}, bf16[64,128]{1,0:T(8,128)(2,1)S(1)}, u32[]{:S(2)}, u32[]{:S(2)}) collective-permute-start(bf16[64,128]{1,0:T(8,128)(2,1)S(1)} %shard_map.160), channel_id=1, source_target_pairs={{0,7},{1,2},{2,1},{3,4},{4,3},{5,6},{6,5},{7,0},{8,15},{9,10},{10,... | collective-permute-start | bytes 49160 | tf_op jit(solution)/shard_map/ppermute | solution.py:128
  38.9 5.4 %collective-permute-start.16 = (bf16[304,128]{1,0:T(8,128)(2,1)S(1)}, bf16[304,128]{1,0:T(8,128)(2,1)S(1)}, u32[]{:S(2)}, u32[]{:S(2)}) collective-permute-start(bf16[304,128]{1,0:T(8,128)(2,1)S(1)} %shard_map.166.refs_0_), channel_id=1, source_target_pairs={{0,17},{1,16},{2,19},{3,18},{4,21},{5,20},{6,23},{7,22},{8,25},{9,... | collective-permute-start | bytes 233480 | tf_op jit(solution)/shard_map/ppermute | solution.py:128
  38.9 5.3 %collective-permute-start.15 = (bf16[304,128]{1,0:T(8,128)(2,1)S(1)}, bf16[304,128]{1,0:T(8,128)(2,1)S(1)}, u32[]{:S(2)}, u32[]{:S(2)}) collective-permute-start(bf16[304,128]{1,0:T(8,128)(2,1)S(1)} %shard_map.166.refs_0_), channel_id=1, source_target_pairs={{0,16},{1,17},{2,18},{3,19},{4,20},{5,21},{6,22},{7,23},{8,24},{9,... | collective-permute-start | bytes 233480 | tf_op jit(solution)/shard_map/ppermute | solution.py:128
  40.0 5.1 %collective-permute-start.14 = (bf16[304,128]{1,0:T(8,128)(2,1)S(1)}, bf16[304,128]{1,0:T(8,128)(2,1)S(1)}, u32[]{:S(2)}, u32[]{:S(2)}) collective-permute-start(bf16[304,128]{1,0:T(8,128)(2,1)S(1)} %shard_map.166.refs_0_), channel_id=1, source_target_pairs={{0,1},{1,0},{2,3},{3,2},{4,5},{5,4},{6,7},{7,6},{8,9},{9,8},{10,11... | collective-permute-start | bytes 233480 | tf_op jit(solution)/shard_map/ppermute | solution.py:128
  45.1 1.7 %collective-permute-start.17 = (bf16[4,304,128]{2,1,0:T(8,128)(2,1)S(1)}, bf16[4,304,128]{2,1,0:T(8,128)(2,1)S(1)}, u32[]{:S(2)}, u32[]{:S(2)}) collective-permute-start(bf16[4,304,128]{2,1,0:T(8,128)(2,1)S(1)} %shard_map.167.own), channel_id=1, source_target_pairs={{0,8},{1,9},{2,10},{3,11},{4,12},{5,13},{6,14},{7,15},{8,0},{9,1},... | collective-permute-start | bytes 933896 | tf_op jit(solution)/shard_map/ppermute | solution.py:128

commit v7 on v5

--- a/solution.py
+++ b/solution.py
@@ -461,8 +461,8 @@
     row_count,
     edge,
     second,
+    inner_column,
     outer_column,
-    inner_column,
     weights,
     bias_wide,
     readout_wide,
@@ -890,8 +890,8 @@
     )(
         edge,
         second,
+        inner_column,
         outer_column,
-        inner_column,
         weights_here,
         bias_wide,
         readout_wide,

time: 47 us -> 47.6 us (1.013)
  waiting for transfers between devices: 8.2 us -> 10.4 us
  starting transfers between devices: 24.9 us -> 23.3 us
    ppermute x18, waiting for transfers between devices: 8.2 us -> 10.4 us  [permuted(): return lax.ppermute(value, AXES, pairs)]
    ppermute x18, starting transfers between devices: 24.9 us -> 23.3 us  [permuted(): return lax.ppermute(value, AXES, pairs)]
  transfers between devices with their start and end apart: 18 -> 18, of which waited for: 11 -> 10; matrix products, arithmetic and copies ran while one was open for 0% -> 0% of each run, Pallas kernels for 21% -> 21%
where the time goes in v7:
time: 47.6 us; the launch traced here: 47.5 us
  starting transfers between devices  23.3 us (49%)
  Pallas kernels  13 us (27%)
  waiting for transfers between devices  10.4 us (22%)
  between operations  0.78 us (2%)
    ppermute x18, starting transfers between devices, permuted(): return lax.ppermute(value, AXES, pairs)  23.3 us
    pallas_call x17, Pallas kernels, run(): pl.pallas_call(kernel, out_shape=out_shape, in_specs=[VMEM] * near + [HBM...  13 us
    ppermute x18, waiting for transfers between devices, permuted(): return lax.ppermute(value, AXES, pairs)  10.4 us
  transfers between devices with their start and end apart: 18, of which 10 were waited for; matrix products, arithmetic and copies ran while one was open for 0% of the time, Pallas kernels for 21%

profile of v7, /device:TPU:0, one launch (start us, length us, event | category | flops | bytes accessed | tf_op | source)
XLA Modules:
  0.0 47.5 jit_solution(14030107003056717388)
XLA Ops:
  0.6 1.0 %shard_map.153 = (bf16[128,128]{1,0:T(8,128)(2,1)S(1)}, bf16[128,128]{1,0:T(8,128)(2,1)S(1)}, f32[1024,128]{1,0:T(8,128)S(1)}) custom-call(bf16[64,8,128]{2,1,0:T(8,128)(2,1)} %below.1, bf16[64,8,128]{2,1,0:T(8,128)(2,1)} %hidden.1), custom_call_target="tpu_custom_call" | custom-call | bytes 524288 | tf_op jit(solution)/shard_map/pallas_call | solution.py:45
  1.7 0.5 %collective-permute-start = (bf16[128,128]{1,0:T(8,128)(2,1)S(1)}, bf16[128,128]{1,0:T(8,128)(2,1)S(1)}, u32[]{:S(2)}, u32[]{:S(2)}) collective-permute-start(bf16[128,128]{1,0:T(8,128)(2,1)S(1)} %get-tuple-element.62), channel_id=1, source_target_pairs={{0,8},{1,9},{2,10},{3,11},{4,12},{5,13},{6,14},{7,15},{8,0},{9,1},... | collective-permute-start | bytes 98312 | tf_op jit(solution)/shard_map/ppermute | solution.py:128
  2.2 3.7 %collective-permute-start.1 = (bf16[128,128]{1,0:T(8,128)(2,1)S(1)}, bf16[128,128]{1,0:T(8,128)(2,1)S(1)}, u32[]{:S(2)}, u32[]{:S(2)}) collective-permute-start(bf16[128,128]{1,0:T(8,128)(2,1)S(1)} %get-tuple-element.63), channel_id=1, source_target_pairs={{0,4},{1,5},{2,6},{3,7},{4,0},{5,1},{6,2},{7,3},{8,16},{9,17},{10,... | collective-permute-start | bytes 98312 | tf_op jit(solution)/shard_map/ppermute | solution.py:128
  5.8 2.2 %shard_map.154 = (bf16[8,128,128]{2,1,0:T(8,128)(2,1)S(1)}, f32[128,128]{1,0:T(8,128)S(1)}, f32[128,128]{1,0:T(8,128)S(1)}, f32[64,128]{1,0:T(8,128)S(1)}, f32[6...) custom-call(f32[1024,128]{1,0:T(8,128)S(1)} %get-tuple-element.60.wi, ...), custom_call_target="tpu_custom_call" | custom-call | bytes 6000000 | tf_op jit(solution)/shard_map/pallas_call | solution.py:45
  8.0 0.0 collective-permute-done.inner_row.inner
  8.0 0.0 collective-permute-done.1.outer_row.outer
  8.0 0.2 shard_map.156
  8.2 4.8 %collective-permute-start.3 = (bf16[32,128]{1,0:T(8,128)(2,1)S(1)}, bf16[32,128]{1,0:T(8,128)(2,1)S(1)}, u32[]{:S(2)}, u32[]{:S(2)}) collective-permute-start(bf16[32,128]{1,0:T(8,128)(2,1)S(1)} %get-tuple-element.80), channel_id=1, source_target_pairs={{0,7},{1,2},{2,1},{3,4},{4,3},{5,6},{6,5},{7,0},{8,15},{9,10},{10,... | collective-permute-start | bytes 24584 | tf_op jit(solution)/shard_map/ppermute | solution.py:128
  13.0 0.0 collective-permute-start.2
  13.0 2.2 %shard_map.155 = (f32[512,128]{1,0:T(8,128)S(1)}, f32[512,128]{1,0:T(8,128)S(1)}, f32[512,128]{1,0:T(8,128)S(1)}, bf16[256,1024]{1,0:T(8,128)(2,1)S(1)}, bf16[12...) custom-call(bf16[8,128,128]{2,1,0:T(8,128)(2,1)S(1)} %get-tuple-element.61.rows_in, ...), custom_call_target="tpu_custom_call" | custom-call | flops 1207959552 | bytes 6000000 | tf_op jit(solution)/shard_map/pallas_call | solution.py:45
  15.3 0.0 collective-permute-done.3.outer_column
  15.3 1.4 %collective-permute-done.2.inner_column = bf16[32,128]{1,0:T(8,128)(2,1)S(1)} collective-permute-done((bf16[32,128]{1,0:T(8,128)(2,1)S(1)}, bf16[32,128]{1,0:T(8,128)(2,1)S(1)}, u32[]{:S(2)}, u32[]{:S(2)}) %collective-permute-start.2) | collective-permute-done | bytes 8224 | tf_op jit(solution)/shard_map/ppermute | solution.py:128
  16.7 0.9 %shard_map.157 = (bf16[1152,128]{1,0:T(8,128)(2,1)S(1)}, bf16[256,128]{1,0:T(8,128)(2,1)S(1)}, f32[256,128]{1,0:T(8,128)S(1)}, bf16[1152,128]{1,0:T(8,128)(2,1)S...) custom-call(bf16[128,128]{1,0:T(8,128)(2,1)S(1)} %get-tuple-element.78.edge, ...), custom_call_target="tpu_custom_call" | custom-call | tf_op jit(solution)/shard_map/pallas_call | solution.py:45
  17.6 0.1 collective-permute-start.8
  17.6 0.3 shard_map.162
  17.9 1.3 %collective-permute-done.8.received = bf16[1152,128]{1,0:T(8,128)(2,1)S(1)} collective-permute-done((bf16[1152,128]{1,0:T(8,128)(2,1)S(1)}, bf16[1152,128]{1,0:T(8,128)(2,1)S(1)}, u32[]{:S(2)}, u32[]{:S(2)}) %collective-permute-start.8) | collective-permute-done | bytes 294944 | tf_op jit(solution)/shard_map/ppermute | solution.py:128
  19.2 0.1 shard_map.163
  19.3 0.1 collective-permute-start.9
  19.4 2.1 %collective-permute-start.10 = (bf16[304,128]{1,0:T(8,128)(2,1)S(1)}, bf16[304,128]{1,0:T(8,128)(2,1)S(1)}, u32[]{:S(2)}, u32[]{:S(2)}) collective-permute-start(bf16[304,128]{1,0:T(8,128)(2,1)S(1)} %get-tuple-element.107), channel_id=1, source_target_pairs={{0,16},{1,17},{2,18},{3,19},{4,20},{5,21},{6,22},{7,23},{8,24},{9,... | collective-permute-start | bytes 233480 | tf_op jit(solution)/shard_map/ppermute | solution.py:128
  21.5 1.4 %collective-permute-start.11 = (bf16[304,128]{1,0:T(8,128)(2,1)S(1)}, bf16[304,128]{1,0:T(8,128)(2,1)S(1)}, u32[]{:S(2)}, u32[]{:S(2)}) collective-permute-start(bf16[304,128]{1,0:T(8,128)(2,1)S(1)} %get-tuple-element.108), channel_id=1, source_target_pairs={{0,1},{1,0},{2,3},{3,2},{4,5},{5,4},{6,7},{7,6},{8,9},{9,8},{10,11... | collective-permute-start | bytes 233480 | tf_op jit(solution)/shard_map/ppermute | solution.py:128
  22.9 1.4 %shard_map.158 = (bf16[64,8,128]{2,1,0:T(8,128)(2,1)}, f32[512,128]{1,0:T(8,128)}, f32[512,128]{1,0:T(8,128)}, bf16[256,1024]{1,0:T(8,128)(2,1)S(1)}, bf16[256,1...) custom-call(f32[512,128]{1,0:T(8,128)S(1)} %get-tuple-element.73.hidden, f32[512,128]{1,0:T(8,128)S(1)} %get-tuple-element.74.cell, ...), custom_call_target="tpu_custom_call" | custom-call | bytes 4000000 | tf_op jit(solution)/shard_map/pallas_call | solution.py:45
  24.2 1.1 %shard_map.159 = (f32[1024,128]{1,0:T(8,128)S(1)}, bf16[3,128,768]{2,1,0:T(8,128)(2,1)S(1)}, f32[8,128]{1,0:T(8,128)S(1)}) custom-call(bf16[256,1024]{1,0:T(8,128)(2,1)S(1)} %get-tuple-element.91.pre, bf16[9,256,128]{2,1,0:T(8,128)(2,1)S(1)} %get-tuple-element.66.weights), custom_call_target="tpu_custom_call" | custom-call | flops 603979776 | bytes 3000000 | tf_op jit(solution)/shard_map/pallas_call | solution.py:45
  25.4 0.1 collective-permute-done.9.refs_0_
  25.5 0.0 collective-permute-done.10.refs_1_
  25.5 0.8 %collective-permute-done.11.refs_2_ = bf16[304,128]{1,0:T(8,128)(2,1)S(1)} collective-permute-done((bf16[304,128]{1,0:T(8,128)(2,1)S(1)}, bf16[304,128]{1,0:T(8,128)(2,1)S(1)}, u32[]{:S(2)}, u32[]{:S(2)}) %collective-permute-start.11) | collective-permute-done | bytes 77856 | tf_op jit(solution)/shard_map/ppermute | solution.py:128
  26.4 0.1 collective-permute-start.12
  26.5 2.7 %collective-permute-start.4 = (bf16[256,128]{1,0:T(8,128)(2,1)S(1)}, bf16[256,128]{1,0:T(8,128)(2,1)S(1)}, u32[]{:S(2)}, u32[]{:S(2)}) collective-permute-start(bf16[256,128]{1,0:T(8,128)(2,1)S(1)} %get-tuple-element.94), channel_id=1, source_target_pairs={{0,4},{1,5},{2,6},{3,7},{4,0},{5,1},{6,2},{7,3},{8,16},{9,17},{10,... | collective-permute-start | bytes 196616 | tf_op jit(solution)/shard_map/ppermute | solution.py:128
  29.2 0.0 collective-permute-start.5
  29.2 1.9 %collective-permute-done.12.received = bf16[304,128]{1,0:T(8,128)(2,1)S(1)} collective-permute-done((bf16[304,128]{1,0:T(8,128)(2,1)S(1)}, bf16[304,128]{1,0:T(8,128)(2,1)S(1)}, u32[]{:S(2)}, u32[]{:S(2)}) %collective-permute-start.12) | collective-permute-done | bytes 77856 | tf_op jit(solution)/shard_map/ppermute | solution.py:128
  31.1 0.5 %collective-permute-start.13 = (bf16[304,128]{1,0:T(8,128)(2,1)S(1)}, bf16[304,128]{1,0:T(8,128)(2,1)S(1)}, u32[]{:S(2)}, u32[]{:S(2)}) collective-permute-start(bf16[304,128]{1,0:T(8,128)(2,1)S(1)} %shard_map.165.own), channel_id=1, source_target_pairs={{0,4},{1,5},{2,6},{3,7},{4,0},{5,1},{6,2},{7,3},{8,10},{9,11},{10,... | collective-permute-start | bytes 233480 | tf_op jit(solution)/shard_map/ppermute | solution.py:128
  31.6 0.1 collective-permute-done.4.outer.outer_row
  31.8 0.0 collective-permute-done.5.inner.inner_row
  31.8 0.2 shard_map.160
  32.0 1.9 %collective-permute-start.7 = (bf16[64,128]{1,0:T(8,128)(2,1)S(1)}, bf16[64,128]{1,0:T(8,128)(2,1)S(1)}, u32[]{:S(2)}, u32[]{:S(2)}) collective-permute-start(bf16[64,128]{1,0:T(8,128)(2,1)S(1)} %shard_map.160), channel_id=1, source_target_pairs={{0,1},{1,0},{2,3},{3,2},{4,5},{5,4},{6,7},{7,6},{8,9},{9,8},{10,11... | collective-permute-start | bytes 49160 | tf_op jit(solution)/shard_map/ppermute | solution.py:128
  33.9 1.7 %collective-permute-start.6 = (bf16[64,128]{1,0:T(8,128)(2,1)S(1)}, bf16[64,128]{1,0:T(8,128)(2,1)S(1)}, u32[]{:S(2)}, u32[]{:S(2)}) collective-permute-start(bf16[64,128]{1,0:T(8,128)(2,1)S(1)} %shard_map.160), channel_id=1, source_target_pairs={{0,7},{1,2},{2,1},{3,4},{4,3},{5,6},{6,5},{7,0},{8,15},{9,10},{10,... | collective-permute-start | bytes 49160 | tf_op jit(solution)/shard_map/ppermute | solution.py:128
  35.6 1.1 %collective-permute-done.13.received = bf16[304,128]{1,0:T(8,128)(2,1)S(1)} collective-permute-done((bf16[304,128]{1,0:T(8,128)(2,1)S(1)}, bf16[304,128]{1,0:T(8,128)(2,1)S(1)}, u32[]{:S(2)}, u32[]{:S(2)}) %collective-permute-start.13) | collective-permute-done | bytes 77856 | tf_op jit(solution)/shard_map/ppermute | solution.py:128
  36.7 1.4 %collective-permute-start.16 = (bf16[304,128]{1,0:T(8,128)(2,1)S(1)}, bf16[304,128]{1,0:T(8,128)(2,1)S(1)}, u32[]{:S(2)}, u32[]{:S(2)}) collective-permute-start(bf16[304,128]{1,0:T(8,128)(2,1)S(1)} %shard_map.166.refs_0_), channel_id=1, source_target_pairs={{0,17},{1,16},{2,19},{3,18},{4,21},{5,20},{6,23},{7,22},{8,25},{9,... | collective-permute-start | bytes 233480 | tf_op jit(solution)/shard_map/ppermute | solution.py:128
  38.1 2.4 %collective-permute-start.15 = (bf16[304,128]{1,0:T(8,128)(2,1)S(1)}, bf16[304,128]{1,0:T(8,128)(2,1)S(1)}, u32[]{:S(2)}, u32[]{:S(2)}) collective-permute-start(bf16[304,128]{1,0:T(8,128)(2,1)S(1)} %shard_map.166.refs_0_), channel_id=1, source_target_pairs={{0,16},{1,17},{2,18},{3,19},{4,20},{5,21},{6,22},{7,23},{8,24},{9,... | collective-permute-start | bytes 233480 | tf_op jit(solution)/shard_map/ppermute | solution.py:128
  40.5 0.0 collective-permute-done.7.inner_column
  40.5 0.0 collective-permute-done.6.outer_column
  40.5 1.6 %shard_map.161 = (bf16[64,8,128]{2,1,0:T(8,128)(2,1)}, bf16[64,8,128]{2,1,0:T(8,128)(2,1)}, f32[8,128]{1,0:T(8,128)S(1)}) custom-call(f32[1024,128]{1,0:T(8,128)S(1)} %get-tuple-element.92.wide, bf16[3,128,768]{2,1,0:T(8,128)(2,1)S(1)} %get-tuple-element.93.turned, bf16[256,128]{1,0:T(8,128)(2,1)S(1)} %collective-permute-done.4.outer.outer_row, ...), custom_call_target="tpu_custom_call" | custom-call | flops 12079595520 | bytes 2000000 | tf_op jit(solution)/shard_map/pallas_call | solution.py:45
  42.1 0.0 collective-permute-done.16.refs_3_
  42.1 1.6 %collective-permute-done.15.refs_2_ = bf16[304,128]{1,0:T(8,128)(2,1)S(1)} collective-permute-done((bf16[304,128]{1,0:T(8,128)(2,1)S(1)}, bf16[304,128]{1,0:T(8,128)(2,1)S(1)}, u32[]{:S(2)}, u32[]{:S(2)}) %collective-permute-start.15) | collective-permute-done | bytes 77856 | tf_op jit(solution)/shard_map/ppermute | solution.py:128
  43.7 1.2 %collective-permute-done.14.refs_1_ = bf16[304,128]{1,0:T(8,128)(2,1)S(1)} collective-permute-done((bf16[304,128]{1,0:T(8,128)(2,1)S(1)}, bf16[304,128]{1,0:T(8,128)(2,1)S(1)}, u32[]{:S(2)}, u32[]{:S(2)}) %collective-permute-start.14) | collective-permute-done | bytes 77856 | tf_op jit(solution)/shard_map/ppermute | solution.py:128
  44.9 0.1 collective-permute-start.17
  45.0 0.9 %shard_map.168.out_before = f32[9,256,128]{2,1,0:T(8,128)} custom-call(bf16[4,304,128]{2,1,0:T(8,128)(2,1)S(1)} %shard_map.167.own), custom_call_target="tpu_custom_call" | custom-call | bytes 884736 | tf_op jit(solution)/shard_map/pallas_call | solution.py:45
  45.9 0.7 %collective-permute-done.17.received = bf16[4,304,128]{2,1,0:T(8,128)(2,1)S(1)} collective-permute-done((bf16[4,304,128]{2,1,0:T(8,128)(2,1)S(1)}, bf16[4,304,128]{2,1,0:T(8,128)(2,1)S(1)}, u32[]{:S(2)}, u32[]{:S(2)}) %collective-permute-start.17) | collective-permute-done | bytes 311328 | tf_op jit(solution)/shard_map/ppermute | solution.py:128
  46.6 0.9 %shard_map.169 = (f32[9,256,128]{2,1,0:T(8,128)}, f32[256]{0:T(256)}) custom-call(bf16[4,304,128]{2,1,0:T(8,128)(2,1)S(1)} %shard_map.167.own, bf16[4,304,128]{2,1,0:T(8,128)(2,1)S(1)} %collective-permute-done.17.received, f32[8,128]{1,0:T(8,128)S(1)} %get-tuple-element.68.target.after, ...), custom_call_target="tpu_custom_call", output_to_operand_aliasing={{0}: (3, {})} | custom-call | bytes 884736 | tf_op jit(solution)/shard_map/pallas_call | solution.py:45
  (5 shorter events, 0.1 us)
Async XLA Ops:
  1.7 6.4 %collective-permute-start = (bf16[128,128]{1,0:T(8,128)(2,1)S(1)}, bf16[128,128]{1,0:T(8,128)(2,1)S(1)}, u32[]{:S(2)}, u32[]{:S(2)}) collective-permute-start(bf16[128,128]{1,0:T(8,128)(2,1)S(1)} %get-tuple-element.62), channel_id=1, source_target_pairs={{0,8},{1,9},{2,10},{3,11},{4,12},{5,13},{6,14},{7,15},{8,0},{9,1},... | collective-permute-start | bytes 98312 | tf_op jit(solution)/shard_map/ppermute | solution.py:128
  2.2 5.9 %collective-permute-start.1 = (bf16[128,128]{1,0:T(8,128)(2,1)S(1)}, bf16[128,128]{1,0:T(8,128)(2,1)S(1)}, u32[]{:S(2)}, u32[]{:S(2)}) collective-permute-start(bf16[128,128]{1,0:T(8,128)(2,1)S(1)} %get-tuple-element.63), channel_id=1, source_target_pairs={{0,4},{1,5},{2,6},{3,7},{4,0},{5,1},{6,2},{7,3},{8,16},{9,17},{10,... | collective-permute-start | bytes 98312 | tf_op jit(solution)/shard_map/ppermute | solution.py:128
  8.2 7.0 %collective-permute-start.3 = (bf16[32,128]{1,0:T(8,128)(2,1)S(1)}, bf16[32,128]{1,0:T(8,128)(2,1)S(1)}, u32[]{:S(2)}, u32[]{:S(2)}) collective-permute-start(bf16[32,128]{1,0:T(8,128)(2,1)S(1)} %get-tuple-element.80), channel_id=1, source_target_pairs={{0,7},{1,2},{2,1},{3,4},{4,3},{5,6},{6,5},{7,0},{8,15},{9,10},{10,... | collective-permute-start | bytes 24584 | tf_op jit(solution)/shard_map/ppermute | solution.py:128
  13.0 3.7 %collective-permute-start.2 = (bf16[32,128]{1,0:T(8,128)(2,1)S(1)}, bf16[32,128]{1,0:T(8,128)(2,1)S(1)}, u32[]{:S(2)}, u32[]{:S(2)}) collective-permute-start(bf16[32,128]{1,0:T(8,128)(2,1)S(1)} %get-tuple-element.80), channel_id=1, source_target_pairs={{0,1},{1,0},{2,3},{3,2},{4,5},{5,4},{6,7},{7,6},{8,9},{9,8},{10,11... | collective-permute-start | bytes 24584 | tf_op jit(solution)/shard_map/ppermute | solution.py:128
  17.6 1.6 %collective-permute-start.8 = (bf16[1152,128]{1,0:T(8,128)(2,1)S(1)}, bf16[1152,128]{1,0:T(8,128)(2,1)S(1)}, u32[]{:S(2)}, u32[]{:S(2)}) collective-permute-start(bf16[1152,128]{1,0:T(8,128)(2,1)S(1)} %get-tuple-element.104), channel_id=1, source_target_pairs={{0,8},{1,9},{2,10},{3,11},{4,12},{5,13},{6,14},{7,15},{8,0},{9,1},... | collective-permute-start | bytes 884744 | tf_op jit(solution)/shard_map/ppermute | solution.py:128
  19.3 6.2 %collective-permute-start.9 = (bf16[304,128]{1,0:T(8,128)(2,1)S(1)}, bf16[304,128]{1,0:T(8,128)(2,1)S(1)}, u32[]{:S(2)}, u32[]{:S(2)}) collective-permute-start(bf16[304,128]{1,0:T(8,128)(2,1)S(1)} %get-tuple-element.106), channel_id=1, source_target_pairs={{0,17},{1,16},{2,19},{3,18},{4,21},{5,20},{6,23},{7,22},{8,25},{9,... | collective-permute-start | bytes 233480 | tf_op jit(solution)/shard_map/ppermute | solution.py:128
  19.4 6.1 %collective-permute-start.10 = (bf16[304,128]{1,0:T(8,128)(2,1)S(1)}, bf16[304,128]{1,0:T(8,128)(2,1)S(1)}, u32[]{:S(2)}, u32[]{:S(2)}) collective-permute-start(bf16[304,128]{1,0:T(8,128)(2,1)S(1)} %get-tuple-element.107), channel_id=1, source_target_pairs={{0,16},{1,17},{2,18},{3,19},{4,20},{5,21},{6,22},{7,23},{8,24},{9,... | collective-permute-start | bytes 233480 | tf_op jit(solution)/shard_map/ppermute | solution.py:128
  21.5 4.9 %collective-permute-start.11 = (bf16[304,128]{1,0:T(8,128)(2,1)S(1)}, bf16[304,128]{1,0:T(8,128)(2,1)S(1)}, u32[]{:S(2)}, u32[]{:S(2)}) collective-permute-start(bf16[304,128]{1,0:T(8,128)(2,1)S(1)} %get-tuple-element.108), channel_id=1, source_target_pairs={{0,1},{1,0},{2,3},{3,2},{4,5},{5,4},{6,7},{7,6},{8,9},{9,8},{10,11... | collective-permute-start | bytes 233480 | tf_op jit(solution)/shard_map/ppermute | solution.py:128
  26.4 4.7 %collective-permute-start.12 = (bf16[304,128]{1,0:T(8,128)(2,1)S(1)}, bf16[304,128]{1,0:T(8,128)(2,1)S(1)}, u32[]{:S(2)}, u32[]{:S(2)}) collective-permute-start(bf16[304,128]{1,0:T(8,128)(2,1)S(1)} %shard_map.164.own), channel_id=1, source_target_pairs={{0,2},{1,3},{2,0},{3,1},{4,6},{5,7},{6,4},{7,5},{8,12},{9,13},{10,... | collective-permute-start | bytes 233480 | tf_op jit(solution)/shard_map/ppermute | solution.py:128
  26.5 5.3 %collective-permute-start.4 = (bf16[256,128]{1,0:T(8,128)(2,1)S(1)}, bf16[256,128]{1,0:T(8,128)(2,1)S(1)}, u32[]{:S(2)}, u32[]{:S(2)}) collective-permute-start(bf16[256,128]{1,0:T(8,128)(2,1)S(1)} %get-tuple-element.94), channel_id=1, source_target_pairs={{0,4},{1,5},{2,6},{3,7},{4,0},{5,1},{6,2},{7,3},{8,16},{9,17},{10,... | collective-permute-start | bytes 196616 | tf_op jit(solution)/shard_map/ppermute | solution.py:128
  29.2 2.6 %collective-permute-start.5 = (bf16[256,128]{1,0:T(8,128)(2,1)S(1)}, bf16[256,128]{1,0:T(8,128)(2,1)S(1)}, u32[]{:S(2)}, u32[]{:S(2)}) collective-permute-start(bf16[256,128]{1,0:T(8,128)(2,1)S(1)} %get-tuple-element.95), channel_id=1, source_target_pairs={{0,8},{1,9},{2,10},{3,11},{4,12},{5,13},{6,14},{7,15},{8,0},{9,1},... | collective-permute-start | bytes 196616 | tf_op jit(solution)/shard_map/ppermute | solution.py:128
  31.1 5.6 %collective-permute-start.13 = (bf16[304,128]{1,0:T(8,128)(2,1)S(1)}, bf16[304,128]{1,0:T(8,128)(2,1)S(1)}, u32[]{:S(2)}, u32[]{:S(2)}) collective-permute-start(bf16[304,128]{1,0:T(8,128)(2,1)S(1)} %shard_map.165.own), channel_id=1, source_target_pairs={{0,4},{1,5},{2,6},{3,7},{4,0},{5,1},{6,2},{7,3},{8,10},{9,11},{10,... | collective-permute-start | bytes 233480 | tf_op jit(solution)/shard_map/ppermute | solution.py:128
  32.0 8.5 %collective-permute-start.7 = (bf16[64,128]{1,0:T(8,128)(2,1)S(1)}, bf16[64,128]{1,0:T(8,128)(2,1)S(1)}, u32[]{:S(2)}, u32[]{:S(2)}) collective-permute-start(bf16[64,128]{1,0:T(8,128)(2,1)S(1)} %shard_map.160), channel_id=1, source_target_pairs={{0,1},{1,0},{2,3},{3,2},{4,5},{5,4},{6,7},{7,6},{8,9},{9,8},{10,11... | collective-permute-start | bytes 49160 | tf_op jit(solution)/shard_map/ppermute | solution.py:128
  33.9 6.6 %collective-permute-start.6 = (bf16[64,128]{1,0:T(8,128)(2,1)S(1)}, bf16[64,128]{1,0:T(8,128)(2,1)S(1)}, u32[]{:S(2)}, u32[]{:S(2)}) collective-permute-start(bf16[64,128]{1,0:T(8,128)(2,1)S(1)} %shard_map.160), channel_id=1, source_target_pairs={{0,7},{1,2},{2,1},{3,4},{4,3},{5,6},{6,5},{7,0},{8,15},{9,10},{10,... | collective-permute-start | bytes 49160 | tf_op jit(solution)/shard_map/ppermute | solution.py:128
  36.7 5.4 %collective-permute-start.16 = (bf16[304,128]{1,0:T(8,128)(2,1)S(1)}, bf16[304,128]{1,0:T(8,128)(2,1)S(1)}, u32[]{:S(2)}, u32[]{:S(2)}) collective-permute-start(bf16[304,128]{1,0:T(8,128)(2,1)S(1)} %shard_map.166.refs_0_), channel_id=1, source_target_pairs={{0,17},{1,16},{2,19},{3,18},{4,21},{5,20},{6,23},{7,22},{8,25},{9,... | collective-permute-start | bytes 233480 | tf_op jit(solution)/shard_map/ppermute | solution.py:128
  38.1 5.6 %collective-permute-start.15 = (bf16[304,128]{1,0:T(8,128)(2,1)S(1)}, bf16[304,128]{1,0:T(8,128)(2,1)S(1)}, u32[]{:S(2)}, u32[]{:S(2)}) collective-permute-start(bf16[304,128]{1,0:T(8,128)(2,1)S(1)} %shard_map.166.refs_0_), channel_id=1, source_target_pairs={{0,16},{1,17},{2,18},{3,19},{4,20},{5,21},{6,22},{7,23},{8,24},{9,... | collective-permute-start | bytes 233480 | tf_op jit(solution)/shard_map/ppermute | solution.py:128
  40.5 4.4 %collective-permute-start.14 = (bf16[304,128]{1,0:T(8,128)(2,1)S(1)}, bf16[304,128]{1,0:T(8,128)(2,1)S(1)}, u32[]{:S(2)}, u32[]{:S(2)}) collective-permute-start(bf16[304,128]{1,0:T(8,128)(2,1)S(1)} %shard_map.166.refs_0_), channel_id=1, source_target_pairs={{0,1},{1,0},{2,3},{3,2},{4,5},{5,4},{6,7},{7,6},{8,9},{9,8},{10,11... | collective-permute-start | bytes 233480 | tf_op jit(solution)/shard_map/ppermute | solution.py:128
  44.9 1.7 %collective-permute-start.17 = (bf16[4,304,128]{2,1,0:T(8,128)(2,1)S(1)}, bf16[4,304,128]{2,1,0:T(8,128)(2,1)S(1)}, u32[]{:S(2)}, u32[]{:S(2)}) collective-permute-start(bf16[4,304,128]{2,1,0:T(8,128)(2,1)S(1)} %shard_map.167.own), channel_id=1, source_target_pairs={{0,8},{1,9},{2,10},{3,11},{4,12},{5,13},{6,14},{7,15},{8,0},{9,1},... | collective-permute-start | bytes 933896 | tf_op jit(solution)/shard_map/ppermute | solution.py:128

commit v8 on v5

--- a/solution.py
+++ b/solution.py
@@ -599,11 +599,10 @@
     out[BIAS_ROWS:, :] = total.astype(BF16)
 
 
-def join_kernel(place, *refs):
+def join_kernel(*refs):
     blocks, out = refs[:-2], refs[-1]
-    rank = place.plane_rank()
-    for step, block in enumerate(blocks):
-        out[rank ^ step] = block[...]
+    for index, block in enumerate(blocks):
+        out[index] = block[...]
 
 
 def add_kernel(scale, own, received, out):
@@ -616,35 +615,50 @@
 def store_half(place, half, blocks, out, wide, left):
     chunk, half_gates = place.chunk, place.half_gates
     gates = pl.ds(pl.multiple_of(half * half_gates, half_gates), half_gates)
+    rank = place.plane_rank()
+    for step, block in enumerate(blocks):
+        at = pl.ds(pl.multiple_of((rank ^ step) * chunk, 8), chunk)
+        wide[at, :] = block[BIAS_ROWS:, :].astype(F32)
     copies = []
-    for index in range(place.plane):
-        wide[index * chunk : (index + 1) * chunk, :] = blocks[index, BIAS_ROWS:, :].astype(F32)
-        while len(copies) < min(place.taps, (index + 1) * chunk // half_gates):
-            tap = len(copies)
-            source = wide.at[tap * half_gates : (tap + 1) * half_gates, :]
-            copies.append(pltpu.make_async_copy(source, out.at[tap, gates, :], left.at[tap]))
-            copies[-1].start()
+    for tap in range(place.taps):
+        source = wide.at[tap * half_gates : (tap + 1) * half_gates, :]
+        copies.append(pltpu.make_async_copy(source, out.at[tap, gates, :], left.at[tap]))
+        copies[-1].start()
     return copies
 
 
-def own_half_kernel(place, own, out, wide, left):
-    for copy in store_half(place, place.rank(0), own, out, wide, left):
+def in_steps(place, early, late):
+    return [early.at[0], late] + [early.at[index] for index in range(1, place.plane - 1)]
+
+
+def own_half_kernel(place, late, early, out, bias_out, wide, left):
+    blocks = in_steps(place, early, late)
+    copies = store_half(place, place.rank(0), blocks, out, wide, left)
+    rank = place.plane_rank()
+    bias = decode(blocks[0][0:BIAS_ROWS, :].astype(F32))
+    for step in range(1, place.plane):
+        bias = pick(rank == step, decode(blocks[step][0:BIAS_ROWS, :].astype(F32)), bias)
+    bias_out[...] = bias
+    for copy in copies:
         copy.wait()
 
 
 def other_half_kernel(
-    place, own, received, after, out_before, out, bias_out, wide, bias_here, left
+    place, bias_own, early, late, after, out_before, out, bias_out, wide, bias_here, left
 ):
     del after, out_before
-    rank = place.rank(0)
-    here, there = own[0, 0:BIAS_ROWS, :].astype(F32), received[0, 0:BIAS_ROWS, :].astype(F32)
-    bias = decode(here) + decode(there)
+    blocks = in_steps(place, early, late)
+    copies = store_half(place, 1 - place.rank(0), blocks, out, wide, left)
+    rank = place.plane_rank()
+    bias = decode(blocks[0][0:BIAS_ROWS, :].astype(F32))
+    for step in range(1, place.plane):
+        bias = pick(rank == step, decode(blocks[step][0:BIAS_ROWS, :].astype(F32)), bias)
+    bias += bias_own[...]
     width = bias.shape[1]
     for index in range(bias_here.shape[0] // width):
         bias_here[pl.ds(index * width, width)] = bias[index]
     bias_copy = pltpu.make_async_copy(bias_here, bias_out, left.at[place.taps])
     bias_copy.start()
-    copies = store_half(place, 1 - rank, received, out, wide, left)
     bias_copy.wait()
     for copy in copies:
         copy.wait()
@@ -971,27 +985,30 @@
         flops=40 * gate_count * channels * cells * 9,
         moved=2_000_000,
     )(field, turned, pre_outer, pre_inner, pre_outer_columns, pre_inner_columns)
-    gathered = call(bind(join_kernel, place), sds((place.plane, *block.shape), BF16))(
-        part, *received, field_done
+    early = call(join_kernel, sds((place.plane - 1, *block.shape), BF16))(
+        part, *received[1:], field_done
     )
-    received = permuted(gathered, place.phase_pairs(0))
+    late = received[0]
+    early_other = permuted(early, place.phase_pairs(0))
+    late_other = permuted(late, place.phase_pairs(0))
     half = [pltpu.VMEM((place.half_rows, channels), F32)]
-    grad_kernel = call(
+    grad_kernel, bias = call(
         bind(own_half_kernel, place),
-        (sds(kernel_weights.shape, F32),),
+        (sds(kernel_weights.shape, F32), sds((8, channels), F32)),
         half + [pltpu.SemaphoreType.DMA((place.taps,))],
         leaving=1,
+        flops=40 * gate_count * channels * cells * 9,
         moved=6 * place.half_rows * channels,
-    )(gathered)[0]
+    )(late, early)
     grad_kernel, grad_bias = call(
         bind(other_half_kernel, place),
         (sds(kernel_weights.shape, F32), sds((gate_count,), F32)),
         half + [pltpu.VMEM((gate_count,), F32), pltpu.SemaphoreType.DMA((place.taps + 1,))],
         remote=1,
         leaving=2,
-        aliases={3: 0},
+        aliases={4: 0},
         moved=6 * place.half_rows * channels,
-    )(gathered, received, target_here, grad_kernel)
+    )(bias, early_other, late_other, target_here, grad_kernel)
     shape = hidden_prev.shape
     return (
         hidden_next,

time: 47 us -> 46.6 us (level)
    ppermute x18 -> x19, waiting for transfers between devices: 8.2 us -> 7.74 us  [permuted(): return lax.ppermute(value, AXES, pairs)]
    ppermute x18 -> x19, starting transfers between devices: 24.9 us -> 24.9 us  [permuted(): return lax.ppermute(value, AXES, pairs)]
  transfers between devices with their start and end apart: 18 -> 19, of which waited for: 11 -> 11; matrix products, arithmetic and copies ran while one was open for 0% -> 0% of each run, Pallas kernels for 21% -> 21%
where the time goes in v8:
time: 46.6 us; the launch traced here: 46.5 us
  starting transfers between devices  24.9 us (53%)
  Pallas kernels  13 us (28%)
  waiting for transfers between devices  7.74 us (17%)
  between operations  0.78 us (2%)
    ppermute x19, starting transfers between devices, permuted(): return lax.ppermute(value, AXES, pairs)  24.9 us
    pallas_call x17, Pallas kernels, run(): pl.pallas_call(kernel, out_shape=out_shape, in_specs=[VMEM] * near + [HBM...  13 us
    ppermute x19, waiting for transfers between devices, permuted(): return lax.ppermute(value, AXES, pairs)  7.74 us
  transfers between devices with their start and end apart: 19, of which 11 were waited for; matrix products, arithmetic and copies ran while one was open for 0% of the time, Pallas kernels for 21%

profile of v8, /device:TPU:0, one launch (start us, length us, event | category | flops | bytes accessed | tf_op | source)
XLA Modules:
  0.0 46.5 jit_solution(15808893499577362800)
XLA Ops:
  0.6 1.0 %shard_map.153 = (bf16[128,128]{1,0:T(8,128)(2,1)S(1)}, bf16[128,128]{1,0:T(8,128)(2,1)S(1)}, f32[1024,128]{1,0:T(8,128)S(1)}) custom-call(bf16[64,8,128]{2,1,0:T(8,128)(2,1)} %below.1, bf16[64,8,128]{2,1,0:T(8,128)(2,1)} %hidden.1), custom_call_target="tpu_custom_call" | custom-call | bytes 524288 | tf_op jit(solution)/shard_map/pallas_call | solution.py:45
  1.7 0.5 %collective-permute-start = (bf16[128,128]{1,0:T(8,128)(2,1)S(1)}, bf16[128,128]{1,0:T(8,128)(2,1)S(1)}, u32[]{:S(2)}, u32[]{:S(2)}) collective-permute-start(bf16[128,128]{1,0:T(8,128)(2,1)S(1)} %get-tuple-element.64), channel_id=1, source_target_pairs={{0,8},{1,9},{2,10},{3,11},{4,12},{5,13},{6,14},{7,15},{8,0},{9,1},... | collective-permute-start | bytes 98312 | tf_op jit(solution)/shard_map/ppermute | solution.py:128
  2.2 3.7 %collective-permute-start.1 = (bf16[128,128]{1,0:T(8,128)(2,1)S(1)}, bf16[128,128]{1,0:T(8,128)(2,1)S(1)}, u32[]{:S(2)}, u32[]{:S(2)}) collective-permute-start(bf16[128,128]{1,0:T(8,128)(2,1)S(1)} %get-tuple-element.65), channel_id=1, source_target_pairs={{0,4},{1,5},{2,6},{3,7},{4,0},{5,1},{6,2},{7,3},{8,16},{9,17},{10,... | collective-permute-start | bytes 98312 | tf_op jit(solution)/shard_map/ppermute | solution.py:128
  5.8 2.2 %shard_map.154 = (bf16[8,128,128]{2,1,0:T(8,128)(2,1)S(1)}, f32[128,128]{1,0:T(8,128)S(1)}, f32[128,128]{1,0:T(8,128)S(1)}, f32[64,128]{1,0:T(8,128)S(1)}, f32[6...) custom-call(f32[1024,128]{1,0:T(8,128)S(1)} %get-tuple-element.62.wi, ...), custom_call_target="tpu_custom_call" | custom-call | bytes 6000000 | tf_op jit(solution)/shard_map/pallas_call | solution.py:45
  8.0 0.0 collective-permute-done.inner_row.inner
  8.0 0.0 collective-permute-done.1.outer_row.outer
  8.0 0.2 shard_map.156
  8.2 1.5 %collective-permute-start.3 = (bf16[32,128]{1,0:T(8,128)(2,1)S(1)}, bf16[32,128]{1,0:T(8,128)(2,1)S(1)}, u32[]{:S(2)}, u32[]{:S(2)}) collective-permute-start(bf16[32,128]{1,0:T(8,128)(2,1)S(1)} %get-tuple-element.82), channel_id=1, source_target_pairs={{0,1},{1,0},{2,3},{3,2},{4,5},{5,4},{6,7},{7,6},{8,9},{9,8},{10,11... | collective-permute-start | bytes 24584 | tf_op jit(solution)/shard_map/ppermute | solution.py:128
  9.8 3.8 %collective-permute-start.2 = (bf16[32,128]{1,0:T(8,128)(2,1)S(1)}, bf16[32,128]{1,0:T(8,128)(2,1)S(1)}, u32[]{:S(2)}, u32[]{:S(2)}) collective-permute-start(bf16[32,128]{1,0:T(8,128)(2,1)S(1)} %get-tuple-element.82), channel_id=1, source_target_pairs={{0,7},{1,2},{2,1},{3,4},{4,3},{5,6},{6,5},{7,0},{8,15},{9,10},{10,... | collective-permute-start | bytes 24584 | tf_op jit(solution)/shard_map/ppermute | solution.py:128
  13.5 2.2 %shard_map.155 = (f32[512,128]{1,0:T(8,128)S(1)}, f32[512,128]{1,0:T(8,128)S(1)}, f32[512,128]{1,0:T(8,128)S(1)}, bf16[256,1024]{1,0:T(8,128)(2,1)S(1)}, bf16[12...) custom-call(bf16[8,128,128]{2,1,0:T(8,128)(2,1)S(1)} %get-tuple-element.63.rows_in, ...), custom_call_target="tpu_custom_call" | custom-call | flops 1207959552 | bytes 6000000 | tf_op jit(solution)/shard_map/pallas_call | solution.py:45
  15.8 0.0 collective-permute-done.3.inner_column
  15.8 0.3 collective-permute-done.2.outer_column
  16.1 0.9 %shard_map.157 = (bf16[1152,128]{1,0:T(8,128)(2,1)S(1)}, bf16[256,128]{1,0:T(8,128)(2,1)S(1)}, f32[256,128]{1,0:T(8,128)S(1)}, bf16[1152,128]{1,0:T(8,128)(2,1)S...) custom-call(bf16[128,128]{1,0:T(8,128)(2,1)S(1)} %get-tuple-element.80.edge, ...), custom_call_target="tpu_custom_call" | custom-call | tf_op jit(solution)/shard_map/pallas_call | solution.py:45
  17.0 0.1 collective-permute-start.8
  17.1 0.3 shard_map.162
  17.3 1.3 %collective-permute-done.8.received = bf16[1152,128]{1,0:T(8,128)(2,1)S(1)} collective-permute-done((bf16[1152,128]{1,0:T(8,128)(2,1)S(1)}, bf16[1152,128]{1,0:T(8,128)(2,1)S(1)}, u32[]{:S(2)}, u32[]{:S(2)}) %collective-permute-start.8) | collective-permute-done | bytes 294944 | tf_op jit(solution)/shard_map/ppermute | solution.py:128
  18.6 0.1 shard_map.163
  18.7 0.1 collective-permute-start.9
  18.8 0.4 collective-permute-start.10
  19.2 3.1 %collective-permute-start.11 = (bf16[304,128]{1,0:T(8,128)(2,1)S(1)}, bf16[304,128]{1,0:T(8,128)(2,1)S(1)}, u32[]{:S(2)}, u32[]{:S(2)}) collective-permute-start(bf16[304,128]{1,0:T(8,128)(2,1)S(1)} %get-tuple-element.110), channel_id=1, source_target_pairs={{0,1},{1,0},{2,3},{3,2},{4,5},{5,4},{6,7},{7,6},{8,9},{9,8},{10,11... | collective-permute-start | bytes 233480 | tf_op jit(solution)/shard_map/ppermute | solution.py:128
  22.3 1.4 %shard_map.158 = (bf16[64,8,128]{2,1,0:T(8,128)(2,1)}, f32[512,128]{1,0:T(8,128)}, f32[512,128]{1,0:T(8,128)}, bf16[256,1024]{1,0:T(8,128)(2,1)S(1)}, bf16[256,1...) custom-call(f32[512,128]{1,0:T(8,128)S(1)} %get-tuple-element.75.hidden, f32[512,128]{1,0:T(8,128)S(1)} %get-tuple-element.76.cell, ...), custom_call_target="tpu_custom_call" | custom-call | bytes 4000000 | tf_op jit(solution)/shard_map/pallas_call | solution.py:45
  23.6 1.1 %shard_map.159 = (f32[1024,128]{1,0:T(8,128)S(1)}, bf16[3,128,768]{2,1,0:T(8,128)(2,1)S(1)}, f32[8,128]{1,0:T(8,128)S(1)}) custom-call(bf16[256,1024]{1,0:T(8,128)(2,1)S(1)} %get-tuple-element.93.pre, bf16[9,256,128]{2,1,0:T(8,128)(2,1)S(1)} %get-tuple-element.68.weights), custom_call_target="tpu_custom_call" | custom-call | flops 603979776 | bytes 3000000 | tf_op jit(solution)/shard_map/pallas_call | solution.py:45
  24.8 0.1 collective-permute-done.9.refs_0_
  24.9 0.0 collective-permute-done.10.refs_1_
  24.9 0.9 %collective-permute-done.11.refs_2_ = bf16[304,128]{1,0:T(8,128)(2,1)S(1)} collective-permute-done((bf16[304,128]{1,0:T(8,128)(2,1)S(1)}, bf16[304,128]{1,0:T(8,128)(2,1)S(1)}, u32[]{:S(2)}, u32[]{:S(2)}) %collective-permute-start.11) | collective-permute-done | bytes 77856 | tf_op jit(solution)/shard_map/ppermute | solution.py:128
  25.8 0.1 collective-permute-start.12
  25.9 3.8 %collective-permute-start.4 = (bf16[256,128]{1,0:T(8,128)(2,1)S(1)}, bf16[256,128]{1,0:T(8,128)(2,1)S(1)}, u32[]{:S(2)}, u32[]{:S(2)}) collective-permute-start(bf16[256,128]{1,0:T(8,128)(2,1)S(1)} %get-tuple-element.96), channel_id=1, source_target_pairs={{0,4},{1,5},{2,6},{3,7},{4,0},{5,1},{6,2},{7,3},{8,16},{9,17},{10,... | collective-permute-start | bytes 196616 | tf_op jit(solution)/shard_map/ppermute | solution.py:128
  29.7 0.0 collective-permute-start.5
  29.7 1.4 %collective-permute-done.12.received = bf16[304,128]{1,0:T(8,128)(2,1)S(1)} collective-permute-done((bf16[304,128]{1,0:T(8,128)(2,1)S(1)}, bf16[304,128]{1,0:T(8,128)(2,1)S(1)}, u32[]{:S(2)}, u32[]{:S(2)}) %collective-permute-start.12) | collective-permute-done | bytes 77856 | tf_op jit(solution)/shard_map/ppermute | solution.py:128
  31.1 1.0 %collective-permute-start.13 = (bf16[304,128]{1,0:T(8,128)(2,1)S(1)}, bf16[304,128]{1,0:T(8,128)(2,1)S(1)}, u32[]{:S(2)}, u32[]{:S(2)}) collective-permute-start(bf16[304,128]{1,0:T(8,128)(2,1)S(1)} %shard_map.165.own), channel_id=1, source_target_pairs={{0,4},{1,5},{2,6},{3,7},{4,0},{5,1},{6,2},{7,3},{8,10},{9,11},{10,... | collective-permute-start | bytes 233480 | tf_op jit(solution)/shard_map/ppermute | solution.py:128
  32.1 0.5 %collective-permute-done.4.outer.outer_row = bf16[256,128]{1,0:T(8,128)(2,1)S(1)} collective-permute-done((bf16[256,128]{1,0:T(8,128)(2,1)S(1)}, bf16[256,128]{1,0:T(8,128)(2,1)S(1)}, u32[]{:S(2)}, u32[]{:S(2)}) %collective-permute-start.4) | collective-permute-done | bytes 65568 | tf_op jit(solution)/shard_map/ppermute | solution.py:128
  32.6 0.0 collective-permute-done.5.inner.inner_row
  32.6 0.2 shard_map.160
  32.8 1.6 %collective-permute-start.7 = (bf16[64,128]{1,0:T(8,128)(2,1)S(1)}, bf16[64,128]{1,0:T(8,128)(2,1)S(1)}, u32[]{:S(2)}, u32[]{:S(2)}) collective-permute-start(bf16[64,128]{1,0:T(8,128)(2,1)S(1)} %shard_map.160), channel_id=1, source_target_pairs={{0,1},{1,0},{2,3},{3,2},{4,5},{5,4},{6,7},{7,6},{8,9},{9,8},{10,11... | collective-permute-start | bytes 49160 | tf_op jit(solution)/shard_map/ppermute | solution.py:128
  34.4 1.7 %collective-permute-start.6 = (bf16[64,128]{1,0:T(8,128)(2,1)S(1)}, bf16[64,128]{1,0:T(8,128)(2,1)S(1)}, u32[]{:S(2)}, u32[]{:S(2)}) collective-permute-start(bf16[64,128]{1,0:T(8,128)(2,1)S(1)} %shard_map.160), channel_id=1, source_target_pairs={{0,7},{1,2},{2,1},{3,4},{4,3},{5,6},{6,5},{7,0},{8,15},{9,10},{10,... | collective-permute-start | bytes 49160 | tf_op jit(solution)/shard_map/ppermute | solution.py:128
  36.1 0.9 %collective-permute-done.13.received = bf16[304,128]{1,0:T(8,128)(2,1)S(1)} collective-permute-done((bf16[304,128]{1,0:T(8,128)(2,1)S(1)}, bf16[304,128]{1,0:T(8,128)(2,1)S(1)}, u32[]{:S(2)}, u32[]{:S(2)}) %collective-permute-start.13) | collective-permute-done | bytes 77856 | tf_op jit(solution)/shard_map/ppermute | solution.py:128
  37.0 0.5 %collective-permute-start.16 = (bf16[304,128]{1,0:T(8,128)(2,1)S(1)}, bf16[304,128]{1,0:T(8,128)(2,1)S(1)}, u32[]{:S(2)}, u32[]{:S(2)}) collective-permute-start(bf16[304,128]{1,0:T(8,128)(2,1)S(1)} %shard_map.166.refs_0_), channel_id=1, source_target_pairs={{0,17},{1,16},{2,19},{3,18},{4,21},{5,20},{6,23},{7,22},{8,25},{9,... | collective-permute-start | bytes 233480 | tf_op jit(solution)/shard_map/ppermute | solution.py:128
  37.5 2.3 %collective-permute-start.15 = (bf16[304,128]{1,0:T(8,128)(2,1)S(1)}, bf16[304,128]{1,0:T(8,128)(2,1)S(1)}, u32[]{:S(2)}, u32[]{:S(2)}) collective-permute-start(bf16[304,128]{1,0:T(8,128)(2,1)S(1)} %shard_map.166.refs_0_), channel_id=1, source_target_pairs={{0,16},{1,17},{2,18},{3,19},{4,20},{5,21},{6,22},{7,23},{8,24},{9,... | collective-permute-start | bytes 233480 | tf_op jit(solution)/shard_map/ppermute | solution.py:128
  39.9 0.7 %collective-permute-start.14 = (bf16[304,128]{1,0:T(8,128)(2,1)S(1)}, bf16[304,128]{1,0:T(8,128)(2,1)S(1)}, u32[]{:S(2)}, u32[]{:S(2)}) collective-permute-start(bf16[304,128]{1,0:T(8,128)(2,1)S(1)} %shard_map.166.refs_0_), channel_id=1, source_target_pairs={{0,1},{1,0},{2,3},{3,2},{4,5},{5,4},{6,7},{7,6},{8,9},{9,8},{10,11... | collective-permute-start | bytes 233480 | tf_op jit(solution)/shard_map/ppermute | solution.py:128
  40.6 0.3 collective-permute-done.6.outer_column
  40.8 1.6 %shard_map.161 = (bf16[64,8,128]{2,1,0:T(8,128)(2,1)}, bf16[64,8,128]{2,1,0:T(8,128)(2,1)}, f32[8,128]{1,0:T(8,128)S(1)}) custom-call(f32[1024,128]{1,0:T(8,128)S(1)} %get-tuple-element.94.wide, bf16[3,128,768]{2,1,0:T(8,128)(2,1)S(1)} %get-tuple-element.95.turned, bf16[256,128]{1,0:T(8,128)(2,1)S(1)} %collective-permute-done.4.outer.outer_row, ...), custom_call_target="tpu_custom_call" | custom-call | flops 12079595520 | bytes 2000000 | tf_op jit(solution)/shard_map/pallas_call | solution.py:45
  42.4 0.7 %collective-permute-done.15.refs_1_ = bf16[304,128]{1,0:T(8,128)(2,1)S(1)} collective-permute-done((bf16[304,128]{1,0:T(8,128)(2,1)S(1)}, bf16[304,128]{1,0:T(8,128)(2,1)S(1)}, u32[]{:S(2)}, u32[]{:S(2)}) %collective-permute-start.15) | collective-permute-done | bytes 77856 | tf_op jit(solution)/shard_map/ppermute | solution.py:128
  43.1 0.1 collective-permute-start.17
  43.2 1.1 %collective-permute-done.14.late = bf16[304,128]{1,0:T(8,128)(2,1)S(1)} collective-permute-done((bf16[304,128]{1,0:T(8,128)(2,1)S(1)}, bf16[304,128]{1,0:T(8,128)(2,1)S(1)}, u32[]{:S(2)}, u32[]{:S(2)}) %collective-permute-start.14) | collective-permute-done | bytes 77856 | tf_op jit(solution)/shard_map/ppermute | solution.py:128
  44.3 0.0 collective-permute-start.18
  44.3 0.9 %shard_map.168 = (f32[9,256,128]{2,1,0:T(8,128)}, f32[8,128]{1,0:T(8,128)S(1)}) custom-call(bf16[304,128]{1,0:T(8,128)(2,1)S(1)} %collective-permute-done.14.late, bf16[3,304,128]{2,1,0:T(8,128)(2,1)S(1)} %shard_map.167.early), custom_call_target="tpu_custom_call" | custom-call | flops 12079595520 | bytes 884736 | tf_op jit(solution)/shard_map/pallas_call | solution.py:45
  45.2 0.3 collective-permute-done.18.late
  45.5 0.9 %shard_map.169 = (f32[9,256,128]{2,1,0:T(8,128)}, f32[256]{0:T(256)}) custom-call(f32[8,128]{1,0:T(8,128)S(1)} %get-tuple-element.113.bias_own, bf16[3,304,128]{2,1,0:T(8,128)(2,1)S(1)} %collective-permute-done.17.early, bf16[304,128]{1,0:T(8,128)(2,1)S(1)} %collective-permute-done.18.late, ...), custom_call_target="tpu_custom_call", output_to_operand_aliasing={{0}: (4, {})} | custom-call | bytes 884736 | tf_op jit(solution)/shard_map/pallas_call | solution.py:45
  (7 shorter events, 0.1 us)
Async XLA Ops:
  1.7 6.4 %collective-permute-start = (bf16[128,128]{1,0:T(8,128)(2,1)S(1)}, bf16[128,128]{1,0:T(8,128)(2,1)S(1)}, u32[]{:S(2)}, u32[]{:S(2)}) collective-permute-start(bf16[128,128]{1,0:T(8,128)(2,1)S(1)} %get-tuple-element.64), channel_id=1, source_target_pairs={{0,8},{1,9},{2,10},{3,11},{4,12},{5,13},{6,14},{7,15},{8,0},{9,1},... | collective-permute-start | bytes 98312 | tf_op jit(solution)/shard_map/ppermute | solution.py:128
  2.2 5.9 %collective-permute-start.1 = (bf16[128,128]{1,0:T(8,128)(2,1)S(1)}, bf16[128,128]{1,0:T(8,128)(2,1)S(1)}, u32[]{:S(2)}, u32[]{:S(2)}) collective-permute-start(bf16[128,128]{1,0:T(8,128)(2,1)S(1)} %get-tuple-element.65), channel_id=1, source_target_pairs={{0,4},{1,5},{2,6},{3,7},{4,0},{5,1},{6,2},{7,3},{8,16},{9,17},{10,... | collective-permute-start | bytes 98312 | tf_op jit(solution)/shard_map/ppermute | solution.py:128
  8.2 7.6 %collective-permute-start.3 = (bf16[32,128]{1,0:T(8,128)(2,1)S(1)}, bf16[32,128]{1,0:T(8,128)(2,1)S(1)}, u32[]{:S(2)}, u32[]{:S(2)}) collective-permute-start(bf16[32,128]{1,0:T(8,128)(2,1)S(1)} %get-tuple-element.82), channel_id=1, source_target_pairs={{0,1},{1,0},{2,3},{3,2},{4,5},{5,4},{6,7},{7,6},{8,9},{9,8},{10,11... | collective-permute-start | bytes 24584 | tf_op jit(solution)/shard_map/ppermute | solution.py:128
  9.8 6.3 %collective-permute-start.2 = (bf16[32,128]{1,0:T(8,128)(2,1)S(1)}, bf16[32,128]{1,0:T(8,128)(2,1)S(1)}, u32[]{:S(2)}, u32[]{:S(2)}) collective-permute-start(bf16[32,128]{1,0:T(8,128)(2,1)S(1)} %get-tuple-element.82), channel_id=1, source_target_pairs={{0,7},{1,2},{2,1},{3,4},{4,3},{5,6},{6,5},{7,0},{8,15},{9,10},{10,... | collective-permute-start | bytes 24584 | tf_op jit(solution)/shard_map/ppermute | solution.py:128
  17.0 1.6 %collective-permute-start.8 = (bf16[1152,128]{1,0:T(8,128)(2,1)S(1)}, bf16[1152,128]{1,0:T(8,128)(2,1)S(1)}, u32[]{:S(2)}, u32[]{:S(2)}) collective-permute-start(bf16[1152,128]{1,0:T(8,128)(2,1)S(1)} %get-tuple-element.106), channel_id=1, source_target_pairs={{0,8},{1,9},{2,10},{3,11},{4,12},{5,13},{6,14},{7,15},{8,0},{9,1},... | collective-permute-start | bytes 884744 | tf_op jit(solution)/shard_map/ppermute | solution.py:128
  18.7 6.2 %collective-permute-start.9 = (bf16[304,128]{1,0:T(8,128)(2,1)S(1)}, bf16[304,128]{1,0:T(8,128)(2,1)S(1)}, u32[]{:S(2)}, u32[]{:S(2)}) collective-permute-start(bf16[304,128]{1,0:T(8,128)(2,1)S(1)} %get-tuple-element.108), channel_id=1, source_target_pairs={{0,17},{1,16},{2,19},{3,18},{4,21},{5,20},{6,23},{7,22},{8,25},{9,... | collective-permute-start | bytes 233480 | tf_op jit(solution)/shard_map/ppermute | solution.py:128
  18.8 6.1 %collective-permute-start.10 = (bf16[304,128]{1,0:T(8,128)(2,1)S(1)}, bf16[304,128]{1,0:T(8,128)(2,1)S(1)}, u32[]{:S(2)}, u32[]{:S(2)}) collective-permute-start(bf16[304,128]{1,0:T(8,128)(2,1)S(1)} %get-tuple-element.109), channel_id=1, source_target_pairs={{0,16},{1,17},{2,18},{3,19},{4,20},{5,21},{6,22},{7,23},{8,24},{9,... | collective-permute-start | bytes 233480 | tf_op jit(solution)/shard_map/ppermute | solution.py:128
  19.2 6.6 %collective-permute-start.11 = (bf16[304,128]{1,0:T(8,128)(2,1)S(1)}, bf16[304,128]{1,0:T(8,128)(2,1)S(1)}, u32[]{:S(2)}, u32[]{:S(2)}) collective-permute-start(bf16[304,128]{1,0:T(8,128)(2,1)S(1)} %get-tuple-element.110), channel_id=1, source_target_pairs={{0,1},{1,0},{2,3},{3,2},{4,5},{5,4},{6,7},{7,6},{8,9},{9,8},{10,11... | collective-permute-start | bytes 233480 | tf_op jit(solution)/shard_map/ppermute | solution.py:128
  25.8 5.3 %collective-permute-start.12 = (bf16[304,128]{1,0:T(8,128)(2,1)S(1)}, bf16[304,128]{1,0:T(8,128)(2,1)S(1)}, u32[]{:S(2)}, u32[]{:S(2)}) collective-permute-start(bf16[304,128]{1,0:T(8,128)(2,1)S(1)} %shard_map.164.own), channel_id=1, source_target_pairs={{0,2},{1,3},{2,0},{3,1},{4,6},{5,7},{6,4},{7,5},{8,12},{9,13},{10,... | collective-permute-start | bytes 233480 | tf_op jit(solution)/shard_map/ppermute | solution.py:128
  25.9 6.7 %collective-permute-start.4 = (bf16[256,128]{1,0:T(8,128)(2,1)S(1)}, bf16[256,128]{1,0:T(8,128)(2,1)S(1)}, u32[]{:S(2)}, u32[]{:S(2)}) collective-permute-start(bf16[256,128]{1,0:T(8,128)(2,1)S(1)} %get-tuple-element.96), channel_id=1, source_target_pairs={{0,4},{1,5},{2,6},{3,7},{4,0},{5,1},{6,2},{7,3},{8,16},{9,17},{10,... | collective-permute-start | bytes 196616 | tf_op jit(solution)/shard_map/ppermute | solution.py:128
  29.7 2.9 %collective-permute-start.5 = (bf16[256,128]{1,0:T(8,128)(2,1)S(1)}, bf16[256,128]{1,0:T(8,128)(2,1)S(1)}, u32[]{:S(2)}, u32[]{:S(2)}) collective-permute-start(bf16[256,128]{1,0:T(8,128)(2,1)S(1)} %get-tuple-element.97), channel_id=1, source_target_pairs={{0,8},{1,9},{2,10},{3,11},{4,12},{5,13},{6,14},{7,15},{8,0},{9,1},... | collective-permute-start | bytes 196616 | tf_op jit(solution)/shard_map/ppermute | solution.py:128
  31.1 5.9 %collective-permute-start.13 = (bf16[304,128]{1,0:T(8,128)(2,1)S(1)}, bf16[304,128]{1,0:T(8,128)(2,1)S(1)}, u32[]{:S(2)}, u32[]{:S(2)}) collective-permute-start(bf16[304,128]{1,0:T(8,128)(2,1)S(1)} %shard_map.165.own), channel_id=1, source_target_pairs={{0,4},{1,5},{2,6},{3,7},{4,0},{5,1},{6,2},{7,3},{8,10},{9,11},{10,... | collective-permute-start | bytes 233480 | tf_op jit(solution)/shard_map/ppermute | solution.py:128
  32.8 7.8 %collective-permute-start.7 = (bf16[64,128]{1,0:T(8,128)(2,1)S(1)}, bf16[64,128]{1,0:T(8,128)(2,1)S(1)}, u32[]{:S(2)}, u32[]{:S(2)}) collective-permute-start(bf16[64,128]{1,0:T(8,128)(2,1)S(1)} %shard_map.160), channel_id=1, source_target_pairs={{0,1},{1,0},{2,3},{3,2},{4,5},{5,4},{6,7},{7,6},{8,9},{9,8},{10,11... | collective-permute-start | bytes 49160 | tf_op jit(solution)/shard_map/ppermute | solution.py:128
  34.4 6.4 %collective-permute-start.6 = (bf16[64,128]{1,0:T(8,128)(2,1)S(1)}, bf16[64,128]{1,0:T(8,128)(2,1)S(1)}, u32[]{:S(2)}, u32[]{:S(2)}) collective-permute-start(bf16[64,128]{1,0:T(8,128)(2,1)S(1)} %shard_map.160), channel_id=1, source_target_pairs={{0,7},{1,2},{2,1},{3,4},{4,3},{5,6},{6,5},{7,0},{8,15},{9,10},{10,... | collective-permute-start | bytes 49160 | tf_op jit(solution)/shard_map/ppermute | solution.py:128
  37.0 5.4 %collective-permute-start.16 = (bf16[304,128]{1,0:T(8,128)(2,1)S(1)}, bf16[304,128]{1,0:T(8,128)(2,1)S(1)}, u32[]{:S(2)}, u32[]{:S(2)}) collective-permute-start(bf16[304,128]{1,0:T(8,128)(2,1)S(1)} %shard_map.166.refs_0_), channel_id=1, source_target_pairs={{0,17},{1,16},{2,19},{3,18},{4,21},{5,20},{6,23},{7,22},{8,25},{9,... | collective-permute-start | bytes 233480 | tf_op jit(solution)/shard_map/ppermute | solution.py:128
  37.5 5.5 %collective-permute-start.15 = (bf16[304,128]{1,0:T(8,128)(2,1)S(1)}, bf16[304,128]{1,0:T(8,128)(2,1)S(1)}, u32[]{:S(2)}, u32[]{:S(2)}) collective-permute-start(bf16[304,128]{1,0:T(8,128)(2,1)S(1)} %shard_map.166.refs_0_), channel_id=1, source_target_pairs={{0,16},{1,17},{2,18},{3,19},{4,20},{5,21},{6,22},{7,23},{8,24},{9,... | collective-permute-start | bytes 233480 | tf_op jit(solution)/shard_map/ppermute | solution.py:128
  39.9 4.4 %collective-permute-start.14 = (bf16[304,128]{1,0:T(8,128)(2,1)S(1)}, bf16[304,128]{1,0:T(8,128)(2,1)S(1)}, u32[]{:S(2)}, u32[]{:S(2)}) collective-permute-start(bf16[304,128]{1,0:T(8,128)(2,1)S(1)} %shard_map.166.refs_0_), channel_id=1, source_target_pairs={{0,1},{1,0},{2,3},{3,2},{4,5},{5,4},{6,7},{7,6},{8,9},{9,8},{10,11... | collective-permute-start | bytes 233480 | tf_op jit(solution)/shard_map/ppermute | solution.py:128
  43.1 2.4 %collective-permute-start.17 = (bf16[3,304,128]{2,1,0:T(8,128)(2,1)S(1)}, bf16[3,304,128]{2,1,0:T(8,128)(2,1)S(1)}, u32[]{:S(2)}, u32[]{:S(2)}) collective-permute-start(bf16[3,304,128]{2,1,0:T(8,128)(2,1)S(1)} %shard_map.167.early), channel_id=1, source_target_pairs={{0,8},{1,9},{2,10},{3,11},{4,12},{5,13},{6,14},{7,15},{8,0},{9,1},... | collective-permute-start | bytes 700424 | tf_op jit(solution)/shard_map/ppermute | solution.py:128
  44.3 1.3 %collective-permute-start.18 = (bf16[304,128]{1,0:T(8,128)(2,1)S(1)}, bf16[304,128]{1,0:T(8,128)(2,1)S(1)}, u32[]{:S(2)}, u32[]{:S(2)}) collective-permute-start(bf16[304,128]{1,0:T(8,128)(2,1)S(1)} %collective-permute-done.14.late), channel_id=1, source_target_pairs={{0,8},{1,9},{2,10},{3,11},{4,12},{5,13},{6,14},{7,15},{8,0},{9,1},... | collective-permute-start | bytes 233480 | tf_op jit(solution)/shard_map/ppermute | solution.py:128

commit v9 on v8

--- a/solution.py
+++ b/solution.py
@@ -582,7 +582,7 @@
     rank = place.plane_rank()
     scratch[...] = keep[...] + received[...].astype(F32)
     block = encode(bias[...]).astype(BF16)
-    for step, send in zip(range(place.plane - 1, 0, -1), sends):
+    for step, send in zip([*range(2, place.plane), 1], sends):
         send[0:BIAS_ROWS, :] = block
         at = pl.ds(pl.multiple_of((rank ^ step) * chunk, 8), chunk)
         send[BIAS_ROWS:, :] = scratch[at, :].astype(BF16)
@@ -628,7 +628,7 @@
 
 
 def in_steps(place, early, late):
-    return [early.at[0], late] + [early.at[index] for index in range(1, place.plane - 1)]
+    return [early.at[0], late] + [early.at[index] for index in range(place.plane - 2, 0, -1)]
 
 
 def own_half_kernel(place, late, early, out, bias_out, wide, left):
@@ -946,7 +946,7 @@
 
     block = sds((BIAS_ROWS + place.chunk, channels), BF16)
     token = sds((8, width), F32)
-    steps = range(place.plane - 1, 0, -1)
+    steps = [*range(2, place.plane), 1]
     *sends, keep = call(
         bind(pair_kernel, place),
         (*[block for _ in steps], sds((place.chunk, channels), F32)),
@@ -973,7 +973,7 @@
         part = call(bind(add_kernel, scaling if is_last else 1.0), block)(
             part, permuted(part, place.phase_pairs(phase))
         )
-    received = [permuted(part, place.plane_pairs(step)) for step in steps[::-1]]
+    late, *received = [permuted(part, place.plane_pairs(step)) for step in steps[::-1]]
     grad_inputs, grad_hidden, field_done = call(
         bind(field_halo_kernel, place),
         (
@@ -986,9 +986,8 @@
         moved=2_000_000,
     )(field, turned, pre_outer, pre_inner, pre_outer_columns, pre_inner_columns)
     early = call(join_kernel, sds((place.plane - 1, *block.shape), BF16))(
-        part, *received[1:], field_done
+        part, *received, field_done
     )
-    late = received[0]
     early_other = permuted(early, place.phase_pairs(0))
     late_other = permuted(late, place.phase_pairs(0))
     half = [pltpu.VMEM((place.half_rows, channels), F32)]

time: 46.6 us -> 46.9 us (level)
  starting transfers between devices: 24.9 us -> 26.5 us
  waiting for transfers between devices: 7.74 us -> 6.41 us
    ppermute x19, starting transfers between devices: 24.9 us -> 26.5 us  [permuted(): return lax.ppermute(value, AXES, pairs)]
    ppermute x19, waiting for transfers between devices: 7.74 us -> 6.41 us  [permuted(): return lax.ppermute(value, AXES, pairs)]
  transfers between devices with their start and end apart: 19 -> 19, of which waited for: 11 -> 10; matrix products, arithmetic and copies ran while one was open for 0% -> 0% of each run, Pallas kernels for 21% -> 21%
where the time goes in v9:
time: 46.9 us; the launch traced here: 46.7 us
  starting transfers between devices  26.5 us (57%)
  Pallas kernels  13 us (28%)
  waiting for transfers between devices  6.41 us (14%)
  between operations  0.78 us (2%)
    ppermute x19, starting transfers between devices, permuted(): return lax.ppermute(value, AXES, pairs)  26.5 us
    pallas_call x17, Pallas kernels, run(): pl.pallas_call(kernel, out_shape=out_shape, in_specs=[VMEM] * near + [HBM...  13 us
    ppermute x19, waiting for transfers between devices, permuted(): return lax.ppermute(value, AXES, pairs)  6.41 us
  transfers between devices with their start and end apart: 19, of which 10 were waited for; matrix products, arithmetic and copies ran while one was open for 0% of the time, Pallas kernels for 21%

profile of v9, /device:TPU:0, one launch (start us, length us, event | category | flops | bytes accessed | tf_op | source)
XLA Modules:
  0.0 46.7 jit_solution(11987067820816833889)
XLA Ops:
  0.6 1.0 %shard_map.153 = (bf16[128,128]{1,0:T(8,128)(2,1)S(1)}, bf16[128,128]{1,0:T(8,128)(2,1)S(1)}, f32[1024,128]{1,0:T(8,128)S(1)}) custom-call(bf16[64,8,128]{2,1,0:T(8,128)(2,1)} %below.1, bf16[64,8,128]{2,1,0:T(8,128)(2,1)} %hidden.1), custom_call_target="tpu_custom_call" | custom-call | bytes 524288 | tf_op jit(solution)/shard_map/pallas_call | solution.py:45
  1.7 0.5 %collective-permute-start = (bf16[128,128]{1,0:T(8,128)(2,1)S(1)}, bf16[128,128]{1,0:T(8,128)(2,1)S(1)}, u32[]{:S(2)}, u32[]{:S(2)}) collective-permute-start(bf16[128,128]{1,0:T(8,128)(2,1)S(1)} %get-tuple-element.64), channel_id=1, source_target_pairs={{0,8},{1,9},{2,10},{3,11},{4,12},{5,13},{6,14},{7,15},{8,0},{9,1},... | collective-permute-start | bytes 98312 | tf_op jit(solution)/shard_map/ppermute | solution.py:128
  2.2 3.7 %collective-permute-start.1 = (bf16[128,128]{1,0:T(8,128)(2,1)S(1)}, bf16[128,128]{1,0:T(8,128)(2,1)S(1)}, u32[]{:S(2)}, u32[]{:S(2)}) collective-permute-start(bf16[128,128]{1,0:T(8,128)(2,1)S(1)} %get-tuple-element.65), channel_id=1, source_target_pairs={{0,4},{1,5},{2,6},{3,7},{4,0},{5,1},{6,2},{7,3},{8,16},{9,17},{10,... | collective-permute-start | bytes 98312 | tf_op jit(solution)/shard_map/ppermute | solution.py:128
  5.8 2.2 %shard_map.154 = (bf16[8,128,128]{2,1,0:T(8,128)(2,1)S(1)}, f32[128,128]{1,0:T(8,128)S(1)}, f32[128,128]{1,0:T(8,128)S(1)}, f32[64,128]{1,0:T(8,128)S(1)}, f32[6...) custom-call(f32[1024,128]{1,0:T(8,128)S(1)} %get-tuple-element.62.wi, ...), custom_call_target="tpu_custom_call" | custom-call | bytes 6000000 | tf_op jit(solution)/shard_map/pallas_call | solution.py:45
  8.0 0.0 collective-permute-done.inner_row.inner
  8.0 0.0 collective-permute-done.1.outer_row.outer
  8.0 0.2 shard_map.156
  8.2 1.5 %collective-permute-start.3 = (bf16[32,128]{1,0:T(8,128)(2,1)S(1)}, bf16[32,128]{1,0:T(8,128)(2,1)S(1)}, u32[]{:S(2)}, u32[]{:S(2)}) collective-permute-start(bf16[32,128]{1,0:T(8,128)(2,1)S(1)} %get-tuple-element.82), channel_id=1, source_target_pairs={{0,1},{1,0},{2,3},{3,2},{4,5},{5,4},{6,7},{7,6},{8,9},{9,8},{10,11... | collective-permute-start | bytes 24584 | tf_op jit(solution)/shard_map/ppermute | solution.py:128
  9.8 3.8 %collective-permute-start.2 = (bf16[32,128]{1,0:T(8,128)(2,1)S(1)}, bf16[32,128]{1,0:T(8,128)(2,1)S(1)}, u32[]{:S(2)}, u32[]{:S(2)}) collective-permute-start(bf16[32,128]{1,0:T(8,128)(2,1)S(1)} %get-tuple-element.82), channel_id=1, source_target_pairs={{0,7},{1,2},{2,1},{3,4},{4,3},{5,6},{6,5},{7,0},{8,15},{9,10},{10,... | collective-permute-start | bytes 24584 | tf_op jit(solution)/shard_map/ppermute | solution.py:128
  13.5 2.2 %shard_map.155 = (f32[512,128]{1,0:T(8,128)S(1)}, f32[512,128]{1,0:T(8,128)S(1)}, f32[512,128]{1,0:T(8,128)S(1)}, bf16[256,1024]{1,0:T(8,128)(2,1)S(1)}, bf16[12...) custom-call(bf16[8,128,128]{2,1,0:T(8,128)(2,1)S(1)} %get-tuple-element.63.rows_in, ...), custom_call_target="tpu_custom_call" | custom-call | flops 1207959552 | bytes 6000000 | tf_op jit(solution)/shard_map/pallas_call | solution.py:45
  15.8 0.0 collective-permute-done.3.inner_column
  15.8 0.3 collective-permute-done.2.outer_column
  16.1 0.9 %shard_map.157 = (bf16[1152,128]{1,0:T(8,128)(2,1)S(1)}, bf16[256,128]{1,0:T(8,128)(2,1)S(1)}, f32[256,128]{1,0:T(8,128)S(1)}, bf16[1152,128]{1,0:T(8,128)(2,1)S...) custom-call(bf16[128,128]{1,0:T(8,128)(2,1)S(1)} %get-tuple-element.80.edge, ...), custom_call_target="tpu_custom_call" | custom-call | tf_op jit(solution)/shard_map/pallas_call | solution.py:45
  17.0 0.1 collective-permute-start.8
  17.1 0.3 shard_map.162
  17.3 1.3 %collective-permute-done.8.received = bf16[1152,128]{1,0:T(8,128)(2,1)S(1)} collective-permute-done((bf16[1152,128]{1,0:T(8,128)(2,1)S(1)}, bf16[1152,128]{1,0:T(8,128)(2,1)S(1)}, u32[]{:S(2)}, u32[]{:S(2)}) %collective-permute-start.8) | collective-permute-done | bytes 294944 | tf_op jit(solution)/shard_map/ppermute | solution.py:128
  18.6 0.1 shard_map.163
  18.7 0.1 collective-permute-start.9
  18.8 0.4 collective-permute-start.10
  19.2 3.1 %collective-permute-start.11 = (bf16[304,128]{1,0:T(8,128)(2,1)S(1)}, bf16[304,128]{1,0:T(8,128)(2,1)S(1)}, u32[]{:S(2)}, u32[]{:S(2)}) collective-permute-start(bf16[304,128]{1,0:T(8,128)(2,1)S(1)} %get-tuple-element.110), channel_id=1, source_target_pairs={{0,1},{1,0},{2,3},{3,2},{4,5},{5,4},{6,7},{7,6},{8,9},{9,8},{10,11... | collective-permute-start | bytes 233480 | tf_op jit(solution)/shard_map/ppermute | solution.py:128
  22.3 1.4 %shard_map.158 = (bf16[64,8,128]{2,1,0:T(8,128)(2,1)}, f32[512,128]{1,0:T(8,128)}, f32[512,128]{1,0:T(8,128)}, bf16[256,1024]{1,0:T(8,128)(2,1)S(1)}, bf16[256,1...) custom-call(f32[512,128]{1,0:T(8,128)S(1)} %get-tuple-element.75.hidden, f32[512,128]{1,0:T(8,128)S(1)} %get-tuple-element.76.cell, ...), custom_call_target="tpu_custom_call" | custom-call | bytes 4000000 | tf_op jit(solution)/shard_map/pallas_call | solution.py:45
  23.6 1.1 %shard_map.159 = (f32[1024,128]{1,0:T(8,128)S(1)}, bf16[3,128,768]{2,1,0:T(8,128)(2,1)S(1)}, f32[8,128]{1,0:T(8,128)S(1)}) custom-call(bf16[256,1024]{1,0:T(8,128)(2,1)S(1)} %get-tuple-element.93.pre, bf16[9,256,128]{2,1,0:T(8,128)(2,1)S(1)} %get-tuple-element.68.weights), custom_call_target="tpu_custom_call" | custom-call | flops 603979776 | bytes 3000000 | tf_op jit(solution)/shard_map/pallas_call | solution.py:45
  24.8 0.0 collective-permute-done.9.refs_0_
  24.8 1.0 %collective-permute-done.11.refs_2_ = bf16[304,128]{1,0:T(8,128)(2,1)S(1)} collective-permute-done((bf16[304,128]{1,0:T(8,128)(2,1)S(1)}, bf16[304,128]{1,0:T(8,128)(2,1)S(1)}, u32[]{:S(2)}, u32[]{:S(2)}) %collective-permute-start.11) | collective-permute-done | bytes 77856 | tf_op jit(solution)/shard_map/ppermute | solution.py:128
  25.9 0.2 collective-permute-start.12
  26.1 4.4 %collective-permute-start.4 = (bf16[256,128]{1,0:T(8,128)(2,1)S(1)}, bf16[256,128]{1,0:T(8,128)(2,1)S(1)}, u32[]{:S(2)}, u32[]{:S(2)}) collective-permute-start(bf16[256,128]{1,0:T(8,128)(2,1)S(1)} %get-tuple-element.96), channel_id=1, source_target_pairs={{0,4},{1,5},{2,6},{3,7},{4,0},{5,1},{6,2},{7,3},{8,16},{9,17},{10,... | collective-permute-start | bytes 196616 | tf_op jit(solution)/shard_map/ppermute | solution.py:128
  30.5 0.0 collective-permute-start.5
  30.5 0.6 %collective-permute-done.12.received = bf16[304,128]{1,0:T(8,128)(2,1)S(1)} collective-permute-done((bf16[304,128]{1,0:T(8,128)(2,1)S(1)}, bf16[304,128]{1,0:T(8,128)(2,1)S(1)}, u32[]{:S(2)}, u32[]{:S(2)}) %collective-permute-start.12) | collective-permute-done | bytes 77856 | tf_op jit(solution)/shard_map/ppermute | solution.py:128
  31.1 1.8 %collective-permute-start.13 = (bf16[304,128]{1,0:T(8,128)(2,1)S(1)}, bf16[304,128]{1,0:T(8,128)(2,1)S(1)}, u32[]{:S(2)}, u32[]{:S(2)}) collective-permute-start(bf16[304,128]{1,0:T(8,128)(2,1)S(1)} %shard_map.165.own), channel_id=1, source_target_pairs={{0,4},{1,5},{2,6},{3,7},{4,0},{5,1},{6,2},{7,3},{8,10},{9,11},{10,... | collective-permute-start | bytes 233480 | tf_op jit(solution)/shard_map/ppermute | solution.py:128
  33.0 0.5 %collective-permute-done.4.outer.outer_row = bf16[256,128]{1,0:T(8,128)(2,1)S(1)} collective-permute-done((bf16[256,128]{1,0:T(8,128)(2,1)S(1)}, bf16[256,128]{1,0:T(8,128)(2,1)S(1)}, u32[]{:S(2)}, u32[]{:S(2)}) %collective-permute-start.4) | collective-permute-done | bytes 65568 | tf_op jit(solution)/shard_map/ppermute | solution.py:128
  33.4 0.0 collective-permute-done.5.inner.inner_row
  33.4 0.2 shard_map.160
  33.6 1.0 %collective-permute-start.7 = (bf16[64,128]{1,0:T(8,128)(2,1)S(1)}, bf16[64,128]{1,0:T(8,128)(2,1)S(1)}, u32[]{:S(2)}, u32[]{:S(2)}) collective-permute-start(bf16[64,128]{1,0:T(8,128)(2,1)S(1)} %shard_map.160), channel_id=1, source_target_pairs={{0,1},{1,0},{2,3},{3,2},{4,5},{5,4},{6,7},{7,6},{8,9},{9,8},{10,11... | collective-permute-start | bytes 49160 | tf_op jit(solution)/shard_map/ppermute | solution.py:128
  34.7 2.3 %collective-permute-start.6 = (bf16[64,128]{1,0:T(8,128)(2,1)S(1)}, bf16[64,128]{1,0:T(8,128)(2,1)S(1)}, u32[]{:S(2)}, u32[]{:S(2)}) collective-permute-start(bf16[64,128]{1,0:T(8,128)(2,1)S(1)} %shard_map.160), channel_id=1, source_target_pairs={{0,7},{1,2},{2,1},{3,4},{4,3},{5,6},{6,5},{7,0},{8,15},{9,10},{10,... | collective-permute-start | bytes 49160 | tf_op jit(solution)/shard_map/ppermute | solution.py:128
  37.0 0.5 %collective-permute-done.13.received = bf16[304,128]{1,0:T(8,128)(2,1)S(1)} collective-permute-done((bf16[304,128]{1,0:T(8,128)(2,1)S(1)}, bf16[304,128]{1,0:T(8,128)(2,1)S(1)}, u32[]{:S(2)}, u32[]{:S(2)}) %collective-permute-start.13) | collective-permute-done | bytes 77856 | tf_op jit(solution)/shard_map/ppermute | solution.py:128
  37.5 0.5 %collective-permute-start.16 = (bf16[304,128]{1,0:T(8,128)(2,1)S(1)}, bf16[304,128]{1,0:T(8,128)(2,1)S(1)}, u32[]{:S(2)}, u32[]{:S(2)}) collective-permute-start(bf16[304,128]{1,0:T(8,128)(2,1)S(1)} %shard_map.166.refs_0_), channel_id=1, source_target_pairs={{0,16},{1,17},{2,18},{3,19},{4,20},{5,21},{6,22},{7,23},{8,24},{9,... | collective-permute-start | bytes 233480 | tf_op jit(solution)/shard_map/ppermute | solution.py:128
  38.1 2.0 %collective-permute-start.15 = (bf16[304,128]{1,0:T(8,128)(2,1)S(1)}, bf16[304,128]{1,0:T(8,128)(2,1)S(1)}, u32[]{:S(2)}, u32[]{:S(2)}) collective-permute-start(bf16[304,128]{1,0:T(8,128)(2,1)S(1)} %shard_map.166.refs_0_), channel_id=1, source_target_pairs={{0,17},{1,16},{2,19},{3,18},{4,21},{5,20},{6,23},{7,22},{8,25},{9,... | collective-permute-start | bytes 233480 | tf_op jit(solution)/shard_map/ppermute | solution.py:128
  40.1 1.0 %collective-permute-start.14 = (bf16[304,128]{1,0:T(8,128)(2,1)S(1)}, bf16[304,128]{1,0:T(8,128)(2,1)S(1)}, u32[]{:S(2)}, u32[]{:S(2)}) collective-permute-start(bf16[304,128]{1,0:T(8,128)(2,1)S(1)} %shard_map.166.refs_0_), channel_id=1, source_target_pairs={{0,1},{1,0},{2,3},{3,2},{4,5},{5,4},{6,7},{7,6},{8,9},{9,8},{10,11... | collective-permute-start | bytes 233480 | tf_op jit(solution)/shard_map/ppermute | solution.py:128
  41.1 0.1 collective-permute-done.6.outer_column
  41.2 1.6 %shard_map.161 = (bf16[64,8,128]{2,1,0:T(8,128)(2,1)}, bf16[64,8,128]{2,1,0:T(8,128)(2,1)}, f32[8,128]{1,0:T(8,128)S(1)}) custom-call(f32[1024,128]{1,0:T(8,128)S(1)} %get-tuple-element.94.wide, bf16[3,128,768]{2,1,0:T(8,128)(2,1)S(1)} %get-tuple-element.95.turned, bf16[256,128]{1,0:T(8,128)(2,1)S(1)} %collective-permute-done.4.outer.outer_row, ...), custom_call_target="tpu_custom_call" | custom-call | flops 12079595520 | bytes 2000000 | tf_op jit(solution)/shard_map/pallas_call | solution.py:45
  42.8 0.0 collective-permute-done.16.refs_2_
  42.8 0.6 %collective-permute-done.15.refs_1_ = bf16[304,128]{1,0:T(8,128)(2,1)S(1)} collective-permute-done((bf16[304,128]{1,0:T(8,128)(2,1)S(1)}, bf16[304,128]{1,0:T(8,128)(2,1)S(1)}, u32[]{:S(2)}, u32[]{:S(2)}) %collective-permute-start.15) | collective-permute-done | bytes 77856 | tf_op jit(solution)/shard_map/ppermute | solution.py:128
  43.4 0.1 collective-permute-start.17
  43.5 1.1 %collective-permute-done.14.late = bf16[304,128]{1,0:T(8,128)(2,1)S(1)} collective-permute-done((bf16[304,128]{1,0:T(8,128)(2,1)S(1)}, bf16[304,128]{1,0:T(8,128)(2,1)S(1)}, u32[]{:S(2)}, u32[]{:S(2)}) %collective-permute-start.14) | collective-permute-done | bytes 77856 | tf_op jit(solution)/shard_map/ppermute | solution.py:128
  44.5 0.9 %shard_map.168 = (f32[9,256,128]{2,1,0:T(8,128)}, f32[8,128]{1,0:T(8,128)S(1)}) custom-call(bf16[304,128]{1,0:T(8,128)(2,1)S(1)} %collective-permute-done.14.late, bf16[3,304,128]{2,1,0:T(8,128)(2,1)S(1)} %shard_map.167.early), custom_call_target="tpu_custom_call" | custom-call | flops 12079595520 | bytes 884736 | tf_op jit(solution)/shard_map/pallas_call | solution.py:45
  45.5 0.3 collective-permute-done.18.late
  45.8 0.0 collective-permute-done.17.early
  45.8 0.9 %shard_map.169 = (f32[9,256,128]{2,1,0:T(8,128)}, f32[256]{0:T(256)}) custom-call(f32[8,128]{1,0:T(8,128)S(1)} %get-tuple-element.113.bias_own, bf16[3,304,128]{2,1,0:T(8,128)(2,1)S(1)} %collective-permute-done.17.early, bf16[304,128]{1,0:T(8,128)(2,1)S(1)} %collective-permute-done.18.late, ...), custom_call_target="tpu_custom_call", output_to_operand_aliasing={{0}: (4, {})} | custom-call | bytes 884736 | tf_op jit(solution)/shard_map/pallas_call | solution.py:45
  (7 shorter events, 0.1 us)
Async XLA Ops:
  1.7 6.4 %collective-permute-start = (bf16[128,128]{1,0:T(8,128)(2,1)S(1)}, bf16[128,128]{1,0:T(8,128)(2,1)S(1)}, u32[]{:S(2)}, u32[]{:S(2)}) collective-permute-start(bf16[128,128]{1,0:T(8,128)(2,1)S(1)} %get-tuple-element.64), channel_id=1, source_target_pairs={{0,8},{1,9},{2,10},{3,11},{4,12},{5,13},{6,14},{7,15},{8,0},{9,1},... | collective-permute-start | bytes 98312 | tf_op jit(solution)/shard_map/ppermute | solution.py:128
  2.2 5.9 %collective-permute-start.1 = (bf16[128,128]{1,0:T(8,128)(2,1)S(1)}, bf16[128,128]{1,0:T(8,128)(2,1)S(1)}, u32[]{:S(2)}, u32[]{:S(2)}) collective-permute-start(bf16[128,128]{1,0:T(8,128)(2,1)S(1)} %get-tuple-element.65), channel_id=1, source_target_pairs={{0,4},{1,5},{2,6},{3,7},{4,0},{5,1},{6,2},{7,3},{8,16},{9,17},{10,... | collective-permute-start | bytes 98312 | tf_op jit(solution)/shard_map/ppermute | solution.py:128
  8.2 7.6 %collective-permute-start.3 = (bf16[32,128]{1,0:T(8,128)(2,1)S(1)}, bf16[32,128]{1,0:T(8,128)(2,1)S(1)}, u32[]{:S(2)}, u32[]{:S(2)}) collective-permute-start(bf16[32,128]{1,0:T(8,128)(2,1)S(1)} %get-tuple-element.82), channel_id=1, source_target_pairs={{0,1},{1,0},{2,3},{3,2},{4,5},{5,4},{6,7},{7,6},{8,9},{9,8},{10,11... | collective-permute-start | bytes 24584 | tf_op jit(solution)/shard_map/ppermute | solution.py:128
  9.8 6.3 %collective-permute-start.2 = (bf16[32,128]{1,0:T(8,128)(2,1)S(1)}, bf16[32,128]{1,0:T(8,128)(2,1)S(1)}, u32[]{:S(2)}, u32[]{:S(2)}) collective-permute-start(bf16[32,128]{1,0:T(8,128)(2,1)S(1)} %get-tuple-element.82), channel_id=1, source_target_pairs={{0,7},{1,2},{2,1},{3,4},{4,3},{5,6},{6,5},{7,0},{8,15},{9,10},{10,... | collective-permute-start | bytes 24584 | tf_op jit(solution)/shard_map/ppermute | solution.py:128
  17.0 1.6 %collective-permute-start.8 = (bf16[1152,128]{1,0:T(8,128)(2,1)S(1)}, bf16[1152,128]{1,0:T(8,128)(2,1)S(1)}, u32[]{:S(2)}, u32[]{:S(2)}) collective-permute-start(bf16[1152,128]{1,0:T(8,128)(2,1)S(1)} %get-tuple-element.106), channel_id=1, source_target_pairs={{0,8},{1,9},{2,10},{3,11},{4,12},{5,13},{6,14},{7,15},{8,0},{9,1},... | collective-permute-start | bytes 884744 | tf_op jit(solution)/shard_map/ppermute | solution.py:128
  18.7 6.1 %collective-permute-start.9 = (bf16[304,128]{1,0:T(8,128)(2,1)S(1)}, bf16[304,128]{1,0:T(8,128)(2,1)S(1)}, u32[]{:S(2)}, u32[]{:S(2)}) collective-permute-start(bf16[304,128]{1,0:T(8,128)(2,1)S(1)} %get-tuple-element.108), channel_id=1, source_target_pairs={{0,16},{1,17},{2,18},{3,19},{4,20},{5,21},{6,22},{7,23},{8,24},{9,... | collective-permute-start | bytes 233480 | tf_op jit(solution)/shard_map/ppermute | solution.py:128
  18.8 6.0 %collective-permute-start.10 = (bf16[304,128]{1,0:T(8,128)(2,1)S(1)}, bf16[304,128]{1,0:T(8,128)(2,1)S(1)}, u32[]{:S(2)}, u32[]{:S(2)}) collective-permute-start(bf16[304,128]{1,0:T(8,128)(2,1)S(1)} %get-tuple-element.109), channel_id=1, source_target_pairs={{0,17},{1,16},{2,19},{3,18},{4,21},{5,20},{6,23},{7,22},{8,25},{9,... | collective-permute-start | bytes 233480 | tf_op jit(solution)/shard_map/ppermute | solution.py:128
  19.2 6.6 %collective-permute-start.11 = (bf16[304,128]{1,0:T(8,128)(2,1)S(1)}, bf16[304,128]{1,0:T(8,128)(2,1)S(1)}, u32[]{:S(2)}, u32[]{:S(2)}) collective-permute-start(bf16[304,128]{1,0:T(8,128)(2,1)S(1)} %get-tuple-element.110), channel_id=1, source_target_pairs={{0,1},{1,0},{2,3},{3,2},{4,5},{5,4},{6,7},{7,6},{8,9},{9,8},{10,11... | collective-permute-start | bytes 233480 | tf_op jit(solution)/shard_map/ppermute | solution.py:128
  25.9 5.2 %collective-permute-start.12 = (bf16[304,128]{1,0:T(8,128)(2,1)S(1)}, bf16[304,128]{1,0:T(8,128)(2,1)S(1)}, u32[]{:S(2)}, u32[]{:S(2)}) collective-permute-start(bf16[304,128]{1,0:T(8,128)(2,1)S(1)} %shard_map.164.own), channel_id=1, source_target_pairs={{0,2},{1,3},{2,0},{3,1},{4,6},{5,7},{6,4},{7,5},{8,12},{9,13},{10,... | collective-permute-start | bytes 233480 | tf_op jit(solution)/shard_map/ppermute | solution.py:128
  26.1 7.3 %collective-permute-start.4 = (bf16[256,128]{1,0:T(8,128)(2,1)S(1)}, bf16[256,128]{1,0:T(8,128)(2,1)S(1)}, u32[]{:S(2)}, u32[]{:S(2)}) collective-permute-start(bf16[256,128]{1,0:T(8,128)(2,1)S(1)} %get-tuple-element.96), channel_id=1, source_target_pairs={{0,4},{1,5},{2,6},{3,7},{4,0},{5,1},{6,2},{7,3},{8,16},{9,17},{10,... | collective-permute-start | bytes 196616 | tf_op jit(solution)/shard_map/ppermute | solution.py:128
  30.5 2.9 %collective-permute-start.5 = (bf16[256,128]{1,0:T(8,128)(2,1)S(1)}, bf16[256,128]{1,0:T(8,128)(2,1)S(1)}, u32[]{:S(2)}, u32[]{:S(2)}) collective-permute-start(bf16[256,128]{1,0:T(8,128)(2,1)S(1)} %get-tuple-element.97), channel_id=1, source_target_pairs={{0,8},{1,9},{2,10},{3,11},{4,12},{5,13},{6,14},{7,15},{8,0},{9,1},... | collective-permute-start | bytes 196616 | tf_op jit(solution)/shard_map/ppermute | solution.py:128
  31.1 6.3 %collective-permute-start.13 = (bf16[304,128]{1,0:T(8,128)(2,1)S(1)}, bf16[304,128]{1,0:T(8,128)(2,1)S(1)}, u32[]{:S(2)}, u32[]{:S(2)}) collective-permute-start(bf16[304,128]{1,0:T(8,128)(2,1)S(1)} %shard_map.165.own), channel_id=1, source_target_pairs={{0,4},{1,5},{2,6},{3,7},{4,0},{5,1},{6,2},{7,3},{8,10},{9,11},{10,... | collective-permute-start | bytes 233480 | tf_op jit(solution)/shard_map/ppermute | solution.py:128
  33.6 7.5 %collective-permute-start.7 = (bf16[64,128]{1,0:T(8,128)(2,1)S(1)}, bf16[64,128]{1,0:T(8,128)(2,1)S(1)}, u32[]{:S(2)}, u32[]{:S(2)}) collective-permute-start(bf16[64,128]{1,0:T(8,128)(2,1)S(1)} %shard_map.160), channel_id=1, source_target_pairs={{0,1},{1,0},{2,3},{3,2},{4,5},{5,4},{6,7},{7,6},{8,9},{9,8},{10,11... | collective-permute-start | bytes 49160 | tf_op jit(solution)/shard_map/ppermute | solution.py:128
  34.7 6.5 %collective-permute-start.6 = (bf16[64,128]{1,0:T(8,128)(2,1)S(1)}, bf16[64,128]{1,0:T(8,128)(2,1)S(1)}, u32[]{:S(2)}, u32[]{:S(2)}) collective-permute-start(bf16[64,128]{1,0:T(8,128)(2,1)S(1)} %shard_map.160), channel_id=1, source_target_pairs={{0,7},{1,2},{2,1},{3,4},{4,3},{5,6},{6,5},{7,0},{8,15},{9,10},{10,... | collective-permute-start | bytes 49160 | tf_op jit(solution)/shard_map/ppermute | solution.py:128
  37.5 5.2 %collective-permute-start.16 = (bf16[304,128]{1,0:T(8,128)(2,1)S(1)}, bf16[304,128]{1,0:T(8,128)(2,1)S(1)}, u32[]{:S(2)}, u32[]{:S(2)}) collective-permute-start(bf16[304,128]{1,0:T(8,128)(2,1)S(1)} %shard_map.166.refs_0_), channel_id=1, source_target_pairs={{0,16},{1,17},{2,18},{3,19},{4,20},{5,21},{6,22},{7,23},{8,24},{9,... | collective-permute-start | bytes 233480 | tf_op jit(solution)/shard_map/ppermute | solution.py:128
  38.1 5.3 %collective-permute-start.15 = (bf16[304,128]{1,0:T(8,128)(2,1)S(1)}, bf16[304,128]{1,0:T(8,128)(2,1)S(1)}, u32[]{:S(2)}, u32[]{:S(2)}) collective-permute-start(bf16[304,128]{1,0:T(8,128)(2,1)S(1)} %shard_map.166.refs_0_), channel_id=1, source_target_pairs={{0,17},{1,16},{2,19},{3,18},{4,21},{5,20},{6,23},{7,22},{8,25},{9,... | collective-permute-start | bytes 233480 | tf_op jit(solution)/shard_map/ppermute | solution.py:128
  40.1 4.4 %collective-permute-start.14 = (bf16[304,128]{1,0:T(8,128)(2,1)S(1)}, bf16[304,128]{1,0:T(8,128)(2,1)S(1)}, u32[]{:S(2)}, u32[]{:S(2)}) collective-permute-start(bf16[304,128]{1,0:T(8,128)(2,1)S(1)} %shard_map.166.refs_0_), channel_id=1, source_target_pairs={{0,1},{1,0},{2,3},{3,2},{4,5},{5,4},{6,7},{7,6},{8,9},{9,8},{10,11... | collective-permute-start | bytes 233480 | tf_op jit(solution)/shard_map/ppermute | solution.py:128
  43.4 2.4 %collective-permute-start.17 = (bf16[3,304,128]{2,1,0:T(8,128)(2,1)S(1)}, bf16[3,304,128]{2,1,0:T(8,128)(2,1)S(1)}, u32[]{:S(2)}, u32[]{:S(2)}) collective-permute-start(bf16[3,304,128]{2,1,0:T(8,128)(2,1)S(1)} %shard_map.167.early), channel_id=1, source_target_pairs={{0,8},{1,9},{2,10},{3,11},{4,12},{5,13},{6,14},{7,15},{8,0},{9,1},... | collective-permute-start | bytes 700424 | tf_op jit(solution)/shard_map/ppermute | solution.py:128
  44.5 1.3 %collective-permute-start.18 = (bf16[304,128]{1,0:T(8,128)(2,1)S(1)}, bf16[304,128]{1,0:T(8,128)(2,1)S(1)}, u32[]{:S(2)}, u32[]{:S(2)}) collective-permute-start(bf16[304,128]{1,0:T(8,128)(2,1)S(1)} %collective-permute-done.14.late), channel_id=1, source_target_pairs={{0,8},{1,9},{2,10},{3,11},{4,12},{5,13},{6,14},{7,15},{8,0},{9,1},... | collective-permute-start | bytes 233480 | tf_op jit(solution)/shard_map/ppermute | solution.py:128

commit v10 on v8

--- a/solution.py
+++ b/solution.py
@@ -143,12 +143,6 @@
     return jnp.where(lane == LAST + position, rolled(row, LAST + position + 1), columns)
 
 
-def second_columns(row, position, columns):
-    lane = lanes(row.shape)
-    columns = jnp.where(lane == position, rolled(row, position - 1), columns)
-    return jnp.where(lane == LAST + position, rolled(row, LAST + position + 2), columns)
-
-
 def at_edges(row, position, columns):
     lane = lanes(row.shape)
     width = row.shape[1]
@@ -166,6 +160,7 @@
 
 def row_sends(first, last, inner_out, outer_out):
     odd = is_odd("core")
+    first, last = first.astype(F32), last.astype(F32)
     inner_out[...] = pick(odd, first, last).astype(BF16)
     outer_out[...] = pick(odd, last, first).astype(BF16)
 
@@ -197,7 +192,7 @@
     return unpacked(pick(odd, inner, outer), groups), unpacked(pick(odd, outer, inner), groups)
 
 
-def pack_kernel(below, hidden, inner_out, outer_out, wide_out, below_here, hidden_here, arrived):
+def pack_kernel(below, hidden, columns_out, wide_out, below_here, hidden_here, arrived):
     first = pltpu.make_async_copy(below, below_here, arrived.at[0])
     second = pltpu.make_async_copy(hidden, hidden_here, arrived.at[1])
     first.start()
@@ -208,9 +203,23 @@
     wide_out[0:size, :] = below_here[...].astype(F32).reshape(size, width)
     second.wait()
     wide_out[size : 2 * size, :] = hidden_here[...].astype(F32).reshape(size, width)
-    edges = [
-        wide_out[pl.ds(index, 2 * channels, stride=row_count), :] for index in (0, row_count - 1)
-    ]
+    columns = jnp.zeros((2 * channels, width), F32)
+    for index in range(row_count):
+        row = wide_out[pl.ds(index, 2 * channels, stride=row_count), :]
+        columns = edge_columns(row, index + 1, columns)
+    columns_out[...] = packed(columns, GROUPS).astype(BF16)
+
+
+def rows_kernel(row_count, wide, inner_column, outer_column, inner_out, outer_out):
+    west, east = column_halo(inner_column, outer_column, GROUPS)
+    channels = west.shape[0]
+    lane = lanes(west.shape)
+    edges = []
+    for index in (0, row_count - 1):
+        row = wide[pl.ds(index, channels, stride=row_count), :]
+        ends = jnp.where(lane == 0, rolled(west, -LAST - index - 1), 0.0)
+        ends = jnp.where(lane == LAST, rolled(east, LAST - index - 1), ends)
+        edges.append(jnp.concatenate([row, packed(ends, GROUPS)], axis=0))
     row_sends(edges[0], edges[1], inner_out, outer_out)
 
 
@@ -230,11 +239,6 @@
     gate_bias_hbm,
     readout_hbm,
     rows_out,
-    columns_out,
-    second_out,
-    cell_strip_out,
-    hidden_grad_strip_out,
-    fields_strip_out,
     cell_out,
     weights_out,
     hidden_grad_out,
@@ -266,44 +270,20 @@
     for copy in copies:
         copy.start()
     row_count, channels, width = rows_out.shape
-    columns = jnp.zeros((channels, width), F32)
-    second = jnp.zeros((channels, width), F32)
     for index in range(row_count):
-        row = wide[pl.ds(index, channels, stride=row_count), :]
-        rows_out[index] = row.astype(BF16)
-        columns = edge_columns(row, index + 1, columns)
-        second = second_columns(row, index + 1, second)
-    columns_out[...] = columns
-    second_out[...] = second
+        rows_out[index] = wide[pl.ds(index, channels, stride=row_count), :].astype(BF16)
     for copy in copies:
         copy.wait()
     hidden_grad_out[...] = hidden_grad_here[...].astype(F32).reshape(hidden_grad_out.shape)
     bias_wide_out[...] = down_rows(gate_bias_here[...], width)
     readout_wide_out[...] = down_rows(readout_here[...], width)
-    hid = hidden_grad_here.shape[0]
-    cell_strip = jnp.zeros((hid, width), F32)
-    hidden_grad_strip = jnp.zeros((hid, width), F32)
-    fields_strip = jnp.zeros((8, width), F32)
-    for index in range(row_count):
-        strided = pl.ds(index, hid, stride=row_count)
-        cell_strip = edge_columns(cell_out[strided, :], index + 1, cell_strip)
-        hidden_grad_strip = edge_columns(hidden_grad_out[strided, :], index + 1, hidden_grad_strip)
-        at = slice(index, index + 1)
-        fields = [target_out[at, :], land_out[at, :].astype(F32), fire_out[at, :].astype(F32)]
-        fields = jnp.concatenate(fields + [jnp.zeros((5, width), F32)], axis=0)
-        fields_strip = edge_columns(fields, index + 1, fields_strip)
-    cell_strip_out[...] = cell_strip
-    hidden_grad_strip_out[...] = hidden_grad_strip
-    fields_strip_out[...] = fields_strip
-
-
-def columns_kernel(row_count, groups, columns, outer, inner, packed_out, *whole_out):
+
+
+def columns_kernel(row_count, groups, columns, outer, inner, packed_out):
     north, south = row_halo(inner, outer)
     value = edge_columns(north, 0, columns[...].astype(F32))
     value = edge_columns(south, row_count + 1, value)
     packed_out[...] = packed(value, groups).astype(BF16)
-    for out in whole_out:
-        out[...] = value.astype(BF16)
 
 
 def encode(bias):
@@ -339,12 +319,24 @@
     return hidden_next, cell_next, cell_grad * forget_gate, pre_grad
 
 
+def beside(row, left, right):
+    lane = lanes(row.shape)
+    width = row.shape[1]
+    return jnp.concatenate(
+        [
+            jnp.where(lane == 0, left, rolled(row, 1)),
+            row,
+            jnp.where(lane == width - 1, right, rolled(row, -1)),
+        ],
+        axis=0,
+    ).astype(BF16)
+
+
 def gates_kernel(
     place,
     rows_in,
-    inner_row,
-    outer_row,
-    second,
+    outer_column,
+    inner_column,
     cell_prev,
     weights,
     hidden_grad,
@@ -357,40 +349,30 @@
     cell_out,
     grad_cell_out,
     pre_out,
-    second_out,
+    shifted,
     sums,
     bias_out,
-    shifted,
 ):
     row_count, channels, width = rows_in.shape
     gate_count = weights.shape[1]
     hid = gate_count // 4
     half_gates = place.half_gates
-    north, south = row_halo(inner_row, outer_row)
-    columns = second_columns(north, 0, second[...])
-    second_out[...] = second_columns(south, row_count + 1, columns).astype(BF16)
-    for position in range(row_count + 2):
-        if position == 0:
-            row = north
-        elif position == row_count + 1:
-            row = south
-        else:
-            row = rows_in[position - 1].astype(F32)
-        at = pl.ds(position * width, width)
-        shifted[0:channels, at] = rolled(row, 1).astype(BF16)
-        shifted[channels : 2 * channels, at] = row.astype(BF16)
-        shifted[2 * channels : 3 * channels, at] = rolled(row, -1).astype(BF16)
+    west, east = column_halo(inner_column, outer_column, GROUPS)
+    for index in range(row_count):
+        shifted[:, pl.ds((index + 1) * width, width)] = beside(
+            rows_in[index].astype(F32),
+            rolled(west, -LAST - index - 1),
+            rolled(east, width - 2 - index),
+        )
 
     taps = [
         jnp.concatenate([weights[3 * a], weights[3 * a + 1], weights[3 * a + 2]], axis=1)
         for a in range(3)
     ]
     bias_total = jnp.zeros((gate_count, width), F32)
-    lane = lanes((gate_count, width))
-    inside = (lane > 0) & (lane < width - 1)
     readout = readout_wide[...]
     pair = 2 if row_count % 2 == 0 else 1
-    for base in range(0, row_count, pair):
+    for base in range(1, row_count - 1, pair):
         preact = jnp.zeros((gate_count, pair * width), F32)
         for a in range(3):
             preact += jnp.dot(
@@ -414,15 +396,14 @@
             hidden_out[strided, :] = hidden_next
             cell_out[strided, :] = cell_next
             grad_cell_out[strided, :] = grad_cell
-            pre_grad = jnp.where(inside, pre_grad, 0.0)
             bias_total += pre_grad
             pre_out[:, pl.ds(index * width, width)] = pre_grad.astype(BF16)
     bias_out[...] = bias_total
 
     for a in range(3):
         product = lax.dot_general(
-            pre_out[...],
-            shifted[:, pl.ds(a * width, row_count * width)],
+            pre_out[:, pl.ds(width, (row_count - 2) * width)],
+            shifted[:, pl.ds((a + 1) * width, (row_count - 2) * width)],
             ACROSS,
             preferred_element_type=F32,
         )
@@ -459,16 +440,17 @@
 def strip_kernel(
     place,
     row_count,
-    edge,
-    second,
-    outer_column,
-    inner_column,
+    outer_row,
+    inner_row,
+    shifted,
     weights,
     bias_wide,
     readout_wide,
-    cell_strip,
-    hidden_grad_strip,
-    fields_strip,
+    cell_prev,
+    hidden_grad,
+    target,
+    land,
+    fire,
     sums,
     send_out,
     pre_out,
@@ -478,36 +460,49 @@
     cell_out,
     grad_cell_out,
 ):
-    channels, width = edge.shape
-    west, east = column_halo(inner_column, outer_column, GROUPS)
-    near_first = lanes((channels, width)) < LAST
-    inner = second[...].astype(F32)
-    columns = (
-        jnp.where(near_first, rolled(west, -LAST), inner),
-        edge[...].astype(F32),
-        jnp.where(near_first, inner, rolled(east, LAST)),
-    )
+    channels = weights.shape[2]
+    hid, width = readout_wide.shape
+    block = 3 * channels
+    halo = []
+    for value in row_halo(inner_row, outer_row):
+        ends = unpacked(value[channels:], GROUPS)
+        halo.append(beside(value[0:channels], ends, rolled(ends, width - 1 - LAST)))
     for a in range(3):
-        for b in range(3):
-            at = (3 * a + b) * channels
-            patches[at : at + channels, :] = rolled(columns[b], 1 - a).astype(BF16)
+        at = slice(a * block, (a + 1) * block)
+        north = a == 0
+        south = a == 2
+        patches[at, 0:width] = halo[0] if north else shifted[:, a * width : (a + 1) * width]
+        from_row = (row_count - 1 + a) * width
+        patches[at, width : 2 * width] = (
+            halo[1] if south else shifted[:, from_row : from_row + width]
+        )
     taps = jnp.concatenate([weights[tap] for tap in range(place.taps)], axis=1)
-    preact = jnp.dot(taps, patches[...], preferred_element_type=F32) + bias_wide[...]
+    preact = jnp.dot(taps, patches[...], preferred_element_type=F32)
+
+    def both(value):
+        return jnp.concatenate([value, value], axis=1)
+
+    def edges(ref):
+        return jnp.concatenate(
+            [ref[pl.ds(index, hid, stride=row_count), :] for index in (0, row_count - 1)], axis=1
+        )
+
+    def edge_fields(ref):
+        rows = [ref[index : index + 1, :].astype(F32) for index in (0, row_count - 1)]
+        return jnp.concatenate(rows, axis=1)
+
     hidden_next, cell_next, grad_cell, pre_grad = cell_step(
-        preact,
-        cell_strip[...],
-        hidden_grad_strip[...],
-        fields_strip[0:1, :],
-        fields_strip[1:2, :],
-        fields_strip[2:3, :],
-        readout_wide[...],
+        preact + both(bias_wide[...]),
+        edges(cell_prev),
+        edges(hidden_grad),
+        edge_fields(target),
+        edge_fields(land),
+        edge_fields(fire),
+        both(readout_wide[...]),
     )
     hidden_out[...] = hidden_next
     cell_out[...] = cell_next
     grad_cell_out[...] = grad_cell
-    lane = lanes(pre_grad.shape)
-    lane = jnp.where(lane >= LAST, lane - LAST, lane)
-    pre_grad = jnp.where((lane >= 1) & (lane <= row_count), pre_grad, 0.0)
     pre_out[...] = pre_grad.astype(BF16)
     pre_wide_out[...] = pre_grad
     add_strip(place, 1 - place.rank(0), sums, pre_out, patches, send_out)
@@ -516,7 +511,8 @@
 def keep_kernel(place, sums, pre_strip, patches, bias_partial, pre_wide, out, bias_out):
     add_strip(place, place.rank(0), sums, pre_strip, patches, out)
     channels = sums.shape[1]
-    bias_total = bias_partial[...] + pre_wide[...]
+    width = bias_partial.shape[1]
+    bias_total = bias_partial[...] + pre_wide[:, 0:width] + pre_wide[:, width : 2 * width]
     ones = jnp.ones((8, bias_total.shape[1]), BF16)
     high = bias_total.astype(BF16)
     low = (bias_total - high.astype(F32)).astype(BF16)
@@ -540,6 +536,7 @@
     cell_hbm,
     grad_cell_hbm,
     pre_out,
+    columns_out,
     inner_out,
     outer_out,
     hidden_low,
@@ -549,29 +546,29 @@
     left,
 ):
     hid, _, width = hidden_low.shape
+    halves = ((0, slice(0, width)), (row_count - 1, slice(width, 2 * width)))
     leaving = []
     for source, strip, here, ready, target in (
         (cell, cell_strip, cell_here, cell_here, cell_hbm),
         (grad_cell, grad_cell_strip, grad_cell_here, grad_cell_here, grad_cell_hbm),
         (hidden, hidden_strip, hidden_here, hidden_low, hidden_hbm),
     ):
-        columns = strip[...]
-        for index in range(row_count):
-            strided = pl.ds(index, hid, stride=row_count)
-            here[strided, :] = at_edges(source[strided, :], index + 1, columns)
+        here[...] = source[...]
+        for index, half in halves:
+            here[pl.ds(index, hid, stride=row_count), :] = strip[:, half]
         if ready is hidden_low:
             hidden_low[...] = here[...].reshape(hidden_low.shape).astype(BF16)
         leaving.append(pltpu.make_async_copy(ready, target, left.at[len(leaving)]))
         leaving[-1].start()
-    first, last = None, None
-    columns = pre_strip[...].astype(F32)
+    pre_out[...] = pre[...]
+    for index, half in halves:
+        pre_out[:, pl.ds(index * width, width)] = pre_strip[:, half]
+    row_sends(pre_strip[:, 0:width], pre_strip[:, width : 2 * width], inner_out, outer_out)
+    columns = jnp.zeros(columns_out.shape, F32)
     for index in range(row_count):
-        at = pl.ds(index * width, width)
-        row = at_edges(pre[:, at].astype(F32), index + 1, columns)
-        pre_out[:, at] = row.astype(BF16)
-        first = row if index == 0 else first
-        last = row
-    row_sends(first, last, inner_out, outer_out)
+        row = pre_out[:, pl.ds(index * width, width)].astype(F32)
+        columns = edge_columns(row, index + 1, columns)
+    columns_out[...] = columns.astype(BF16)
     for copy in leaving:
         copy.wait()
 
@@ -785,13 +782,12 @@
     inner_columns = place.pairs(place.inner_columns)
     outer_columns = place.pairs(place.outer_columns)
     flat = sds((hid * row_count, width), F32)
-    strip = sds((hid, width), F32)
-
-    inner, outer, wide = call(
+    strip = sds((hid, 2 * width), F32)
+
+    columns, wide = call(
         pack_kernel,
         (
-            sds((channels, width), BF16),
-            sds((channels, width), BF16),
+            sds((channels // GROUPS, width), BF16),
             sds((channels * row_count, width), F32),
         ),
         [
@@ -802,14 +798,10 @@
         remote=2,
         moved=4 * channels * cells,
     )(inputs_below, hidden_prev)
-    inner, outer = permuted(inner, inner_rows), permuted(outer, outer_rows)
+    inner_column = permuted(columns, inner_columns)
+    outer_column = permuted(columns, outer_columns)
     (
         rows,
-        columns,
-        second,
-        cell_strip,
-        hidden_grad_strip,
-        fields_strip,
         cell_here,
         weights_here,
         hidden_grad_here,
@@ -822,11 +814,6 @@
         prepare_kernel,
         (
             sds((row_count, channels, width), BF16),
-            sds((channels, width), F32),
-            sds((channels, width), F32),
-            strip,
-            strip,
-            sds((8, width), F32),
             flat,
             sds(kernel_weights.shape, BF16),
             flat,
@@ -855,32 +842,29 @@
         gate_bias,
         readout,
     )
-    columns, edge = call(
-        bind(columns_kernel, row_count, GROUPS),
-        (sds((channels // GROUPS, width), BF16), sds((channels, width), BF16)),
-    )(columns, outer, inner)
-    inner_column = permuted(columns, inner_columns)
-    outer_column = permuted(columns, outer_columns)
-    hidden_rows, cell_rows, grad_cell_rows, pre, second, sums, bias = call(
+    edge = sds((channels + channels // GROUPS, width), BF16)
+    inner, outer = call(bind(rows_kernel, row_count), (edge, edge))(
+        wide, inner_column, outer_column
+    )
+    inner, outer = permuted(inner, inner_rows), permuted(outer, outer_rows)
+    hidden_rows, cell_rows, grad_cell_rows, pre, shifted, sums, bias = call(
         bind(gates_kernel, place),
         (
             flat,
             flat,
             flat,
             sds((gate_count, cells), BF16),
-            sds((channels, width), BF16),
+            sds((3 * channels, halo_cells), BF16),
             sds((2 * place.half_rows, channels), F32),
             sds((gate_count, width), F32),
         ),
-        [pltpu.VMEM((3 * channels, halo_cells), BF16)],
         flops=4 * 9 * gate_count * channels * cells,
         moved=6_000_000,
         transcendentals=5 * hid * cells,
     )(
         rows,
-        inner,
-        outer,
-        second,
+        outer_column,
+        inner_column,
         cell_here,
         weights_here,
         hidden_grad_here,
@@ -894,37 +878,39 @@
         bind(strip_kernel, place, row_count),
         (
             sds((place.half_rows, channels), BF16),
-            sds((gate_count, width), BF16),
-            sds((gate_count, width), F32),
-            sds((place.taps * channels, width), BF16),
+            sds((gate_count, 2 * width), BF16),
+            sds((gate_count, 2 * width), F32),
+            sds((place.taps * channels, 2 * width), BF16),
             strip,
             strip,
             strip,
         ),
     )(
-        edge,
-        second,
-        outer_column,
-        inner_column,
+        outer,
+        inner,
+        shifted,
         weights_here,
         bias_wide,
         readout_wide,
-        cell_strip,
-        hidden_grad_strip,
-        fields_strip,
+        cell_here,
+        hidden_grad_here,
+        target_here,
+        land_here,
+        fire_here,
         sums,
     )
     keep, bias = call(
         bind(keep_kernel, place),
         (sds((place.half_rows, channels), F32), sds((8, channels), F32)),
     )(sums, pre_strip, patches, bias, pre_wide)
-    hidden_next, cell_next, grad_cell, pre, pre_inner, pre_outer = call(
+    hidden_next, cell_next, grad_cell, pre, pre_columns, pre_inner, pre_outer = call(
         bind(edges_kernel, row_count),
         (
             sds((hid, row_count, width), BF16),
             flat,
             flat,
             sds((gate_count, cells), BF16),
+            sds((gate_count, width), BF16),
             sds((gate_count, width), BF16),
             sds((gate_count, width), BF16),
         ),
@@ -942,7 +928,7 @@
     pre_columns = call(
         bind(columns_kernel, row_count, PRE_GROUPS),
         (sds((gate_count // PRE_GROUPS, width), BF16),),
-    )(pre_strip, pre_outer, pre_inner)[0]
+    )(pre_columns, pre_outer, pre_inner)[0]
 
     block = sds((BIAS_ROWS + place.chunk, channels), BF16)
     token = sds((8, width), F32)

time: 46.6 us -> 46.9 us (level)
  waiting for transfers between devices: 7.74 us -> 9.78 us
  starting transfers between devices: 24.9 us -> 23.6 us
    ppermute x19, waiting for transfers between devices: 7.74 us -> 9.78 us  [permuted(): return lax.ppermute(value, AXES, pairs)]
    ppermute x19, starting transfers between devices: 24.9 us -> 23.6 us  [permuted(): return lax.ppermute(value, AXES, pairs)]
  transfers between devices with their start and end apart: 19 -> 19, of which waited for: 11 -> 12; matrix products, arithmetic and copies ran while one was open for 0% -> 0% of each run, Pallas kernels for 21% -> 19%
where the time goes in v10:
time: 46.9 us; the launch traced here: 46.8 us
  starting transfers between devices  23.6 us (50%)
  Pallas kernels  12.6 us (27%)
  waiting for transfers between devices  9.78 us (21%)
  between operations  0.76 us (2%)
    ppermute x19, starting transfers between devices, permuted(): return lax.ppermute(value, AXES, pairs)  23.6 us
    pallas_call x17, Pallas kernels, run(): pl.pallas_call(kernel, out_shape=out_shape, in_specs=[VMEM] * near + [HBM...  12.6 us
    ppermute x19, waiting for transfers between devices, permuted(): return lax.ppermute(value, AXES, pairs)  9.78 us
  transfers between devices with their start and end apart: 19, of which 12 were waited for; matrix products, arithmetic and copies ran while one was open for 0% of the time, Pallas kernels for 19%

profile of v10, /device:TPU:0, one launch (start us, length us, event | category | flops | bytes accessed | tf_op | source)
XLA Modules:
  0.0 46.8 jit_solution(5294743887589807983)
XLA Ops:
  0.6 1.3 %shard_map.153 = (bf16[32,128]{1,0:T(8,128)(2,1)S(1)}, f32[1024,128]{1,0:T(8,128)S(1)}) custom-call(bf16[64,8,128]{2,1,0:T(8,128)(2,1)} %below.1, bf16[64,8,128]{2,1,0:T(8,128)(2,1)} %hidden.1), custom_call_target="tpu_custom_call" | custom-call | bytes 524288 | tf_op jit(solution)/shard_map/pallas_call | solution.py:45
  1.9 3.0 %collective-permute-start.1 = (bf16[32,128]{1,0:T(8,128)(2,1)S(1)}, bf16[32,128]{1,0:T(8,128)(2,1)S(1)}, u32[]{:S(2)}, u32[]{:S(2)}) collective-permute-start(bf16[32,128]{1,0:T(8,128)(2,1)S(1)} %get-tuple-element.59), channel_id=1, source_target_pairs={{0,1},{1,0},{2,3},{3,2},{4,5},{5,4},{6,7},{7,6},{8,9},{9,8},{10,11... | collective-permute-start | bytes 24584 | tf_op jit(solution)/shard_map/ppermute | solution.py:128
  5.0 3.5 %collective-permute-start = (bf16[32,128]{1,0:T(8,128)(2,1)S(1)}, bf16[32,128]{1,0:T(8,128)(2,1)S(1)}, u32[]{:S(2)}, u32[]{:S(2)}) collective-permute-start(bf16[32,128]{1,0:T(8,128)(2,1)S(1)} %get-tuple-element.59), channel_id=1, source_target_pairs={{0,7},{1,2},{2,1},{3,4},{4,3},{5,6},{6,5},{7,0},{8,15},{9,10},{10,... | collective-permute-start | bytes 24584 | tf_op jit(solution)/shard_map/ppermute | solution.py:128
  8.5 1.4 %shard_map.154 = (bf16[8,128,128]{2,1,0:T(8,128)(2,1)S(1)}, f32[512,128]{1,0:T(8,128)S(1)}, bf16[9,256,128]{2,1,0:T(8,128)(2,1)S(1)}, f32[512,128]{1,0:T(8,128)S...) custom-call(f32[1024,128]{1,0:T(8,128)S(1)} %get-tuple-element.57.wi, ...), custom_call_target="tpu_custom_call" | custom-call | bytes 6000000 | tf_op jit(solution)/shard_map/pallas_call | solution.py:45
  9.9 0.0 collective-permute-done.1.inner_column
  9.9 1.4 %collective-permute-done.outer_column = bf16[32,128]{1,0:T(8,128)(2,1)S(1)} collective-permute-done((bf16[32,128]{1,0:T(8,128)(2,1)S(1)}, bf16[32,128]{1,0:T(8,128)(2,1)S(1)}, u32[]{:S(2)}, u32[]{:S(2)}) %collective-permute-start) | collective-permute-done | bytes 8224 | tf_op jit(solution)/shard_map/ppermute | solution.py:128
  11.3 0.2 shard_map.156
  11.5 0.9 %collective-permute-start.2 = (bf16[160,128]{1,0:T(8,128)(2,1)S(1)}, bf16[160,128]{1,0:T(8,128)(2,1)S(1)}, u32[]{:S(2)}, u32[]{:S(2)}) collective-permute-start(bf16[160,128]{1,0:T(8,128)(2,1)S(1)} %get-tuple-element.72), channel_id=1, source_target_pairs={{0,4},{1,5},{2,6},{3,7},{4,0},{5,1},{6,2},{7,3},{8,16},{9,17},{10,... | collective-permute-start | bytes 122888 | tf_op jit(solution)/shard_map/ppermute | solution.py:128
  12.4 0.8 %collective-permute-start.3 = (bf16[160,128]{1,0:T(8,128)(2,1)S(1)}, bf16[160,128]{1,0:T(8,128)(2,1)S(1)}, u32[]{:S(2)}, u32[]{:S(2)}) collective-permute-start(bf16[160,128]{1,0:T(8,128)(2,1)S(1)} %get-tuple-element.73), channel_id=1, source_target_pairs={{0,8},{1,9},{2,10},{3,11},{4,12},{5,13},{6,14},{7,15},{8,0},{9,1},... | collective-permute-start | bytes 122888 | tf_op jit(solution)/shard_map/ppermute | solution.py:128
  13.2 2.2 %shard_map.155 = (f32[512,128]{1,0:T(8,128)S(1)}, f32[512,128]{1,0:T(8,128)S(1)}, f32[512,128]{1,0:T(8,128)S(1)}, bf16[256,1024]{1,0:T(8,128)(2,1)S(1)}, bf16[38...) custom-call(bf16[8,128,128]{2,1,0:T(8,128)(2,1)S(1)} %get-tuple-element.58.rows_in, ...), custom_call_target="tpu_custom_call" | custom-call | flops 1207959552 | bytes 6000000 | tf_op jit(solution)/shard_map/pallas_call | solution.py:45
  15.4 1.1 %collective-permute-done.2.outer_row = bf16[160,128]{1,0:T(8,128)(2,1)S(1)} collective-permute-done((bf16[160,128]{1,0:T(8,128)(2,1)S(1)}, bf16[160,128]{1,0:T(8,128)(2,1)S(1)}, u32[]{:S(2)}, u32[]{:S(2)}) %collective-permute-start.2) | collective-permute-done | bytes 40992 | tf_op jit(solution)/shard_map/ppermute | solution.py:128
  16.5 0.0 collective-permute-done.3.inner_row
  16.5 1.0 %shard_map.157 = (bf16[1152,128]{1,0:T(8,128)(2,1)S(1)}, bf16[256,256]{1,0:T(8,128)(2,1)S(1)}, f32[256,256]{1,0:T(8,128)S(1)}, bf16[1152,256]{1,0:T(8,128)(2,1)S...) custom-call(bf16[160,128]{1,0:T(8,128)(2,1)S(1)} %collective-permute-done.2.outer_row, ...), custom_call_target="tpu_custom_call" | custom-call | tf_op jit(solution)/shard_map/pallas_call | solution.py:45
  17.5 0.1 collective-permute-start.8
  17.6 0.4 shard_map.162
  17.9 1.2 %collective-permute-done.8.received = bf16[1152,128]{1,0:T(8,128)(2,1)S(1)} collective-permute-done((bf16[1152,128]{1,0:T(8,128)(2,1)S(1)}, bf16[1152,128]{1,0:T(8,128)(2,1)S(1)}, u32[]{:S(2)}, u32[]{:S(2)}) %collective-permute-start.8) | collective-permute-done | bytes 294944 | tf_op jit(solution)/shard_map/ppermute | solution.py:128
  19.2 0.1 shard_map.163
  19.3 0.1 collective-permute-start.9
  19.3 0.2 collective-permute-start.10
  19.6 3.2 %collective-permute-start.11 = (bf16[304,128]{1,0:T(8,128)(2,1)S(1)}, bf16[304,128]{1,0:T(8,128)(2,1)S(1)}, u32[]{:S(2)}, u32[]{:S(2)}) collective-permute-start(bf16[304,128]{1,0:T(8,128)(2,1)S(1)} %get-tuple-element.100), channel_id=1, source_target_pairs={{0,1},{1,0},{2,3},{3,2},{4,5},{5,4},{6,7},{7,6},{8,9},{9,8},{10,11... | collective-permute-start | bytes 233480 | tf_op jit(solution)/shard_map/ppermute | solution.py:128
  22.8 1.2 %shard_map.158 = (bf16[64,8,128]{2,1,0:T(8,128)(2,1)}, f32[512,128]{1,0:T(8,128)}, f32[512,128]{1,0:T(8,128)}, bf16[256,1024]{1,0:T(8,128)(2,1)S(1)}, bf16[256,1...) custom-call(f32[512,128]{1,0:T(8,128)S(1)} %get-tuple-element.68.hidden, ...), custom_call_target="tpu_custom_call" | custom-call | bytes 4000000 | tf_op jit(solution)/shard_map/pallas_call | solution.py:45
  24.1 1.1 %shard_map.159 = (f32[1024,128]{1,0:T(8,128)S(1)}, bf16[3,128,768]{2,1,0:T(8,128)(2,1)S(1)}, f32[8,128]{1,0:T(8,128)S(1)}) custom-call(bf16[256,1024]{1,0:T(8,128)(2,1)S(1)} %get-tuple-element.82.pre, bf16[9,256,128]{2,1,0:T(8,128)(2,1)S(1)} %get-tuple-element.61.weights), custom_call_target="tpu_custom_call" | custom-call | flops 603979776 | bytes 3000000 | tf_op jit(solution)/shard_map/pallas_call | solution.py:45
  25.2 0.2 collective-permute-done.9.refs_0_
  25.4 0.9 %collective-permute-done.11.refs_2_ = bf16[304,128]{1,0:T(8,128)(2,1)S(1)} collective-permute-done((bf16[304,128]{1,0:T(8,128)(2,1)S(1)}, bf16[304,128]{1,0:T(8,128)(2,1)S(1)}, u32[]{:S(2)}, u32[]{:S(2)}) %collective-permute-start.11) | collective-permute-done | bytes 77856 | tf_op jit(solution)/shard_map/ppermute | solution.py:128
  26.3 1.1 %collective-permute-start.12 = (bf16[304,128]{1,0:T(8,128)(2,1)S(1)}, bf16[304,128]{1,0:T(8,128)(2,1)S(1)}, u32[]{:S(2)}, u32[]{:S(2)}) collective-permute-start(bf16[304,128]{1,0:T(8,128)(2,1)S(1)} %shard_map.164.own), channel_id=1, source_target_pairs={{0,2},{1,3},{2,0},{3,1},{4,6},{5,7},{6,4},{7,5},{8,12},{9,13},{10,... | collective-permute-start | bytes 233480 | tf_op jit(solution)/shard_map/ppermute | solution.py:128
  27.4 2.5 %collective-permute-start.4 = (bf16[256,128]{1,0:T(8,128)(2,1)S(1)}, bf16[256,128]{1,0:T(8,128)(2,1)S(1)}, u32[]{:S(2)}, u32[]{:S(2)}) collective-permute-start(bf16[256,128]{1,0:T(8,128)(2,1)S(1)} %get-tuple-element.85), channel_id=1, source_target_pairs={{0,4},{1,5},{2,6},{3,7},{4,0},{5,1},{6,2},{7,3},{8,16},{9,17},{10,... | collective-permute-start | bytes 196616 | tf_op jit(solution)/shard_map/ppermute | solution.py:128
  30.0 0.0 collective-permute-start.5
  30.0 0.8 %collective-permute-done.12.received = bf16[304,128]{1,0:T(8,128)(2,1)S(1)} collective-permute-done((bf16[304,128]{1,0:T(8,128)(2,1)S(1)}, bf16[304,128]{1,0:T(8,128)(2,1)S(1)}, u32[]{:S(2)}, u32[]{:S(2)}) %collective-permute-start.12) | collective-permute-done | bytes 77856 | tf_op jit(solution)/shard_map/ppermute | solution.py:128
  30.8 1.6 %collective-permute-start.13 = (bf16[304,128]{1,0:T(8,128)(2,1)S(1)}, bf16[304,128]{1,0:T(8,128)(2,1)S(1)}, u32[]{:S(2)}, u32[]{:S(2)}) collective-permute-start(bf16[304,128]{1,0:T(8,128)(2,1)S(1)} %shard_map.165.own), channel_id=1, source_target_pairs={{0,4},{1,5},{2,6},{3,7},{4,0},{5,1},{6,2},{7,3},{8,10},{9,11},{10,... | collective-permute-start | bytes 233480 | tf_op jit(solution)/shard_map/ppermute | solution.py:128
  32.4 0.9 %collective-permute-done.4.outer.outer_row = bf16[256,128]{1,0:T(8,128)(2,1)S(1)} collective-permute-done((bf16[256,128]{1,0:T(8,128)(2,1)S(1)}, bf16[256,128]{1,0:T(8,128)(2,1)S(1)}, u32[]{:S(2)}, u32[]{:S(2)}) %collective-permute-start.4) | collective-permute-done | bytes 65568 | tf_op jit(solution)/shard_map/ppermute | solution.py:128
  33.3 0.0 collective-permute-done.5.inner.inner_row
  33.3 0.2 shard_map.160
  33.5 1.4 %collective-permute-start.7 = (bf16[64,128]{1,0:T(8,128)(2,1)S(1)}, bf16[64,128]{1,0:T(8,128)(2,1)S(1)}, u32[]{:S(2)}, u32[]{:S(2)}) collective-permute-start(bf16[64,128]{1,0:T(8,128)(2,1)S(1)} %shard_map.160), channel_id=1, source_target_pairs={{0,1},{1,0},{2,3},{3,2},{4,5},{5,4},{6,7},{7,6},{8,9},{9,8},{10,11... | collective-permute-start | bytes 49160 | tf_op jit(solution)/shard_map/ppermute | solution.py:128
  34.9 1.4 %collective-permute-start.6 = (bf16[64,128]{1,0:T(8,128)(2,1)S(1)}, bf16[64,128]{1,0:T(8,128)(2,1)S(1)}, u32[]{:S(2)}, u32[]{:S(2)}) collective-permute-start(bf16[64,128]{1,0:T(8,128)(2,1)S(1)} %shard_map.160), channel_id=1, source_target_pairs={{0,7},{1,2},{2,1},{3,4},{4,3},{5,6},{6,5},{7,0},{8,15},{9,10},{10,... | collective-permute-start | bytes 49160 | tf_op jit(solution)/shard_map/ppermute | solution.py:128
  36.4 0.8 %collective-permute-done.13.received = bf16[304,128]{1,0:T(8,128)(2,1)S(1)} collective-permute-done((bf16[304,128]{1,0:T(8,128)(2,1)S(1)}, bf16[304,128]{1,0:T(8,128)(2,1)S(1)}, u32[]{:S(2)}, u32[]{:S(2)}) %collective-permute-start.13) | collective-permute-done | bytes 77856 | tf_op jit(solution)/shard_map/ppermute | solution.py:128
  37.2 1.0 %collective-permute-start.16 = (bf16[304,128]{1,0:T(8,128)(2,1)S(1)}, bf16[304,128]{1,0:T(8,128)(2,1)S(1)}, u32[]{:S(2)}, u32[]{:S(2)}) collective-permute-start(bf16[304,128]{1,0:T(8,128)(2,1)S(1)} %shard_map.166.refs_0_), channel_id=1, source_target_pairs={{0,17},{1,16},{2,19},{3,18},{4,21},{5,20},{6,23},{7,22},{8,25},{9,... | collective-permute-start | bytes 233480 | tf_op jit(solution)/shard_map/ppermute | solution.py:128
  38.2 1.9 %collective-permute-start.15 = (bf16[304,128]{1,0:T(8,128)(2,1)S(1)}, bf16[304,128]{1,0:T(8,128)(2,1)S(1)}, u32[]{:S(2)}, u32[]{:S(2)}) collective-permute-start(bf16[304,128]{1,0:T(8,128)(2,1)S(1)} %shard_map.166.refs_0_), channel_id=1, source_target_pairs={{0,16},{1,17},{2,18},{3,19},{4,20},{5,21},{6,22},{7,23},{8,24},{9,... | collective-permute-start | bytes 233480 | tf_op jit(solution)/shard_map/ppermute | solution.py:128
  40.1 0.6 %collective-permute-start.14 = (bf16[304,128]{1,0:T(8,128)(2,1)S(1)}, bf16[304,128]{1,0:T(8,128)(2,1)S(1)}, u32[]{:S(2)}, u32[]{:S(2)}) collective-permute-start(bf16[304,128]{1,0:T(8,128)(2,1)S(1)} %shard_map.166.refs_0_), channel_id=1, source_target_pairs={{0,1},{1,0},{2,3},{3,2},{4,5},{5,4},{6,7},{7,6},{8,9},{9,8},{10,11... | collective-permute-start | bytes 233480 | tf_op jit(solution)/shard_map/ppermute | solution.py:128
  40.8 0.6 %collective-permute-done.6.outer_column = bf16[64,128]{1,0:T(8,128)(2,1)S(1)} collective-permute-done((bf16[64,128]{1,0:T(8,128)(2,1)S(1)}, bf16[64,128]{1,0:T(8,128)(2,1)S(1)}, u32[]{:S(2)}, u32[]{:S(2)}) %collective-permute-start.6) | collective-permute-done | bytes 16416 | tf_op jit(solution)/shard_map/ppermute | solution.py:128
  41.4 1.6 %shard_map.161 = (bf16[64,8,128]{2,1,0:T(8,128)(2,1)}, bf16[64,8,128]{2,1,0:T(8,128)(2,1)}, f32[8,128]{1,0:T(8,128)S(1)}) custom-call(f32[1024,128]{1,0:T(8,128)S(1)} %get-tuple-element.83.wide, bf16[3,128,768]{2,1,0:T(8,128)(2,1)S(1)} %get-tuple-element.84.turned, bf16[256,128]{1,0:T(8,128)(2,1)S(1)} %collective-permute-done.4.outer.outer_row, ...), custom_call_target="tpu_custom_call" | custom-call | flops 12079595520 | bytes 2000000 | tf_op jit(solution)/shard_map/pallas_call | solution.py:45
  42.9 0.4 collective-permute-done.15.refs_1_
  43.4 0.1 collective-permute-start.17
  43.5 1.1 %collective-permute-done.14.late = bf16[304,128]{1,0:T(8,128)(2,1)S(1)} collective-permute-done((bf16[304,128]{1,0:T(8,128)(2,1)S(1)}, bf16[304,128]{1,0:T(8,128)(2,1)S(1)}, u32[]{:S(2)}, u32[]{:S(2)}) %collective-permute-start.14) | collective-permute-done | bytes 77856 | tf_op jit(solution)/shard_map/ppermute | solution.py:128
  44.5 0.0 collective-permute-start.18
  44.5 0.9 %shard_map.168 = (f32[9,256,128]{2,1,0:T(8,128)}, f32[8,128]{1,0:T(8,128)S(1)}) custom-call(bf16[304,128]{1,0:T(8,128)(2,1)S(1)} %collective-permute-done.14.late, bf16[3,304,128]{2,1,0:T(8,128)(2,1)S(1)} %shard_map.167.early), custom_call_target="tpu_custom_call" | custom-call | flops 12079595520 | bytes 884736 | tf_op jit(solution)/shard_map/pallas_call | solution.py:45
  45.5 0.3 collective-permute-done.18.late
  45.8 0.0 collective-permute-done.17.early
  45.8 0.9 %shard_map.169 = (f32[9,256,128]{2,1,0:T(8,128)}, f32[256]{0:T(256)}) custom-call(f32[8,128]{1,0:T(8,128)S(1)} %get-tuple-element.103.bias_own, bf16[3,304,128]{2,1,0:T(8,128)(2,1)S(1)} %collective-permute-done.17.early, bf16[304,128]{1,0:T(8,128)(2,1)S(1)} %collective-permute-done.18.late, ...), custom_call_target="tpu_custom_call", output_to_operand_aliasing={{0}: (4, {})} | custom-call | bytes 884736 | tf_op jit(solution)/shard_map/pallas_call | solution.py:45
  (7 shorter events, 0.1 us)
Async XLA Ops:
  1.9 8.0 %collective-permute-start.1 = (bf16[32,128]{1,0:T(8,128)(2,1)S(1)}, bf16[32,128]{1,0:T(8,128)(2,1)S(1)}, u32[]{:S(2)}, u32[]{:S(2)}) collective-permute-start(bf16[32,128]{1,0:T(8,128)(2,1)S(1)} %get-tuple-element.59), channel_id=1, source_target_pairs={{0,1},{1,0},{2,3},{3,2},{4,5},{5,4},{6,7},{7,6},{8,9},{9,8},{10,11... | collective-permute-start | bytes 24584 | tf_op jit(solution)/shard_map/ppermute | solution.py:128
  5.0 6.3 %collective-permute-start = (bf16[32,128]{1,0:T(8,128)(2,1)S(1)}, bf16[32,128]{1,0:T(8,128)(2,1)S(1)}, u32[]{:S(2)}, u32[]{:S(2)}) collective-permute-start(bf16[32,128]{1,0:T(8,128)(2,1)S(1)} %get-tuple-element.59), channel_id=1, source_target_pairs={{0,7},{1,2},{2,1},{3,4},{4,3},{5,6},{6,5},{7,0},{8,15},{9,10},{10,... | collective-permute-start | bytes 24584 | tf_op jit(solution)/shard_map/ppermute | solution.py:128
  11.5 5.0 %collective-permute-start.2 = (bf16[160,128]{1,0:T(8,128)(2,1)S(1)}, bf16[160,128]{1,0:T(8,128)(2,1)S(1)}, u32[]{:S(2)}, u32[]{:S(2)}) collective-permute-start(bf16[160,128]{1,0:T(8,128)(2,1)S(1)} %get-tuple-element.72), channel_id=1, source_target_pairs={{0,4},{1,5},{2,6},{3,7},{4,0},{5,1},{6,2},{7,3},{8,16},{9,17},{10,... | collective-permute-start | bytes 122888 | tf_op jit(solution)/shard_map/ppermute | solution.py:128
  12.4 4.1 %collective-permute-start.3 = (bf16[160,128]{1,0:T(8,128)(2,1)S(1)}, bf16[160,128]{1,0:T(8,128)(2,1)S(1)}, u32[]{:S(2)}, u32[]{:S(2)}) collective-permute-start(bf16[160,128]{1,0:T(8,128)(2,1)S(1)} %get-tuple-element.73), channel_id=1, source_target_pairs={{0,8},{1,9},{2,10},{3,11},{4,12},{5,13},{6,14},{7,15},{8,0},{9,1},... | collective-permute-start | bytes 122888 | tf_op jit(solution)/shard_map/ppermute | solution.py:128
  17.5 1.6 %collective-permute-start.8 = (bf16[1152,128]{1,0:T(8,128)(2,1)S(1)}, bf16[1152,128]{1,0:T(8,128)(2,1)S(1)}, u32[]{:S(2)}, u32[]{:S(2)}) collective-permute-start(bf16[1152,128]{1,0:T(8,128)(2,1)S(1)} %get-tuple-element.96), channel_id=1, source_target_pairs={{0,8},{1,9},{2,10},{3,11},{4,12},{5,13},{6,14},{7,15},{8,0},{9,1},... | collective-permute-start | bytes 884744 | tf_op jit(solution)/shard_map/ppermute | solution.py:128
  19.3 6.2 %collective-permute-start.9 = (bf16[304,128]{1,0:T(8,128)(2,1)S(1)}, bf16[304,128]{1,0:T(8,128)(2,1)S(1)}, u32[]{:S(2)}, u32[]{:S(2)}) collective-permute-start(bf16[304,128]{1,0:T(8,128)(2,1)S(1)} %get-tuple-element.98), channel_id=1, source_target_pairs={{0,17},{1,16},{2,19},{3,18},{4,21},{5,20},{6,23},{7,22},{8,25},{9,... | collective-permute-start | bytes 233480 | tf_op jit(solution)/shard_map/ppermute | solution.py:128
  19.3 6.1 %collective-permute-start.10 = (bf16[304,128]{1,0:T(8,128)(2,1)S(1)}, bf16[304,128]{1,0:T(8,128)(2,1)S(1)}, u32[]{:S(2)}, u32[]{:S(2)}) collective-permute-start(bf16[304,128]{1,0:T(8,128)(2,1)S(1)} %get-tuple-element.99), channel_id=1, source_target_pairs={{0,16},{1,17},{2,18},{3,19},{4,20},{5,21},{6,22},{7,23},{8,24},{9,... | collective-permute-start | bytes 233480 | tf_op jit(solution)/shard_map/ppermute | solution.py:128
  19.6 6.7 %collective-permute-start.11 = (bf16[304,128]{1,0:T(8,128)(2,1)S(1)}, bf16[304,128]{1,0:T(8,128)(2,1)S(1)}, u32[]{:S(2)}, u32[]{:S(2)}) collective-permute-start(bf16[304,128]{1,0:T(8,128)(2,1)S(1)} %get-tuple-element.100), channel_id=1, source_target_pairs={{0,1},{1,0},{2,3},{3,2},{4,5},{5,4},{6,7},{7,6},{8,9},{9,8},{10,11... | collective-permute-start | bytes 233480 | tf_op jit(solution)/shard_map/ppermute | solution.py:128
  26.3 4.5 %collective-permute-start.12 = (bf16[304,128]{1,0:T(8,128)(2,1)S(1)}, bf16[304,128]{1,0:T(8,128)(2,1)S(1)}, u32[]{:S(2)}, u32[]{:S(2)}) collective-permute-start(bf16[304,128]{1,0:T(8,128)(2,1)S(1)} %shard_map.164.own), channel_id=1, source_target_pairs={{0,2},{1,3},{2,0},{3,1},{4,6},{5,7},{6,4},{7,5},{8,12},{9,13},{10,... | collective-permute-start | bytes 233480 | tf_op jit(solution)/shard_map/ppermute | solution.py:128
  27.4 5.9 %collective-permute-start.4 = (bf16[256,128]{1,0:T(8,128)(2,1)S(1)}, bf16[256,128]{1,0:T(8,128)(2,1)S(1)}, u32[]{:S(2)}, u32[]{:S(2)}) collective-permute-start(bf16[256,128]{1,0:T(8,128)(2,1)S(1)} %get-tuple-element.85), channel_id=1, source_target_pairs={{0,4},{1,5},{2,6},{3,7},{4,0},{5,1},{6,2},{7,3},{8,16},{9,17},{10,... | collective-permute-start | bytes 196616 | tf_op jit(solution)/shard_map/ppermute | solution.py:128
  30.0 3.3 %collective-permute-start.5 = (bf16[256,128]{1,0:T(8,128)(2,1)S(1)}, bf16[256,128]{1,0:T(8,128)(2,1)S(1)}, u32[]{:S(2)}, u32[]{:S(2)}) collective-permute-start(bf16[256,128]{1,0:T(8,128)(2,1)S(1)} %get-tuple-element.86), channel_id=1, source_target_pairs={{0,8},{1,9},{2,10},{3,11},{4,12},{5,13},{6,14},{7,15},{8,0},{9,1},... | collective-permute-start | bytes 196616 | tf_op jit(solution)/shard_map/ppermute | solution.py:128
  30.8 6.4 %collective-permute-start.13 = (bf16[304,128]{1,0:T(8,128)(2,1)S(1)}, bf16[304,128]{1,0:T(8,128)(2,1)S(1)}, u32[]{:S(2)}, u32[]{:S(2)}) collective-permute-start(bf16[304,128]{1,0:T(8,128)(2,1)S(1)} %shard_map.165.own), channel_id=1, source_target_pairs={{0,4},{1,5},{2,6},{3,7},{4,0},{5,1},{6,2},{7,3},{8,10},{9,11},{10,... | collective-permute-start | bytes 233480 | tf_op jit(solution)/shard_map/ppermute | solution.py:128
  33.5 7.3 %collective-permute-start.7 = (bf16[64,128]{1,0:T(8,128)(2,1)S(1)}, bf16[64,128]{1,0:T(8,128)(2,1)S(1)}, u32[]{:S(2)}, u32[]{:S(2)}) collective-permute-start(bf16[64,128]{1,0:T(8,128)(2,1)S(1)} %shard_map.160), channel_id=1, source_target_pairs={{0,1},{1,0},{2,3},{3,2},{4,5},{5,4},{6,7},{7,6},{8,9},{9,8},{10,11... | collective-permute-start | bytes 49160 | tf_op jit(solution)/shard_map/ppermute | solution.py:128
  34.9 6.4 %collective-permute-start.6 = (bf16[64,128]{1,0:T(8,128)(2,1)S(1)}, bf16[64,128]{1,0:T(8,128)(2,1)S(1)}, u32[]{:S(2)}, u32[]{:S(2)}) collective-permute-start(bf16[64,128]{1,0:T(8,128)(2,1)S(1)} %shard_map.160), channel_id=1, source_target_pairs={{0,7},{1,2},{2,1},{3,4},{4,3},{5,6},{6,5},{7,0},{8,15},{9,10},{10,... | collective-permute-start | bytes 49160 | tf_op jit(solution)/shard_map/ppermute | solution.py:128
  37.2 5.7 %collective-permute-start.16 = (bf16[304,128]{1,0:T(8,128)(2,1)S(1)}, bf16[304,128]{1,0:T(8,128)(2,1)S(1)}, u32[]{:S(2)}, u32[]{:S(2)}) collective-permute-start(bf16[304,128]{1,0:T(8,128)(2,1)S(1)} %shard_map.166.refs_0_), channel_id=1, source_target_pairs={{0,17},{1,16},{2,19},{3,18},{4,21},{5,20},{6,23},{7,22},{8,25},{9,... | collective-permute-start | bytes 233480 | tf_op jit(solution)/shard_map/ppermute | solution.py:128
  38.2 5.1 %collective-permute-start.15 = (bf16[304,128]{1,0:T(8,128)(2,1)S(1)}, bf16[304,128]{1,0:T(8,128)(2,1)S(1)}, u32[]{:S(2)}, u32[]{:S(2)}) collective-permute-start(bf16[304,128]{1,0:T(8,128)(2,1)S(1)} %shard_map.166.refs_0_), channel_id=1, source_target_pairs={{0,16},{1,17},{2,18},{3,19},{4,20},{5,21},{6,22},{7,23},{8,24},{9,... | collective-permute-start | bytes 233480 | tf_op jit(solution)/shard_map/ppermute | solution.py:128
  40.1 4.4 %collective-permute-start.14 = (bf16[304,128]{1,0:T(8,128)(2,1)S(1)}, bf16[304,128]{1,0:T(8,128)(2,1)S(1)}, u32[]{:S(2)}, u32[]{:S(2)}) collective-permute-start(bf16[304,128]{1,0:T(8,128)(2,1)S(1)} %shard_map.166.refs_0_), channel_id=1, source_target_pairs={{0,1},{1,0},{2,3},{3,2},{4,5},{5,4},{6,7},{7,6},{8,9},{9,8},{10,11... | collective-permute-start | bytes 233480 | tf_op jit(solution)/shard_map/ppermute | solution.py:128
  43.4 2.4 %collective-permute-start.17 = (bf16[3,304,128]{2,1,0:T(8,128)(2,1)S(1)}, bf16[3,304,128]{2,1,0:T(8,128)(2,1)S(1)}, u32[]{:S(2)}, u32[]{:S(2)}) collective-permute-start(bf16[3,304,128]{2,1,0:T(8,128)(2,1)S(1)} %shard_map.167.early), channel_id=1, source_target_pairs={{0,8},{1,9},{2,10},{3,11},{4,12},{5,13},{6,14},{7,15},{8,0},{9,1},... | collective-permute-start | bytes 700424 | tf_op jit(solution)/shard_map/ppermute | solution.py:128
  44.5 1.3 %collective-permute-start.18 = (bf16[304,128]{1,0:T(8,128)(2,1)S(1)}, bf16[304,128]{1,0:T(8,128)(2,1)S(1)}, u32[]{:S(2)}, u32[]{:S(2)}) collective-permute-start(bf16[304,128]{1,0:T(8,128)(2,1)S(1)} %collective-permute-done.14.late), channel_id=1, source_target_pairs={{0,8},{1,9},{2,10},{3,11},{4,12},{5,13},{6,14},{7,15},{8,0},{9,1},... | collective-permute-start | bytes 233480 | tf_op jit(solution)/shard_map/ppermute | solution.py:128

commit v11 on v8

--- a/solution.py
+++ b/solution.py
@@ -198,16 +198,22 @@
 
 
 def pack_kernel(below, hidden, inner_out, outer_out, wide_out, below_here, hidden_here, arrived):
-    first = pltpu.make_async_copy(below, below_here, arrived.at[0])
-    second = pltpu.make_async_copy(hidden, hidden_here, arrived.at[1])
-    first.start()
-    second.start()
     channels, row_count, width = below.shape
     size = channels * row_count
-    first.wait()
-    wide_out[0:size, :] = below_here[...].astype(F32).reshape(size, width)
-    second.wait()
-    wide_out[size : 2 * size, :] = hidden_here[...].astype(F32).reshape(size, width)
+    part = channels // 2
+    copies = []
+    for source, here in ((below, below_here), (hidden, hidden_here)):
+        for at in (pl.ds(0, part), pl.ds(part, part)):
+            copies.append(
+                pltpu.make_async_copy(source.at[at], here.at[at], arrived.at[len(copies)])
+            )
+            copies[-1].start()
+    for index, copy in enumerate(copies):
+        here = (below_here, hidden_here)[index // 2]
+        copy.wait()
+        value = here[pl.ds(index % 2 * part, part)].astype(F32)
+        at = pl.ds(index * part * row_count, part * row_count)
+        wide_out[at, :] = value.reshape(part * row_count, width)
     edges = [
         wide_out[pl.ds(index, 2 * channels, stride=row_count), :] for index in (0, row_count - 1)
     ]
@@ -248,12 +254,16 @@
     readout_here,
     arrived,
 ):
+    row_count, channels, width = rows_out.shape
     copies = [
         pltpu.make_async_copy(source, target, arrived.at[index])
         for index, (source, target) in enumerate(
             (
                 (cell_hbm, cell_out),
-                (weights_hbm, weights_out),
+                *(
+                    (weights_hbm.at[tap], weights_out.at[:, pl.ds(tap * channels, channels)])
+                    for tap in range(weights_hbm.shape[0])
+                ),
                 (hidden_grad_hbm, hidden_grad_here),
                 (target_hbm, target_out),
                 (land_hbm, land_out),
@@ -265,7 +275,6 @@
     ]
     for copy in copies:
         copy.start()
-    row_count, channels, width = rows_out.shape
     columns = jnp.zeros((channels, width), F32)
     second = jnp.zeros((channels, width), F32)
     for index in range(row_count):
@@ -363,7 +372,7 @@
     shifted,
 ):
     row_count, channels, width = rows_in.shape
-    gate_count = weights.shape[1]
+    gate_count = weights.shape[0]
     hid = gate_count // 4
     half_gates = place.half_gates
     north, south = row_halo(inner_row, outer_row)
@@ -381,10 +390,6 @@
         shifted[channels : 2 * channels, at] = row.astype(BF16)
         shifted[2 * channels : 3 * channels, at] = rolled(row, -1).astype(BF16)
 
-    taps = [
-        jnp.concatenate([weights[3 * a], weights[3 * a + 1], weights[3 * a + 2]], axis=1)
-        for a in range(3)
-    ]
     bias_total = jnp.zeros((gate_count, width), F32)
     lane = lanes((gate_count, width))
     inside = (lane > 0) & (lane < width - 1)
@@ -394,7 +399,7 @@
         preact = jnp.zeros((gate_count, pair * width), F32)
         for a in range(3):
             preact += jnp.dot(
-                taps[a],
+                weights[:, pl.ds(3 * a * channels, 3 * channels)],
                 shifted[:, pl.ds((base + a) * width, pair * width)],
                 preferred_element_type=F32,
             )
@@ -491,8 +496,7 @@
         for b in range(3):
             at = (3 * a + b) * channels
             patches[at : at + channels, :] = rolled(columns[b], 1 - a).astype(BF16)
-    taps = jnp.concatenate([weights[tap] for tap in range(place.taps)], axis=1)
-    preact = jnp.dot(taps, patches[...], preferred_element_type=F32) + bias_wide[...]
+    preact = jnp.dot(weights[...], patches[...], preferred_element_type=F32) + bias_wide[...]
     hidden_next, cell_next, grad_cell, pre_grad = cell_step(
         preact,
         cell_strip[...],
@@ -667,7 +671,8 @@
 def field_kernel(pre, weights, wide_out, turned_out, done_out, shifted):
     done_out[...] = jnp.zeros(done_out.shape, F32)
     gate_count, cells = pre.shape
-    channels, width = weights.shape[2], wide_out.shape[1]
+    width = wide_out.shape[1]
+    channels = weights.shape[1] // 9
     row_count = cells // width
     lane = lanes((gate_count, width))
     for index in range(row_count):
@@ -680,7 +685,9 @@
         shifted[2 * gate_count : 3 * gate_count, at] = left.astype(BF16)
     for a in range(3):
         for b in range(3):
-            turned_out[a, :, b * gate_count : (b + 1) * gate_count] = weights[3 * a + b].T
+            turned_out[a, :, b * gate_count : (b + 1) * gate_count] = (
+                weights[:, pl.ds((3 * a + b) * channels, channels)].T
+            )
 
     def product(a, index, count):
         return jnp.dot(
@@ -797,7 +804,7 @@
         [
             pltpu.VMEM(inputs_below.shape, BF16),
             pltpu.VMEM(hidden_prev.shape, BF16),
-            pltpu.SemaphoreType.DMA((2,)),
+            pltpu.SemaphoreType.DMA((4,)),
         ],
         remote=2,
         moved=4 * channels * cells,
@@ -828,7 +835,7 @@
             strip,
             sds((8, width), F32),
             flat,
-            sds(kernel_weights.shape, BF16),
+            sds((gate_count, place.taps * channels), BF16),
             flat,
             sds(target_field.shape, F32),
             sds(land_mask.shape, jnp.int32),
@@ -840,7 +847,7 @@
             pltpu.VMEM(hidden_grad.shape, BF16),
             pltpu.VMEM(gate_bias.shape, F32),
             pltpu.VMEM(readout.shape, F32),
-            pltpu.SemaphoreType.DMA((8,)),
+            pltpu.SemaphoreType.DMA((7 + place.taps,)),
         ],
         remote=8,
         moved=6_000_000,

time: 46.6 us -> 46.7 us (level)
  transfers between devices with their start and end apart: 19 -> 19, of which waited for: 11 -> 10; matrix products, arithmetic and copies ran while one was open for 0% -> 0% of each run, Pallas kernels for 21% -> 22%
where the time goes in v11:
time: 46.7 us; the launch traced here: 46.5 us
  starting transfers between devices  25.1 us (54%)
  Pallas kernels  13.1 us (28%)
  waiting for transfers between devices  7.49 us (16%)
  between operations  0.78 us (2%)
    ppermute x19, starting transfers between devices, permuted(): return lax.ppermute(value, AXES, pairs)  25.1 us
    pallas_call x17, Pallas kernels, run(): pl.pallas_call(kernel, out_shape=out_shape, in_specs=[VMEM] * near + [HBM...  13.1 us
    ppermute x19, waiting for transfers between devices, permuted(): return lax.ppermute(value, AXES, pairs)  7.49 us
  transfers between devices with their start and end apart: 19, of which 10 were waited for; matrix products, arithmetic and copies ran while one was open for 0% of the time, Pallas kernels for 22%

profile of v11, /device:TPU:0, one launch (start us, length us, event | category | flops | bytes accessed | tf_op | source)
XLA Modules:
  0.0 46.5 jit_solution(16206710592182339717)
XLA Ops:
  0.6 1.0 %shard_map.153 = (bf16[128,128]{1,0:T(8,128)(2,1)S(1)}, bf16[128,128]{1,0:T(8,128)(2,1)S(1)}, f32[1024,128]{1,0:T(8,128)S(1)}) custom-call(bf16[64,8,128]{2,1,0:T(8,128)(2,1)} %below.1, bf16[64,8,128]{2,1,0:T(8,128)(2,1)} %hidden.1), custom_call_target="tpu_custom_call" | custom-call | bytes 524288 | tf_op jit(solution)/shard_map/pallas_call | solution.py:45
  1.6 0.5 %collective-permute-start = (bf16[128,128]{1,0:T(8,128)(2,1)S(1)}, bf16[128,128]{1,0:T(8,128)(2,1)S(1)}, u32[]{:S(2)}, u32[]{:S(2)}) collective-permute-start(bf16[128,128]{1,0:T(8,128)(2,1)S(1)} %get-tuple-element.64), channel_id=1, source_target_pairs={{0,8},{1,9},{2,10},{3,11},{4,12},{5,13},{6,14},{7,15},{8,0},{9,1},... | collective-permute-start | bytes 98312 | tf_op jit(solution)/shard_map/ppermute | solution.py:128
  2.2 3.7 %collective-permute-start.1 = (bf16[128,128]{1,0:T(8,128)(2,1)S(1)}, bf16[128,128]{1,0:T(8,128)(2,1)S(1)}, u32[]{:S(2)}, u32[]{:S(2)}) collective-permute-start(bf16[128,128]{1,0:T(8,128)(2,1)S(1)} %get-tuple-element.65), channel_id=1, source_target_pairs={{0,4},{1,5},{2,6},{3,7},{4,0},{5,1},{6,2},{7,3},{8,16},{9,17},{10,... | collective-permute-start | bytes 98312 | tf_op jit(solution)/shard_map/ppermute | solution.py:128
  5.8 2.3 %shard_map.154 = (bf16[8,128,128]{2,1,0:T(8,128)(2,1)S(1)}, f32[128,128]{1,0:T(8,128)S(1)}, f32[128,128]{1,0:T(8,128)S(1)}, f32[64,128]{1,0:T(8,128)S(1)}, f32[6...) custom-call(f32[1024,128]{1,0:T(8,128)S(1)} %get-tuple-element.62.wi, ...), custom_call_target="tpu_custom_call" | custom-call | bytes 6000000 | tf_op jit(solution)/shard_map/pallas_call | solution.py:45
  8.1 0.0 collective-permute-done.inner_row.inner
  8.1 0.0 collective-permute-done.1.outer_row.outer
  8.1 0.2 shard_map.156
  8.3 1.5 %collective-permute-start.3 = (bf16[32,128]{1,0:T(8,128)(2,1)S(1)}, bf16[32,128]{1,0:T(8,128)(2,1)S(1)}, u32[]{:S(2)}, u32[]{:S(2)}) collective-permute-start(bf16[32,128]{1,0:T(8,128)(2,1)S(1)} %get-tuple-element.82), channel_id=1, source_target_pairs={{0,1},{1,0},{2,3},{3,2},{4,5},{5,4},{6,7},{7,6},{8,9},{9,8},{10,11... | collective-permute-start | bytes 24584 | tf_op jit(solution)/shard_map/ppermute | solution.py:128
  9.8 3.7 %collective-permute-start.2 = (bf16[32,128]{1,0:T(8,128)(2,1)S(1)}, bf16[32,128]{1,0:T(8,128)(2,1)S(1)}, u32[]{:S(2)}, u32[]{:S(2)}) collective-permute-start(bf16[32,128]{1,0:T(8,128)(2,1)S(1)} %get-tuple-element.82), channel_id=1, source_target_pairs={{0,7},{1,2},{2,1},{3,4},{4,3},{5,6},{6,5},{7,0},{8,15},{9,10},{10,... | collective-permute-start | bytes 24584 | tf_op jit(solution)/shard_map/ppermute | solution.py:128
  13.5 2.2 %shard_map.155 = (f32[512,128]{1,0:T(8,128)S(1)}, f32[512,128]{1,0:T(8,128)S(1)}, f32[512,128]{1,0:T(8,128)S(1)}, bf16[256,1024]{1,0:T(8,128)(2,1)S(1)}, bf16[12...) custom-call(bf16[8,128,128]{2,1,0:T(8,128)(2,1)S(1)} %get-tuple-element.63.rows_in, ...), custom_call_target="tpu_custom_call" | custom-call | flops 1207959552 | bytes 6000000 | tf_op jit(solution)/shard_map/pallas_call | solution.py:45
  15.7 0.0 collective-permute-done.3.inner_column
  15.7 0.4 collective-permute-done.2.outer_column
  16.2 0.9 %shard_map.157 = (bf16[1152,128]{1,0:T(8,128)(2,1)S(1)}, bf16[256,128]{1,0:T(8,128)(2,1)S(1)}, f32[256,128]{1,0:T(8,128)S(1)}, bf16[1152,128]{1,0:T(8,128)(2,1)S...) custom-call(bf16[128,128]{1,0:T(8,128)(2,1)S(1)} %get-tuple-element.80.edge, ...), custom_call_target="tpu_custom_call" | custom-call | tf_op jit(solution)/shard_map/pallas_call | solution.py:45
  17.1 0.1 collective-permute-start.8
  17.1 0.3 shard_map.162
  17.4 1.3 %collective-permute-done.8.received = bf16[1152,128]{1,0:T(8,128)(2,1)S(1)} collective-permute-done((bf16[1152,128]{1,0:T(8,128)(2,1)S(1)}, bf16[1152,128]{1,0:T(8,128)(2,1)S(1)}, u32[]{:S(2)}, u32[]{:S(2)}) %collective-permute-start.8) | collective-permute-done | bytes 294944 | tf_op jit(solution)/shard_map/ppermute | solution.py:128
  18.7 0.1 shard_map.163
  18.8 0.1 collective-permute-start.9
  18.9 0.4 collective-permute-start.10
  19.3 3.1 %collective-permute-start.11 = (bf16[304,128]{1,0:T(8,128)(2,1)S(1)}, bf16[304,128]{1,0:T(8,128)(2,1)S(1)}, u32[]{:S(2)}, u32[]{:S(2)}) collective-permute-start(bf16[304,128]{1,0:T(8,128)(2,1)S(1)} %get-tuple-element.110), channel_id=1, source_target_pairs={{0,1},{1,0},{2,3},{3,2},{4,5},{5,4},{6,7},{7,6},{8,9},{9,8},{10,11... | collective-permute-start | bytes 233480 | tf_op jit(solution)/shard_map/ppermute | solution.py:128
  22.4 1.4 %shard_map.158 = (bf16[64,8,128]{2,1,0:T(8,128)(2,1)}, f32[512,128]{1,0:T(8,128)}, f32[512,128]{1,0:T(8,128)}, bf16[256,1024]{1,0:T(8,128)(2,1)S(1)}, bf16[256,1...) custom-call(f32[512,128]{1,0:T(8,128)S(1)} %get-tuple-element.75.hidden, f32[512,128]{1,0:T(8,128)S(1)} %get-tuple-element.76.cell, ...), custom_call_target="tpu_custom_call" | custom-call | bytes 4000000 | tf_op jit(solution)/shard_map/pallas_call | solution.py:45
  23.7 1.1 %shard_map.159 = (f32[1024,128]{1,0:T(8,128)S(1)}, bf16[3,128,768]{2,1,0:T(8,128)(2,1)S(1)}, f32[8,128]{1,0:T(8,128)S(1)}) custom-call(bf16[256,1024]{1,0:T(8,128)(2,1)S(1)} %get-tuple-element.93.pre, bf16[256,1152]{1,0:T(8,128)(2,1)S(1)} %get-tuple-element.68.weights), custom_call_target="tpu_custom_call" | custom-call | flops 603979776 | bytes 3000000 | tf_op jit(solution)/shard_map/pallas_call | solution.py:45
  24.9 0.1 collective-permute-done.9.refs_0_
  25.0 0.0 collective-permute-done.10.refs_1_
  25.0 0.9 %collective-permute-done.11.refs_2_ = bf16[304,128]{1,0:T(8,128)(2,1)S(1)} collective-permute-done((bf16[304,128]{1,0:T(8,128)(2,1)S(1)}, bf16[304,128]{1,0:T(8,128)(2,1)S(1)}, u32[]{:S(2)}, u32[]{:S(2)}) %collective-permute-start.11) | collective-permute-done | bytes 77856 | tf_op jit(solution)/shard_map/ppermute | solution.py:128
  25.9 0.1 collective-permute-start.12
  26.0 3.7 %collective-permute-start.4 = (bf16[256,128]{1,0:T(8,128)(2,1)S(1)}, bf16[256,128]{1,0:T(8,128)(2,1)S(1)}, u32[]{:S(2)}, u32[]{:S(2)}) collective-permute-start(bf16[256,128]{1,0:T(8,128)(2,1)S(1)} %get-tuple-element.96), channel_id=1, source_target_pairs={{0,4},{1,5},{2,6},{3,7},{4,0},{5,1},{6,2},{7,3},{8,16},{9,17},{10,... | collective-permute-start | bytes 196616 | tf_op jit(solution)/shard_map/ppermute | solution.py:128
  29.7 0.0 collective-permute-start.5
  29.7 1.5 %collective-permute-done.12.received = bf16[304,128]{1,0:T(8,128)(2,1)S(1)} collective-permute-done((bf16[304,128]{1,0:T(8,128)(2,1)S(1)}, bf16[304,128]{1,0:T(8,128)(2,1)S(1)}, u32[]{:S(2)}, u32[]{:S(2)}) %collective-permute-start.12) | collective-permute-done | bytes 77856 | tf_op jit(solution)/shard_map/ppermute | solution.py:128
  31.2 0.9 %collective-permute-start.13 = (bf16[304,128]{1,0:T(8,128)(2,1)S(1)}, bf16[304,128]{1,0:T(8,128)(2,1)S(1)}, u32[]{:S(2)}, u32[]{:S(2)}) collective-permute-start(bf16[304,128]{1,0:T(8,128)(2,1)S(1)} %shard_map.165.own), channel_id=1, source_target_pairs={{0,4},{1,5},{2,6},{3,7},{4,0},{5,1},{6,2},{7,3},{8,10},{9,11},{10,... | collective-permute-start | bytes 233480 | tf_op jit(solution)/shard_map/ppermute | solution.py:128
  32.1 0.0 collective-permute-done.4.outer.outer_row
  32.1 0.0 collective-permute-done.5.inner.inner_row
  32.1 0.2 shard_map.160
  32.3 2.1 %collective-permute-start.7 = (bf16[64,128]{1,0:T(8,128)(2,1)S(1)}, bf16[64,128]{1,0:T(8,128)(2,1)S(1)}, u32[]{:S(2)}, u32[]{:S(2)}) collective-permute-start(bf16[64,128]{1,0:T(8,128)(2,1)S(1)} %shard_map.160), channel_id=1, source_target_pairs={{0,1},{1,0},{2,3},{3,2},{4,5},{5,4},{6,7},{7,6},{8,9},{9,8},{10,11... | collective-permute-start | bytes 49160 | tf_op jit(solution)/shard_map/ppermute | solution.py:128
  34.4 1.7 %collective-permute-start.6 = (bf16[64,128]{1,0:T(8,128)(2,1)S(1)}, bf16[64,128]{1,0:T(8,128)(2,1)S(1)}, u32[]{:S(2)}, u32[]{:S(2)}) collective-permute-start(bf16[64,128]{1,0:T(8,128)(2,1)S(1)} %shard_map.160), channel_id=1, source_target_pairs={{0,7},{1,2},{2,1},{3,4},{4,3},{5,6},{6,5},{7,0},{8,15},{9,10},{10,... | collective-permute-start | bytes 49160 | tf_op jit(solution)/shard_map/ppermute | solution.py:128
  36.1 0.9 %collective-permute-done.13.received = bf16[304,128]{1,0:T(8,128)(2,1)S(1)} collective-permute-done((bf16[304,128]{1,0:T(8,128)(2,1)S(1)}, bf16[304,128]{1,0:T(8,128)(2,1)S(1)}, u32[]{:S(2)}, u32[]{:S(2)}) %collective-permute-start.13) | collective-permute-done | bytes 77856 | tf_op jit(solution)/shard_map/ppermute | solution.py:128
  37.0 0.4 collective-permute-start.16
  37.4 2.5 %collective-permute-start.15 = (bf16[304,128]{1,0:T(8,128)(2,1)S(1)}, bf16[304,128]{1,0:T(8,128)(2,1)S(1)}, u32[]{:S(2)}, u32[]{:S(2)}) collective-permute-start(bf16[304,128]{1,0:T(8,128)(2,1)S(1)} %shard_map.166.refs_0_), channel_id=1, source_target_pairs={{0,16},{1,17},{2,18},{3,19},{4,20},{5,21},{6,22},{7,23},{8,24},{9,... | collective-permute-start | bytes 233480 | tf_op jit(solution)/shard_map/ppermute | solution.py:128
  39.9 0.7 %collective-permute-start.14 = (bf16[304,128]{1,0:T(8,128)(2,1)S(1)}, bf16[304,128]{1,0:T(8,128)(2,1)S(1)}, u32[]{:S(2)}, u32[]{:S(2)}) collective-permute-start(bf16[304,128]{1,0:T(8,128)(2,1)S(1)} %shard_map.166.refs_0_), channel_id=1, source_target_pairs={{0,1},{1,0},{2,3},{3,2},{4,5},{5,4},{6,7},{7,6},{8,9},{9,8},{10,11... | collective-permute-start | bytes 233480 | tf_op jit(solution)/shard_map/ppermute | solution.py:128
  40.6 0.3 collective-permute-done.6.outer_column
  40.8 1.6 %shard_map.161 = (bf16[64,8,128]{2,1,0:T(8,128)(2,1)}, bf16[64,8,128]{2,1,0:T(8,128)(2,1)}, f32[8,128]{1,0:T(8,128)S(1)}) custom-call(f32[1024,128]{1,0:T(8,128)S(1)} %get-tuple-element.94.wide, bf16[3,128,768]{2,1,0:T(8,128)(2,1)S(1)} %get-tuple-element.95.turned, bf16[256,128]{1,0:T(8,128)(2,1)S(1)} %collective-permute-done.4.outer.outer_row, ...), custom_call_target="tpu_custom_call" | custom-call | flops 12079595520 | bytes 2000000 | tf_op jit(solution)/shard_map/pallas_call | solution.py:45
  42.4 0.7 %collective-permute-done.15.refs_1_ = bf16[304,128]{1,0:T(8,128)(2,1)S(1)} collective-permute-done((bf16[304,128]{1,0:T(8,128)(2,1)S(1)}, bf16[304,128]{1,0:T(8,128)(2,1)S(1)}, u32[]{:S(2)}, u32[]{:S(2)}) %collective-permute-start.15) | collective-permute-done | bytes 77856 | tf_op jit(solution)/shard_map/ppermute | solution.py:128
  43.1 0.1 collective-permute-start.17
  43.2 1.1 %collective-permute-done.14.late = bf16[304,128]{1,0:T(8,128)(2,1)S(1)} collective-permute-done((bf16[304,128]{1,0:T(8,128)(2,1)S(1)}, bf16[304,128]{1,0:T(8,128)(2,1)S(1)}, u32[]{:S(2)}, u32[]{:S(2)}) %collective-permute-start.14) | collective-permute-done | bytes 77856 | tf_op jit(solution)/shard_map/ppermute | solution.py:128
  44.3 0.0 collective-permute-start.18
  44.3 0.9 %shard_map.168 = (f32[9,256,128]{2,1,0:T(8,128)}, f32[8,128]{1,0:T(8,128)S(1)}) custom-call(bf16[304,128]{1,0:T(8,128)(2,1)S(1)} %collective-permute-done.14.late, bf16[3,304,128]{2,1,0:T(8,128)(2,1)S(1)} %shard_map.167.early), custom_call_target="tpu_custom_call" | custom-call | flops 12079595520 | bytes 884736 | tf_op jit(solution)/shard_map/pallas_call | solution.py:45
  45.2 0.3 collective-permute-done.18.late
  45.5 0.9 %shard_map.169 = (f32[9,256,128]{2,1,0:T(8,128)}, f32[256]{0:T(256)}) custom-call(f32[8,128]{1,0:T(8,128)S(1)} %get-tuple-element.113.bias_own, bf16[3,304,128]{2,1,0:T(8,128)(2,1)S(1)} %collective-permute-done.17.early, bf16[304,128]{1,0:T(8,128)(2,1)S(1)} %collective-permute-done.18.late, ...), custom_call_target="tpu_custom_call", output_to_operand_aliasing={{0}: (4, {})} | custom-call | bytes 884736 | tf_op jit(solution)/shard_map/pallas_call | solution.py:45
  (7 shorter events, 0.1 us)
Async XLA Ops:
  1.6 6.5 %collective-permute-start = (bf16[128,128]{1,0:T(8,128)(2,1)S(1)}, bf16[128,128]{1,0:T(8,128)(2,1)S(1)}, u32[]{:S(2)}, u32[]{:S(2)}) collective-permute-start(bf16[128,128]{1,0:T(8,128)(2,1)S(1)} %get-tuple-element.64), channel_id=1, source_target_pairs={{0,8},{1,9},{2,10},{3,11},{4,12},{5,13},{6,14},{7,15},{8,0},{9,1},... | collective-permute-start | bytes 98312 | tf_op jit(solution)/shard_map/ppermute | solution.py:128
  2.2 6.0 %collective-permute-start.1 = (bf16[128,128]{1,0:T(8,128)(2,1)S(1)}, bf16[128,128]{1,0:T(8,128)(2,1)S(1)}, u32[]{:S(2)}, u32[]{:S(2)}) collective-permute-start(bf16[128,128]{1,0:T(8,128)(2,1)S(1)} %get-tuple-element.65), channel_id=1, source_target_pairs={{0,4},{1,5},{2,6},{3,7},{4,0},{5,1},{6,2},{7,3},{8,16},{9,17},{10,... | collective-permute-start | bytes 98312 | tf_op jit(solution)/shard_map/ppermute | solution.py:128
  8.3 7.4 %collective-permute-start.3 = (bf16[32,128]{1,0:T(8,128)(2,1)S(1)}, bf16[32,128]{1,0:T(8,128)(2,1)S(1)}, u32[]{:S(2)}, u32[]{:S(2)}) collective-permute-start(bf16[32,128]{1,0:T(8,128)(2,1)S(1)} %get-tuple-element.82), channel_id=1, source_target_pairs={{0,1},{1,0},{2,3},{3,2},{4,5},{5,4},{6,7},{7,6},{8,9},{9,8},{10,11... | collective-permute-start | bytes 24584 | tf_op jit(solution)/shard_map/ppermute | solution.py:128
  9.8 6.3 %collective-permute-start.2 = (bf16[32,128]{1,0:T(8,128)(2,1)S(1)}, bf16[32,128]{1,0:T(8,128)(2,1)S(1)}, u32[]{:S(2)}, u32[]{:S(2)}) collective-permute-start(bf16[32,128]{1,0:T(8,128)(2,1)S(1)} %get-tuple-element.82), channel_id=1, source_target_pairs={{0,7},{1,2},{2,1},{3,4},{4,3},{5,6},{6,5},{7,0},{8,15},{9,10},{10,... | collective-permute-start | bytes 24584 | tf_op jit(solution)/shard_map/ppermute | solution.py:128
  17.1 1.6 %collective-permute-start.8 = (bf16[1152,128]{1,0:T(8,128)(2,1)S(1)}, bf16[1152,128]{1,0:T(8,128)(2,1)S(1)}, u32[]{:S(2)}, u32[]{:S(2)}) collective-permute-start(bf16[1152,128]{1,0:T(8,128)(2,1)S(1)} %get-tuple-element.106), channel_id=1, source_target_pairs={{0,8},{1,9},{2,10},{3,11},{4,12},{5,13},{6,14},{7,15},{8,0},{9,1},... | collective-permute-start | bytes 884744 | tf_op jit(solution)/shard_map/ppermute | solution.py:128
  18.8 6.2 %collective-permute-start.9 = (bf16[304,128]{1,0:T(8,128)(2,1)S(1)}, bf16[304,128]{1,0:T(8,128)(2,1)S(1)}, u32[]{:S(2)}, u32[]{:S(2)}) collective-permute-start(bf16[304,128]{1,0:T(8,128)(2,1)S(1)} %get-tuple-element.108), channel_id=1, source_target_pairs={{0,17},{1,16},{2,19},{3,18},{4,21},{5,20},{6,23},{7,22},{8,25},{9,... | collective-permute-start | bytes 233480 | tf_op jit(solution)/shard_map/ppermute | solution.py:128
  18.9 6.1 %collective-permute-start.10 = (bf16[304,128]{1,0:T(8,128)(2,1)S(1)}, bf16[304,128]{1,0:T(8,128)(2,1)S(1)}, u32[]{:S(2)}, u32[]{:S(2)}) collective-permute-start(bf16[304,128]{1,0:T(8,128)(2,1)S(1)} %get-tuple-element.109), channel_id=1, source_target_pairs={{0,16},{1,17},{2,18},{3,19},{4,20},{5,21},{6,22},{7,23},{8,24},{9,... | collective-permute-start | bytes 233480 | tf_op jit(solution)/shard_map/ppermute | solution.py:128
  19.3 6.6 %collective-permute-start.11 = (bf16[304,128]{1,0:T(8,128)(2,1)S(1)}, bf16[304,128]{1,0:T(8,128)(2,1)S(1)}, u32[]{:S(2)}, u32[]{:S(2)}) collective-permute-start(bf16[304,128]{1,0:T(8,128)(2,1)S(1)} %get-tuple-element.110), channel_id=1, source_target_pairs={{0,1},{1,0},{2,3},{3,2},{4,5},{5,4},{6,7},{7,6},{8,9},{9,8},{10,11... | collective-permute-start | bytes 233480 | tf_op jit(solution)/shard_map/ppermute | solution.py:128
  25.9 5.3 %collective-permute-start.12 = (bf16[304,128]{1,0:T(8,128)(2,1)S(1)}, bf16[304,128]{1,0:T(8,128)(2,1)S(1)}, u32[]{:S(2)}, u32[]{:S(2)}) collective-permute-start(bf16[304,128]{1,0:T(8,128)(2,1)S(1)} %shard_map.164.own), channel_id=1, source_target_pairs={{0,2},{1,3},{2,0},{3,1},{4,6},{5,7},{6,4},{7,5},{8,12},{9,13},{10,... | collective-permute-start | bytes 233480 | tf_op jit(solution)/shard_map/ppermute | solution.py:128
  26.0 6.2 %collective-permute-start.4 = (bf16[256,128]{1,0:T(8,128)(2,1)S(1)}, bf16[256,128]{1,0:T(8,128)(2,1)S(1)}, u32[]{:S(2)}, u32[]{:S(2)}) collective-permute-start(bf16[256,128]{1,0:T(8,128)(2,1)S(1)} %get-tuple-element.96), channel_id=1, source_target_pairs={{0,4},{1,5},{2,6},{3,7},{4,0},{5,1},{6,2},{7,3},{8,16},{9,17},{10,... | collective-permute-start | bytes 196616 | tf_op jit(solution)/shard_map/ppermute | solution.py:128
  29.7 2.5 %collective-permute-start.5 = (bf16[256,128]{1,0:T(8,128)(2,1)S(1)}, bf16[256,128]{1,0:T(8,128)(2,1)S(1)}, u32[]{:S(2)}, u32[]{:S(2)}) collective-permute-start(bf16[256,128]{1,0:T(8,128)(2,1)S(1)} %get-tuple-element.97), channel_id=1, source_target_pairs={{0,8},{1,9},{2,10},{3,11},{4,12},{5,13},{6,14},{7,15},{8,0},{9,1},... | collective-permute-start | bytes 196616 | tf_op jit(solution)/shard_map/ppermute | solution.py:128
  31.2 5.8 %collective-permute-start.13 = (bf16[304,128]{1,0:T(8,128)(2,1)S(1)}, bf16[304,128]{1,0:T(8,128)(2,1)S(1)}, u32[]{:S(2)}, u32[]{:S(2)}) collective-permute-start(bf16[304,128]{1,0:T(8,128)(2,1)S(1)} %shard_map.165.own), channel_id=1, source_target_pairs={{0,4},{1,5},{2,6},{3,7},{4,0},{5,1},{6,2},{7,3},{8,10},{9,11},{10,... | collective-permute-start | bytes 233480 | tf_op jit(solution)/shard_map/ppermute | solution.py:128
  32.3 8.2 %collective-permute-start.7 = (bf16[64,128]{1,0:T(8,128)(2,1)S(1)}, bf16[64,128]{1,0:T(8,128)(2,1)S(1)}, u32[]{:S(2)}, u32[]{:S(2)}) collective-permute-start(bf16[64,128]{1,0:T(8,128)(2,1)S(1)} %shard_map.160), channel_id=1, source_target_pairs={{0,1},{1,0},{2,3},{3,2},{4,5},{5,4},{6,7},{7,6},{8,9},{9,8},{10,11... | collective-permute-start | bytes 49160 | tf_op jit(solution)/shard_map/ppermute | solution.py:128
  34.4 6.4 %collective-permute-start.6 = (bf16[64,128]{1,0:T(8,128)(2,1)S(1)}, bf16[64,128]{1,0:T(8,128)(2,1)S(1)}, u32[]{:S(2)}, u32[]{:S(2)}) collective-permute-start(bf16[64,128]{1,0:T(8,128)(2,1)S(1)} %shard_map.160), channel_id=1, source_target_pairs={{0,7},{1,2},{2,1},{3,4},{4,3},{5,6},{6,5},{7,0},{8,15},{9,10},{10,... | collective-permute-start | bytes 49160 | tf_op jit(solution)/shard_map/ppermute | solution.py:128
  37.0 5.4 %collective-permute-start.16 = (bf16[304,128]{1,0:T(8,128)(2,1)S(1)}, bf16[304,128]{1,0:T(8,128)(2,1)S(1)}, u32[]{:S(2)}, u32[]{:S(2)}) collective-permute-start(bf16[304,128]{1,0:T(8,128)(2,1)S(1)} %shard_map.166.refs_0_), channel_id=1, source_target_pairs={{0,17},{1,16},{2,19},{3,18},{4,21},{5,20},{6,23},{7,22},{8,25},{9,... | collective-permute-start | bytes 233480 | tf_op jit(solution)/shard_map/ppermute | solution.py:128
  37.4 5.7 %collective-permute-start.15 = (bf16[304,128]{1,0:T(8,128)(2,1)S(1)}, bf16[304,128]{1,0:T(8,128)(2,1)S(1)}, u32[]{:S(2)}, u32[]{:S(2)}) collective-permute-start(bf16[304,128]{1,0:T(8,128)(2,1)S(1)} %shard_map.166.refs_0_), channel_id=1, source_target_pairs={{0,16},{1,17},{2,18},{3,19},{4,20},{5,21},{6,22},{7,23},{8,24},{9,... | collective-permute-start | bytes 233480 | tf_op jit(solution)/shard_map/ppermute | solution.py:128
  39.9 4.4 %collective-permute-start.14 = (bf16[304,128]{1,0:T(8,128)(2,1)S(1)}, bf16[304,128]{1,0:T(8,128)(2,1)S(1)}, u32[]{:S(2)}, u32[]{:S(2)}) collective-permute-start(bf16[304,128]{1,0:T(8,128)(2,1)S(1)} %shard_map.166.refs_0_), channel_id=1, source_target_pairs={{0,1},{1,0},{2,3},{3,2},{4,5},{5,4},{6,7},{7,6},{8,9},{9,8},{10,11... | collective-permute-start | bytes 233480 | tf_op jit(solution)/shard_map/ppermute | solution.py:128
  43.1 2.4 %collective-permute-start.17 = (bf16[3,304,128]{2,1,0:T(8,128)(2,1)S(1)}, bf16[3,304,128]{2,1,0:T(8,128)(2,1)S(1)}, u32[]{:S(2)}, u32[]{:S(2)}) collective-permute-start(bf16[3,304,128]{2,1,0:T(8,128)(2,1)S(1)} %shard_map.167.early), channel_id=1, source_target_pairs={{0,8},{1,9},{2,10},{3,11},{4,12},{5,13},{6,14},{7,15},{8,0},{9,1},... | collective-permute-start | bytes 700424 | tf_op jit(solution)/shard_map/ppermute | solution.py:128
  44.3 1.3 %collective-permute-start.18 = (bf16[304,128]{1,0:T(8,128)(2,1)S(1)}, bf16[304,128]{1,0:T(8,128)(2,1)S(1)}, u32[]{:S(2)}, u32[]{:S(2)}) collective-permute-start(bf16[304,128]{1,0:T(8,128)(2,1)S(1)} %collective-permute-done.14.late), channel_id=1, source_target_pairs={{0,8},{1,9},{2,10},{3,11},{4,12},{5,13},{6,14},{7,15},{8,0},{9,1},... | collective-permute-start | bytes 233480 | tf_op jit(solution)/shard_map/ppermute | solution.py:128

commit v12 on v11

--- a/solution.py
+++ b/solution.py
@@ -66,9 +66,9 @@
         self.plane = lat_count
         whole = [("lon", 1 << k) for k in range(1, lon_count.bit_length() - 1)]
         self.orders = ([("lat", 1)] + whole, [("lat", 1)] + whole[::-1])
-        step = 8 * self.plane
-        self.half_rows = -(-taps * self.half_gates // step) * step
+        self.half_rows = taps * self.half_gates
         self.chunk = self.half_rows // self.plane
+        self.chunk_gates = self.half_gates // self.plane
 
     def position(self):
         lat = 2 * lax.axis_index("band") + lax.axis_index("core")
@@ -437,13 +437,6 @@
                 sums[at : at + half_gates, :] = product[
                     half * half_gates : (half + 1) * half_gates, b * channels : (b + 1) * channels
                 ]
-    used = place.taps * half_gates
-    if place.half_rows > used:
-        for half in range(2):
-            at = half * place.half_rows
-            sums[at + used : at + place.half_rows, :] = jnp.zeros(
-                (place.half_rows - used, channels), F32
-            )
 
 
 def add_strip(place, half, sums, pre_strip, patches, out):
@@ -451,14 +444,14 @@
     gates = pre_strip[pl.ds(pl.multiple_of(half * half_gates, half_gates), half_gates), :]
     product = lax.dot_general(gates, patches[...], ACROSS, preferred_element_type=F32)
     base = half * place.half_rows
+    size = place.chunk_gates
     for tap in range(place.taps):
         at = pl.ds(pl.multiple_of(base + tap * half_gates, 8), half_gates)
         value = sums[at, :] + product[:, tap * channels : (tap + 1) * channels]
-        out[tap * half_gates : (tap + 1) * half_gates, :] = value.astype(out.dtype)
-    used = place.taps * half_gates
-    if place.half_rows > used:
-        rest = jnp.zeros((place.half_rows - used, channels), out.dtype)
-        out[used:, :] = rest
+        value = value.astype(out.dtype)
+        for index in range(place.plane):
+            to = (index * place.taps + tap) * size
+            out[to : to + size, :] = value[index * size : (index + 1) * size]
 
 
 def strip_kernel(
@@ -604,7 +597,7 @@
 
 
 def join_kernel(*refs):
-    blocks, out = refs[:-2], refs[-1]
+    blocks, out = refs[:-3], refs[-1]
     for index, block in enumerate(blocks):
         out[index] = block[...]
 
@@ -616,54 +609,60 @@
     out[BIAS_ROWS:, :] = ((here[BIAS_ROWS:] + there[BIAS_ROWS:]) * scale).astype(BF16)
 
 
-def store_half(place, half, blocks, out, wide, left):
-    chunk, half_gates = place.chunk, place.half_gates
-    gates = pl.ds(pl.multiple_of(half * half_gates, half_gates), half_gates)
+def store_blocks(place, half, blocks, out, wide, left):
+    size = place.chunk_gates
     rank = place.plane_rank()
-    for step, block in enumerate(blocks):
-        at = pl.ds(pl.multiple_of((rank ^ step) * chunk, 8), chunk)
-        wide[at, :] = block[BIAS_ROWS:, :].astype(F32)
     copies = []
-    for tap in range(place.taps):
-        source = wide.at[tap * half_gates : (tap + 1) * half_gates, :]
-        copies.append(pltpu.make_async_copy(source, out.at[tap, gates, :], left.at[tap]))
+    for step, block in blocks:
+        index = len(copies)
+        value = block[BIAS_ROWS:, :].astype(F32)
+        wide[index] = value.reshape(place.taps, size, value.shape[1])
+        first = pl.multiple_of(half * place.half_gates + (rank ^ step) * size, 8)
+        target = out.at[:, pl.ds(first, size), :]
+        copies.append(pltpu.make_async_copy(wide.at[index], target, left.at[index]))
         copies[-1].start()
     return copies
 
 
-def in_steps(place, early, late):
-    return [early.at[0], late] + [early.at[index] for index in range(1, place.plane - 1)]
-
-
-def own_half_kernel(place, late, early, out, bias_out, wide, left):
-    blocks = in_steps(place, early, late)
-    copies = store_half(place, place.rank(0), blocks, out, wide, left)
+def plane_bias(place, blocks):
     rank = place.plane_rank()
-    bias = decode(blocks[0][0:BIAS_ROWS, :].astype(F32))
-    for step in range(1, place.plane):
-        bias = pick(rank == step, decode(blocks[step][0:BIAS_ROWS, :].astype(F32)), bias)
-    bias_out[...] = bias
+    bias = jnp.zeros((8, blocks[0][1].shape[1]), F32)
+    for step, block in blocks:
+        bias = pick(rank == step, decode(block[0:BIAS_ROWS, :].astype(F32)), bias)
+    return bias
+
+
+def first_store_kernel(place, part, last, out, done_out, wide, left):
+    done_out[...] = jnp.zeros(done_out.shape, F32)
+    blocks = [(0, part), (place.plane - 1, last)]
+    for copy in store_blocks(place, place.rank(0), blocks, out, wide, left):
+        copy.wait()
+
+
+def second_store_kernel(place, *refs):
+    count = place.plane
+    own, early, out, bias_out, wide, left = refs[:count], refs[count], *refs[-4:]
+    rank = place.rank(0)
+    own = list(enumerate(own))
+    other = [(0, early.at[0]), (count - 1, early.at[1])]
+    copies = store_blocks(place, rank, own[1:-1], out, wide.at[0], left.at[0])
+    copies += store_blocks(place, 1 - rank, other, out, wide.at[1], left.at[1])
+    bias_out[...] = plane_bias(place, own) + plane_bias(place, other)
     for copy in copies:
         copy.wait()
 
 
-def other_half_kernel(
-    place, bias_own, early, late, after, out_before, out, bias_out, wide, bias_here, left
-):
-    del after, out_before
-    blocks = in_steps(place, early, late)
-    copies = store_half(place, 1 - place.rank(0), blocks, out, wide, left)
-    rank = place.plane_rank()
-    bias = decode(blocks[0][0:BIAS_ROWS, :].astype(F32))
-    for step in range(1, place.plane):
-        bias = pick(rank == step, decode(blocks[step][0:BIAS_ROWS, :].astype(F32)), bias)
-    bias += bias_own[...]
+def third_store_kernel(place, bias_before, late, out_before, out, bias_out, wide, bias_here, left):
+    del out_before
+    rank = place.rank(0)
+    blocks = [(step, late.at[step - 1]) for step in range(1, place.plane - 1)]
+    copies = store_blocks(place, 1 - rank, blocks, out, wide, left)
+    bias = bias_before[...] + plane_bias(place, blocks)
     width = bias.shape[1]
     for index in range(bias_here.shape[0] // width):
         bias_here[pl.ds(index * width, width)] = bias[index]
-    bias_copy = pltpu.make_async_copy(bias_here, bias_out, left.at[place.taps])
-    bias_copy.start()
-    bias_copy.wait()
+    copies.append(pltpu.make_async_copy(bias_here, bias_out, left.at[len(copies)]))
+    copies[-1].start()
     for copy in copies:
         copy.wait()
 
@@ -992,30 +991,43 @@
         flops=40 * gate_count * channels * cells * 9,
         moved=2_000_000,
     )(field, turned, pre_outer, pre_inner, pre_outer_columns, pre_inner_columns)
-    early = call(join_kernel, sds((place.plane - 1, *block.shape), BF16))(
-        part, *received[1:], field_done
+    last = received[-1]
+    early = call(join_kernel, sds((2, *block.shape), BF16))(part, last, target_here, target_here)
+    early_other = permuted(early, place.phase_pairs(0))
+    wide_block = (place.taps, place.chunk_gates, channels)
+    grad_kernel, stored = call(
+        bind(first_store_kernel, place),
+        (sds(kernel_weights.shape, F32), token),
+        [pltpu.VMEM((2, *wide_block), F32), pltpu.SemaphoreType.DMA((2,))],
+        leaving=1,
+    )(part, last)
+    late = call(join_kernel, sds((place.plane - 2, *block.shape), BF16))(
+        *received[:-1], field_done, stored
     )
-    late = received[0]
-    early_other = permuted(early, place.phase_pairs(0))
     late_other = permuted(late, place.phase_pairs(0))
-    half = [pltpu.VMEM((place.half_rows, channels), F32)]
     grad_kernel, bias = call(
-        bind(own_half_kernel, place),
+        bind(second_store_kernel, place),
         (sds(kernel_weights.shape, F32), sds((8, channels), F32)),
-        half + [pltpu.SemaphoreType.DMA((place.taps,))],
+        [
+            pltpu.VMEM((2, place.plane, *wide_block), F32),
+            pltpu.SemaphoreType.DMA((2, place.plane)),
+        ],
+        remote=1,
         leaving=1,
-        flops=40 * gate_count * channels * cells * 9,
-        moved=6 * place.half_rows * channels,
-    )(late, early)
+        aliases={place.plane + 1: 0},
+    )(part, *received, early_other, grad_kernel)
     grad_kernel, grad_bias = call(
-        bind(other_half_kernel, place),
+        bind(third_store_kernel, place),
         (sds(kernel_weights.shape, F32), sds((gate_count,), F32)),
-        half + [pltpu.VMEM((gate_count,), F32), pltpu.SemaphoreType.DMA((place.taps + 1,))],
+        [
+            pltpu.VMEM((place.plane - 2, *wide_block), F32),
+            pltpu.VMEM((gate_count,), F32),
+            pltpu.SemaphoreType.DMA((place.plane - 1,)),
+        ],
         remote=1,
         leaving=2,
-        aliases={4: 0},
-        moved=6 * place.half_rows * channels,
-    )(bias, early_other, late_other, target_here, grad_kernel)
+        aliases={2: 0},
+    )(bias, late_other, grad_kernel)
     shape = hidden_prev.shape
     return (
         hidden_next,

time: 46.7 us -> 46.7 us (level)
  waiting for transfers between devices: 7.49 us -> 6.92 us
  Pallas kernels: 13.1 us -> 13.6 us
    ppermute x19, waiting for transfers between devices: 7.49 us -> 6.92 us  [permuted(): return lax.ppermute(value, AXES, pairs)]
    pallas_call x17 -> x19, Pallas kernels: 13.1 us -> 13.6 us  [run(): pl.pallas_call(kernel, out_shape=out_shape, in_specs=[VMEM] * near + [HBM...]
  transfers between devices with their start and end apart: 19 -> 19, of which waited for: 10 -> 9; matrix products, arithmetic and copies ran while one was open for 0% -> 0% of each run, Pallas kernels for 22% -> 23%
where the time goes in v12:
time: 46.7 us; the launch traced here: 46.5 us
  starting transfers between devices  25.1 us (54%)
  Pallas kernels  13.6 us (29%)
  waiting for transfers between devices  6.92 us (15%)
  between operations  0.81 us (2%)
    ppermute x19, starting transfers between devices, permuted(): return lax.ppermute(value, AXES, pairs)  25.1 us
    pallas_call x19, Pallas kernels, run(): pl.pallas_call(kernel, out_shape=out_shape, in_specs=[VMEM] * near + [HBM...  13.6 us
    ppermute x19, waiting for transfers between devices, permuted(): return lax.ppermute(value, AXES, pairs)  6.92 us
  transfers between devices with their start and end apart: 19, of which 9 were waited for; matrix products, arithmetic and copies ran while one was open for 0% of the time, Pallas kernels for 23%

profile of v12, /device:TPU:0, one launch (start us, length us, event | category | flops | bytes accessed | tf_op | source)
XLA Modules:
  0.0 46.5 jit_solution(11379559802270643785)
XLA Ops:
  0.6 1.0 %shard_map.153 = (bf16[128,128]{1,0:T(8,128)(2,1)S(1)}, bf16[128,128]{1,0:T(8,128)(2,1)S(1)}, f32[1024,128]{1,0:T(8,128)S(1)}) custom-call(bf16[64,8,128]{2,1,0:T(8,128)(2,1)} %below.1, bf16[64,8,128]{2,1,0:T(8,128)(2,1)} %hidden.1), custom_call_target="tpu_custom_call" | custom-call | bytes 524288 | tf_op jit(solution)/shard_map/pallas_call | solution.py:45
  1.6 0.5 %collective-permute-start = (bf16[128,128]{1,0:T(8,128)(2,1)S(1)}, bf16[128,128]{1,0:T(8,128)(2,1)S(1)}, u32[]{:S(2)}, u32[]{:S(2)}) collective-permute-start(bf16[128,128]{1,0:T(8,128)(2,1)S(1)} %get-tuple-element.66), channel_id=1, source_target_pairs={{0,8},{1,9},{2,10},{3,11},{4,12},{5,13},{6,14},{7,15},{8,0},{9,1},... | collective-permute-start | bytes 98312 | tf_op jit(solution)/shard_map/ppermute | solution.py:128
  2.2 3.7 %collective-permute-start.1 = (bf16[128,128]{1,0:T(8,128)(2,1)S(1)}, bf16[128,128]{1,0:T(8,128)(2,1)S(1)}, u32[]{:S(2)}, u32[]{:S(2)}) collective-permute-start(bf16[128,128]{1,0:T(8,128)(2,1)S(1)} %get-tuple-element.67), channel_id=1, source_target_pairs={{0,4},{1,5},{2,6},{3,7},{4,0},{5,1},{6,2},{7,3},{8,16},{9,17},{10,... | collective-permute-start | bytes 98312 | tf_op jit(solution)/shard_map/ppermute | solution.py:128
  5.8 2.3 %shard_map.154 = (bf16[8,128,128]{2,1,0:T(8,128)(2,1)S(1)}, f32[128,128]{1,0:T(8,128)S(1)}, f32[128,128]{1,0:T(8,128)S(1)}, f32[64,128]{1,0:T(8,128)S(1)}, f32[6...) custom-call(f32[1024,128]{1,0:T(8,128)S(1)} %get-tuple-element.64.wi, ...), custom_call_target="tpu_custom_call" | custom-call | bytes 6000000 | tf_op jit(solution)/shard_map/pallas_call | solution.py:45
  8.1 0.0 collective-permute-done.inner_row.inner
  8.1 0.2 shard_map.156
  8.3 1.5 %collective-permute-start.3 = (bf16[32,128]{1,0:T(8,128)(2,1)S(1)}, bf16[32,128]{1,0:T(8,128)(2,1)S(1)}, u32[]{:S(2)}, u32[]{:S(2)}) collective-permute-start(bf16[32,128]{1,0:T(8,128)(2,1)S(1)} %get-tuple-element.84), channel_id=1, source_target_pairs={{0,1},{1,0},{2,3},{3,2},{4,5},{5,4},{6,7},{7,6},{8,9},{9,8},{10,11... | collective-permute-start | bytes 24584 | tf_op jit(solution)/shard_map/ppermute | solution.py:128
  9.8 3.7 %collective-permute-start.2 = (bf16[32,128]{1,0:T(8,128)(2,1)S(1)}, bf16[32,128]{1,0:T(8,128)(2,1)S(1)}, u32[]{:S(2)}, u32[]{:S(2)}) collective-permute-start(bf16[32,128]{1,0:T(8,128)(2,1)S(1)} %get-tuple-element.84), channel_id=1, source_target_pairs={{0,7},{1,2},{2,1},{3,4},{4,3},{5,6},{6,5},{7,0},{8,15},{9,10},{10,... | collective-permute-start | bytes 24584 | tf_op jit(solution)/shard_map/ppermute | solution.py:128
  13.5 2.2 %shard_map.155 = (f32[512,128]{1,0:T(8,128)S(1)}, f32[512,128]{1,0:T(8,128)S(1)}, f32[512,128]{1,0:T(8,128)S(1)}, bf16[256,1024]{1,0:T(8,128)(2,1)S(1)}, bf16[12...) custom-call(bf16[8,128,128]{2,1,0:T(8,128)(2,1)S(1)} %get-tuple-element.65.rows_in, ...), custom_call_target="tpu_custom_call" | custom-call | flops 1207959552 | bytes 6000000 | tf_op jit(solution)/shard_map/pallas_call | solution.py:45
  15.7 0.4 collective-permute-done.2.outer_column
  16.2 0.9 %shard_map.157 = (bf16[1152,128]{1,0:T(8,128)(2,1)S(1)}, bf16[256,128]{1,0:T(8,128)(2,1)S(1)}, f32[256,128]{1,0:T(8,128)S(1)}, bf16[1152,128]{1,0:T(8,128)(2,1)S...) custom-call(bf16[128,128]{1,0:T(8,128)(2,1)S(1)} %get-tuple-element.82.edge, ...), custom_call_target="tpu_custom_call" | custom-call | tf_op jit(solution)/shard_map/pallas_call | solution.py:45
  17.1 0.1 collective-permute-start.8
  17.1 0.3 shard_map.162
  17.4 1.3 %collective-permute-done.8.received = bf16[1152,128]{1,0:T(8,128)(2,1)S(1)} collective-permute-done((bf16[1152,128]{1,0:T(8,128)(2,1)S(1)}, bf16[1152,128]{1,0:T(8,128)(2,1)S(1)}, u32[]{:S(2)}, u32[]{:S(2)}) %collective-permute-start.8) | collective-permute-done | bytes 294944 | tf_op jit(solution)/shard_map/ppermute | solution.py:128
  18.7 0.1 shard_map.163
  18.8 0.1 collective-permute-start.9
  18.9 0.4 collective-permute-start.10
  19.3 3.1 %collective-permute-start.11 = (bf16[304,128]{1,0:T(8,128)(2,1)S(1)}, bf16[304,128]{1,0:T(8,128)(2,1)S(1)}, u32[]{:S(2)}, u32[]{:S(2)}) collective-permute-start(bf16[304,128]{1,0:T(8,128)(2,1)S(1)} %get-tuple-element.112), channel_id=1, source_target_pairs={{0,1},{1,0},{2,3},{3,2},{4,5},{5,4},{6,7},{7,6},{8,9},{9,8},{10,11... | collective-permute-start | bytes 233480 | tf_op jit(solution)/shard_map/ppermute | solution.py:128
  22.4 1.4 %shard_map.158 = (bf16[64,8,128]{2,1,0:T(8,128)(2,1)}, f32[512,128]{1,0:T(8,128)}, f32[512,128]{1,0:T(8,128)}, bf16[256,1024]{1,0:T(8,128)(2,1)S(1)}, bf16[256,1...) custom-call(f32[512,128]{1,0:T(8,128)S(1)} %get-tuple-element.77.hidden, f32[512,128]{1,0:T(8,128)S(1)} %get-tuple-element.78.cell, ...), custom_call_target="tpu_custom_call" | custom-call | bytes 4000000 | tf_op jit(solution)/shard_map/pallas_call | solution.py:45
  23.7 1.1 %shard_map.159 = (f32[1024,128]{1,0:T(8,128)S(1)}, bf16[3,128,768]{2,1,0:T(8,128)(2,1)S(1)}, f32[8,128]{1,0:T(8,128)S(1)}) custom-call(bf16[256,1024]{1,0:T(8,128)(2,1)S(1)} %get-tuple-element.95.pre, bf16[256,1152]{1,0:T(8,128)(2,1)S(1)} %get-tuple-element.70.weights), custom_call_target="tpu_custom_call" | custom-call | flops 603979776 | bytes 3000000 | tf_op jit(solution)/shard_map/pallas_call | solution.py:45
  24.8 0.2 collective-permute-done.9.refs_0_
  25.0 0.0 collective-permute-done.10.refs_1_
  25.0 0.9 %collective-permute-done.11.refs_2_ = bf16[304,128]{1,0:T(8,128)(2,1)S(1)} collective-permute-done((bf16[304,128]{1,0:T(8,128)(2,1)S(1)}, bf16[304,128]{1,0:T(8,128)(2,1)S(1)}, u32[]{:S(2)}, u32[]{:S(2)}) %collective-permute-start.11) | collective-permute-done | bytes 77856 | tf_op jit(solution)/shard_map/ppermute | solution.py:128
  25.9 0.1 collective-permute-start.12
  26.0 3.7 %collective-permute-start.4 = (bf16[256,128]{1,0:T(8,128)(2,1)S(1)}, bf16[256,128]{1,0:T(8,128)(2,1)S(1)}, u32[]{:S(2)}, u32[]{:S(2)}) collective-permute-start(bf16[256,128]{1,0:T(8,128)(2,1)S(1)} %get-tuple-element.98), channel_id=1, source_target_pairs={{0,4},{1,5},{2,6},{3,7},{4,0},{5,1},{6,2},{7,3},{8,16},{9,17},{10,... | collective-permute-start | bytes 196616 | tf_op jit(solution)/shard_map/ppermute | solution.py:128
  29.7 0.0 collective-permute-start.5
  29.7 1.5 %collective-permute-done.12.received = bf16[304,128]{1,0:T(8,128)(2,1)S(1)} collective-permute-done((bf16[304,128]{1,0:T(8,128)(2,1)S(1)}, bf16[304,128]{1,0:T(8,128)(2,1)S(1)}, u32[]{:S(2)}, u32[]{:S(2)}) %collective-permute-start.12) | collective-permute-done | bytes 77856 | tf_op jit(solution)/shard_map/ppermute | solution.py:128
  31.2 0.9 %collective-permute-start.13 = (bf16[304,128]{1,0:T(8,128)(2,1)S(1)}, bf16[304,128]{1,0:T(8,128)(2,1)S(1)}, u32[]{:S(2)}, u32[]{:S(2)}) collective-permute-start(bf16[304,128]{1,0:T(8,128)(2,1)S(1)} %shard_map.165.own), channel_id=1, source_target_pairs={{0,4},{1,5},{2,6},{3,7},{4,0},{5,1},{6,2},{7,3},{8,10},{9,11},{10,... | collective-permute-start | bytes 233480 | tf_op jit(solution)/shard_map/ppermute | solution.py:128
  32.1 0.0 collective-permute-done.4.outer.outer_row
  32.1 0.0 collective-permute-done.5.inner.inner_row
  32.1 0.2 shard_map.160
  32.3 2.1 %collective-permute-start.7 = (bf16[64,128]{1,0:T(8,128)(2,1)S(1)}, bf16[64,128]{1,0:T(8,128)(2,1)S(1)}, u32[]{:S(2)}, u32[]{:S(2)}) collective-permute-start(bf16[64,128]{1,0:T(8,128)(2,1)S(1)} %shard_map.160), channel_id=1, source_target_pairs={{0,1},{1,0},{2,3},{3,2},{4,5},{5,4},{6,7},{7,6},{8,9},{9,8},{10,11... | collective-permute-start | bytes 49160 | tf_op jit(solution)/shard_map/ppermute | solution.py:128
  34.4 1.7 %collective-permute-start.6 = (bf16[64,128]{1,0:T(8,128)(2,1)S(1)}, bf16[64,128]{1,0:T(8,128)(2,1)S(1)}, u32[]{:S(2)}, u32[]{:S(2)}) collective-permute-start(bf16[64,128]{1,0:T(8,128)(2,1)S(1)} %shard_map.160), channel_id=1, source_target_pairs={{0,7},{1,2},{2,1},{3,4},{4,3},{5,6},{6,5},{7,0},{8,15},{9,10},{10,... | collective-permute-start | bytes 49160 | tf_op jit(solution)/shard_map/ppermute | solution.py:128
  36.1 0.9 %collective-permute-done.13.received = bf16[304,128]{1,0:T(8,128)(2,1)S(1)} collective-permute-done((bf16[304,128]{1,0:T(8,128)(2,1)S(1)}, bf16[304,128]{1,0:T(8,128)(2,1)S(1)}, u32[]{:S(2)}, u32[]{:S(2)}) %collective-permute-start.13) | collective-permute-done | bytes 77856 | tf_op jit(solution)/shard_map/ppermute | solution.py:128
  37.0 0.4 collective-permute-start.16
  37.4 2.5 %collective-permute-start.15 = (bf16[304,128]{1,0:T(8,128)(2,1)S(1)}, bf16[304,128]{1,0:T(8,128)(2,1)S(1)}, u32[]{:S(2)}, u32[]{:S(2)}) collective-permute-start(bf16[304,128]{1,0:T(8,128)(2,1)S(1)} %shard_map.166.refs_0_.part), channel_id=1, source_target_pairs={{0,16},{1,17},{2,18},{3,19},{4,20},{5,21},{6,22},{7,23},{8,24},{9,... | collective-permute-start | bytes 233480 | tf_op jit(solution)/shard_map/ppermute | solution.py:128
  39.9 0.7 %collective-permute-start.14 = (bf16[304,128]{1,0:T(8,128)(2,1)S(1)}, bf16[304,128]{1,0:T(8,128)(2,1)S(1)}, u32[]{:S(2)}, u32[]{:S(2)}) collective-permute-start(bf16[304,128]{1,0:T(8,128)(2,1)S(1)} %shard_map.166.refs_0_.part), channel_id=1, source_target_pairs={{0,1},{1,0},{2,3},{3,2},{4,5},{5,4},{6,7},{7,6},{8,9},{9,8},{10,11... | collective-permute-start | bytes 233480 | tf_op jit(solution)/shard_map/ppermute | solution.py:128
  40.6 0.3 collective-permute-done.6.outer_column
  40.8 1.6 %shard_map.161 = (bf16[64,8,128]{2,1,0:T(8,128)(2,1)}, bf16[64,8,128]{2,1,0:T(8,128)(2,1)}, f32[8,128]{1,0:T(8,128)S(1)}) custom-call(f32[1024,128]{1,0:T(8,128)S(1)} %get-tuple-element.96.wide, bf16[3,128,768]{2,1,0:T(8,128)(2,1)S(1)} %get-tuple-element.97.turned, bf16[256,128]{1,0:T(8,128)(2,1)S(1)} %collective-permute-done.4.outer.outer_row, ...), custom_call_target="tpu_custom_call" | custom-call | flops 12079595520 | bytes 2000000 | tf_op jit(solution)/shard_map/pallas_call | solution.py:45
  42.4 0.0 collective-permute-done.16.refs_1_.last.refs_3_
  42.4 0.1 collective-permute-start.17
  42.5 0.7 %shard_map.168 = (f32[9,256,128]{2,1,0:T(8,128)}, f32[8,128]{1,0:T(8,128)S(1)}) custom-call(bf16[304,128]{1,0:T(8,128)(2,1)S(1)} %shard_map.166.refs_0_.part, bf16[304,128]{1,0:T(8,128)(2,1)S(1)} %collective-permute-done.16.refs_1_.last.refs_3_), custom_call_target="tpu_custom_call" | custom-call | tf_op jit(solution)/shard_map/pallas_call | solution.py:45
  43.2 0.0 collective-permute-done.15.refs_2_.refs_1_
  43.2 1.0 %collective-permute-done.14.refs_1_.refs_0_ = bf16[304,128]{1,0:T(8,128)(2,1)S(1)} collective-permute-done((bf16[304,128]{1,0:T(8,128)(2,1)S(1)}, bf16[304,128]{1,0:T(8,128)(2,1)S(1)}, u32[]{:S(2)}, u32[]{:S(2)}) %collective-permute-start.14) | collective-permute-done | bytes 77856 | tf_op jit(solution)/shard_map/ppermute | solution.py:128
  44.3 0.1 collective-permute-start.18
  44.4 0.9 %shard_map.169 = (f32[9,256,128]{2,1,0:T(8,128)}, f32[8,128]{1,0:T(8,128)S(1)}) custom-call(bf16[304,128]{1,0:T(8,128)(2,1)S(1)} %shard_map.166.refs_0_.part, bf16[304,128]{1,0:T(8,128)(2,1)S(1)} %collective-permute-done.14.refs_1_.refs_0_, bf16[304,128]{1,0:T(8,128)(2,1)S(1)} %collective-permute-done.15.refs_2_.refs_1_, ...), custom_call_target="tpu_custom_call", output_to_operand_aliasing={{0}: (5, {})} | custom-call | tf_op jit(solution)/shard_map/pallas_call | solution.py:45
  45.3 0.5 collective-permute-done.18.late
  45.7 0.8 %shard_map.171 = (f32[9,256,128]{2,1,0:T(8,128)}, f32[256]{0:T(256)}) custom-call(f32[8,128]{1,0:T(8,128)S(1)} %get-tuple-element.115.bias_before, bf16[2,304,128]{2,1,0:T(8,128)(2,1)S(1)} %collective-permute-done.18.late, f32[9,256,128]{2,1,0:T(8,128)} %get-tuple-element.118.out_before), custom_call_target="tpu_custom_call", output_to_operand_aliasing={{0}: (2, {})} | custom-call | tf_op jit(solution)/shard_map/pallas_call | solution.py:45
  (9 shorter events, 0.1 us)
Async XLA Ops:
  1.6 6.5 %collective-permute-start = (bf16[128,128]{1,0:T(8,128)(2,1)S(1)}, bf16[128,128]{1,0:T(8,128)(2,1)S(1)}, u32[]{:S(2)}, u32[]{:S(2)}) collective-permute-start(bf16[128,128]{1,0:T(8,128)(2,1)S(1)} %get-tuple-element.66), channel_id=1, source_target_pairs={{0,8},{1,9},{2,10},{3,11},{4,12},{5,13},{6,14},{7,15},{8,0},{9,1},... | collective-permute-start | bytes 98312 | tf_op jit(solution)/shard_map/ppermute | solution.py:128
  2.2 6.0 %collective-permute-start.1 = (bf16[128,128]{1,0:T(8,128)(2,1)S(1)}, bf16[128,128]{1,0:T(8,128)(2,1)S(1)}, u32[]{:S(2)}, u32[]{:S(2)}) collective-permute-start(bf16[128,128]{1,0:T(8,128)(2,1)S(1)} %get-tuple-element.67), channel_id=1, source_target_pairs={{0,4},{1,5},{2,6},{3,7},{4,0},{5,1},{6,2},{7,3},{8,16},{9,17},{10,... | collective-permute-start | bytes 98312 | tf_op jit(solution)/shard_map/ppermute | solution.py:128
  8.3 7.4 %collective-permute-start.3 = (bf16[32,128]{1,0:T(8,128)(2,1)S(1)}, bf16[32,128]{1,0:T(8,128)(2,1)S(1)}, u32[]{:S(2)}, u32[]{:S(2)}) collective-permute-start(bf16[32,128]{1,0:T(8,128)(2,1)S(1)} %get-tuple-element.84), channel_id=1, source_target_pairs={{0,1},{1,0},{2,3},{3,2},{4,5},{5,4},{6,7},{7,6},{8,9},{9,8},{10,11... | collective-permute-start | bytes 24584 | tf_op jit(solution)/shard_map/ppermute | solution.py:128
  9.8 6.3 %collective-permute-start.2 = (bf16[32,128]{1,0:T(8,128)(2,1)S(1)}, bf16[32,128]{1,0:T(8,128)(2,1)S(1)}, u32[]{:S(2)}, u32[]{:S(2)}) collective-permute-start(bf16[32,128]{1,0:T(8,128)(2,1)S(1)} %get-tuple-element.84), channel_id=1, source_target_pairs={{0,7},{1,2},{2,1},{3,4},{4,3},{5,6},{6,5},{7,0},{8,15},{9,10},{10,... | collective-permute-start | bytes 24584 | tf_op jit(solution)/shard_map/ppermute | solution.py:128
  17.1 1.6 %collective-permute-start.8 = (bf16[1152,128]{1,0:T(8,128)(2,1)S(1)}, bf16[1152,128]{1,0:T(8,128)(2,1)S(1)}, u32[]{:S(2)}, u32[]{:S(2)}) collective-permute-start(bf16[1152,128]{1,0:T(8,128)(2,1)S(1)} %get-tuple-element.108), channel_id=1, source_target_pairs={{0,8},{1,9},{2,10},{3,11},{4,12},{5,13},{6,14},{7,15},{8,0},{9,1},... | collective-permute-start | bytes 884744 | tf_op jit(solution)/shard_map/ppermute | solution.py:128
  18.8 6.2 %collective-permute-start.9 = (bf16[304,128]{1,0:T(8,128)(2,1)S(1)}, bf16[304,128]{1,0:T(8,128)(2,1)S(1)}, u32[]{:S(2)}, u32[]{:S(2)}) collective-permute-start(bf16[304,128]{1,0:T(8,128)(2,1)S(1)} %get-tuple-element.110), channel_id=1, source_target_pairs={{0,17},{1,16},{2,19},{3,18},{4,21},{5,20},{6,23},{7,22},{8,25},{9,... | collective-permute-start | bytes 233480 | tf_op jit(solution)/shard_map/ppermute | solution.py:128
  18.9 6.1 %collective-permute-start.10 = (bf16[304,128]{1,0:T(8,128)(2,1)S(1)}, bf16[304,128]{1,0:T(8,128)(2,1)S(1)}, u32[]{:S(2)}, u32[]{:S(2)}) collective-permute-start(bf16[304,128]{1,0:T(8,128)(2,1)S(1)} %get-tuple-element.111), channel_id=1, source_target_pairs={{0,16},{1,17},{2,18},{3,19},{4,20},{5,21},{6,22},{7,23},{8,24},{9,... | collective-permute-start | bytes 233480 | tf_op jit(solution)/shard_map/ppermute | solution.py:128
  19.3 6.6 %collective-permute-start.11 = (bf16[304,128]{1,0:T(8,128)(2,1)S(1)}, bf16[304,128]{1,0:T(8,128)(2,1)S(1)}, u32[]{:S(2)}, u32[]{:S(2)}) collective-permute-start(bf16[304,128]{1,0:T(8,128)(2,1)S(1)} %get-tuple-element.112), channel_id=1, source_target_pairs={{0,1},{1,0},{2,3},{3,2},{4,5},{5,4},{6,7},{7,6},{8,9},{9,8},{10,11... | collective-permute-start | bytes 233480 | tf_op jit(solution)/shard_map/ppermute | solution.py:128
  25.9 5.3 %collective-permute-start.12 = (bf16[304,128]{1,0:T(8,128)(2,1)S(1)}, bf16[304,128]{1,0:T(8,128)(2,1)S(1)}, u32[]{:S(2)}, u32[]{:S(2)}) collective-permute-start(bf16[304,128]{1,0:T(8,128)(2,1)S(1)} %shard_map.164.own), channel_id=1, source_target_pairs={{0,2},{1,3},{2,0},{3,1},{4,6},{5,7},{6,4},{7,5},{8,12},{9,13},{10,... | collective-permute-start | bytes 233480 | tf_op jit(solution)/shard_map/ppermute | solution.py:128
  26.0 6.2 %collective-permute-start.4 = (bf16[256,128]{1,0:T(8,128)(2,1)S(1)}, bf16[256,128]{1,0:T(8,128)(2,1)S(1)}, u32[]{:S(2)}, u32[]{:S(2)}) collective-permute-start(bf16[256,128]{1,0:T(8,128)(2,1)S(1)} %get-tuple-element.98), channel_id=1, source_target_pairs={{0,4},{1,5},{2,6},{3,7},{4,0},{5,1},{6,2},{7,3},{8,16},{9,17},{10,... | collective-permute-start | bytes 196616 | tf_op jit(solution)/shard_map/ppermute | solution.py:128
  29.7 2.5 %collective-permute-start.5 = (bf16[256,128]{1,0:T(8,128)(2,1)S(1)}, bf16[256,128]{1,0:T(8,128)(2,1)S(1)}, u32[]{:S(2)}, u32[]{:S(2)}) collective-permute-start(bf16[256,128]{1,0:T(8,128)(2,1)S(1)} %get-tuple-element.99), channel_id=1, source_target_pairs={{0,8},{1,9},{2,10},{3,11},{4,12},{5,13},{6,14},{7,15},{8,0},{9,1},... | collective-permute-start | bytes 196616 | tf_op jit(solution)/shard_map/ppermute | solution.py:128
  31.2 5.8 %collective-permute-start.13 = (bf16[304,128]{1,0:T(8,128)(2,1)S(1)}, bf16[304,128]{1,0:T(8,128)(2,1)S(1)}, u32[]{:S(2)}, u32[]{:S(2)}) collective-permute-start(bf16[304,128]{1,0:T(8,128)(2,1)S(1)} %shard_map.165.own), channel_id=1, source_target_pairs={{0,4},{1,5},{2,6},{3,7},{4,0},{5,1},{6,2},{7,3},{8,10},{9,11},{10,... | collective-permute-start | bytes 233480 | tf_op jit(solution)/shard_map/ppermute | solution.py:128
  32.3 8.2 %collective-permute-start.7 = (bf16[64,128]{1,0:T(8,128)(2,1)S(1)}, bf16[64,128]{1,0:T(8,128)(2,1)S(1)}, u32[]{:S(2)}, u32[]{:S(2)}) collective-permute-start(bf16[64,128]{1,0:T(8,128)(2,1)S(1)} %shard_map.160), channel_id=1, source_target_pairs={{0,1},{1,0},{2,3},{3,2},{4,5},{5,4},{6,7},{7,6},{8,9},{9,8},{10,11... | collective-permute-start | bytes 49160 | tf_op jit(solution)/shard_map/ppermute | solution.py:128
  34.4 6.4 %collective-permute-start.6 = (bf16[64,128]{1,0:T(8,128)(2,1)S(1)}, bf16[64,128]{1,0:T(8,128)(2,1)S(1)}, u32[]{:S(2)}, u32[]{:S(2)}) collective-permute-start(bf16[64,128]{1,0:T(8,128)(2,1)S(1)} %shard_map.160), channel_id=1, source_target_pairs={{0,7},{1,2},{2,1},{3,4},{4,3},{5,6},{6,5},{7,0},{8,15},{9,10},{10,... | collective-permute-start | bytes 49160 | tf_op jit(solution)/shard_map/ppermute | solution.py:128
  37.0 5.4 %collective-permute-start.16 = (bf16[304,128]{1,0:T(8,128)(2,1)S(1)}, bf16[304,128]{1,0:T(8,128)(2,1)S(1)}, u32[]{:S(2)}, u32[]{:S(2)}) collective-permute-start(bf16[304,128]{1,0:T(8,128)(2,1)S(1)} %shard_map.166.refs_0_.part), channel_id=1, source_target_pairs={{0,17},{1,16},{2,19},{3,18},{4,21},{5,20},{6,23},{7,22},{8,25},{9,... | collective-permute-start | bytes 233480 | tf_op jit(solution)/shard_map/ppermute | solution.py:128
  37.4 5.8 %collective-permute-start.15 = (bf16[304,128]{1,0:T(8,128)(2,1)S(1)}, bf16[304,128]{1,0:T(8,128)(2,1)S(1)}, u32[]{:S(2)}, u32[]{:S(2)}) collective-permute-start(bf16[304,128]{1,0:T(8,128)(2,1)S(1)} %shard_map.166.refs_0_.part), channel_id=1, source_target_pairs={{0,16},{1,17},{2,18},{3,19},{4,20},{5,21},{6,22},{7,23},{8,24},{9,... | collective-permute-start | bytes 233480 | tf_op jit(solution)/shard_map/ppermute | solution.py:128
  39.9 4.4 %collective-permute-start.14 = (bf16[304,128]{1,0:T(8,128)(2,1)S(1)}, bf16[304,128]{1,0:T(8,128)(2,1)S(1)}, u32[]{:S(2)}, u32[]{:S(2)}) collective-permute-start(bf16[304,128]{1,0:T(8,128)(2,1)S(1)} %shard_map.166.refs_0_.part), channel_id=1, source_target_pairs={{0,1},{1,0},{2,3},{3,2},{4,5},{5,4},{6,7},{7,6},{8,9},{9,8},{10,11... | collective-permute-start | bytes 233480 | tf_op jit(solution)/shard_map/ppermute | solution.py:128
  42.4 1.9 %collective-permute-start.17 = (bf16[2,304,128]{2,1,0:T(8,128)(2,1)S(1)}, bf16[2,304,128]{2,1,0:T(8,128)(2,1)S(1)}, u32[]{:S(2)}, u32[]{:S(2)}) collective-permute-start(bf16[2,304,128]{2,1,0:T(8,128)(2,1)S(1)} %shard_map.167), channel_id=1, source_target_pairs={{0,8},{1,9},{2,10},{3,11},{4,12},{5,13},{6,14},{7,15},{8,0},{9,1},... | collective-permute-start | bytes 466952 | tf_op jit(solution)/shard_map/ppermute | solution.py:128
  44.3 1.4 %collective-permute-start.18 = (bf16[2,304,128]{2,1,0:T(8,128)(2,1)S(1)}, bf16[2,304,128]{2,1,0:T(8,128)(2,1)S(1)}, u32[]{:S(2)}, u32[]{:S(2)}) collective-permute-start(bf16[2,304,128]{2,1,0:T(8,128)(2,1)S(1)} %shard_map.170), channel_id=1, source_target_pairs={{0,8},{1,9},{2,10},{3,11},{4,12},{5,13},{6,14},{7,15},{8,0},{9,1},... | collective-permute-start | bytes 466952 | tf_op jit(solution)/shard_map/ppermute | solution.py:128

commit v13 on v11

--- a/solution.py
+++ b/solution.py
@@ -64,6 +64,7 @@
         self.half = lon_count // 2
         self.taps, self.half_gates = taps, gate_count // 2
         self.plane = lat_count
+        self.scatter_steps = [self.plane - 1, *range(1, self.plane - 1)]
         whole = [("lon", 1 << k) for k in range(1, lon_count.bit_length() - 1)]
         self.orders = ([("lat", 1)] + whole, [("lat", 1)] + whole[::-1])
         step = 8 * self.plane
@@ -586,7 +587,7 @@
     rank = place.plane_rank()
     scratch[...] = keep[...] + received[...].astype(F32)
     block = encode(bias[...]).astype(BF16)
-    for step, send in zip(range(place.plane - 1, 0, -1), sends):
+    for step, send in zip(place.scatter_steps, sends):
         send[0:BIAS_ROWS, :] = block
         at = pl.ds(pl.multiple_of((rank ^ step) * chunk, 8), chunk)
         send[BIAS_ROWS:, :] = scratch[at, :].astype(BF16)
@@ -959,7 +960,9 @@
         (*[block for _ in steps], sds((place.chunk, channels), F32)),
         [pltpu.VMEM((place.half_rows, channels), F32)],
     )(keep, bias, permuted(send, place.phase_pairs(0)))
-    received = [permuted(send, place.plane_pairs(step)) for step, send in zip(steps, sends)]
+    received = [
+        permuted(send, place.plane_pairs(step)) for step, send in zip(place.scatter_steps, sends)
+    ]
     field, turned, field_done = call(
         field_kernel,
         (

time: 46.7 us -> 46.2 us (0.989)
  waiting for transfers between devices: 7.49 us -> 5.65 us
  starting transfers between devices: 25.1 us -> 26.4 us
    ppermute x19, waiting for transfers between devices: 7.49 us -> 5.65 us  [permuted(): return lax.ppermute(value, AXES, pairs)]
    ppermute x19, starting transfers between devices: 25.1 us -> 26.4 us  [permuted(): return lax.ppermute(value, AXES, pairs)]
  transfers between devices with their start and end apart: 19 -> 19, of which waited for: 10 -> 9; matrix products, arithmetic and copies ran while one was open for 0% -> 0% of each run, Pallas kernels for 22% -> 22%
where the time goes in v13:
time: 46.2 us; the launch traced here: 46 us
  starting transfers between devices  26.4 us (57%)
  Pallas kernels  13.1 us (28%)
  waiting for transfers between devices  5.65 us (12%)
  between operations  0.78 us (2%)
    ppermute x19, starting transfers between devices, permuted(): return lax.ppermute(value, AXES, pairs)  26.4 us
    pallas_call x17, Pallas kernels, run(): pl.pallas_call(kernel, out_shape=out_shape, in_specs=[VMEM] * near + [HBM...  13.1 us
    ppermute x19, waiting for transfers between devices, permuted(): return lax.ppermute(value, AXES, pairs)  5.65 us
  transfers between devices with their start and end apart: 19, of which 9 were waited for; matrix products, arithmetic and copies ran while one was open for 0% of the time, Pallas kernels for 22%

profile of v13, /device:TPU:0, one launch (start us, length us, event | category | flops | bytes accessed | tf_op | source)
XLA Modules:
  0.0 46.0 jit_solution(18400447703953444674)
XLA Ops:
  0.6 1.0 %shard_map.153 = (bf16[128,128]{1,0:T(8,128)(2,1)S(1)}, bf16[128,128]{1,0:T(8,128)(2,1)S(1)}, f32[1024,128]{1,0:T(8,128)S(1)}) custom-call(bf16[64,8,128]{2,1,0:T(8,128)(2,1)} %below.1, bf16[64,8,128]{2,1,0:T(8,128)(2,1)} %hidden.1), custom_call_target="tpu_custom_call" | custom-call | bytes 524288 | tf_op jit(solution)/shard_map/pallas_call | solution.py:45
  1.6 0.5 %collective-permute-start = (bf16[128,128]{1,0:T(8,128)(2,1)S(1)}, bf16[128,128]{1,0:T(8,128)(2,1)S(1)}, u32[]{:S(2)}, u32[]{:S(2)}) collective-permute-start(bf16[128,128]{1,0:T(8,128)(2,1)S(1)} %get-tuple-element.64), channel_id=1, source_target_pairs={{0,8},{1,9},{2,10},{3,11},{4,12},{5,13},{6,14},{7,15},{8,0},{9,1},... | collective-permute-start | bytes 98312 | tf_op jit(solution)/shard_map/ppermute | solution.py:129
  2.2 3.7 %collective-permute-start.1 = (bf16[128,128]{1,0:T(8,128)(2,1)S(1)}, bf16[128,128]{1,0:T(8,128)(2,1)S(1)}, u32[]{:S(2)}, u32[]{:S(2)}) collective-permute-start(bf16[128,128]{1,0:T(8,128)(2,1)S(1)} %get-tuple-element.65), channel_id=1, source_target_pairs={{0,4},{1,5},{2,6},{3,7},{4,0},{5,1},{6,2},{7,3},{8,16},{9,17},{10,... | collective-permute-start | bytes 98312 | tf_op jit(solution)/shard_map/ppermute | solution.py:129
  5.8 2.3 %shard_map.154 = (bf16[8,128,128]{2,1,0:T(8,128)(2,1)S(1)}, f32[128,128]{1,0:T(8,128)S(1)}, f32[128,128]{1,0:T(8,128)S(1)}, f32[64,128]{1,0:T(8,128)S(1)}, f32[6...) custom-call(f32[1024,128]{1,0:T(8,128)S(1)} %get-tuple-element.62.wi, ...), custom_call_target="tpu_custom_call" | custom-call | bytes 6000000 | tf_op jit(solution)/shard_map/pallas_call | solution.py:45
  8.1 0.0 collective-permute-done.inner_row.inner
  8.1 0.0 collective-permute-done.1.outer_row.outer
  8.1 0.2 shard_map.156
  8.3 1.5 %collective-permute-start.3 = (bf16[32,128]{1,0:T(8,128)(2,1)S(1)}, bf16[32,128]{1,0:T(8,128)(2,1)S(1)}, u32[]{:S(2)}, u32[]{:S(2)}) collective-permute-start(bf16[32,128]{1,0:T(8,128)(2,1)S(1)} %get-tuple-element.82), channel_id=1, source_target_pairs={{0,1},{1,0},{2,3},{3,2},{4,5},{5,4},{6,7},{7,6},{8,9},{9,8},{10,11... | collective-permute-start | bytes 24584 | tf_op jit(solution)/shard_map/ppermute | solution.py:129
  9.8 3.7 %collective-permute-start.2 = (bf16[32,128]{1,0:T(8,128)(2,1)S(1)}, bf16[32,128]{1,0:T(8,128)(2,1)S(1)}, u32[]{:S(2)}, u32[]{:S(2)}) collective-permute-start(bf16[32,128]{1,0:T(8,128)(2,1)S(1)} %get-tuple-element.82), channel_id=1, source_target_pairs={{0,7},{1,2},{2,1},{3,4},{4,3},{5,6},{6,5},{7,0},{8,15},{9,10},{10,... | collective-permute-start | bytes 24584 | tf_op jit(solution)/shard_map/ppermute | solution.py:129
  13.5 2.2 %shard_map.155 = (f32[512,128]{1,0:T(8,128)S(1)}, f32[512,128]{1,0:T(8,128)S(1)}, f32[512,128]{1,0:T(8,128)S(1)}, bf16[256,1024]{1,0:T(8,128)(2,1)S(1)}, bf16[12...) custom-call(bf16[8,128,128]{2,1,0:T(8,128)(2,1)S(1)} %get-tuple-element.63.rows_in, ...), custom_call_target="tpu_custom_call" | custom-call | flops 1207959552 | bytes 6000000 | tf_op jit(solution)/shard_map/pallas_call | solution.py:45
  15.7 0.0 collective-permute-done.3.inner_column
  15.7 0.4 collective-permute-done.2.outer_column
  16.2 0.9 %shard_map.157 = (bf16[1152,128]{1,0:T(8,128)(2,1)S(1)}, bf16[256,128]{1,0:T(8,128)(2,1)S(1)}, f32[256,128]{1,0:T(8,128)S(1)}, bf16[1152,128]{1,0:T(8,128)(2,1)S...) custom-call(bf16[128,128]{1,0:T(8,128)(2,1)S(1)} %get-tuple-element.80.edge, ...), custom_call_target="tpu_custom_call" | custom-call | tf_op jit(solution)/shard_map/pallas_call | solution.py:45
  17.1 0.1 collective-permute-start.8
  17.1 0.3 shard_map.162
  17.4 1.3 %collective-permute-done.8.received = bf16[1152,128]{1,0:T(8,128)(2,1)S(1)} collective-permute-done((bf16[1152,128]{1,0:T(8,128)(2,1)S(1)}, bf16[1152,128]{1,0:T(8,128)(2,1)S(1)}, u32[]{:S(2)}, u32[]{:S(2)}) %collective-permute-start.8) | collective-permute-done | bytes 294944 | tf_op jit(solution)/shard_map/ppermute | solution.py:129
  18.7 0.1 shard_map.163
  18.8 0.1 collective-permute-start.9
  18.9 1.4 %collective-permute-start.10 = (bf16[304,128]{1,0:T(8,128)(2,1)S(1)}, bf16[304,128]{1,0:T(8,128)(2,1)S(1)}, u32[]{:S(2)}, u32[]{:S(2)}) collective-permute-start(bf16[304,128]{1,0:T(8,128)(2,1)S(1)} %get-tuple-element.109), channel_id=1, source_target_pairs={{0,1},{1,0},{2,3},{3,2},{4,5},{5,4},{6,7},{7,6},{8,9},{9,8},{10,11... | collective-permute-start | bytes 233480 | tf_op jit(solution)/shard_map/ppermute | solution.py:129
  20.3 2.1 %collective-permute-start.11 = (bf16[304,128]{1,0:T(8,128)(2,1)S(1)}, bf16[304,128]{1,0:T(8,128)(2,1)S(1)}, u32[]{:S(2)}, u32[]{:S(2)}) collective-permute-start(bf16[304,128]{1,0:T(8,128)(2,1)S(1)} %get-tuple-element.110), channel_id=1, source_target_pairs={{0,16},{1,17},{2,18},{3,19},{4,20},{5,21},{6,22},{7,23},{8,24},{9,... | collective-permute-start | bytes 233480 | tf_op jit(solution)/shard_map/ppermute | solution.py:129
  22.4 1.4 %shard_map.158 = (bf16[64,8,128]{2,1,0:T(8,128)(2,1)}, f32[512,128]{1,0:T(8,128)}, f32[512,128]{1,0:T(8,128)}, bf16[256,1024]{1,0:T(8,128)(2,1)S(1)}, bf16[256,1...) custom-call(f32[512,128]{1,0:T(8,128)S(1)} %get-tuple-element.75.hidden, f32[512,128]{1,0:T(8,128)S(1)} %get-tuple-element.76.cell, ...), custom_call_target="tpu_custom_call" | custom-call | bytes 4000000 | tf_op jit(solution)/shard_map/pallas_call | solution.py:45
  23.7 1.1 %shard_map.159 = (f32[1024,128]{1,0:T(8,128)S(1)}, bf16[3,128,768]{2,1,0:T(8,128)(2,1)S(1)}, f32[8,128]{1,0:T(8,128)S(1)}) custom-call(bf16[256,1024]{1,0:T(8,128)(2,1)S(1)} %get-tuple-element.93.pre, bf16[256,1152]{1,0:T(8,128)(2,1)S(1)} %get-tuple-element.68.weights), custom_call_target="tpu_custom_call" | custom-call | flops 603979776 | bytes 3000000 | tf_op jit(solution)/shard_map/pallas_call | solution.py:45
  24.9 0.1 collective-permute-done.9.refs_0_
  25.0 0.0 collective-permute-done.10.refs_1_
  25.0 0.0 collective-permute-done.11.refs_2_
  25.1 0.1 collective-permute-start.12
  25.1 4.1 %collective-permute-start.4 = (bf16[256,128]{1,0:T(8,128)(2,1)S(1)}, bf16[256,128]{1,0:T(8,128)(2,1)S(1)}, u32[]{:S(2)}, u32[]{:S(2)}) collective-permute-start(bf16[256,128]{1,0:T(8,128)(2,1)S(1)} %get-tuple-element.96), channel_id=1, source_target_pairs={{0,4},{1,5},{2,6},{3,7},{4,0},{5,1},{6,2},{7,3},{8,16},{9,17},{10,... | collective-permute-start | bytes 196616 | tf_op jit(solution)/shard_map/ppermute | solution.py:129
  29.3 0.2 collective-permute-done.12.received
  29.6 2.2 %collective-permute-start.13 = (bf16[304,128]{1,0:T(8,128)(2,1)S(1)}, bf16[304,128]{1,0:T(8,128)(2,1)S(1)}, u32[]{:S(2)}, u32[]{:S(2)}) collective-permute-start(bf16[304,128]{1,0:T(8,128)(2,1)S(1)} %shard_map.165.own), channel_id=1, source_target_pairs={{0,4},{1,5},{2,6},{3,7},{4,0},{5,1},{6,2},{7,3},{8,10},{9,11},{10,... | collective-permute-start | bytes 233480 | tf_op jit(solution)/shard_map/ppermute | solution.py:129
  31.8 0.5 %collective-permute-done.4.outer.outer_row = bf16[256,128]{1,0:T(8,128)(2,1)S(1)} collective-permute-done((bf16[256,128]{1,0:T(8,128)(2,1)S(1)}, bf16[256,128]{1,0:T(8,128)(2,1)S(1)}, u32[]{:S(2)}, u32[]{:S(2)}) %collective-permute-start.4) | collective-permute-done | bytes 65568 | tf_op jit(solution)/shard_map/ppermute | solution.py:129
  32.2 0.0 collective-permute-done.5.inner.inner_row
  32.2 0.2 shard_map.160
  32.4 0.2 collective-permute-start.7
  32.7 3.0 %collective-permute-start.6 = (bf16[64,128]{1,0:T(8,128)(2,1)S(1)}, bf16[64,128]{1,0:T(8,128)(2,1)S(1)}, u32[]{:S(2)}, u32[]{:S(2)}) collective-permute-start(bf16[64,128]{1,0:T(8,128)(2,1)S(1)} %shard_map.160), channel_id=1, source_target_pairs={{0,7},{1,2},{2,1},{3,4},{4,3},{5,6},{6,5},{7,0},{8,15},{9,10},{10,... | collective-permute-start | bytes 49160 | tf_op jit(solution)/shard_map/ppermute | solution.py:129
  35.7 0.0 collective-permute-done.13.received
  35.7 2.4 %collective-permute-start.16 = (bf16[304,128]{1,0:T(8,128)(2,1)S(1)}, bf16[304,128]{1,0:T(8,128)(2,1)S(1)}, u32[]{:S(2)}, u32[]{:S(2)}) collective-permute-start(bf16[304,128]{1,0:T(8,128)(2,1)S(1)} %shard_map.166.refs_0_), channel_id=1, source_target_pairs={{0,17},{1,16},{2,19},{3,18},{4,21},{5,20},{6,23},{7,22},{8,25},{9,... | collective-permute-start | bytes 233480 | tf_op jit(solution)/shard_map/ppermute | solution.py:129
  38.2 1.2 %collective-permute-start.15 = (bf16[304,128]{1,0:T(8,128)(2,1)S(1)}, bf16[304,128]{1,0:T(8,128)(2,1)S(1)}, u32[]{:S(2)}, u32[]{:S(2)}) collective-permute-start(bf16[304,128]{1,0:T(8,128)(2,1)S(1)} %shard_map.166.refs_0_), channel_id=1, source_target_pairs={{0,16},{1,17},{2,18},{3,19},{4,20},{5,21},{6,22},{7,23},{8,24},{9,... | collective-permute-start | bytes 233480 | tf_op jit(solution)/shard_map/ppermute | solution.py:129
  39.4 0.0 collective-permute-start.14
  39.4 0.0 collective-permute-done.7.inner_column
  39.4 1.6 %shard_map.161 = (bf16[64,8,128]{2,1,0:T(8,128)(2,1)}, bf16[64,8,128]{2,1,0:T(8,128)(2,1)}, f32[8,128]{1,0:T(8,128)S(1)}) custom-call(f32[1024,128]{1,0:T(8,128)S(1)} %get-tuple-element.94.wide, bf16[3,128,768]{2,1,0:T(8,128)(2,1)S(1)} %get-tuple-element.95.turned, bf16[256,128]{1,0:T(8,128)(2,1)S(1)} %collective-permute-done.4.outer.outer_row, ...), custom_call_target="tpu_custom_call" | custom-call | flops 12079595520 | bytes 2000000 | tf_op jit(solution)/shard_map/pallas_call | solution.py:45
  41.0 0.1 collective-permute-done.16.refs_2_
  41.1 1.5 %collective-permute-done.15.refs_1_ = bf16[304,128]{1,0:T(8,128)(2,1)S(1)} collective-permute-done((bf16[304,128]{1,0:T(8,128)(2,1)S(1)}, bf16[304,128]{1,0:T(8,128)(2,1)S(1)}, u32[]{:S(2)}, u32[]{:S(2)}) %collective-permute-start.15) | collective-permute-done | bytes 77856 | tf_op jit(solution)/shard_map/ppermute | solution.py:129
  42.6 0.1 collective-permute-start.17
  42.7 1.1 %collective-permute-done.14.late = bf16[304,128]{1,0:T(8,128)(2,1)S(1)} collective-permute-done((bf16[304,128]{1,0:T(8,128)(2,1)S(1)}, bf16[304,128]{1,0:T(8,128)(2,1)S(1)}, u32[]{:S(2)}, u32[]{:S(2)}) %collective-permute-start.14) | collective-permute-done | bytes 77856 | tf_op jit(solution)/shard_map/ppermute | solution.py:129
  43.8 0.9 %shard_map.168 = (f32[9,256,128]{2,1,0:T(8,128)}, f32[8,128]{1,0:T(8,128)S(1)}) custom-call(bf16[304,128]{1,0:T(8,128)(2,1)S(1)} %collective-permute-done.14.late, bf16[3,304,128]{2,1,0:T(8,128)(2,1)S(1)} %shard_map.167.early), custom_call_target="tpu_custom_call" | custom-call | flops 12079595520 | bytes 884736 | tf_op jit(solution)/shard_map/pallas_call | solution.py:45
  44.7 0.3 collective-permute-done.18.late
  45.0 0.0 collective-permute-done.17.early
  45.0 0.9 %shard_map.169 = (f32[9,256,128]{2,1,0:T(8,128)}, f32[256]{0:T(256)}) custom-call(f32[8,128]{1,0:T(8,128)S(1)} %get-tuple-element.113.bias_own, bf16[3,304,128]{2,1,0:T(8,128)(2,1)S(1)} %collective-permute-done.17.early, bf16[304,128]{1,0:T(8,128)(2,1)S(1)} %collective-permute-done.18.late, ...), custom_call_target="tpu_custom_call", output_to_operand_aliasing={{0}: (4, {})} | custom-call | bytes 884736 | tf_op jit(solution)/shard_map/pallas_call | solution.py:45
  (7 shorter events, 0.1 us)
Async XLA Ops:
  1.6 6.5 %collective-permute-start = (bf16[128,128]{1,0:T(8,128)(2,1)S(1)}, bf16[128,128]{1,0:T(8,128)(2,1)S(1)}, u32[]{:S(2)}, u32[]{:S(2)}) collective-permute-start(bf16[128,128]{1,0:T(8,128)(2,1)S(1)} %get-tuple-element.64), channel_id=1, source_target_pairs={{0,8},{1,9},{2,10},{3,11},{4,12},{5,13},{6,14},{7,15},{8,0},{9,1},... | collective-permute-start | bytes 98312 | tf_op jit(solution)/shard_map/ppermute | solution.py:129
  2.2 6.0 %collective-permute-start.1 = (bf16[128,128]{1,0:T(8,128)(2,1)S(1)}, bf16[128,128]{1,0:T(8,128)(2,1)S(1)}, u32[]{:S(2)}, u32[]{:S(2)}) collective-permute-start(bf16[128,128]{1,0:T(8,128)(2,1)S(1)} %get-tuple-element.65), channel_id=1, source_target_pairs={{0,4},{1,5},{2,6},{3,7},{4,0},{5,1},{6,2},{7,3},{8,16},{9,17},{10,... | collective-permute-start | bytes 98312 | tf_op jit(solution)/shard_map/ppermute | solution.py:129
  8.3 7.4 %collective-permute-start.3 = (bf16[32,128]{1,0:T(8,128)(2,1)S(1)}, bf16[32,128]{1,0:T(8,128)(2,1)S(1)}, u32[]{:S(2)}, u32[]{:S(2)}) collective-permute-start(bf16[32,128]{1,0:T(8,128)(2,1)S(1)} %get-tuple-element.82), channel_id=1, source_target_pairs={{0,1},{1,0},{2,3},{3,2},{4,5},{5,4},{6,7},{7,6},{8,9},{9,8},{10,11... | collective-permute-start | bytes 24584 | tf_op jit(solution)/shard_map/ppermute | solution.py:129
  9.8 6.3 %collective-permute-start.2 = (bf16[32,128]{1,0:T(8,128)(2,1)S(1)}, bf16[32,128]{1,0:T(8,128)(2,1)S(1)}, u32[]{:S(2)}, u32[]{:S(2)}) collective-permute-start(bf16[32,128]{1,0:T(8,128)(2,1)S(1)} %get-tuple-element.82), channel_id=1, source_target_pairs={{0,7},{1,2},{2,1},{3,4},{4,3},{5,6},{6,5},{7,0},{8,15},{9,10},{10,... | collective-permute-start | bytes 24584 | tf_op jit(solution)/shard_map/ppermute | solution.py:129
  17.1 1.6 %collective-permute-start.8 = (bf16[1152,128]{1,0:T(8,128)(2,1)S(1)}, bf16[1152,128]{1,0:T(8,128)(2,1)S(1)}, u32[]{:S(2)}, u32[]{:S(2)}) collective-permute-start(bf16[1152,128]{1,0:T(8,128)(2,1)S(1)} %get-tuple-element.106), channel_id=1, source_target_pairs={{0,8},{1,9},{2,10},{3,11},{4,12},{5,13},{6,14},{7,15},{8,0},{9,1},... | collective-permute-start | bytes 884744 | tf_op jit(solution)/shard_map/ppermute | solution.py:129
  18.8 6.2 %collective-permute-start.9 = (bf16[304,128]{1,0:T(8,128)(2,1)S(1)}, bf16[304,128]{1,0:T(8,128)(2,1)S(1)}, u32[]{:S(2)}, u32[]{:S(2)}) collective-permute-start(bf16[304,128]{1,0:T(8,128)(2,1)S(1)} %get-tuple-element.108), channel_id=1, source_target_pairs={{0,17},{1,16},{2,19},{3,18},{4,21},{5,20},{6,23},{7,22},{8,25},{9,... | collective-permute-start | bytes 233480 | tf_op jit(solution)/shard_map/ppermute | solution.py:129
  18.9 6.1 %collective-permute-start.10 = (bf16[304,128]{1,0:T(8,128)(2,1)S(1)}, bf16[304,128]{1,0:T(8,128)(2,1)S(1)}, u32[]{:S(2)}, u32[]{:S(2)}) collective-permute-start(bf16[304,128]{1,0:T(8,128)(2,1)S(1)} %get-tuple-element.109), channel_id=1, source_target_pairs={{0,1},{1,0},{2,3},{3,2},{4,5},{5,4},{6,7},{7,6},{8,9},{9,8},{10,11... | collective-permute-start | bytes 233480 | tf_op jit(solution)/shard_map/ppermute | solution.py:129
  20.3 4.8 %collective-permute-start.11 = (bf16[304,128]{1,0:T(8,128)(2,1)S(1)}, bf16[304,128]{1,0:T(8,128)(2,1)S(1)}, u32[]{:S(2)}, u32[]{:S(2)}) collective-permute-start(bf16[304,128]{1,0:T(8,128)(2,1)S(1)} %get-tuple-element.110), channel_id=1, source_target_pairs={{0,16},{1,17},{2,18},{3,19},{4,20},{5,21},{6,22},{7,23},{8,24},{9,... | collective-permute-start | bytes 233480 | tf_op jit(solution)/shard_map/ppermute | solution.py:129
  25.1 4.5 %collective-permute-start.12 = (bf16[304,128]{1,0:T(8,128)(2,1)S(1)}, bf16[304,128]{1,0:T(8,128)(2,1)S(1)}, u32[]{:S(2)}, u32[]{:S(2)}) collective-permute-start(bf16[304,128]{1,0:T(8,128)(2,1)S(1)} %shard_map.164.own), channel_id=1, source_target_pairs={{0,2},{1,3},{2,0},{3,1},{4,6},{5,7},{6,4},{7,5},{8,12},{9,13},{10,... | collective-permute-start | bytes 233480 | tf_op jit(solution)/shard_map/ppermute | solution.py:129
  25.1 7.1 %collective-permute-start.4 = (bf16[256,128]{1,0:T(8,128)(2,1)S(1)}, bf16[256,128]{1,0:T(8,128)(2,1)S(1)}, u32[]{:S(2)}, u32[]{:S(2)}) collective-permute-start(bf16[256,128]{1,0:T(8,128)(2,1)S(1)} %get-tuple-element.96), channel_id=1, source_target_pairs={{0,4},{1,5},{2,6},{3,7},{4,0},{5,1},{6,2},{7,3},{8,16},{9,17},{10,... | collective-permute-start | bytes 196616 | tf_op jit(solution)/shard_map/ppermute | solution.py:129
  29.3 2.9 %collective-permute-start.5 = (bf16[256,128]{1,0:T(8,128)(2,1)S(1)}, bf16[256,128]{1,0:T(8,128)(2,1)S(1)}, u32[]{:S(2)}, u32[]{:S(2)}) collective-permute-start(bf16[256,128]{1,0:T(8,128)(2,1)S(1)} %get-tuple-element.97), channel_id=1, source_target_pairs={{0,8},{1,9},{2,10},{3,11},{4,12},{5,13},{6,14},{7,15},{8,0},{9,1},... | collective-permute-start | bytes 196616 | tf_op jit(solution)/shard_map/ppermute | solution.py:129
  29.6 6.2 %collective-permute-start.13 = (bf16[304,128]{1,0:T(8,128)(2,1)S(1)}, bf16[304,128]{1,0:T(8,128)(2,1)S(1)}, u32[]{:S(2)}, u32[]{:S(2)}) collective-permute-start(bf16[304,128]{1,0:T(8,128)(2,1)S(1)} %shard_map.165.own), channel_id=1, source_target_pairs={{0,4},{1,5},{2,6},{3,7},{4,0},{5,1},{6,2},{7,3},{8,10},{9,11},{10,... | collective-permute-start | bytes 233480 | tf_op jit(solution)/shard_map/ppermute | solution.py:129
  32.4 6.9 %collective-permute-start.7 = (bf16[64,128]{1,0:T(8,128)(2,1)S(1)}, bf16[64,128]{1,0:T(8,128)(2,1)S(1)}, u32[]{:S(2)}, u32[]{:S(2)}) collective-permute-start(bf16[64,128]{1,0:T(8,128)(2,1)S(1)} %shard_map.160), channel_id=1, source_target_pairs={{0,1},{1,0},{2,3},{3,2},{4,5},{5,4},{6,7},{7,6},{8,9},{9,8},{10,11... | collective-permute-start | bytes 49160 | tf_op jit(solution)/shard_map/ppermute | solution.py:129
  32.7 6.7 %collective-permute-start.6 = (bf16[64,128]{1,0:T(8,128)(2,1)S(1)}, bf16[64,128]{1,0:T(8,128)(2,1)S(1)}, u32[]{:S(2)}, u32[]{:S(2)}) collective-permute-start(bf16[64,128]{1,0:T(8,128)(2,1)S(1)} %shard_map.160), channel_id=1, source_target_pairs={{0,7},{1,2},{2,1},{3,4},{4,3},{5,6},{6,5},{7,0},{8,15},{9,10},{10,... | collective-permute-start | bytes 49160 | tf_op jit(solution)/shard_map/ppermute | solution.py:129
  35.7 5.4 %collective-permute-start.16 = (bf16[304,128]{1,0:T(8,128)(2,1)S(1)}, bf16[304,128]{1,0:T(8,128)(2,1)S(1)}, u32[]{:S(2)}, u32[]{:S(2)}) collective-permute-start(bf16[304,128]{1,0:T(8,128)(2,1)S(1)} %shard_map.166.refs_0_), channel_id=1, source_target_pairs={{0,17},{1,16},{2,19},{3,18},{4,21},{5,20},{6,23},{7,22},{8,25},{9,... | collective-permute-start | bytes 233480 | tf_op jit(solution)/shard_map/ppermute | solution.py:129
  38.2 4.4 %collective-permute-start.15 = (bf16[304,128]{1,0:T(8,128)(2,1)S(1)}, bf16[304,128]{1,0:T(8,128)(2,1)S(1)}, u32[]{:S(2)}, u32[]{:S(2)}) collective-permute-start(bf16[304,128]{1,0:T(8,128)(2,1)S(1)} %shard_map.166.refs_0_), channel_id=1, source_target_pairs={{0,16},{1,17},{2,18},{3,19},{4,20},{5,21},{6,22},{7,23},{8,24},{9,... | collective-permute-start | bytes 233480 | tf_op jit(solution)/shard_map/ppermute | solution.py:129
  39.4 4.4 %collective-permute-start.14 = (bf16[304,128]{1,0:T(8,128)(2,1)S(1)}, bf16[304,128]{1,0:T(8,128)(2,1)S(1)}, u32[]{:S(2)}, u32[]{:S(2)}) collective-permute-start(bf16[304,128]{1,0:T(8,128)(2,1)S(1)} %shard_map.166.refs_0_), channel_id=1, source_target_pairs={{0,1},{1,0},{2,3},{3,2},{4,5},{5,4},{6,7},{7,6},{8,9},{9,8},{10,11... | collective-permute-start | bytes 233480 | tf_op jit(solution)/shard_map/ppermute | solution.py:129
  42.6 2.4 %collective-permute-start.17 = (bf16[3,304,128]{2,1,0:T(8,128)(2,1)S(1)}, bf16[3,304,128]{2,1,0:T(8,128)(2,1)S(1)}, u32[]{:S(2)}, u32[]{:S(2)}) collective-permute-start(bf16[3,304,128]{2,1,0:T(8,128)(2,1)S(1)} %shard_map.167.early), channel_id=1, source_target_pairs={{0,8},{1,9},{2,10},{3,11},{4,12},{5,13},{6,14},{7,15},{8,0},{9,1},... | collective-permute-start | bytes 700424 | tf_op jit(solution)/shard_map/ppermute | solution.py:129
  43.8 1.3 %collective-permute-start.18 = (bf16[304,128]{1,0:T(8,128)(2,1)S(1)}, bf16[304,128]{1,0:T(8,128)(2,1)S(1)}, u32[]{:S(2)}, u32[]{:S(2)}) collective-permute-start(bf16[304,128]{1,0:T(8,128)(2,1)S(1)} %collective-permute-done.14.late), channel_id=1, source_target_pairs={{0,8},{1,9},{2,10},{3,11},{4,12},{5,13},{6,14},{7,15},{8,0},{9,1},... | collective-permute-start | bytes 233480 | tf_op jit(solution)/shard_map/ppermute | solution.py:129

commit v14 on v13

--- a/solution.py
+++ b/solution.py
@@ -633,7 +633,8 @@
 
 
 def in_steps(place, early, late):
-    return [early.at[0], late] + [early.at[index] for index in range(1, place.plane - 1)]
+    blocks = [early.at[index] for index in range(place.plane - 1)]
+    return blocks[:-1] + [late] + blocks[-1:]
 
 
 def own_half_kernel(place, late, early, out, bias_out, wide, left):
@@ -996,9 +997,9 @@
         moved=2_000_000,
     )(field, turned, pre_outer, pre_inner, pre_outer_columns, pre_inner_columns)
     early = call(join_kernel, sds((place.plane - 1, *block.shape), BF16))(
-        part, *received[1:], field_done
+        part, *received[:-2], received[-1], field_done
     )
-    late = received[0]
+    late = received[-2]
     early_other = permuted(early, place.phase_pairs(0))
     late_other = permuted(late, place.phase_pairs(0))
     half = [pltpu.VMEM((place.half_rows, channels), F32)]

time: 46.2 us -> 45.8 us (level)
  no operation moved by 1% of the time
where the time goes in v14:
time: 45.8 us; the launch traced here: 45.6 us
  starting transfers between devices  26.4 us (58%)
  Pallas kernels  13.1 us (29%)
  waiting for transfers between devices  5.32 us (12%)
  between operations  0.78 us (2%)
    ppermute x19, starting transfers between devices, permuted(): return lax.ppermute(value, AXES, pairs)  26.4 us
    pallas_call x17, Pallas kernels, run(): pl.pallas_call(kernel, out_shape=out_shape, in_specs=[VMEM] * near + [HBM...  13.1 us
    ppermute x19, waiting for transfers between devices, permuted(): return lax.ppermute(value, AXES, pairs)  5.32 us
  transfers between devices with their start and end apart: 19, of which 9 were waited for; matrix products, arithmetic and copies ran while one was open for 0% of the time, Pallas kernels for 22%

profile of v14, /device:TPU:0, one launch (start us, length us, event | category | flops | bytes accessed | tf_op | source)
XLA Modules:
  0.0 45.6 jit_solution(7267395447667494215)
XLA Ops:
  0.6 1.0 %shard_map.153 = (bf16[128,128]{1,0:T(8,128)(2,1)S(1)}, bf16[128,128]{1,0:T(8,128)(2,1)S(1)}, f32[1024,128]{1,0:T(8,128)S(1)}) custom-call(bf16[64,8,128]{2,1,0:T(8,128)(2,1)} %below.1, bf16[64,8,128]{2,1,0:T(8,128)(2,1)} %hidden.1), custom_call_target="tpu_custom_call" | custom-call | bytes 524288 | tf_op jit(solution)/shard_map/pallas_call | solution.py:45
  1.6 0.5 %collective-permute-start = (bf16[128,128]{1,0:T(8,128)(2,1)S(1)}, bf16[128,128]{1,0:T(8,128)(2,1)S(1)}, u32[]{:S(2)}, u32[]{:S(2)}) collective-permute-start(bf16[128,128]{1,0:T(8,128)(2,1)S(1)} %get-tuple-element.64), channel_id=1, source_target_pairs={{0,8},{1,9},{2,10},{3,11},{4,12},{5,13},{6,14},{7,15},{8,0},{9,1},... | collective-permute-start | bytes 98312 | tf_op jit(solution)/shard_map/ppermute | solution.py:129
  2.2 3.7 %collective-permute-start.1 = (bf16[128,128]{1,0:T(8,128)(2,1)S(1)}, bf16[128,128]{1,0:T(8,128)(2,1)S(1)}, u32[]{:S(2)}, u32[]{:S(2)}) collective-permute-start(bf16[128,128]{1,0:T(8,128)(2,1)S(1)} %get-tuple-element.65), channel_id=1, source_target_pairs={{0,4},{1,5},{2,6},{3,7},{4,0},{5,1},{6,2},{7,3},{8,16},{9,17},{10,... | collective-permute-start | bytes 98312 | tf_op jit(solution)/shard_map/ppermute | solution.py:129
  5.8 2.3 %shard_map.154 = (bf16[8,128,128]{2,1,0:T(8,128)(2,1)S(1)}, f32[128,128]{1,0:T(8,128)S(1)}, f32[128,128]{1,0:T(8,128)S(1)}, f32[64,128]{1,0:T(8,128)S(1)}, f32[6...) custom-call(f32[1024,128]{1,0:T(8,128)S(1)} %get-tuple-element.62.wi, ...), custom_call_target="tpu_custom_call" | custom-call | bytes 6000000 | tf_op jit(solution)/shard_map/pallas_call | solution.py:45
  8.1 0.0 collective-permute-done.inner_row.inner
  8.1 0.0 collective-permute-done.1.outer_row.outer
  8.1 0.2 shard_map.156
  8.3 1.5 %collective-permute-start.3 = (bf16[32,128]{1,0:T(8,128)(2,1)S(1)}, bf16[32,128]{1,0:T(8,128)(2,1)S(1)}, u32[]{:S(2)}, u32[]{:S(2)}) collective-permute-start(bf16[32,128]{1,0:T(8,128)(2,1)S(1)} %get-tuple-element.82), channel_id=1, source_target_pairs={{0,1},{1,0},{2,3},{3,2},{4,5},{5,4},{6,7},{7,6},{8,9},{9,8},{10,11... | collective-permute-start | bytes 24584 | tf_op jit(solution)/shard_map/ppermute | solution.py:129
  9.8 3.7 %collective-permute-start.2 = (bf16[32,128]{1,0:T(8,128)(2,1)S(1)}, bf16[32,128]{1,0:T(8,128)(2,1)S(1)}, u32[]{:S(2)}, u32[]{:S(2)}) collective-permute-start(bf16[32,128]{1,0:T(8,128)(2,1)S(1)} %get-tuple-element.82), channel_id=1, source_target_pairs={{0,7},{1,2},{2,1},{3,4},{4,3},{5,6},{6,5},{7,0},{8,15},{9,10},{10,... | collective-permute-start | bytes 24584 | tf_op jit(solution)/shard_map/ppermute | solution.py:129
  13.5 2.2 %shard_map.155 = (f32[512,128]{1,0:T(8,128)S(1)}, f32[512,128]{1,0:T(8,128)S(1)}, f32[512,128]{1,0:T(8,128)S(1)}, bf16[256,1024]{1,0:T(8,128)(2,1)S(1)}, bf16[12...) custom-call(bf16[8,128,128]{2,1,0:T(8,128)(2,1)S(1)} %get-tuple-element.63.rows_in, ...), custom_call_target="tpu_custom_call" | custom-call | flops 1207959552 | bytes 6000000 | tf_op jit(solution)/shard_map/pallas_call | solution.py:45
  15.7 0.0 collective-permute-done.3.inner_column
  15.7 0.4 collective-permute-done.2.outer_column
  16.2 0.9 %shard_map.157 = (bf16[1152,128]{1,0:T(8,128)(2,1)S(1)}, bf16[256,128]{1,0:T(8,128)(2,1)S(1)}, f32[256,128]{1,0:T(8,128)S(1)}, bf16[1152,128]{1,0:T(8,128)(2,1)S...) custom-call(bf16[128,128]{1,0:T(8,128)(2,1)S(1)} %get-tuple-element.80.edge, ...), custom_call_target="tpu_custom_call" | custom-call | tf_op jit(solution)/shard_map/pallas_call | solution.py:45
  17.1 0.1 collective-permute-start.8
  17.1 0.3 shard_map.162
  17.4 1.3 %collective-permute-done.8.received = bf16[1152,128]{1,0:T(8,128)(2,1)S(1)} collective-permute-done((bf16[1152,128]{1,0:T(8,128)(2,1)S(1)}, bf16[1152,128]{1,0:T(8,128)(2,1)S(1)}, u32[]{:S(2)}, u32[]{:S(2)}) %collective-permute-start.8) | collective-permute-done | bytes 294944 | tf_op jit(solution)/shard_map/ppermute | solution.py:129
  18.7 0.1 shard_map.163
  18.8 0.1 collective-permute-start.9
  18.9 1.4 %collective-permute-start.10 = (bf16[304,128]{1,0:T(8,128)(2,1)S(1)}, bf16[304,128]{1,0:T(8,128)(2,1)S(1)}, u32[]{:S(2)}, u32[]{:S(2)}) collective-permute-start(bf16[304,128]{1,0:T(8,128)(2,1)S(1)} %get-tuple-element.109), channel_id=1, source_target_pairs={{0,1},{1,0},{2,3},{3,2},{4,5},{5,4},{6,7},{7,6},{8,9},{9,8},{10,11... | collective-permute-start | bytes 233480 | tf_op jit(solution)/shard_map/ppermute | solution.py:129
  20.3 2.1 %collective-permute-start.11 = (bf16[304,128]{1,0:T(8,128)(2,1)S(1)}, bf16[304,128]{1,0:T(8,128)(2,1)S(1)}, u32[]{:S(2)}, u32[]{:S(2)}) collective-permute-start(bf16[304,128]{1,0:T(8,128)(2,1)S(1)} %get-tuple-element.110), channel_id=1, source_target_pairs={{0,16},{1,17},{2,18},{3,19},{4,20},{5,21},{6,22},{7,23},{8,24},{9,... | collective-permute-start | bytes 233480 | tf_op jit(solution)/shard_map/ppermute | solution.py:129
  22.4 1.4 %shard_map.158 = (bf16[64,8,128]{2,1,0:T(8,128)(2,1)}, f32[512,128]{1,0:T(8,128)}, f32[512,128]{1,0:T(8,128)}, bf16[256,1024]{1,0:T(8,128)(2,1)S(1)}, bf16[256,1...) custom-call(f32[512,128]{1,0:T(8,128)S(1)} %get-tuple-element.75.hidden, f32[512,128]{1,0:T(8,128)S(1)} %get-tuple-element.76.cell, ...), custom_call_target="tpu_custom_call" | custom-call | bytes 4000000 | tf_op jit(solution)/shard_map/pallas_call | solution.py:45
  23.7 1.1 %shard_map.159 = (f32[1024,128]{1,0:T(8,128)S(1)}, bf16[3,128,768]{2,1,0:T(8,128)(2,1)S(1)}, f32[8,128]{1,0:T(8,128)S(1)}) custom-call(bf16[256,1024]{1,0:T(8,128)(2,1)S(1)} %get-tuple-element.93.pre, bf16[256,1152]{1,0:T(8,128)(2,1)S(1)} %get-tuple-element.68.weights), custom_call_target="tpu_custom_call" | custom-call | flops 603979776 | bytes 3000000 | tf_op jit(solution)/shard_map/pallas_call | solution.py:45
  24.9 0.1 collective-permute-done.9.refs_0_
  25.0 0.0 collective-permute-done.10.refs_1_
  25.0 0.0 collective-permute-done.11.refs_2_
  25.1 0.1 collective-permute-start.12
  25.1 4.1 %collective-permute-start.4 = (bf16[256,128]{1,0:T(8,128)(2,1)S(1)}, bf16[256,128]{1,0:T(8,128)(2,1)S(1)}, u32[]{:S(2)}, u32[]{:S(2)}) collective-permute-start(bf16[256,128]{1,0:T(8,128)(2,1)S(1)} %get-tuple-element.96), channel_id=1, source_target_pairs={{0,4},{1,5},{2,6},{3,7},{4,0},{5,1},{6,2},{7,3},{8,16},{9,17},{10,... | collective-permute-start | bytes 196616 | tf_op jit(solution)/shard_map/ppermute | solution.py:129
  29.3 0.2 collective-permute-done.12.received
  29.6 2.2 %collective-permute-start.13 = (bf16[304,128]{1,0:T(8,128)(2,1)S(1)}, bf16[304,128]{1,0:T(8,128)(2,1)S(1)}, u32[]{:S(2)}, u32[]{:S(2)}) collective-permute-start(bf16[304,128]{1,0:T(8,128)(2,1)S(1)} %shard_map.165.own), channel_id=1, source_target_pairs={{0,4},{1,5},{2,6},{3,7},{4,0},{5,1},{6,2},{7,3},{8,10},{9,11},{10,... | collective-permute-start | bytes 233480 | tf_op jit(solution)/shard_map/ppermute | solution.py:129
  31.8 0.5 %collective-permute-done.4.outer.outer_row = bf16[256,128]{1,0:T(8,128)(2,1)S(1)} collective-permute-done((bf16[256,128]{1,0:T(8,128)(2,1)S(1)}, bf16[256,128]{1,0:T(8,128)(2,1)S(1)}, u32[]{:S(2)}, u32[]{:S(2)}) %collective-permute-start.4) | collective-permute-done | bytes 65568 | tf_op jit(solution)/shard_map/ppermute | solution.py:129
  32.2 0.2 shard_map.160
  32.4 0.2 collective-permute-start.7
  32.7 3.0 %collective-permute-start.6 = (bf16[64,128]{1,0:T(8,128)(2,1)S(1)}, bf16[64,128]{1,0:T(8,128)(2,1)S(1)}, u32[]{:S(2)}, u32[]{:S(2)}) collective-permute-start(bf16[64,128]{1,0:T(8,128)(2,1)S(1)} %shard_map.160), channel_id=1, source_target_pairs={{0,7},{1,2},{2,1},{3,4},{4,3},{5,6},{6,5},{7,0},{8,15},{9,10},{10,... | collective-permute-start | bytes 49160 | tf_op jit(solution)/shard_map/ppermute | solution.py:129
  35.7 0.0 collective-permute-done.13.received
  35.7 2.4 %collective-permute-start.16 = (bf16[304,128]{1,0:T(8,128)(2,1)S(1)}, bf16[304,128]{1,0:T(8,128)(2,1)S(1)}, u32[]{:S(2)}, u32[]{:S(2)}) collective-permute-start(bf16[304,128]{1,0:T(8,128)(2,1)S(1)} %shard_map.166.refs_0_), channel_id=1, source_target_pairs={{0,17},{1,16},{2,19},{3,18},{4,21},{5,20},{6,23},{7,22},{8,25},{9,... | collective-permute-start | bytes 233480 | tf_op jit(solution)/shard_map/ppermute | solution.py:129
  38.2 0.9 %collective-permute-start.15 = (bf16[304,128]{1,0:T(8,128)(2,1)S(1)}, bf16[304,128]{1,0:T(8,128)(2,1)S(1)}, u32[]{:S(2)}, u32[]{:S(2)}) collective-permute-start(bf16[304,128]{1,0:T(8,128)(2,1)S(1)} %shard_map.166.refs_0_), channel_id=1, source_target_pairs={{0,1},{1,0},{2,3},{3,2},{4,5},{5,4},{6,7},{7,6},{8,9},{9,8},{10,11... | collective-permute-start | bytes 233480 | tf_op jit(solution)/shard_map/ppermute | solution.py:129
  39.0 0.3 collective-permute-start.14
  39.4 0.0 collective-permute-done.7.inner_column
  39.4 0.0 collective-permute-done.6.outer_column
  39.4 1.6 %shard_map.161 = (bf16[64,8,128]{2,1,0:T(8,128)(2,1)}, bf16[64,8,128]{2,1,0:T(8,128)(2,1)}, f32[8,128]{1,0:T(8,128)S(1)}) custom-call(f32[1024,128]{1,0:T(8,128)S(1)} %get-tuple-element.94.wide, bf16[3,128,768]{2,1,0:T(8,128)(2,1)S(1)} %get-tuple-element.95.turned, bf16[256,128]{1,0:T(8,128)(2,1)S(1)} %collective-permute-done.4.outer.outer_row, ...), custom_call_target="tpu_custom_call" | custom-call | flops 12079595520 | bytes 2000000 | tf_op jit(solution)/shard_map/pallas_call | solution.py:45
  40.9 0.2 collective-permute-done.16.refs_2_
  41.1 1.5 %collective-permute-done.15.refs_1_ = bf16[304,128]{1,0:T(8,128)(2,1)S(1)} collective-permute-done((bf16[304,128]{1,0:T(8,128)(2,1)S(1)}, bf16[304,128]{1,0:T(8,128)(2,1)S(1)}, u32[]{:S(2)}, u32[]{:S(2)}) %collective-permute-start.15) | collective-permute-done | bytes 77856 | tf_op jit(solution)/shard_map/ppermute | solution.py:129
  42.6 0.1 collective-permute-start.17
  42.7 0.8 %collective-permute-done.14.late = bf16[304,128]{1,0:T(8,128)(2,1)S(1)} collective-permute-done((bf16[304,128]{1,0:T(8,128)(2,1)S(1)}, bf16[304,128]{1,0:T(8,128)(2,1)S(1)}, u32[]{:S(2)}, u32[]{:S(2)}) %collective-permute-start.14) | collective-permute-done | bytes 77856 | tf_op jit(solution)/shard_map/ppermute | solution.py:129
  43.4 0.9 %shard_map.168 = (f32[9,256,128]{2,1,0:T(8,128)}, f32[8,128]{1,0:T(8,128)S(1)}) custom-call(bf16[304,128]{1,0:T(8,128)(2,1)S(1)} %collective-permute-done.14.late, bf16[3,304,128]{2,1,0:T(8,128)(2,1)S(1)} %shard_map.167.early), custom_call_target="tpu_custom_call" | custom-call | flops 12079595520 | bytes 884736 | tf_op jit(solution)/shard_map/pallas_call | solution.py:45
  44.4 0.3 collective-permute-done.18.late
  44.7 0.0 collective-permute-done.17.early
  44.7 0.9 %shard_map.169 = (f32[9,256,128]{2,1,0:T(8,128)}, f32[256]{0:T(256)}) custom-call(f32[8,128]{1,0:T(8,128)S(1)} %get-tuple-element.113.bias_own, bf16[3,304,128]{2,1,0:T(8,128)(2,1)S(1)} %collective-permute-done.17.early, bf16[304,128]{1,0:T(8,128)(2,1)S(1)} %collective-permute-done.18.late, ...), custom_call_target="tpu_custom_call", output_to_operand_aliasing={{0}: (4, {})} | custom-call | bytes 884736 | tf_op jit(solution)/shard_map/pallas_call | solution.py:45
  (7 shorter events, 0.1 us)
Async XLA Ops:
  1.6 6.5 %collective-permute-start = (bf16[128,128]{1,0:T(8,128)(2,1)S(1)}, bf16[128,128]{1,0:T(8,128)(2,1)S(1)}, u32[]{:S(2)}, u32[]{:S(2)}) collective-permute-start(bf16[128,128]{1,0:T(8,128)(2,1)S(1)} %get-tuple-element.64), channel_id=1, source_target_pairs={{0,8},{1,9},{2,10},{3,11},{4,12},{5,13},{6,14},{7,15},{8,0},{9,1},... | collective-permute-start | bytes 98312 | tf_op jit(solution)/shard_map/ppermute | solution.py:129
  2.2 6.0 %collective-permute-start.1 = (bf16[128,128]{1,0:T(8,128)(2,1)S(1)}, bf16[128,128]{1,0:T(8,128)(2,1)S(1)}, u32[]{:S(2)}, u32[]{:S(2)}) collective-permute-start(bf16[128,128]{1,0:T(8,128)(2,1)S(1)} %get-tuple-element.65), channel_id=1, source_target_pairs={{0,4},{1,5},{2,6},{3,7},{4,0},{5,1},{6,2},{7,3},{8,16},{9,17},{10,... | collective-permute-start | bytes 98312 | tf_op jit(solution)/shard_map/ppermute | solution.py:129
  8.3 7.4 %collective-permute-start.3 = (bf16[32,128]{1,0:T(8,128)(2,1)S(1)}, bf16[32,128]{1,0:T(8,128)(2,1)S(1)}, u32[]{:S(2)}, u32[]{:S(2)}) collective-permute-start(bf16[32,128]{1,0:T(8,128)(2,1)S(1)} %get-tuple-element.82), channel_id=1, source_target_pairs={{0,1},{1,0},{2,3},{3,2},{4,5},{5,4},{6,7},{7,6},{8,9},{9,8},{10,11... | collective-permute-start | bytes 24584 | tf_op jit(solution)/shard_map/ppermute | solution.py:129
  9.8 6.3 %collective-permute-start.2 = (bf16[32,128]{1,0:T(8,128)(2,1)S(1)}, bf16[32,128]{1,0:T(8,128)(2,1)S(1)}, u32[]{:S(2)}, u32[]{:S(2)}) collective-permute-start(bf16[32,128]{1,0:T(8,128)(2,1)S(1)} %get-tuple-element.82), channel_id=1, source_target_pairs={{0,7},{1,2},{2,1},{3,4},{4,3},{5,6},{6,5},{7,0},{8,15},{9,10},{10,... | collective-permute-start | bytes 24584 | tf_op jit(solution)/shard_map/ppermute | solution.py:129
  17.1 1.6 %collective-permute-start.8 = (bf16[1152,128]{1,0:T(8,128)(2,1)S(1)}, bf16[1152,128]{1,0:T(8,128)(2,1)S(1)}, u32[]{:S(2)}, u32[]{:S(2)}) collective-permute-start(bf16[1152,128]{1,0:T(8,128)(2,1)S(1)} %get-tuple-element.106), channel_id=1, source_target_pairs={{0,8},{1,9},{2,10},{3,11},{4,12},{5,13},{6,14},{7,15},{8,0},{9,1},... | collective-permute-start | bytes 884744 | tf_op jit(solution)/shard_map/ppermute | solution.py:129
  18.8 6.2 %collective-permute-start.9 = (bf16[304,128]{1,0:T(8,128)(2,1)S(1)}, bf16[304,128]{1,0:T(8,128)(2,1)S(1)}, u32[]{:S(2)}, u32[]{:S(2)}) collective-permute-start(bf16[304,128]{1,0:T(8,128)(2,1)S(1)} %get-tuple-element.108), channel_id=1, source_target_pairs={{0,17},{1,16},{2,19},{3,18},{4,21},{5,20},{6,23},{7,22},{8,25},{9,... | collective-permute-start | bytes 233480 | tf_op jit(solution)/shard_map/ppermute | solution.py:129
  18.9 6.1 %collective-permute-start.10 = (bf16[304,128]{1,0:T(8,128)(2,1)S(1)}, bf16[304,128]{1,0:T(8,128)(2,1)S(1)}, u32[]{:S(2)}, u32[]{:S(2)}) collective-permute-start(bf16[304,128]{1,0:T(8,128)(2,1)S(1)} %get-tuple-element.109), channel_id=1, source_target_pairs={{0,1},{1,0},{2,3},{3,2},{4,5},{5,4},{6,7},{7,6},{8,9},{9,8},{10,11... | collective-permute-start | bytes 233480 | tf_op jit(solution)/shard_map/ppermute | solution.py:129
  20.3 4.8 %collective-permute-start.11 = (bf16[304,128]{1,0:T(8,128)(2,1)S(1)}, bf16[304,128]{1,0:T(8,128)(2,1)S(1)}, u32[]{:S(2)}, u32[]{:S(2)}) collective-permute-start(bf16[304,128]{1,0:T(8,128)(2,1)S(1)} %get-tuple-element.110), channel_id=1, source_target_pairs={{0,16},{1,17},{2,18},{3,19},{4,20},{5,21},{6,22},{7,23},{8,24},{9,... | collective-permute-start | bytes 233480 | tf_op jit(solution)/shard_map/ppermute | solution.py:129
  25.1 4.5 %collective-permute-start.12 = (bf16[304,128]{1,0:T(8,128)(2,1)S(1)}, bf16[304,128]{1,0:T(8,128)(2,1)S(1)}, u32[]{:S(2)}, u32[]{:S(2)}) collective-permute-start(bf16[304,128]{1,0:T(8,128)(2,1)S(1)} %shard_map.164.own), channel_id=1, source_target_pairs={{0,2},{1,3},{2,0},{3,1},{4,6},{5,7},{6,4},{7,5},{8,12},{9,13},{10,... | collective-permute-start | bytes 233480 | tf_op jit(solution)/shard_map/ppermute | solution.py:129
  25.1 7.1 %collective-permute-start.4 = (bf16[256,128]{1,0:T(8,128)(2,1)S(1)}, bf16[256,128]{1,0:T(8,128)(2,1)S(1)}, u32[]{:S(2)}, u32[]{:S(2)}) collective-permute-start(bf16[256,128]{1,0:T(8,128)(2,1)S(1)} %get-tuple-element.96), channel_id=1, source_target_pairs={{0,4},{1,5},{2,6},{3,7},{4,0},{5,1},{6,2},{7,3},{8,16},{9,17},{10,... | collective-permute-start | bytes 196616 | tf_op jit(solution)/shard_map/ppermute | solution.py:129
  29.3 2.9 %collective-permute-start.5 = (bf16[256,128]{1,0:T(8,128)(2,1)S(1)}, bf16[256,128]{1,0:T(8,128)(2,1)S(1)}, u32[]{:S(2)}, u32[]{:S(2)}) collective-permute-start(bf16[256,128]{1,0:T(8,128)(2,1)S(1)} %get-tuple-element.97), channel_id=1, source_target_pairs={{0,8},{1,9},{2,10},{3,11},{4,12},{5,13},{6,14},{7,15},{8,0},{9,1},... | collective-permute-start | bytes 196616 | tf_op jit(solution)/shard_map/ppermute | solution.py:129
  29.6 6.2 %collective-permute-start.13 = (bf16[304,128]{1,0:T(8,128)(2,1)S(1)}, bf16[304,128]{1,0:T(8,128)(2,1)S(1)}, u32[]{:S(2)}, u32[]{:S(2)}) collective-permute-start(bf16[304,128]{1,0:T(8,128)(2,1)S(1)} %shard_map.165.own), channel_id=1, source_target_pairs={{0,4},{1,5},{2,6},{3,7},{4,0},{5,1},{6,2},{7,3},{8,10},{9,11},{10,... | collective-permute-start | bytes 233480 | tf_op jit(solution)/shard_map/ppermute | solution.py:129
  32.4 6.9 %collective-permute-start.7 = (bf16[64,128]{1,0:T(8,128)(2,1)S(1)}, bf16[64,128]{1,0:T(8,128)(2,1)S(1)}, u32[]{:S(2)}, u32[]{:S(2)}) collective-permute-start(bf16[64,128]{1,0:T(8,128)(2,1)S(1)} %shard_map.160), channel_id=1, source_target_pairs={{0,1},{1,0},{2,3},{3,2},{4,5},{5,4},{6,7},{7,6},{8,9},{9,8},{10,11... | collective-permute-start | bytes 49160 | tf_op jit(solution)/shard_map/ppermute | solution.py:129
  32.7 6.7 %collective-permute-start.6 = (bf16[64,128]{1,0:T(8,128)(2,1)S(1)}, bf16[64,128]{1,0:T(8,128)(2,1)S(1)}, u32[]{:S(2)}, u32[]{:S(2)}) collective-permute-start(bf16[64,128]{1,0:T(8,128)(2,1)S(1)} %shard_map.160), channel_id=1, source_target_pairs={{0,7},{1,2},{2,1},{3,4},{4,3},{5,6},{6,5},{7,0},{8,15},{9,10},{10,... | collective-permute-start | bytes 49160 | tf_op jit(solution)/shard_map/ppermute | solution.py:129
  35.7 5.4 %collective-permute-start.16 = (bf16[304,128]{1,0:T(8,128)(2,1)S(1)}, bf16[304,128]{1,0:T(8,128)(2,1)S(1)}, u32[]{:S(2)}, u32[]{:S(2)}) collective-permute-start(bf16[304,128]{1,0:T(8,128)(2,1)S(1)} %shard_map.166.refs_0_), channel_id=1, source_target_pairs={{0,17},{1,16},{2,19},{3,18},{4,21},{5,20},{6,23},{7,22},{8,25},{9,... | collective-permute-start | bytes 233480 | tf_op jit(solution)/shard_map/ppermute | solution.py:129
  38.2 4.4 %collective-permute-start.15 = (bf16[304,128]{1,0:T(8,128)(2,1)S(1)}, bf16[304,128]{1,0:T(8,128)(2,1)S(1)}, u32[]{:S(2)}, u32[]{:S(2)}) collective-permute-start(bf16[304,128]{1,0:T(8,128)(2,1)S(1)} %shard_map.166.refs_0_), channel_id=1, source_target_pairs={{0,1},{1,0},{2,3},{3,2},{4,5},{5,4},{6,7},{7,6},{8,9},{9,8},{10,11... | collective-permute-start | bytes 233480 | tf_op jit(solution)/shard_map/ppermute | solution.py:129
  39.0 4.4 %collective-permute-start.14 = (bf16[304,128]{1,0:T(8,128)(2,1)S(1)}, bf16[304,128]{1,0:T(8,128)(2,1)S(1)}, u32[]{:S(2)}, u32[]{:S(2)}) collective-permute-start(bf16[304,128]{1,0:T(8,128)(2,1)S(1)} %shard_map.166.refs_0_), channel_id=1, source_target_pairs={{0,16},{1,17},{2,18},{3,19},{4,20},{5,21},{6,22},{7,23},{8,24},{9,... | collective-permute-start | bytes 233480 | tf_op jit(solution)/shard_map/ppermute | solution.py:129
  42.6 2.1 %collective-permute-start.17 = (bf16[3,304,128]{2,1,0:T(8,128)(2,1)S(1)}, bf16[3,304,128]{2,1,0:T(8,128)(2,1)S(1)}, u32[]{:S(2)}, u32[]{:S(2)}) collective-permute-start(bf16[3,304,128]{2,1,0:T(8,128)(2,1)S(1)} %shard_map.167.early), channel_id=1, source_target_pairs={{0,8},{1,9},{2,10},{3,11},{4,12},{5,13},{6,14},{7,15},{8,0},{9,1},... | collective-permute-start | bytes 700424 | tf_op jit(solution)/shard_map/ppermute | solution.py:129
  43.4 1.3 %collective-permute-start.18 = (bf16[304,128]{1,0:T(8,128)(2,1)S(1)}, bf16[304,128]{1,0:T(8,128)(2,1)S(1)}, u32[]{:S(2)}, u32[]{:S(2)}) collective-permute-start(bf16[304,128]{1,0:T(8,128)(2,1)S(1)} %collective-permute-done.14.late), channel_id=1, source_target_pairs={{0,8},{1,9},{2,10},{3,11},{4,12},{5,13},{6,14},{7,15},{8,0},{9,1},... | collective-permute-start | bytes 233480 | tf_op jit(solution)/shard_map/ppermute | solution.py:129

commit v15 on v14

--- a/solution.py
+++ b/solution.py
@@ -64,7 +64,7 @@
         self.half = lon_count // 2
         self.taps, self.half_gates = taps, gate_count // 2
         self.plane = lat_count
-        self.scatter_steps = [self.plane - 1, *range(1, self.plane - 1)]
+        self.scatter_steps = [1, self.plane - 1, *range(2, self.plane - 1)]
         whole = [("lon", 1 << k) for k in range(1, lon_count.bit_length() - 1)]
         self.orders = ([("lat", 1)] + whole, [("lat", 1)] + whole[::-1])
         step = 8 * self.plane

time: 45.8 us -> 46.5 us (1.015)
  waiting for transfers between devices: 5.32 us -> 7.6 us
  starting transfers between devices: 26.4 us -> 24.8 us
    ppermute x19, waiting for transfers between devices: 5.32 us -> 7.6 us  [permuted(): return lax.ppermute(value, AXES, pairs)]
    ppermute x19, starting transfers between devices: 26.4 us -> 24.8 us  [permuted(): return lax.ppermute(value, AXES, pairs)]
  transfers between devices with their start and end apart: 19 -> 19, of which waited for: 9 -> 11; matrix products, arithmetic and copies ran while one was open for 0% -> 0% of each run, Pallas kernels for 22% -> 22%
where the time goes in v15:
time: 46.5 us; the launch traced here: 46.3 us
  starting transfers between devices  24.8 us (53%)
  Pallas kernels  13.1 us (28%)
  waiting for transfers between devices  7.6 us (16%)
  between operations  0.78 us (2%)
    ppermute x19, starting transfers between devices, permuted(): return lax.ppermute(value, AXES, pairs)  24.8 us
    pallas_call x17, Pallas kernels, run(): pl.pallas_call(kernel, out_shape=out_shape, in_specs=[VMEM] * near + [HBM...  13.1 us
    ppermute x19, waiting for transfers between devices, permuted(): return lax.ppermute(value, AXES, pairs)  7.6 us
  transfers between devices with their start and end apart: 19, of which 11 were waited for; matrix products, arithmetic and copies ran while one was open for 0% of the time, Pallas kernels for 22%

profile of v15, /device:TPU:0, one launch (start us, length us, event | category | flops | bytes accessed | tf_op | source)
XLA Modules:
  0.0 46.3 jit_solution(6063632893262353984)
XLA Ops:
  0.6 1.0 %shard_map.153 = (bf16[128,128]{1,0:T(8,128)(2,1)S(1)}, bf16[128,128]{1,0:T(8,128)(2,1)S(1)}, f32[1024,128]{1,0:T(8,128)S(1)}) custom-call(bf16[64,8,128]{2,1,0:T(8,128)(2,1)} %below.1, bf16[64,8,128]{2,1,0:T(8,128)(2,1)} %hidden.1), custom_call_target="tpu_custom_call" | custom-call | bytes 524288 | tf_op jit(solution)/shard_map/pallas_call | solution.py:45
  1.6 0.5 %collective-permute-start = (bf16[128,128]{1,0:T(8,128)(2,1)S(1)}, bf16[128,128]{1,0:T(8,128)(2,1)S(1)}, u32[]{:S(2)}, u32[]{:S(2)}) collective-permute-start(bf16[128,128]{1,0:T(8,128)(2,1)S(1)} %get-tuple-element.64), channel_id=1, source_target_pairs={{0,8},{1,9},{2,10},{3,11},{4,12},{5,13},{6,14},{7,15},{8,0},{9,1},... | collective-permute-start | bytes 98312 | tf_op jit(solution)/shard_map/ppermute | solution.py:129
  2.2 3.7 %collective-permute-start.1 = (bf16[128,128]{1,0:T(8,128)(2,1)S(1)}, bf16[128,128]{1,0:T(8,128)(2,1)S(1)}, u32[]{:S(2)}, u32[]{:S(2)}) collective-permute-start(bf16[128,128]{1,0:T(8,128)(2,1)S(1)} %get-tuple-element.65), channel_id=1, source_target_pairs={{0,4},{1,5},{2,6},{3,7},{4,0},{5,1},{6,2},{7,3},{8,16},{9,17},{10,... | collective-permute-start | bytes 98312 | tf_op jit(solution)/shard_map/ppermute | solution.py:129
  5.8 2.3 %shard_map.154 = (bf16[8,128,128]{2,1,0:T(8,128)(2,1)S(1)}, f32[128,128]{1,0:T(8,128)S(1)}, f32[128,128]{1,0:T(8,128)S(1)}, f32[64,128]{1,0:T(8,128)S(1)}, f32[6...) custom-call(f32[1024,128]{1,0:T(8,128)S(1)} %get-tuple-element.62.wi, ...), custom_call_target="tpu_custom_call" | custom-call | bytes 6000000 | tf_op jit(solution)/shard_map/pallas_call | solution.py:45
  8.1 0.0 collective-permute-done.inner_row.inner
  8.1 0.0 collective-permute-done.1.outer_row.outer
  8.1 0.2 shard_map.156
  8.3 1.5 %collective-permute-start.3 = (bf16[32,128]{1,0:T(8,128)(2,1)S(1)}, bf16[32,128]{1,0:T(8,128)(2,1)S(1)}, u32[]{:S(2)}, u32[]{:S(2)}) collective-permute-start(bf16[32,128]{1,0:T(8,128)(2,1)S(1)} %get-tuple-element.82), channel_id=1, source_target_pairs={{0,1},{1,0},{2,3},{3,2},{4,5},{5,4},{6,7},{7,6},{8,9},{9,8},{10,11... | collective-permute-start | bytes 24584 | tf_op jit(solution)/shard_map/ppermute | solution.py:129
  9.8 3.7 %collective-permute-start.2 = (bf16[32,128]{1,0:T(8,128)(2,1)S(1)}, bf16[32,128]{1,0:T(8,128)(2,1)S(1)}, u32[]{:S(2)}, u32[]{:S(2)}) collective-permute-start(bf16[32,128]{1,0:T(8,128)(2,1)S(1)} %get-tuple-element.82), channel_id=1, source_target_pairs={{0,7},{1,2},{2,1},{3,4},{4,3},{5,6},{6,5},{7,0},{8,15},{9,10},{10,... | collective-permute-start | bytes 24584 | tf_op jit(solution)/shard_map/ppermute | solution.py:129
  13.5 2.2 %shard_map.155 = (f32[512,128]{1,0:T(8,128)S(1)}, f32[512,128]{1,0:T(8,128)S(1)}, f32[512,128]{1,0:T(8,128)S(1)}, bf16[256,1024]{1,0:T(8,128)(2,1)S(1)}, bf16[12...) custom-call(bf16[8,128,128]{2,1,0:T(8,128)(2,1)S(1)} %get-tuple-element.63.rows_in, ...), custom_call_target="tpu_custom_call" | custom-call | flops 1207959552 | bytes 6000000 | tf_op jit(solution)/shard_map/pallas_call | solution.py:45
  15.7 0.0 collective-permute-done.3.inner_column
  15.7 0.4 collective-permute-done.2.outer_column
  16.2 0.9 %shard_map.157 = (bf16[1152,128]{1,0:T(8,128)(2,1)S(1)}, bf16[256,128]{1,0:T(8,128)(2,1)S(1)}, f32[256,128]{1,0:T(8,128)S(1)}, bf16[1152,128]{1,0:T(8,128)(2,1)S...) custom-call(bf16[128,128]{1,0:T(8,128)(2,1)S(1)} %get-tuple-element.80.edge, ...), custom_call_target="tpu_custom_call" | custom-call | tf_op jit(solution)/shard_map/pallas_call | solution.py:45
  17.1 0.1 collective-permute-start.8
  17.1 0.3 shard_map.162
  17.4 1.3 %collective-permute-done.8.received = bf16[1152,128]{1,0:T(8,128)(2,1)S(1)} collective-permute-done((bf16[1152,128]{1,0:T(8,128)(2,1)S(1)}, bf16[1152,128]{1,0:T(8,128)(2,1)S(1)}, u32[]{:S(2)}, u32[]{:S(2)}) %collective-permute-start.8) | collective-permute-done | bytes 294944 | tf_op jit(solution)/shard_map/ppermute | solution.py:129
  18.7 0.1 shard_map.163
  18.8 0.1 collective-permute-start.9
  18.9 1.4 %collective-permute-start.10 = (bf16[304,128]{1,0:T(8,128)(2,1)S(1)}, bf16[304,128]{1,0:T(8,128)(2,1)S(1)}, u32[]{:S(2)}, u32[]{:S(2)}) collective-permute-start(bf16[304,128]{1,0:T(8,128)(2,1)S(1)} %get-tuple-element.109), channel_id=1, source_target_pairs={{0,17},{1,16},{2,19},{3,18},{4,21},{5,20},{6,23},{7,22},{8,25},{9,... | collective-permute-start | bytes 233480 | tf_op jit(solution)/shard_map/ppermute | solution.py:129
  20.3 2.1 %collective-permute-start.11 = (bf16[304,128]{1,0:T(8,128)(2,1)S(1)}, bf16[304,128]{1,0:T(8,128)(2,1)S(1)}, u32[]{:S(2)}, u32[]{:S(2)}) collective-permute-start(bf16[304,128]{1,0:T(8,128)(2,1)S(1)} %get-tuple-element.110), channel_id=1, source_target_pairs={{0,16},{1,17},{2,18},{3,19},{4,20},{5,21},{6,22},{7,23},{8,24},{9,... | collective-permute-start | bytes 233480 | tf_op jit(solution)/shard_map/ppermute | solution.py:129
  22.4 1.4 %shard_map.158 = (bf16[64,8,128]{2,1,0:T(8,128)(2,1)}, f32[512,128]{1,0:T(8,128)}, f32[512,128]{1,0:T(8,128)}, bf16[256,1024]{1,0:T(8,128)(2,1)S(1)}, bf16[256,1...) custom-call(f32[512,128]{1,0:T(8,128)S(1)} %get-tuple-element.75.hidden, f32[512,128]{1,0:T(8,128)S(1)} %get-tuple-element.76.cell, ...), custom_call_target="tpu_custom_call" | custom-call | bytes 4000000 | tf_op jit(solution)/shard_map/pallas_call | solution.py:45
  23.7 1.1 %shard_map.159 = (f32[1024,128]{1,0:T(8,128)S(1)}, bf16[3,128,768]{2,1,0:T(8,128)(2,1)S(1)}, f32[8,128]{1,0:T(8,128)S(1)}) custom-call(bf16[256,1024]{1,0:T(8,128)(2,1)S(1)} %get-tuple-element.93.pre, bf16[256,1152]{1,0:T(8,128)(2,1)S(1)} %get-tuple-element.68.weights), custom_call_target="tpu_custom_call" | custom-call | flops 603979776 | bytes 3000000 | tf_op jit(solution)/shard_map/pallas_call | solution.py:45
  24.9 0.0 collective-permute-done.9.refs_0_
  24.9 0.2 collective-permute-done.10.refs_1_
  25.1 1.1 %collective-permute-done.11.refs_2_ = bf16[304,128]{1,0:T(8,128)(2,1)S(1)} collective-permute-done((bf16[304,128]{1,0:T(8,128)(2,1)S(1)}, bf16[304,128]{1,0:T(8,128)(2,1)S(1)}, u32[]{:S(2)}, u32[]{:S(2)}) %collective-permute-start.11) | collective-permute-done | bytes 77856 | tf_op jit(solution)/shard_map/ppermute | solution.py:129
  26.2 0.1 collective-permute-start.12
  26.2 3.4 %collective-permute-start.4 = (bf16[256,128]{1,0:T(8,128)(2,1)S(1)}, bf16[256,128]{1,0:T(8,128)(2,1)S(1)}, u32[]{:S(2)}, u32[]{:S(2)}) collective-permute-start(bf16[256,128]{1,0:T(8,128)(2,1)S(1)} %get-tuple-element.96), channel_id=1, source_target_pairs={{0,4},{1,5},{2,6},{3,7},{4,0},{5,1},{6,2},{7,3},{8,16},{9,17},{10,... | collective-permute-start | bytes 196616 | tf_op jit(solution)/shard_map/ppermute | solution.py:129
  29.6 0.0 collective-permute-start.5
  29.7 1.4 %collective-permute-done.12.received = bf16[304,128]{1,0:T(8,128)(2,1)S(1)} collective-permute-done((bf16[304,128]{1,0:T(8,128)(2,1)S(1)}, bf16[304,128]{1,0:T(8,128)(2,1)S(1)}, u32[]{:S(2)}, u32[]{:S(2)}) %collective-permute-start.12) | collective-permute-done | bytes 77856 | tf_op jit(solution)/shard_map/ppermute | solution.py:129
  31.1 1.0 %collective-permute-start.13 = (bf16[304,128]{1,0:T(8,128)(2,1)S(1)}, bf16[304,128]{1,0:T(8,128)(2,1)S(1)}, u32[]{:S(2)}, u32[]{:S(2)}) collective-permute-start(bf16[304,128]{1,0:T(8,128)(2,1)S(1)} %shard_map.165.own), channel_id=1, source_target_pairs={{0,4},{1,5},{2,6},{3,7},{4,0},{5,1},{6,2},{7,3},{8,10},{9,11},{10,... | collective-permute-start | bytes 233480 | tf_op jit(solution)/shard_map/ppermute | solution.py:129
  32.1 0.2 shard_map.160
  32.3 1.9 %collective-permute-start.7 = (bf16[64,128]{1,0:T(8,128)(2,1)S(1)}, bf16[64,128]{1,0:T(8,128)(2,1)S(1)}, u32[]{:S(2)}, u32[]{:S(2)}) collective-permute-start(bf16[64,128]{1,0:T(8,128)(2,1)S(1)} %shard_map.160), channel_id=1, source_target_pairs={{0,1},{1,0},{2,3},{3,2},{4,5},{5,4},{6,7},{7,6},{8,9},{9,8},{10,11... | collective-permute-start | bytes 49160 | tf_op jit(solution)/shard_map/ppermute | solution.py:129
  34.3 1.8 %collective-permute-start.6 = (bf16[64,128]{1,0:T(8,128)(2,1)S(1)}, bf16[64,128]{1,0:T(8,128)(2,1)S(1)}, u32[]{:S(2)}, u32[]{:S(2)}) collective-permute-start(bf16[64,128]{1,0:T(8,128)(2,1)S(1)} %shard_map.160), channel_id=1, source_target_pairs={{0,7},{1,2},{2,1},{3,4},{4,3},{5,6},{6,5},{7,0},{8,15},{9,10},{10,... | collective-permute-start | bytes 49160 | tf_op jit(solution)/shard_map/ppermute | solution.py:129
  36.1 0.9 %collective-permute-done.13.received = bf16[304,128]{1,0:T(8,128)(2,1)S(1)} collective-permute-done((bf16[304,128]{1,0:T(8,128)(2,1)S(1)}, bf16[304,128]{1,0:T(8,128)(2,1)S(1)}, u32[]{:S(2)}, u32[]{:S(2)}) %collective-permute-start.13) | collective-permute-done | bytes 77856 | tf_op jit(solution)/shard_map/ppermute | solution.py:129
  37.0 1.2 %collective-permute-start.16 = (bf16[304,128]{1,0:T(8,128)(2,1)S(1)}, bf16[304,128]{1,0:T(8,128)(2,1)S(1)}, u32[]{:S(2)}, u32[]{:S(2)}) collective-permute-start(bf16[304,128]{1,0:T(8,128)(2,1)S(1)} %shard_map.166.refs_0_), channel_id=1, source_target_pairs={{0,17},{1,16},{2,19},{3,18},{4,21},{5,20},{6,23},{7,22},{8,25},{9,... | collective-permute-start | bytes 233480 | tf_op jit(solution)/shard_map/ppermute | solution.py:129
  38.2 1.6 %collective-permute-start.15 = (bf16[304,128]{1,0:T(8,128)(2,1)S(1)}, bf16[304,128]{1,0:T(8,128)(2,1)S(1)}, u32[]{:S(2)}, u32[]{:S(2)}) collective-permute-start(bf16[304,128]{1,0:T(8,128)(2,1)S(1)} %shard_map.166.refs_0_), channel_id=1, source_target_pairs={{0,1},{1,0},{2,3},{3,2},{4,5},{5,4},{6,7},{7,6},{8,9},{9,8},{10,11... | collective-permute-start | bytes 233480 | tf_op jit(solution)/shard_map/ppermute | solution.py:129
  39.7 0.8 %collective-permute-start.14 = (bf16[304,128]{1,0:T(8,128)(2,1)S(1)}, bf16[304,128]{1,0:T(8,128)(2,1)S(1)}, u32[]{:S(2)}, u32[]{:S(2)}) collective-permute-start(bf16[304,128]{1,0:T(8,128)(2,1)S(1)} %shard_map.166.refs_0_), channel_id=1, source_target_pairs={{0,16},{1,17},{2,18},{3,19},{4,20},{5,21},{6,22},{7,23},{8,24},{9,... | collective-permute-start | bytes 233480 | tf_op jit(solution)/shard_map/ppermute | solution.py:129
  40.5 0.0 collective-permute-done.7.inner_column
  40.5 0.1 collective-permute-done.6.outer_column
  40.7 1.6 %shard_map.161 = (bf16[64,8,128]{2,1,0:T(8,128)(2,1)}, bf16[64,8,128]{2,1,0:T(8,128)(2,1)}, f32[8,128]{1,0:T(8,128)S(1)}) custom-call(f32[1024,128]{1,0:T(8,128)S(1)} %get-tuple-element.94.wide, bf16[3,128,768]{2,1,0:T(8,128)(2,1)S(1)} %get-tuple-element.95.turned, bf16[256,128]{1,0:T(8,128)(2,1)S(1)} %collective-permute-done.4.outer.outer_row, ...), custom_call_target="tpu_custom_call" | custom-call | flops 12079595520 | bytes 2000000 | tf_op jit(solution)/shard_map/pallas_call | solution.py:45
  42.3 0.2 collective-permute-done.16.refs_2_
  42.4 0.8 %collective-permute-done.15.refs_1_ = bf16[304,128]{1,0:T(8,128)(2,1)S(1)} collective-permute-done((bf16[304,128]{1,0:T(8,128)(2,1)S(1)}, bf16[304,128]{1,0:T(8,128)(2,1)S(1)}, u32[]{:S(2)}, u32[]{:S(2)}) %collective-permute-start.15) | collective-permute-done | bytes 77856 | tf_op jit(solution)/shard_map/ppermute | solution.py:129
  43.2 0.1 collective-permute-start.17
  43.3 0.8 %collective-permute-done.14.late = bf16[304,128]{1,0:T(8,128)(2,1)S(1)} collective-permute-done((bf16[304,128]{1,0:T(8,128)(2,1)S(1)}, bf16[304,128]{1,0:T(8,128)(2,1)S(1)}, u32[]{:S(2)}, u32[]{:S(2)}) %collective-permute-start.14) | collective-permute-done | bytes 77856 | tf_op jit(solution)/shard_map/ppermute | solution.py:129
  44.1 0.9 %shard_map.168 = (f32[9,256,128]{2,1,0:T(8,128)}, f32[8,128]{1,0:T(8,128)S(1)}) custom-call(bf16[304,128]{1,0:T(8,128)(2,1)S(1)} %collective-permute-done.14.late, bf16[3,304,128]{2,1,0:T(8,128)(2,1)S(1)} %shard_map.167.early), custom_call_target="tpu_custom_call" | custom-call | flops 12079595520 | bytes 884736 | tf_op jit(solution)/shard_map/pallas_call | solution.py:45
  45.1 0.3 collective-permute-done.18.late
  45.4 0.0 collective-permute-done.17.early
  45.4 0.9 %shard_map.169 = (f32[9,256,128]{2,1,0:T(8,128)}, f32[256]{0:T(256)}) custom-call(f32[8,128]{1,0:T(8,128)S(1)} %get-tuple-element.113.bias_own, bf16[3,304,128]{2,1,0:T(8,128)(2,1)S(1)} %collective-permute-done.17.early, bf16[304,128]{1,0:T(8,128)(2,1)S(1)} %collective-permute-done.18.late, ...), custom_call_target="tpu_custom_call", output_to_operand_aliasing={{0}: (4, {})} | custom-call | bytes 884736 | tf_op jit(solution)/shard_map/pallas_call | solution.py:45
  (7 shorter events, 0.1 us)
Async XLA Ops:
  1.6 6.5 %collective-permute-start = (bf16[128,128]{1,0:T(8,128)(2,1)S(1)}, bf16[128,128]{1,0:T(8,128)(2,1)S(1)}, u32[]{:S(2)}, u32[]{:S(2)}) collective-permute-start(bf16[128,128]{1,0:T(8,128)(2,1)S(1)} %get-tuple-element.64), channel_id=1, source_target_pairs={{0,8},{1,9},{2,10},{3,11},{4,12},{5,13},{6,14},{7,15},{8,0},{9,1},... | collective-permute-start | bytes 98312 | tf_op jit(solution)/shard_map/ppermute | solution.py:129
  2.2 6.0 %collective-permute-start.1 = (bf16[128,128]{1,0:T(8,128)(2,1)S(1)}, bf16[128,128]{1,0:T(8,128)(2,1)S(1)}, u32[]{:S(2)}, u32[]{:S(2)}) collective-permute-start(bf16[128,128]{1,0:T(8,128)(2,1)S(1)} %get-tuple-element.65), channel_id=1, source_target_pairs={{0,4},{1,5},{2,6},{3,7},{4,0},{5,1},{6,2},{7,3},{8,16},{9,17},{10,... | collective-permute-start | bytes 98312 | tf_op jit(solution)/shard_map/ppermute | solution.py:129
  8.3 7.4 %collective-permute-start.3 = (bf16[32,128]{1,0:T(8,128)(2,1)S(1)}, bf16[32,128]{1,0:T(8,128)(2,1)S(1)}, u32[]{:S(2)}, u32[]{:S(2)}) collective-permute-start(bf16[32,128]{1,0:T(8,128)(2,1)S(1)} %get-tuple-element.82), channel_id=1, source_target_pairs={{0,1},{1,0},{2,3},{3,2},{4,5},{5,4},{6,7},{7,6},{8,9},{9,8},{10,11... | collective-permute-start | bytes 24584 | tf_op jit(solution)/shard_map/ppermute | solution.py:129
  9.8 6.3 %collective-permute-start.2 = (bf16[32,128]{1,0:T(8,128)(2,1)S(1)}, bf16[32,128]{1,0:T(8,128)(2,1)S(1)}, u32[]{:S(2)}, u32[]{:S(2)}) collective-permute-start(bf16[32,128]{1,0:T(8,128)(2,1)S(1)} %get-tuple-element.82), channel_id=1, source_target_pairs={{0,7},{1,2},{2,1},{3,4},{4,3},{5,6},{6,5},{7,0},{8,15},{9,10},{10,... | collective-permute-start | bytes 24584 | tf_op jit(solution)/shard_map/ppermute | solution.py:129
  17.1 1.6 %collective-permute-start.8 = (bf16[1152,128]{1,0:T(8,128)(2,1)S(1)}, bf16[1152,128]{1,0:T(8,128)(2,1)S(1)}, u32[]{:S(2)}, u32[]{:S(2)}) collective-permute-start(bf16[1152,128]{1,0:T(8,128)(2,1)S(1)} %get-tuple-element.106), channel_id=1, source_target_pairs={{0,8},{1,9},{2,10},{3,11},{4,12},{5,13},{6,14},{7,15},{8,0},{9,1},... | collective-permute-start | bytes 884744 | tf_op jit(solution)/shard_map/ppermute | solution.py:129
  18.8 6.1 %collective-permute-start.9 = (bf16[304,128]{1,0:T(8,128)(2,1)S(1)}, bf16[304,128]{1,0:T(8,128)(2,1)S(1)}, u32[]{:S(2)}, u32[]{:S(2)}) collective-permute-start(bf16[304,128]{1,0:T(8,128)(2,1)S(1)} %get-tuple-element.108), channel_id=1, source_target_pairs={{0,1},{1,0},{2,3},{3,2},{4,5},{5,4},{6,7},{7,6},{8,9},{9,8},{10,11... | collective-permute-start | bytes 233480 | tf_op jit(solution)/shard_map/ppermute | solution.py:129
  18.9 6.2 %collective-permute-start.10 = (bf16[304,128]{1,0:T(8,128)(2,1)S(1)}, bf16[304,128]{1,0:T(8,128)(2,1)S(1)}, u32[]{:S(2)}, u32[]{:S(2)}) collective-permute-start(bf16[304,128]{1,0:T(8,128)(2,1)S(1)} %get-tuple-element.109), channel_id=1, source_target_pairs={{0,17},{1,16},{2,19},{3,18},{4,21},{5,20},{6,23},{7,22},{8,25},{9,... | collective-permute-start | bytes 233480 | tf_op jit(solution)/shard_map/ppermute | solution.py:129
  20.3 5.9 %collective-permute-start.11 = (bf16[304,128]{1,0:T(8,128)(2,1)S(1)}, bf16[304,128]{1,0:T(8,128)(2,1)S(1)}, u32[]{:S(2)}, u32[]{:S(2)}) collective-permute-start(bf16[304,128]{1,0:T(8,128)(2,1)S(1)} %get-tuple-element.110), channel_id=1, source_target_pairs={{0,16},{1,17},{2,18},{3,19},{4,20},{5,21},{6,22},{7,23},{8,24},{9,... | collective-permute-start | bytes 233480 | tf_op jit(solution)/shard_map/ppermute | solution.py:129
  26.2 4.9 %collective-permute-start.12 = (bf16[304,128]{1,0:T(8,128)(2,1)S(1)}, bf16[304,128]{1,0:T(8,128)(2,1)S(1)}, u32[]{:S(2)}, u32[]{:S(2)}) collective-permute-start(bf16[304,128]{1,0:T(8,128)(2,1)S(1)} %shard_map.164.own), channel_id=1, source_target_pairs={{0,2},{1,3},{2,0},{3,1},{4,6},{5,7},{6,4},{7,5},{8,12},{9,13},{10,... | collective-permute-start | bytes 233480 | tf_op jit(solution)/shard_map/ppermute | solution.py:129
  26.2 5.9 %collective-permute-start.4 = (bf16[256,128]{1,0:T(8,128)(2,1)S(1)}, bf16[256,128]{1,0:T(8,128)(2,1)S(1)}, u32[]{:S(2)}, u32[]{:S(2)}) collective-permute-start(bf16[256,128]{1,0:T(8,128)(2,1)S(1)} %get-tuple-element.96), channel_id=1, source_target_pairs={{0,4},{1,5},{2,6},{3,7},{4,0},{5,1},{6,2},{7,3},{8,16},{9,17},{10,... | collective-permute-start | bytes 196616 | tf_op jit(solution)/shard_map/ppermute | solution.py:129
  29.6 2.5 %collective-permute-start.5 = (bf16[256,128]{1,0:T(8,128)(2,1)S(1)}, bf16[256,128]{1,0:T(8,128)(2,1)S(1)}, u32[]{:S(2)}, u32[]{:S(2)}) collective-permute-start(bf16[256,128]{1,0:T(8,128)(2,1)S(1)} %get-tuple-element.97), channel_id=1, source_target_pairs={{0,8},{1,9},{2,10},{3,11},{4,12},{5,13},{6,14},{7,15},{8,0},{9,1},... | collective-permute-start | bytes 196616 | tf_op jit(solution)/shard_map/ppermute | solution.py:129
  31.1 5.8 %collective-permute-start.13 = (bf16[304,128]{1,0:T(8,128)(2,1)S(1)}, bf16[304,128]{1,0:T(8,128)(2,1)S(1)}, u32[]{:S(2)}, u32[]{:S(2)}) collective-permute-start(bf16[304,128]{1,0:T(8,128)(2,1)S(1)} %shard_map.165.own), channel_id=1, source_target_pairs={{0,4},{1,5},{2,6},{3,7},{4,0},{5,1},{6,2},{7,3},{8,10},{9,11},{10,... | collective-permute-start | bytes 233480 | tf_op jit(solution)/shard_map/ppermute | solution.py:129
  32.3 8.2 %collective-permute-start.7 = (bf16[64,128]{1,0:T(8,128)(2,1)S(1)}, bf16[64,128]{1,0:T(8,128)(2,1)S(1)}, u32[]{:S(2)}, u32[]{:S(2)}) collective-permute-start(bf16[64,128]{1,0:T(8,128)(2,1)S(1)} %shard_map.160), channel_id=1, source_target_pairs={{0,1},{1,0},{2,3},{3,2},{4,5},{5,4},{6,7},{7,6},{8,9},{9,8},{10,11... | collective-permute-start | bytes 49160 | tf_op jit(solution)/shard_map/ppermute | solution.py:129
  34.3 6.4 %collective-permute-start.6 = (bf16[64,128]{1,0:T(8,128)(2,1)S(1)}, bf16[64,128]{1,0:T(8,128)(2,1)S(1)}, u32[]{:S(2)}, u32[]{:S(2)}) collective-permute-start(bf16[64,128]{1,0:T(8,128)(2,1)S(1)} %shard_map.160), channel_id=1, source_target_pairs={{0,7},{1,2},{2,1},{3,4},{4,3},{5,6},{6,5},{7,0},{8,15},{9,10},{10,... | collective-permute-start | bytes 49160 | tf_op jit(solution)/shard_map/ppermute | solution.py:129
  37.0 5.4 %collective-permute-start.16 = (bf16[304,128]{1,0:T(8,128)(2,1)S(1)}, bf16[304,128]{1,0:T(8,128)(2,1)S(1)}, u32[]{:S(2)}, u32[]{:S(2)}) collective-permute-start(bf16[304,128]{1,0:T(8,128)(2,1)S(1)} %shard_map.166.refs_0_), channel_id=1, source_target_pairs={{0,17},{1,16},{2,19},{3,18},{4,21},{5,20},{6,23},{7,22},{8,25},{9,... | collective-permute-start | bytes 233480 | tf_op jit(solution)/shard_map/ppermute | solution.py:129
  38.2 5.0 %collective-permute-start.15 = (bf16[304,128]{1,0:T(8,128)(2,1)S(1)}, bf16[304,128]{1,0:T(8,128)(2,1)S(1)}, u32[]{:S(2)}, u32[]{:S(2)}) collective-permute-start(bf16[304,128]{1,0:T(8,128)(2,1)S(1)} %shard_map.166.refs_0_), channel_id=1, source_target_pairs={{0,1},{1,0},{2,3},{3,2},{4,5},{5,4},{6,7},{7,6},{8,9},{9,8},{10,11... | collective-permute-start | bytes 233480 | tf_op jit(solution)/shard_map/ppermute | solution.py:129
  39.7 4.4 %collective-permute-start.14 = (bf16[304,128]{1,0:T(8,128)(2,1)S(1)}, bf16[304,128]{1,0:T(8,128)(2,1)S(1)}, u32[]{:S(2)}, u32[]{:S(2)}) collective-permute-start(bf16[304,128]{1,0:T(8,128)(2,1)S(1)} %shard_map.166.refs_0_), channel_id=1, source_target_pairs={{0,16},{1,17},{2,18},{3,19},{4,20},{5,21},{6,22},{7,23},{8,24},{9,... | collective-permute-start | bytes 233480 | tf_op jit(solution)/shard_map/ppermute | solution.py:129
  43.2 2.2 %collective-permute-start.17 = (bf16[3,304,128]{2,1,0:T(8,128)(2,1)S(1)}, bf16[3,304,128]{2,1,0:T(8,128)(2,1)S(1)}, u32[]{:S(2)}, u32[]{:S(2)}) collective-permute-start(bf16[3,304,128]{2,1,0:T(8,128)(2,1)S(1)} %shard_map.167.early), channel_id=1, source_target_pairs={{0,8},{1,9},{2,10},{3,11},{4,12},{5,13},{6,14},{7,15},{8,0},{9,1},... | collective-permute-start | bytes 700424 | tf_op jit(solution)/shard_map/ppermute | solution.py:129
  44.1 1.3 %collective-permute-start.18 = (bf16[304,128]{1,0:T(8,128)(2,1)S(1)}, bf16[304,128]{1,0:T(8,128)(2,1)S(1)}, u32[]{:S(2)}, u32[]{:S(2)}) collective-permute-start(bf16[304,128]{1,0:T(8,128)(2,1)S(1)} %collective-permute-done.14.late), channel_id=1, source_target_pairs={{0,8},{1,9},{2,10},{3,11},{4,12},{5,13},{6,14},{7,15},{8,0},{9,1},... | collective-permute-start | bytes 233480 | tf_op jit(solution)/shard_map/ppermute | solution.py:129
